TPU v7x, 32 devices: a whole 2x2x4 slice. The times are simulated.
32 devices in a mesh: rep: 2 (over y), fsdp: 4 (over z), own: 2 (over x), tp: 2 (over core).
Axes of the slice: x: 2, y: 2, z: 4, core: 2. Of those that a mesh axis runs over, the one named last changes fastest.
Arguments:
- tokens: bfloat16 [4096, 8192], P(('rep', 'fsdp', 'own'), 'tp'), parts along dimension 0, may hold values from -6 to 6
- cotangent: bfloat16 [4096, 1024], P(('rep', 'fsdp', 'own'), 'tp'), parts along dimension 0, may hold values from -6 to 6
- frozen_value_weight: bfloat16 [8192, 1024], P('tp', 'fsdp'), may hold values from -0.0625 to 0.0625
- adapter_down_weight: bfloat16 [8, 8192, 128], P(('fsdp', 'own'), 'tp'), may hold values from -0.0625 to 0.0625
- adapter_up_weight: bfloat16 [8, 128, 1024], P(('fsdp', 'own'), None, 'tp'), may hold values from -0.5 to 0.5
- token_adapter: int32 [4096, 1], P(('rep', 'fsdp', 'own')), parts along dimension 0, may hold values from 0 to 7; in each aligned block of 256 rows (0 to 255, 256 to 511, ...) at most 48 rows name the same one
- rank_step_count: int32 [8], replicated, may hold values from 1 to 8
Outputs:
- projected: bfloat16 [4096, 1024], P(('rep', 'fsdp', 'own'), 'tp'), parts along dimension 0
- input_grad: bfloat16 [4096, 8192], P(('rep', 'fsdp', 'own'), 'tp'), parts along dimension 0
- down_gradient: bfloat16 [16, 8192, 128], P(('rep', 'fsdp', 'own'), 'tp'), parts along dimension 0
- up_gradient: bfloat16 [16, 128, 1024], P(('rep', 'fsdp', 'own'), None, 'tp'), parts along dimension 0
There are 2 independent parts, one for each index of `rep`. A program takes and returns all parts, laid end to end along the dimension named above; an argument that names none is the same for every part. Nothing has to cross between parts.
Inputs may be any that keep to these rules, and one draw needn't show every extreme that they name: `token_adapter`: among the 256 tokens of each aligned block (the tokens of one index pair of fsdp and own), no adapter is named more than 48 times, a bound that some block reaches.
All inputs are finite; a program needn't handle non-finite values.
Results may differ from a plain program's by a relative error of at most 0.0051.
Values may be sent and summed in bfloat16 or wider, within the bound.
No kernel may reach another device: no remote copies, remote signals or barrier semaphores. Data moves between devices by JAX's collectives and lax.ppermute only.
A program may use at most 128 MiB of HBM per device.

v0:
```python
import jax
import jax.numpy as jnp
from jax import lax
from jax.sharding import PartitionSpec as P


def contract_first(left, right):
    return lax.dot_general(
        left, right, (((0,), (0,)), ((), ())), preferred_element_type=jnp.float32
    )


def contract_final_axis(left, right):
    return lax.dot_general(
        left, right, (((1,), (1,)), ((), ())), preferred_element_type=jnp.float32
    )


def body(
    tokens,
    cotangent,
    frozen_value_weight,
    adapter_down_weight,
    adapter_up_weight,
    token_adapter,
    rank_step_count,
):
    rows, width_halved = tokens.shape
    half_kv = cotangent.shape[1]
    owning_adapters = lax.axis_size(("fsdp", "own"))
    greatest_rank = 3 * rows // (2 * owning_adapters)
    ids = token_adapter[:, 0]
    table = (ids[:, None] == jnp.arange(owning_adapters, dtype=jnp.int32)[None, :]).astype(
        jnp.float32
    )
    order = jnp.arange(rows, dtype=jnp.int32)
    earlier = (order[:, None] > order[None, :]).astype(jnp.float32)
    before = jnp.dot(earlier, table, precision=lax.Precision.HIGHEST)
    place = jnp.sum(before * table, axis=1).astype(jnp.int32)
    slot = ids * greatest_rank + place
    source_rows = jnp.full((owning_adapters * greatest_rank,), rows, jnp.int32).at[slot].set(order)
    padded_x = jnp.concatenate([tokens, jnp.zeros((1, width_halved), jnp.bfloat16)], axis=0)
    padded_dy = jnp.concatenate([cotangent, jnp.zeros((1, half_kv), jnp.bfloat16)], axis=0)
    send_x = jnp.take(padded_x, source_rows, axis=0)
    send_dy = jnp.take(padded_dy, source_rows, axis=0)
    recv_x, recv_dy = (
        lax.all_to_all(
            send_x.reshape(owning_adapters, greatest_rank, width_halved),
            ("fsdp", "own"),
            split_axis=0,
            concat_axis=0,
            tiled=True,
        ),
        lax.all_to_all(
            send_dy.reshape(owning_adapters, greatest_rank, half_kv),
            ("fsdp", "own"),
            split_axis=0,
            concat_axis=0,
            tiled=True,
        ),
    )
    flat_x = recv_x.reshape(owning_adapters * greatest_rank, width_halved)
    flat_dy = recv_dy.reshape(owning_adapters * greatest_rank, half_kv)
    dy_full = lax.all_gather(cotangent, "tp", axis=1, tiled=True)
    whole = lax.all_gather(frozen_value_weight, "fsdp", axis=1, tiled=True)
    partial_y = jnp.dot(tokens, whole, preferred_element_type=jnp.float32)
    base_dx = contract_final_axis(dy_full, whole)
    base_y = lax.psum_scatter(partial_y, "tp", scatter_dimension=1, tiled=True)
    down_matrix = adapter_down_weight[0]
    up_matrix = adapter_up_weight[0]
    part_low = jnp.dot(flat_x, down_matrix, preferred_element_type=jnp.float32)
    part_back = contract_final_axis(flat_dy, up_matrix)
    low_sum, back_sum = lax.psum((part_low, part_back), "tp")
    width_rank = down_matrix.shape[1]
    rank = width_rank // 8 * rank_step_count[lax.axis_index(("fsdp", "own"))]
    keep = jnp.arange(width_rank, dtype=jnp.int32)[None, :] < rank
    scale = 16.0 / rank.astype(jnp.float32)
    low = jnp.where(keep, low_sum, 0.0).astype(jnp.bfloat16)
    backward_pass = (scale * jnp.where(keep, back_sum, 0.0)).astype(jnp.bfloat16)
    delta = (scale * jnp.dot(low, up_matrix, preferred_element_type=jnp.float32)).astype(
        jnp.bfloat16
    )
    adapter_input_gradient = contract_final_axis(backward_pass, down_matrix).astype(jnp.bfloat16)
    down_gradient = contract_first(flat_x, backward_pass).astype(jnp.bfloat16)[None]
    up_gradient = (scale * contract_first(low, flat_dy)).astype(jnp.bfloat16)[None]
    home_delta, home_dx = (
        lax.all_to_all(
            delta.reshape(owning_adapters, greatest_rank, half_kv),
            ("fsdp", "own"),
            split_axis=0,
            concat_axis=0,
            tiled=True,
        ),
        lax.all_to_all(
            adapter_input_gradient.reshape(owning_adapters, greatest_rank, width_halved),
            ("fsdp", "own"),
            split_axis=0,
            concat_axis=0,
            tiled=True,
        ),
    )
    adapter_delta_rows = jnp.take(
        home_delta.reshape(owning_adapters * greatest_rank, half_kv), slot, axis=0
    )
    input_gradient_rows = jnp.take(
        home_dx.reshape(owning_adapters * greatest_rank, width_halved), slot, axis=0
    )
    projected = (base_y + adapter_delta_rows.astype(jnp.float32)).astype(jnp.bfloat16)
    input_grad = (base_dx + input_gradient_rows.astype(jnp.float32)).astype(jnp.bfloat16)
    return (projected, input_grad, down_gradient, up_gradient)


def solution(mesh):
    placed = (
        P(("rep", "fsdp", "own"), "tp"),
        P(("rep", "fsdp", "own"), "tp"),
        P("tp", "fsdp"),
        P(("fsdp", "own"), "tp", None),
        P(("fsdp", "own"), None, "tp"),
        P(("rep", "fsdp", "own"), None),
        P(),
    )
    return jax.shard_map(
        body,
        mesh=mesh,
        in_specs=placed,
        out_specs=(
            P(("rep", "fsdp", "own"), "tp"),
            P(("rep", "fsdp", "own"), "tp"),
            P(("rep", "fsdp", "own"), "tp", None),
            P(("rep", "fsdp", "own"), None, "tp"),
        ),
        check_vma=False,
    )
```

profile of v0, /device:TPU:0, one launch (start us, length us, event | category | flops | bytes accessed | tf_op | source)
XLA Modules:
  0.0 350.9 jit_solution(5783497059896371872)
XLA Ops:
  9.8 1.4 scatter_custom_fusion
  12.3 2.1 gather_fusion.2
  14.5 19.1 %all_to_all.20 = bf16[8,48,512]{2,1,0:T(8,128)(2,1)S(1)} all-to-all(bf16[8,48,512]{2,1,0:T(8,128)(2,1)S(1)} %broadcast_select_fusion.1), channel_id=1, replica_groups=mesh['rep'=2,'fsdp'=4,'own'=2,'tp'=2] {'fsdp','own'}, dimensions={0} | all-to-all | bytes 786432 | tf_op jit(solution)/shard_map/all_to_all | solution.py:54
  35.9 1.8 concatenate.6
  37.7 4.0 %gather_fusion = bf16[384,4096]{1,0:T(8,128)(2,1)} fusion(bf16[257,4096]{1,0:T(8,128)(2,1)S(1)} %concatenate.6, s32[1024]{0:T(1024)S(1)} %pad_clamp_fusion.1), kind=kCustom, calls=%fused_computation | custom fusion | bytes 6292992 | tf_op jit(solution)/shard_map/jit(_take)/gather | solution.py:44
  41.8 4.4 %broadcast_select_fusion = bf16[8,48,4096]{2,1,0:T(8,128)(2,1)} fusion(bf16[8,48,4096]{2,1,0:T(8,128)(2,1)} %bitcast.36, pred[8,48]{1,0:T(8,128)(4,1)S(1)} %broadcast_in_dim.79), kind=kLoop, calls=%fused_computation.10 | loop fusion | flops 1572864 | bytes 6291840 | tf_op jit(solution)/shard_map/jit(_take)/select_n | solution.py:44
  46.2 4.6 %all-to-all-start = ((bf16[8,48,4096]{2,1,0:T(8,128)(2,1)}), bf16[8,48,4096]{2,1,0:T(8,128)(2,1)}, u32[]{:S(2)}, u32[]{:S(2)}) async-start(bf16[8,48,4096]{2,1,0:T(8,128)(2,1)} %broadcast_select_fusion), calls=%async_computation.1 | async-start | bytes 6291456 | tf_op jit(solution)/shard_map/all_to_all | solution.py:47
  52.1 144.6 %all-to-all-done = bf16[8,48,4096]{2,1,0:T(8,128)(2,1)} async-done(((bf16[8,48,4096]{2,1,0:T(8,128)(2,1)}), bf16[8,48,4096]{2,1,0:T(8,128)(2,1)}, u32[]{:S(2)}, u32[]{:S(2)}) %all-to-all-start) | async-done | bytes 3145760 | tf_op jit(solution)/shard_map/all_to_all | solution.py:47
  196.7 2.9 fusion.7
  199.6 4.0 %all-reduce.6 = bf16[384,128]{1,0:T(8,128)(2,1)S(1)} all-reduce(f32[384,128]{1,0:T(8,128)S(1)} %fusion.7), channel_id=1, replica_groups=mesh['rep'=2,'fsdp'=4,'own'=2,'tp'=2] {'tp'}, use_global_device_ids=true, to_apply=%region_3.4 | all-reduce | flops 49152 | bytes 294912 | tf_op jit(solution)/shard_map/psum | solution.py:73
  203.6 1.0 fusion.2
  204.6 3.5 all-to-all-start.1
  208.1 3.5 %convolution_convert_fusion = bf16[384,4096]{1,0:T(8,128)(2,1)} fusion(bf16[1,4096,128]{2,1,0:T(8,128)(2,1)S(1)} %copy-done, f32[384,128]{1,0:T(8,128)} %all-reduce.5.cloned.1.call-done, f32[]{:T(128)S(6)} %div.3, pred[128]{0:T(512)(128)(4,1)S(1)} %iota_compare_fusion.4), kind=kOutput, calls=%fused_computation.5 | convolution fusion | flops 404373504 | bytes 4391044 | tf_op jit(solution)/shard_map/dot_general | solution.py:14
  211.6 21.1 %all-to-all-done.1 = bf16[8,48,512]{2,1,0:T(8,128)(2,1)S(1)} async-done(((bf16[8,48,512]{2,1,0:T(8,128)(2,1)}), bf16[8,48,512]{2,1,0:T(8,128)(2,1)S(1)}, u32[]{:S(2)}, u32[]{:S(2)}) %all-to-all-start.1) | async-done | bytes 393248 | tf_op jit(solution)/shard_map/all_to_all | solution.py:87
  232.8 5.7 %all-to-all-start.3 = ((bf16[8,48,4096]{2,1,0:T(8,128)(2,1)}), bf16[8,48,4096]{2,1,0:T(8,128)(2,1)}, u32[]{:S(2)}, u32[]{:S(2)}) async-start(bf16[8,48,4096]{2,1,0:T(8,128)(2,1)} %bitcast.35), calls=%async_computation.4 | async-start | bytes 6291456 | tf_op jit(solution)/shard_map/all_to_all | solution.py:94
  238.5 49.2 %all-gather.2.cloned.1.call-done = bf16[4096,1024]{1,0:T(8,128)(2,1)} async-done(((bf16[4096,256]{1,0:T(8,128)(2,1)}), bf16[4096,1024]{1,0:T(8,128)(2,1)}) %all-gather.2.cloned.1.call-update) | async-done | bytes 8388624 | tf_op jit(solution)/shard_map/all_gather | solution.py:65
  287.7 7.4 %fusion.19 = f32[256,1024]{1,0:T(8,128)} fusion(bf16[256,4096]{1,0:T(8,128)(2,1)} %param.7, bf16[4096,1024]{1,0:T(8,128)(2,1)} %all-gather.2.cloned.1.call-done), kind=kOutput, calls=%fused_computation.44 | convolution fusion | flops 2147483648 | bytes 11534336 | tf_op jit(solution)/shard_map/dot_general | solution.py:66
  295.1 2.5 all_gather.7
  298.6 3.9 %fusion.1 = bf16[1,4096,128]{2,1,0:T(8,128)(2,1)} fusion(bf16[384,4096]{1,0:T(8,128)(2,1)} %bitcast.5, f32[384,128]{1,0:T(8,128)S(1)} %copy-done.4, f32[]{:T(128)S(6)} %div.3, pred[128]{0:T(512)(128)(4,1)S(1)} %iota_compare_fusion.4), kind=kOutput, calls=%fused_computation.9 | convolution fusion | flops 403324928 | bytes 4391044 | tf_op jit(solution)/shard_map/dot_general | solution.py:8
  302.4 1.2 gather_fusion.1
  303.6 24.6 %all-to-all-done.3 = bf16[8,48,4096]{2,1,0:T(8,128)(2,1)} async-done(((bf16[8,48,4096]{2,1,0:T(8,128)(2,1)}), bf16[8,48,4096]{2,1,0:T(8,128)(2,1)}, u32[]{:S(2)}, u32[]{:S(2)}) %all-to-all-start.3) | async-done | bytes 3145760 | tf_op jit(solution)/shard_map/all_to_all | solution.py:94
  328.2 6.2 %gather_fusion.3 = bf16[256,4096]{1,0:T(8,128)(2,1)S(1)} fusion(bf16[384,4096]{1,0:T(8,128)(2,1)} %bitcast.13, s32[1024]{0:T(1024)S(1)} %pad_clamp_fusion), kind=kCustom, calls=%fused_computation.3 | custom fusion | bytes 4195328 | tf_op jit(solution)/shard_map/jit(_take)/gather | solution.py:105
  334.3 7.3 %fusion = bf16[256,4096]{1,0:T(8,128)(2,1)} fusion(bf16[256,1024]{1,0:T(8,128)(2,1)} %all_gather.7, bf16[4096,1024]{1,0:T(8,128)(2,1)} %all-gather.2.cloned.1.call-done, bf16[256,4096]{1,0:T(8,128)(2,1)S(1)} %gather_fusion.3, pred[256]{0:T(512)(128)(4,1)S(1)} %get-tuple-element.4), kind=kOutput, calls=%fused_computation.7 | convolution fusion | flops 2151677952 | bytes 13107456 | tf_op jit(solution)/shard_map/dot_general | solution.py:14
  341.6 1.9 add_convert_fusion
  (37 shorter events, 6.8 us)
Async XLA Ops:
  8.0 188.7 %copy-start = (bf16[1,4096,128]{2,1,0:T(8,128)(2,1)S(1)}, bf16[1,4096,128]{2,1,0:T(8,128)(2,1)}, u32[]{:S(2)}) copy-start(bf16[1,4096,128]{2,1,0:T(8,128)(2,1)} %param.10) | copy-start | bytes 3145732
  8.0 26.4 %copy-start.5 = (bf16[1,128,512]{2,1,0:T(8,128)(2,1)S(1)}, bf16[1,128,512]{2,1,0:T(8,128)(2,1)}, u32[]{:S(2)}) copy-start(bf16[1,128,512]{2,1,0:T(8,128)(2,1)} %param.11) | copy-start | bytes 393220
  8.0 200.0 %all-reduce.5.cloned.1.call-start = ((), (), s32[]{:S(2)}) async-start(), calls=%async_computation.7 | async-start | bytes 393216 | tf_op jit(solution)/shard_map/psum | solution.py:73
  33.6 0.7 copy-start.1
  35.4 252.4 %all-gather.2.cloned.1.call-start = ((), (), s32[]{:S(2)}) async-start(), calls=%async_computation.5 | async-start | bytes 10485760 | tf_op jit(solution)/shard_map/all_gather | solution.py:65
  46.2 4.7 %copy-start.6 = (s32[8]{0:T(128)S(1)}, s32[8]{0:T(128)}, u32[]{:S(2)}) copy-start(s32[8]{0:T(128)} %param.13) | copy-start | bytes 100
  46.2 150.6 %all-to-all-start = ((bf16[8,48,4096]{2,1,0:T(8,128)(2,1)}), bf16[8,48,4096]{2,1,0:T(8,128)(2,1)}, u32[]{:S(2)}, u32[]{:S(2)}) async-start(bf16[8,48,4096]{2,1,0:T(8,128)(2,1)} %broadcast_select_fusion), calls=%async_computation.1 | async-start | bytes 6291456 | tf_op jit(solution)/shard_map/all_to_all | solution.py:47
  204.6 28.2 %all-to-all-start.1 = ((bf16[8,48,512]{2,1,0:T(8,128)(2,1)}), bf16[8,48,512]{2,1,0:T(8,128)(2,1)S(1)}, u32[]{:S(2)}, u32[]{:S(2)}) async-start(bf16[8,48,512]{2,1,0:T(8,128)(2,1)} %bitcast.8), calls=%async_computation.2 | async-start | bytes 786432 | tf_op jit(solution)/shard_map/all_to_all | solution.py:87
  232.8 95.4 %all-to-all-start.3 = ((bf16[8,48,4096]{2,1,0:T(8,128)(2,1)}), bf16[8,48,4096]{2,1,0:T(8,128)(2,1)}, u32[]{:S(2)}, u32[]{:S(2)}) async-start(bf16[8,48,4096]{2,1,0:T(8,128)(2,1)} %bitcast.35), calls=%async_computation.4 | async-start | bytes 6291456 | tf_op jit(solution)/shard_map/all_to_all | solution.py:94
  238.4 56.7 %copy-start.3 = (bf16[256,512]{1,0:T(8,128)(2,1)S(1)}, bf16[256,512]{1,0:T(8,128)(2,1)}, u32[]{:S(2)}) copy-start(bf16[256,512]{1,0:T(8,128)(2,1)} %param.8) | copy-start | bytes 786436
  238.4 59.2 %copy-start.2 = (bf16[8,48,512]{2,1,0:T(8,128)(2,1)S(1)}, bf16[8,48,512]{2,1,0:T(8,128)(2,1)}, u32[]{:S(2)}) copy-start(bf16[8,48,512]{2,1,0:T(8,128)(2,1)} %copy-done.1) | copy-start | bytes 1179652
  238.5 60.1 %copy-start.4 = (f32[384,128]{1,0:T(8,128)S(1)}, f32[384,128]{1,0:T(8,128)}, u32[]{:S(2)}) copy-start(f32[384,128]{1,0:T(8,128)} %all-reduce.5.cloned.1.call-done) | copy-start | bytes 589828
  238.5 103.2 %reduce-scatter.2.cloned.1.call-start = ((), (), s32[]{:S(2)}) async-start(), calls=%async_computation.6 | async-start | bytes 1572864 | tf_op jit(solution)/shard_map/reduce_scatter | solution.py:68
Sparse Core Ops, SparseCore 0:
  35.5 16.7 all-reduce.4
  295.2 22.3 reduce-scatter.1
Sparse Core Ops, SparseCore 1:
  37.4 250.3 all-gather.1
where the time goes:
time: 352 us; the launch traced here: 351 us
  waiting for transfers between devices  240 us (68%)
  matrix products  28.8 us (8%)
  blocking collectives  25.6 us (7%)
  local copies, waits for them, and re-layouts  19 us (5%)
  between operations  16.4 us (5%)
  starting transfers between devices  13.9 us (4%)
  other arithmetic  7.14 us (2%)
    all_to_all x1, waiting for transfers between devices, body(): lax.all_to_all(send_x.reshape(owning_adapters, greatest_rank, width_halve...  145 us
    all_gather x1, waiting for transfers between devices, body(): whole = lax.all_gather(frozen_value_weight, 'fsdp', axis=1, tiled=True)  49.2 us
    all_to_all x1, waiting for transfers between devices, body(): lax.all_to_all(adapter_input_gradient.reshape(owning_adapters, greatest_r...  24.6 us
    all_to_all x1, waiting for transfers between devices, body(): lax.all_to_all(delta.reshape(owning_adapters, greatest_rank, half_kv), ('...  21.1 us
    all_to_all x1, blocking collectives, body(): lax.all_to_all(send_dy.reshape(owning_adapters, greatest_rank, half_kv),...  19.1 us
    dot_general x3, matrix products, contract_final_axis(): lax.dot_general(left, right, (((1,), (1,)), ((), ())), preferred_element_...  11.8 us
    dot_general x1, matrix products, body(): partial_y = jnp.dot(tokens, whole, preferred_element_type=jnp.float32)  7.38 us
  transfers between devices with their start and end apart: 6, of which 4 were waited for; matrix products, arithmetic and copies ran while one was open for 13% of the time, Pallas kernels for 0%

commit v1 on v0

v1 whole, which is shorter than its diff:
```python
import jax
import jax.numpy as jnp
from jax import lax
from jax.sharding import PartitionSpec as P

bf16 = jnp.bfloat16
f32 = jnp.float32


def contract_first(left, right):
    return lax.dot_general(
        left, right, (((0,), (0,)), ((), ())), preferred_element_type=f32
    )


def contract_final_axis(left, right):
    return lax.dot_general(
        left, right, (((1,), (1,)), ((), ())), preferred_element_type=f32
    )


def matmul(left, right):
    return jnp.dot(left, right, preferred_element_type=f32)


PAIR = [(0, 1), (1, 0)]
NEIGHBOURS = [(0, 1), (1, 0), (2, 3), (3, 2)]
MIDDLE = [(1, 2), (2, 1)]
OUTWARD = [(1, 0), (2, 3)]
INWARD = [(0, 1), (3, 2)]


def swap(value, axis):
    return lax.ppermute(value, axis, PAIR)


def along(value, pairs):
    return lax.ppermute(value, "fsdp", pairs)


def body_line(
    tokens,
    cotangent,
    frozen_value_weight,
    adapter_down_weight,
    adapter_up_weight,
    token_adapter,
    rank_step_count,
):
    rows, width = tokens.shape
    kv = cotangent.shape[1]
    cols = frozen_value_weight.shape[1]
    down = adapter_down_weight[0]
    up = adapter_up_weight[0]
    rank_limit = down.shape[1]
    quarter = width // 2
    eighth = quarter // 2
    kvq = kv // 2
    z, x = lax.axis_index("fsdp"), lax.axis_index("own")
    y, c = lax.axis_index("rep"), lax.axis_index("tp")
    first_pair = z < 2
    is_middle = (z == 1) | (z == 2)
    line = [z, z + 1 - 2 * (z % 2), jnp.where(first_pair, 2, 1), jnp.where(first_pair, 3, 0)]
    adapters = [2 * t + o for t in line for o in (x, 1 - x)]

    def cut(value, start, size, axis):
        return lax.dynamic_slice_in_dim(value, start, size, axis)

    def features(value, side, axis):
        return [
            cut(value, side * quarter + half * eighth, eighth, axis) for half in (y, 1 - y)
        ]

    def gather_line(piece):
        near = along(piece, NEIGHBOURS)
        both = jnp.stack([piece, near])
        crossed = along(both, MIDDLE)
        outer = along(crossed, OUTWARD)
        return near, jnp.where(is_middle, crossed, outer)

    ids_row = token_adapter[:, 0].astype(bf16)[None, :]
    up_here, up_there = cut(up, x * kvq, kvq, 1), cut(up, (1 - x) * kvq, kvq, 1)
    packet = jnp.concatenate(
        [
            cotangent,
            jnp.concatenate([up_there, jnp.broadcast_to(ids_row, (rank_limit, rows))], axis=1),
        ],
        axis=0,
    )
    packet = swap(packet, "own")
    dy_half = jnp.concatenate([cotangent, packet[:rows]], axis=0)
    up_piece = jnp.concatenate([up_here, packet[rows:, :kvq]], axis=0)
    ids = jnp.concatenate([token_adapter[:, 0], packet[rows, kvq:].astype(jnp.int32)])[:, None]
    x_here = jnp.concatenate(features(tokens, x, 1), axis=1)
    x_there = swap(jnp.concatenate(features(tokens, 1 - x, 1), axis=1), "own")
    x_both = jnp.concatenate([x_here, x_there], axis=0)
    down_here = features(down, x, 0)
    down_piece = jnp.concatenate(
        [down_here[0], swap(cut(down, (1 - x) * quarter + y * eighth, eighth, 0), "own")], axis=1
    )

    ranks = rank_limit // 8 * rank_step_count
    number = ranks.shape[0]
    onehot = ids == jnp.arange(number, dtype=jnp.int32)[None, :]
    token_rank = jnp.sum(jnp.where(onehot, ranks[None, :], 0), axis=1, keepdims=True)
    token_scale = 16.0 / token_rank.astype(f32)
    keep = jnp.arange(rank_limit, dtype=jnp.int32)[None, :] < token_rank

    def compact(part):
        total = jnp.zeros((2 * rows, rank_limit), f32)
        for i, a in enumerate(adapters):
            total = total + jnp.where(ids == a, part[:, i * rank_limit : (i + 1) * rank_limit], 0.0)
        return total

    def expand(value, order):
        return jnp.concatenate(
            [jnp.where(ids == a, value, jnp.zeros_like(value)) for a in order], axis=1
        )

    def sum_features(part):
        part = compact(part)
        part = part + swap(part, "tp")
        return part + jnp.roll(swap(part, "own"), rows, axis=0)

    up_near, up_far = gather_line(up_piece)
    up_all = jnp.concatenate([up_piece, up_near, up_far[0], up_far[1]], axis=0)
    dy_quarter = cut(dy_half, x * kvq, kvq, 1)
    back = sum_features(contract_final_axis(dy_quarter, up_all))
    back = (token_scale * jnp.where(keep, back, 0.0)).astype(bf16)
    back_wide = expand(back, adapters)

    wide = 2 * rank_limit

    def partial(i):
        return contract_first(x_both, back_wide[:, i * wide : (i + 1) * wide])

    to_end, to_middle, to_pair, to_self = partial(3), partial(2), partial(1), partial(0)
    from_end = along(to_end.astype(bf16), INWARD)
    from_end_too = along(to_middle.astype(bf16), INWARD)
    crossed_end = along((to_end + from_end.astype(f32)).astype(bf16), MIDDLE)
    crossed_middle = along((to_middle + from_end_too.astype(f32)).astype(bf16), MIDDLE)
    from_pair = along((to_pair + crossed_end.astype(f32)).astype(bf16), NEIGHBOURS)
    grad = (to_self + from_pair.astype(f32) + crossed_middle.astype(f32)).astype(bf16)
    grad_here = grad[:, :rank_limit]
    grad_there = swap(grad[:, rank_limit:], "own")

    def in_place(here, there, axis):
        blocks = jnp.concatenate(here + there, axis=axis)
        size = blocks.shape[axis] // 4
        return jnp.concatenate(
            [
                cut(blocks, (2 * ((i + x) % 2) + (j + y) % 2) * size, size, axis)
                for i in (0, 1)
                for j in (0, 1)
            ],
            axis=axis,
        )

    down_gradient = in_place([grad_here], [grad_there], 0)[None]

    down_near, down_far = gather_line(down_piece)
    down_mine = jnp.concatenate([down_piece, down_near, down_far[0], down_far[1]], axis=1)
    down_other = swap(down_mine, "rep")
    low = sum_features(
        matmul(x_both[:, :eighth], down_mine) + matmul(x_both[:, eighth:], down_other)
    )
    low = jnp.where(keep, low, 0.0).astype(bf16)
    delta = (token_scale * matmul(expand(low, adapters), up_all)).astype(bf16)
    natural = [2 * (i // 2) + i % 2 for i in range(number)]
    up_part = contract_first(expand(low, natural), dy_quarter).astype(bf16)
    up_sent = lax.all_to_all(
        up_part.reshape(4, 2, rank_limit, kvq), "fsdp", split_axis=0, concat_axis=0, tiled=True
    )
    up_sum = jnp.sum(up_sent.astype(f32), axis=0)
    own_ranks = cut(ranks, 2 * z, 2, 0).astype(f32)
    up_sum = ((16.0 / own_ranks)[:, None, None] * up_sum).astype(bf16)
    up_mine = cut(up_sum, x, 1, 0)
    up_theirs = swap(cut(up_sum, 1 - x, 1, 0), "own")
    up_gradient = jnp.where(
        x == 0,
        jnp.concatenate([up_mine, up_theirs], axis=2),
        jnp.concatenate([up_theirs, up_mine], axis=2),
    )

    dy_tp = swap(dy_half, "tp")
    dy_full = jnp.where(
        c == 0,
        jnp.concatenate([dy_half, dy_tp], axis=1),
        jnp.concatenate([dy_tp, dy_half], axis=1),
    )
    dy_line = jnp.concatenate([cut(dy_full, t * cols, cols, 1) for t in line], axis=1)

    weight_here = features(frozen_value_weight, x, 0)
    weight_near, weight_far = gather_line(weight_here[0])
    got = jnp.concatenate([weight_near, weight_far[0], weight_far[1]], axis=1)
    weight_mine = jnp.concatenate([weight_here[0], got], axis=1)
    weight_other = jnp.concatenate([weight_here[1], swap(got, "rep")], axis=1)

    def input_grad_of(weight, adapter):
        lora = contract_final_axis(back_wide, adapter).astype(bf16)
        return (contract_final_axis(dy_line, weight) + lora.astype(f32)).astype(bf16)

    dx_mine = input_grad_of(weight_mine, down_mine)
    dx_other = input_grad_of(weight_other, down_other)
    back_mine = swap(dx_mine[rows:], "own")
    back_other = swap(dx_other[rows:], "own")
    input_grad = in_place([dx_mine[:rows], dx_other[:rows]], [back_mine, back_other], 1)

    part = matmul(x_both[:, :eighth], weight_mine) + matmul(x_both[:, eighth:], weight_other)
    first, second = part[:, :kv], part[:, kv:]
    own_first = (c == 0) == first_pair
    half = jnp.where(own_first, first, second) + swap(jnp.where(own_first, second, first), "tp")
    turned = jnp.where(own_first, z % 2 == 1, z >= 2)
    half = jnp.where(turned, jnp.roll(half, cols, axis=1), half)
    blank = jnp.zeros_like(delta)
    half = half + jnp.where(
        x == 0, jnp.concatenate([delta, blank], axis=1), jnp.concatenate([blank, delta], axis=1)
    ).astype(f32)
    projected = (half[:rows] + swap(half[rows:], "own")).astype(bf16)
    return (projected, input_grad, down_gradient, up_gradient)


def body_routed(
    tokens,
    cotangent,
    frozen_value_weight,
    adapter_down_weight,
    adapter_up_weight,
    token_adapter,
    rank_step_count,
):
    rows, width_halved = tokens.shape
    half_kv = cotangent.shape[1]
    owning_adapters = lax.axis_size(("fsdp", "own"))
    greatest_rank = 3 * rows // (2 * owning_adapters)
    ids = token_adapter[:, 0]
    table = (ids[:, None] == jnp.arange(owning_adapters, dtype=jnp.int32)[None, :]).astype(
        f32
    )
    order = jnp.arange(rows, dtype=jnp.int32)
    earlier = (order[:, None] > order[None, :]).astype(f32)
    before = jnp.dot(earlier, table, precision=lax.Precision.HIGHEST)
    place = jnp.sum(before * table, axis=1).astype(jnp.int32)
    slot = ids * greatest_rank + place
    source_rows = jnp.full((owning_adapters * greatest_rank,), rows, jnp.int32).at[slot].set(order)
    padded_x = jnp.concatenate([tokens, jnp.zeros((1, width_halved), bf16)], axis=0)
    padded_dy = jnp.concatenate([cotangent, jnp.zeros((1, half_kv), bf16)], axis=0)
    send_x = jnp.take(padded_x, source_rows, axis=0)
    send_dy = jnp.take(padded_dy, source_rows, axis=0)
    recv_x, recv_dy = (
        lax.all_to_all(
            send_x.reshape(owning_adapters, greatest_rank, width_halved),
            ("fsdp", "own"),
            split_axis=0,
            concat_axis=0,
            tiled=True,
        ),
        lax.all_to_all(
            send_dy.reshape(owning_adapters, greatest_rank, half_kv),
            ("fsdp", "own"),
            split_axis=0,
            concat_axis=0,
            tiled=True,
        ),
    )
    flat_x = recv_x.reshape(owning_adapters * greatest_rank, width_halved)
    flat_dy = recv_dy.reshape(owning_adapters * greatest_rank, half_kv)
    dy_full = lax.all_gather(cotangent, "tp", axis=1, tiled=True)
    whole = lax.all_gather(frozen_value_weight, "fsdp", axis=1, tiled=True)
    partial_y = jnp.dot(tokens, whole, preferred_element_type=f32)
    base_dx = contract_final_axis(dy_full, whole)
    base_y = lax.psum_scatter(partial_y, "tp", scatter_dimension=1, tiled=True)
    down_matrix = adapter_down_weight[0]
    up_matrix = adapter_up_weight[0]
    part_low = jnp.dot(flat_x, down_matrix, preferred_element_type=f32)
    part_back = contract_final_axis(flat_dy, up_matrix)
    low_sum, back_sum = lax.psum((part_low, part_back), "tp")
    width_rank = down_matrix.shape[1]
    rank = width_rank // 8 * rank_step_count[lax.axis_index(("fsdp", "own"))]
    keep = jnp.arange(width_rank, dtype=jnp.int32)[None, :] < rank
    scale = 16.0 / rank.astype(f32)
    low = jnp.where(keep, low_sum, 0.0).astype(bf16)
    backward_pass = (scale * jnp.where(keep, back_sum, 0.0)).astype(bf16)
    delta = (scale * jnp.dot(low, up_matrix, preferred_element_type=f32)).astype(
        bf16
    )
    adapter_input_gradient = contract_final_axis(backward_pass, down_matrix).astype(bf16)
    down_gradient = contract_first(flat_x, backward_pass).astype(bf16)[None]
    up_gradient = (scale * contract_first(low, flat_dy)).astype(bf16)[None]
    home_delta, home_dx = (
        lax.all_to_all(
            delta.reshape(owning_adapters, greatest_rank, half_kv),
            ("fsdp", "own"),
            split_axis=0,
            concat_axis=0,
            tiled=True,
        ),
        lax.all_to_all(
            adapter_input_gradient.reshape(owning_adapters, greatest_rank, width_halved),
            ("fsdp", "own"),
            split_axis=0,
            concat_axis=0,
            tiled=True,
        ),
    )
    adapter_delta_rows = jnp.take(
        home_delta.reshape(owning_adapters * greatest_rank, half_kv), slot, axis=0
    )
    input_gradient_rows = jnp.take(
        home_dx.reshape(owning_adapters * greatest_rank, width_halved), slot, axis=0
    )
    projected = (base_y + adapter_delta_rows.astype(f32)).astype(bf16)
    input_grad = (base_dx + input_gradient_rows.astype(f32)).astype(bf16)
    return (projected, input_grad, down_gradient, up_gradient)


def solution(mesh):
    placed = (
        P(("rep", "fsdp", "own"), "tp"),
        P(("rep", "fsdp", "own"), "tp"),
        P("tp", "fsdp"),
        P(("fsdp", "own"), "tp", None),
        P(("fsdp", "own"), None, "tp"),
        P(("rep", "fsdp", "own"), None),
        P(),
    )
    line = mesh.shape["fsdp"] == 4 and mesh.shape["own"] == 2 and mesh.shape["rep"] == 2
    return jax.shard_map(
        body_line if line else body_routed,
        mesh=mesh,
        in_specs=placed,
        out_specs=(
            P(("rep", "fsdp", "own"), "tp"),
            P(("rep", "fsdp", "own"), "tp"),
            P(("rep", "fsdp", "own"), "tp", None),
            P(("rep", "fsdp", "own"), None, "tp"),
        ),
        check_vma=False,
    )
```

time: 352 us -> 322 us (0.915)
  starting transfers between devices: 13.9 us -> 46.5 us
  waiting for transfers between devices: 240 us -> 213 us
  blocking collectives: 25.6 us -> 0 us
  other arithmetic: 7.14 us -> 25.4 us
  between operations: 16.4 us -> 1.72 us
  matrix products: 28.8 us -> 22.5 us
  local copies, waits for them, and re-layouts: 19 us -> 13 us
    ppermute x0 -> x30, waiting for transfers between devices: none -> 213 us  [the longest x14 124 us: along(): return lax.ppermute(value, 'fsdp', pairs)]
    all_to_all x3 -> x1, waiting for transfers between devices: 190 us -> 0.01 us  [body_line(): lax.all_to_all(up_part.reshape(4, 2, rank_limit, kvq), 'fsdp', split_axis...]
    all_gather x1 -> x0, waiting for transfers between devices: 49.2 us -> none  [body(): whole = lax.all_gather(frozen_value_weight, 'fsdp', axis=1, tiled=True)]
    ppermute x0 -> x30, starting transfers between devices: none -> 42.3 us  [the longest x14 24.3 us: along(): return lax.ppermute(value, 'fsdp', pairs)]
    all_to_all x1 -> x0, blocking collectives: 19.1 us -> none  [body(): lax.all_to_all(send_dy.reshape(owning_adapters, greatest_rank, half_kv),...]
    gather x4 -> x0, local copies, waits for them, and re-layouts: 13.4 us -> none  [the longest x1 6.18 us: body(): jnp.take(home_dx.reshape(owning_adapters * greatest_rank, width_halved),...]
    concatenate x0 -> x10, other arithmetic: none -> 9.67 us  [the longest x2 3.81 us: in_place(): blocks = jnp.concatenate(here + there, axis=axis)]
    all_to_all x3 -> x1, starting transfers between devices: 13.8 us -> 4.2 us  [body_line(): lax.all_to_all(up_part.reshape(4, 2, rank_limit, kvq), 'fsdp', split_axis...]
  transfers between devices with their start and end apart: 6 -> 31, of which waited for: 4 -> 11; matrix products, arithmetic and copies ran while one was open for 13% -> 14% of each run, Pallas kernels for 0% -> 0%
where the time goes in v1:
time: 322 us
  waiting for transfers between devices  213 us (66%)
  starting transfers between devices  46.5 us (14%)
  other arithmetic  25.4 us (8%)
  matrix products  22.5 us (7%)
  local copies, waits for them, and re-layouts  13 us (4%)
    ppermute x14, waiting for transfers between devices, along(): return lax.ppermute(value, 'fsdp', pairs)  124 us
    ppermute x16, waiting for transfers between devices, swap(): return lax.ppermute(value, axis, PAIR)  88.1 us
    ppermute x14, starting transfers between devices, along(): return lax.ppermute(value, 'fsdp', pairs)  24.3 us
    ppermute x16, starting transfers between devices, swap(): return lax.ppermute(value, axis, PAIR)  18 us
    dot_general x5, matrix products, contract_first(): lax.dot_general(left, right, (((0,), (0,)), ((), ())), preferred_element_...  11.4 us
    dynamic_slice x7, local copies, waits for them, and re-layouts, cut(): return lax.dynamic_slice_in_dim(value, start, size, axis)  6.74 us
  transfers between devices with their start and end apart: 31, of which 11 were waited for; matrix products, arithmetic and copies ran while one was open for 14% of the time, Pallas kernels for 0%

profile of v1, /device:TPU:0, one launch (start us, length us, event | category | flops | bytes accessed | tf_op | source)
XLA Modules:
  0.0 321.6 jit_solution(10923287446568126150)
XLA Ops:
  2.3 2.9 collective-permute-start.7
  5.3 1.7 constant_dynamic-slice_fusion.15
  9.2 1.8 collective-permute-start.6
  11.0 2.1 constant_dynamic-slice_fusion.10
  16.6 26.2 %collective-permute-done.6 = bf16[384,512]{1,0:T(8,128)(2,1)} collective-permute-done((bf16[384,512]{1,0:T(8,128)(2,1)}, bf16[384,512]{1,0:T(8,128)(2,1)}, u32[]{:S(2)}, u32[]{:S(2)}) %collective-permute-start.6) | collective-permute-done | bytes 393248 | tf_op jit(solution)/shard_map/ppermute | solution.py:34
  43.6 1.9 collective-permute-start.14
  52.9 55.3 %collective-permute-done.16 = bf16[2,256,256]{2,1,0:T(8,128)(2,1)S(1)} collective-permute-done((bf16[2,256,256]{2,1,0:T(8,128)(2,1)S(1)}, bf16[2,256,256]{2,1,0:T(8,128)(2,1)S(1)}, u32[]{:S(2)}, u32[]{:S(2)}) %collective-permute-start.16) | collective-permute-done | bytes 262176 | tf_op jit(solution)/shard_map/ppermute | solution.py:38
  111.8 20.9 %collective-permute-done.10 = bf16[2,1024,256]{2,1,0:T(8,128)(2,1)S(1)} collective-permute-done((bf16[2,1024,256]{2,1,0:T(8,128)(2,1)S(1)}, bf16[2,1024,256]{2,1,0:T(8,128)(2,1)S(1)}, u32[]{:S(2)}, u32[]{:S(2)}) %collective-permute-start.10) | collective-permute-done | bytes 1048608 | tf_op jit(solution)/shard_map/ppermute | solution.py:38
  139.7 7.9 %collective-permute-done.4 = bf16[1024,768]{1,0:T(8,128)(2,1)S(1)} collective-permute-done((bf16[1024,768]{1,0:T(8,128)(2,1)S(1)}, bf16[1024,768]{1,0:T(8,128)(2,1)S(1)}, u32[]{:S(2)}, u32[]{:S(2)}) %collective-permute-start.4) | collective-permute-done | bytes 1572896 | tf_op jit(solution)/shard_map/ppermute | solution.py:34
  150.5 38.4 %collective-permute-done.11 = bf16[1024,1024]{1,0:T(8,128)(2,1)S(1)} collective-permute-done((bf16[1024,1024]{1,0:T(8,128)(2,1)S(1)}, bf16[1024,1024]{1,0:T(8,128)(2,1)S(1)}, u32[]{:S(2)}, u32[]{:S(2)}) %collective-permute-start.11) | collective-permute-done | bytes 2097184 | tf_op jit(solution)/shard_map/ppermute | solution.py:34
  196.6 6.4 %collective-permute-done.13 = f32[512,128]{1,0:T(8,128)S(1)} collective-permute-done((f32[512,128]{1,0:T(8,128)S(1)}, f32[512,128]{1,0:T(8,128)S(1)}, u32[]{:S(2)}, u32[]{:S(2)}) %collective-permute-start.13) | collective-permute-done | bytes 262176 | tf_op jit(solution)/shard_map/ppermute | solution.py:34
  211.2 4.2 %all-to-all-start = ((bf16[4,2,128,256]{3,2,1,0:T(8,128)(2,1)}), bf16[4,2,128,256]{3,2,1,0:T(8,128)(2,1)}, u32[]{:S(2)}, u32[]{:S(2)}) async-start(bf16[4,2,128,256]{3,2,1,0:T(8,128)(2,1)} %bitcast.56), calls=%async_computation | async-start | bytes 1048576 | tf_op jit(solution)/shard_map/all_to_all | solution.py:171
  215.4 2.4 fusion.77
  217.8 4.6 %collective-permute-start.23 = (bf16[2048,256]{1,0:T(8,128)(2,1)S(1)}, bf16[2048,256]{1,0:T(8,128)(2,1)S(1)}, u32[]{:S(2)}, u32[]{:S(2)}) collective-permute-start(bf16[2048,256]{1,0:T(8,128)(2,1)S(1)} %get-tuple-element.115), channel_id=1, source_target_pairs={{0,4},{12,8},{1,5},{13,9},{2,6},{14,10},{3,7},{15,11},{16,20},{28,... | collective-permute-start | bytes 3145736 | tf_op jit(solution)/shard_map/ppermute | solution.py:38
  222.4 2.1 fusion.76
  234.6 13.0 %collective-permute-done.23 = bf16[2048,256]{1,0:T(8,128)(2,1)S(1)} collective-permute-done((bf16[2048,256]{1,0:T(8,128)(2,1)S(1)}, bf16[2048,256]{1,0:T(8,128)(2,1)S(1)}, u32[]{:S(2)}, u32[]{:S(2)}) %collective-permute-start.23) | collective-permute-done | bytes 1048608 | tf_op jit(solution)/shard_map/ppermute | solution.py:38
  252.0 16.5 %collective-permute-done.26 = bf16[2048,256]{1,0:T(8,128)(2,1)S(1)} collective-permute-done((bf16[2048,256]{1,0:T(8,128)(2,1)S(1)}, bf16[2048,256]{1,0:T(8,128)(2,1)S(1)}, u32[]{:S(2)}, u32[]{:S(2)}) %collective-permute-start.26) | collective-permute-done | bytes 1048608 | tf_op jit(solution)/shard_map/ppermute | solution.py:38
  270.4 3.0 fusion.2
  273.4 5.7 %collective-permute-start.25 = (bf16[2048,256]{1,0:T(8,128)(2,1)}, bf16[2048,256]{1,0:T(8,128)(2,1)}, u32[]{:S(2)}, u32[]{:S(2)}) collective-permute-start(bf16[2048,256]{1,0:T(8,128)(2,1)} %fusion.2), channel_id=1, source_target_pairs={{0,4},{4,0},{8,12},{12,8},{1,5},{5,1},{9,13},{13,9},{2,6},{6,2},{1... | collective-permute-start | bytes 3145736 | tf_op jit(solution)/shard_map/ppermute | solution.py:38
  282.2 18.6 %collective-permute-done.25 = bf16[2048,256]{1,0:T(8,128)(2,1)} collective-permute-done((bf16[2048,256]{1,0:T(8,128)(2,1)}, bf16[2048,256]{1,0:T(8,128)(2,1)}, u32[]{:S(2)}, u32[]{:S(2)}) %collective-permute-start.25) | collective-permute-done | bytes 1048608 | tf_op jit(solution)/shard_map/ppermute | solution.py:38
  300.8 2.6 fusion.1
  305.8 1.8 fusion.11
  307.6 8.6 %collective-permute-done.29 = bf16[1,128,256]{2,1,0:T(8,128)(2,1)S(1)} collective-permute-done((bf16[1,128,256]{2,1,0:T(8,128)(2,1)S(1)}, bf16[1,128,256]{2,1,0:T(8,128)(2,1)S(1)}, u32[]{:S(2)}, u32[]{:S(2)}) %collective-permute-start.29) | collective-permute-done | bytes 65568 | tf_op jit(solution)/shard_map/ppermute | solution.py:34
  317.0 3.6 %fusion.16 = (bf16[1024,128]{1,0:T(8,128)(2,1)S(1)}, bf16[1024,128]{1,0:T(8,128)(2,1)S(1)}, bf16[1024,128]{1,0:T(8,128)(2,1)S(1)}, bf16[1024,128]{1,0:T(8,128)(2,1)S(1)}) fusion(s32[]{:T(128)S(6)} %select_n.388, bf16[2048,128]{1,0:T(8,128)(2,1)S(1)} %get-tuple-element.42, bf16[2048,128]{1,0:T(8,128)(2,1)S(1)} %collective-permute-done.28, s32[]{:T(128)S(6)} %select_n.390, ...), kind=kLoop, calls=%fused_computation.64 | loop fusion | flops 2097152 | bytes 2097168 | tf_op jit(solution)/shard_map/concatenate | solution.py:148
  (203 shorter events, 67.5 us)
Async XLA Ops:
  2.3 13.6 %collective-permute-start.7 = (bf16[1024,128]{1,0:T(8,128)(2,1)}, bf16[1024,128]{1,0:T(8,128)(2,1)S(1)}, u32[]{:S(2)}, u32[]{:S(2)}) collective-permute-start(bf16[1024,128]{1,0:T(8,128)(2,1)} %dynamic-slice_bitcast_fusion), channel_id=1, source_target_pairs={{0,2},{2,0},{1,3},{3,1},{4,6},{6,4},{5,7},{7,5},{8,10},{10,8},{9,1... | collective-permute-start | bytes 786440 | tf_op jit(solution)/shard_map/ppermute | solution.py:34
  8.1 127.8 %collective-permute-start = (bf16[256,2048]{1,0:T(8,128)(2,1)}, bf16[256,2048]{1,0:T(8,128)(2,1)}, u32[]{:S(2)}, u32[]{:S(2)}) collective-permute-start(bf16[256,2048]{1,0:T(8,128)(2,1)} %pad_maximum_fusion.8), channel_id=1, source_target_pairs={{0,2},{2,0},{1,3},{3,1},{4,6},{6,4},{5,7},{7,5},{8,10},{10,8},{9,1... | collective-permute-start | bytes 3145736 | tf_op jit(solution)/shard_map/ppermute | solution.py:34
  9.2 33.6 %collective-permute-start.6 = (bf16[384,512]{1,0:T(8,128)(2,1)}, bf16[384,512]{1,0:T(8,128)(2,1)}, u32[]{:S(2)}, u32[]{:S(2)}) collective-permute-start(bf16[384,512]{1,0:T(8,128)(2,1)} %maximum_maximum_fusion), channel_id=1, source_target_pairs={{0,2},{2,0},{1,3},{3,1},{4,6},{6,4},{5,7},{7,5},{8,10},{10,8},{9,1... | collective-permute-start | bytes 1179656 | tf_op jit(solution)/shard_map/ppermute | solution.py:34
  13.1 34.1 %collective-permute-start.1 = (bf16[1024,256]{1,0:T(8,128)(2,1)S(1)}, bf16[1024,256]{1,0:T(8,128)(2,1)S(1)}, u32[]{:S(2)}, u32[]{:S(2)}) collective-permute-start(bf16[1024,256]{1,0:T(8,128)(2,1)S(1)} %get-tuple-element.36), channel_id=1, source_target_pairs={{0,4},{4,0},{8,12},{12,8},{1,5},{5,1},{9,13},{13,9},{2,6},{6,2},{1... | collective-permute-start | bytes 1572872 | tf_op jit(solution)/shard_map/ppermute | solution.py:38
  16.0 32.3 %collective-permute-start.8 = (bf16[1024,256]{1,0:T(8,128)(2,1)S(1)}, bf16[1024,256]{1,0:T(8,128)(2,1)S(1)}, u32[]{:S(2)}, u32[]{:S(2)}) collective-permute-start(bf16[1024,256]{1,0:T(8,128)(2,1)S(1)} %get-tuple-element.56), channel_id=1, source_target_pairs={{0,4},{4,0},{8,12},{12,8},{1,5},{5,1},{9,13},{13,9},{2,6},{6,2},{1... | collective-permute-start | bytes 1572872 | tf_op jit(solution)/shard_map/ppermute | solution.py:38
  48.4 59.9 %collective-permute-start.9 = (bf16[2,1024,256]{2,1,0:T(8,128)(2,1)S(1)}, bf16[2,1024,256]{2,1,0:T(8,128)(2,1)S(1)}, u32[]{:S(2)}, u32[]{:S(2)}) collective-permute-start(bf16[2,1024,256]{2,1,0:T(8,128)(2,1)S(1)} %pad_maximum_fusion.10), channel_id=1, source_target_pairs={{4,8},{8,4},{5,9},{9,5},{6,10},{10,6},{7,11},{11,7},{20,24},{24,20... | collective-permute-start | bytes 3145736 | tf_op jit(solution)/shard_map/ppermute | solution.py:38
  49.9 59.9 %collective-permute-start.3 = (bf16[2,1024,256]{2,1,0:T(8,128)(2,1)S(1)}, bf16[2,1024,256]{2,1,0:T(8,128)(2,1)S(1)}, u32[]{:S(2)}, u32[]{:S(2)}) collective-permute-start(bf16[2,1024,256]{2,1,0:T(8,128)(2,1)S(1)} %collective-permute-done.2), channel_id=1, source_target_pairs={{4,0},{8,12},{5,1},{9,13},{6,2},{10,14},{7,3},{11,15},{20,16},{24,... | collective-permute-start | bytes 3145736 | tf_op jit(solution)/shard_map/ppermute | solution.py:38
  51.3 57.0 %collective-permute-start.16 = (bf16[2,256,256]{2,1,0:T(8,128)(2,1)S(1)}, bf16[2,256,256]{2,1,0:T(8,128)(2,1)S(1)}, u32[]{:S(2)}, u32[]{:S(2)}) collective-permute-start(bf16[2,256,256]{2,1,0:T(8,128)(2,1)S(1)} %collective-permute-done.15), channel_id=1, source_target_pairs={{4,0},{8,12},{5,1},{9,13},{6,2},{10,14},{7,3},{11,15},{20,16},{24,... | collective-permute-start | bytes 786440 | tf_op jit(solution)/shard_map/ppermute | solution.py:38
  108.3 24.4 %collective-permute-start.10 = (bf16[2,1024,256]{2,1,0:T(8,128)(2,1)S(1)}, bf16[2,1024,256]{2,1,0:T(8,128)(2,1)S(1)}, u32[]{:S(2)}, u32[]{:S(2)}) collective-permute-start(bf16[2,1024,256]{2,1,0:T(8,128)(2,1)S(1)} %collective-permute-done.9), channel_id=1, source_target_pairs={{4,0},{8,12},{5,1},{9,13},{6,2},{10,14},{7,3},{11,15},{20,16},{24,... | collective-permute-start | bytes 3145736 | tf_op jit(solution)/shard_map/ppermute | solution.py:38
  110.2 37.4 %collective-permute-start.4 = (bf16[1024,768]{1,0:T(8,128)(2,1)S(1)}, bf16[1024,768]{1,0:T(8,128)(2,1)S(1)}, u32[]{:S(2)}, u32[]{:S(2)}) collective-permute-start(bf16[1024,768]{1,0:T(8,128)(2,1)S(1)} %pad_maximum_fusion.5), channel_id=1, source_target_pairs={{0,16},{16,0},{1,17},{17,1},{2,18},{18,2},{3,19},{19,3},{4,20},{20... | collective-permute-start | bytes 4718600 | tf_op jit(solution)/shard_map/ppermute | solution.py:34
  133.0 55.9 %collective-permute-start.11 = (bf16[1024,1024]{1,0:T(8,128)(2,1)S(1)}, bf16[1024,1024]{1,0:T(8,128)(2,1)S(1)}, u32[]{:S(2)}, u32[]{:S(2)}) collective-permute-start(bf16[1024,1024]{1,0:T(8,128)(2,1)S(1)} %fusion.12), channel_id=1, source_target_pairs={{0,16},{16,0},{1,17},{17,1},{2,18},{18,2},{3,19},{19,3},{4,20},{20... | collective-permute-start | bytes 6291464 | tf_op jit(solution)/shard_map/ppermute | solution.py:34
  138.2 55.1 %collective-permute-start.20 = (f32[512,128]{1,0:T(8,128)S(1)}, f32[512,128]{1,0:T(8,128)S(1)}, u32[]{:S(2)}, u32[]{:S(2)}) collective-permute-start(f32[512,128]{1,0:T(8,128)S(1)} %fusion.89), channel_id=1, source_target_pairs={{0,2},{2,0},{1,3},{3,1},{4,6},{6,4},{5,7},{7,5},{8,10},{10,8},{9,1... | collective-permute-start | bytes 786440 | tf_op jit(solution)/shard_map/ppermute | solution.py:34
  150.4 45.8 %collective-permute-start.5 = (f32[512,512]{1,0:T(8,128)S(1)}, f32[512,512]{1,0:T(8,128)S(1)}, u32[]{:S(2)}, u32[]{:S(2)}) collective-permute-start(f32[512,512]{1,0:T(8,128)S(1)} %slice_select_fusion), channel_id=1, source_target_pairs={{0,1},{1,0},{2,3},{3,2},{4,5},{5,4},{6,7},{7,6},{8,9},{9,8},{10,11... | collective-permute-start | bytes 3145736 | tf_op jit(solution)/shard_map/ppermute | solution.py:34
  211.2 69.9 %all-to-all-start = ((bf16[4,2,128,256]{3,2,1,0:T(8,128)(2,1)}), bf16[4,2,128,256]{3,2,1,0:T(8,128)(2,1)}, u32[]{:S(2)}, u32[]{:S(2)}) async-start(bf16[4,2,128,256]{3,2,1,0:T(8,128)(2,1)} %bitcast.56), calls=%async_computation | async-start | bytes 1048576 | tf_op jit(solution)/shard_map/all_to_all | solution.py:171
  217.8 29.8 %collective-permute-start.23 = (bf16[2048,256]{1,0:T(8,128)(2,1)S(1)}, bf16[2048,256]{1,0:T(8,128)(2,1)S(1)}, u32[]{:S(2)}, u32[]{:S(2)}) collective-permute-start(bf16[2048,256]{1,0:T(8,128)(2,1)S(1)} %get-tuple-element.115), channel_id=1, source_target_pairs={{0,4},{12,8},{1,5},{13,9},{2,6},{14,10},{3,7},{15,11},{16,20},{28,... | collective-permute-start | bytes 3145736 | tf_op jit(solution)/shard_map/ppermute | solution.py:38
  224.5 44.0 %collective-permute-start.26 = (bf16[2048,256]{1,0:T(8,128)(2,1)S(1)}, bf16[2048,256]{1,0:T(8,128)(2,1)S(1)}, u32[]{:S(2)}, u32[]{:S(2)}) collective-permute-start(bf16[2048,256]{1,0:T(8,128)(2,1)S(1)} %get-tuple-element.113), channel_id=1, source_target_pairs={{0,4},{12,8},{1,5},{13,9},{2,6},{14,10},{3,7},{15,11},{16,20},{28,... | collective-permute-start | bytes 3145736 | tf_op jit(solution)/shard_map/ppermute | solution.py:38
  228.9 50.2 %collective-permute-start.21 = (bf16[256,1024]{1,0:T(8,128)(2,1)S(1)}, bf16[256,1024]{1,0:T(8,128)(2,1)S(1)}, u32[]{:S(2)}, u32[]{:S(2)}) collective-permute-start(bf16[256,1024]{1,0:T(8,128)(2,1)S(1)} %get-tuple-element.44), channel_id=1, source_target_pairs={{0,2},{2,0},{1,3},{3,1},{4,6},{6,4},{5,7},{7,5},{8,10},{10,8},{9,1... | collective-permute-start | bytes 1572872 | tf_op jit(solution)/shard_map/ppermute | solution.py:34
  233.1 46.0 %collective-permute-start.22 = (bf16[256,1024]{1,0:T(8,128)(2,1)S(1)}, bf16[256,1024]{1,0:T(8,128)(2,1)S(1)}, u32[]{:S(2)}, u32[]{:S(2)}) collective-permute-start(bf16[256,1024]{1,0:T(8,128)(2,1)S(1)} %get-tuple-element.46), channel_id=1, source_target_pairs={{0,2},{2,0},{1,3},{3,1},{4,6},{6,4},{5,7},{7,5},{8,10},{10,8},{9,1... | collective-permute-start | bytes 1572872 | tf_op jit(solution)/shard_map/ppermute | solution.py:34
  247.8 22.6 %collective-permute-start.24 = (bf16[2048,256]{1,0:T(8,128)(2,1)S(1)}, bf16[2048,256]{1,0:T(8,128)(2,1)S(1)}, u32[]{:S(2)}, u32[]{:S(2)}) collective-permute-start(bf16[2048,256]{1,0:T(8,128)(2,1)S(1)} %add_convert_fusion.1), channel_id=1, source_target_pairs={{4,8},{8,4},{5,9},{9,5},{6,10},{10,6},{7,11},{11,7},{20,24},{24,20... | collective-permute-start | bytes 3145736 | tf_op jit(solution)/shard_map/ppermute | solution.py:38
  250.5 55.3 %collective-permute-start.17 = (f32[256,512]{1,0:T(8,128)}, f32[256,512]{1,0:T(8,128)}, u32[]{:S(2)}, u32[]{:S(2)}) collective-permute-start(f32[256,512]{1,0:T(8,128)} %slice.211), channel_id=1, source_target_pairs={{0,2},{2,0},{1,3},{3,1},{4,6},{6,4},{5,7},{7,5},{8,10},{10,8},{9,1... | collective-permute-start | bytes 1572872 | tf_op jit(solution)/shard_map/ppermute | solution.py:34
  268.8 13.4 %collective-permute-start.27 = (bf16[2048,256]{1,0:T(8,128)(2,1)S(1)}, bf16[2048,256]{1,0:T(8,128)(2,1)}, u32[]{:S(2)}, u32[]{:S(2)}) collective-permute-start(bf16[2048,256]{1,0:T(8,128)(2,1)S(1)} %add_convert_fusion), channel_id=1, source_target_pairs={{4,8},{8,4},{5,9},{9,5},{6,10},{10,6},{7,11},{11,7},{20,24},{24,20... | collective-permute-start | bytes 3145736 | tf_op jit(solution)/shard_map/ppermute | solution.py:38
  273.4 27.4 %collective-permute-start.25 = (bf16[2048,256]{1,0:T(8,128)(2,1)}, bf16[2048,256]{1,0:T(8,128)(2,1)}, u32[]{:S(2)}, u32[]{:S(2)}) collective-permute-start(bf16[2048,256]{1,0:T(8,128)(2,1)} %fusion.2), channel_id=1, source_target_pairs={{0,4},{4,0},{8,12},{12,8},{1,5},{5,1},{9,13},{13,9},{2,6},{6,2},{1... | collective-permute-start | bytes 3145736 | tf_op jit(solution)/shard_map/ppermute | solution.py:38
  303.5 13.4 %collective-permute-start.28 = (bf16[2048,128]{1,0:T(8,128)(2,1)S(1)}, bf16[2048,128]{1,0:T(8,128)(2,1)S(1)}, u32[]{:S(2)}, u32[]{:S(2)}) collective-permute-start(bf16[2048,128]{1,0:T(8,128)(2,1)S(1)} %get-tuple-element.41), channel_id=1, source_target_pairs={{0,2},{2,0},{1,3},{3,1},{4,6},{6,4},{5,7},{7,5},{8,10},{10,8},{9,1... | collective-permute-start | bytes 1572872 | tf_op jit(solution)/shard_map/ppermute | solution.py:34
  305.2 11.0 %collective-permute-start.29 = (bf16[1,128,256]{2,1,0:T(8,128)(2,1)S(1)}, bf16[1,128,256]{2,1,0:T(8,128)(2,1)S(1)}, u32[]{:S(2)}, u32[]{:S(2)}) collective-permute-start(bf16[1,128,256]{2,1,0:T(8,128)(2,1)S(1)} %get-tuple-element.64), channel_id=1, source_target_pairs={{0,2},{2,0},{1,3},{3,1},{4,6},{6,4},{5,7},{7,5},{8,10},{10,8},{9,1... | collective-permute-start | bytes 196616 | tf_op jit(solution)/shard_map/ppermute | solution.py:34
  (43 other events, 678.7 us)

commit v2 on v1

--- a/solution.py
+++ b/solution.py
@@ -36,6 +36,10 @@
 
 def along(value, pairs):
     return lax.ppermute(value, "fsdp", pairs)
+
+
+def after(value, *earlier):
+    return lax.optimization_barrier((value, *earlier))[0]
 
 
 def body_line(
@@ -53,6 +57,7 @@
     down = adapter_down_weight[0]
     up = adapter_up_weight[0]
     rank_limit = down.shape[1]
+    wide = 2 * rank_limit
     quarter = width // 2
     eighth = quarter // 2
     kvq = kv // 2
@@ -62,87 +67,127 @@
     is_middle = (z == 1) | (z == 2)
     line = [z, z + 1 - 2 * (z % 2), jnp.where(first_pair, 2, 1), jnp.where(first_pair, 3, 0)]
     adapters = [2 * t + o for t in line for o in (x, 1 - x)]
+    number = len(adapters)
 
     def cut(value, start, size, axis):
         return lax.dynamic_slice_in_dim(value, start, size, axis)
 
-    def features(value, side, axis):
-        return [
-            cut(value, side * quarter + half * eighth, eighth, axis) for half in (y, 1 - y)
-        ]
-
-    def gather_line(piece):
-        near = along(piece, NEIGHBOURS)
-        both = jnp.stack([piece, near])
-        crossed = along(both, MIDDLE)
-        outer = along(crossed, OUTWARD)
-        return near, jnp.where(is_middle, crossed, outer)
-
+    def features(value, side, half, axis):
+        return cut(value, side * quarter + half * eighth, eighth, axis)
+
+    weight_here = features(frozen_value_weight, x, y, 0)
+    weight_near = along(weight_here, NEIGHBOURS)
+    up_sent = jnp.broadcast_to(
+        up.reshape(rank_limit, 2, kvq).transpose(1, 0, 2)[None], (4, 2, rank_limit, kvq)
+    ).reshape(number, rank_limit, kvq)
+    up_all = lax.all_to_all(
+        up_sent, ("fsdp", "own"), split_axis=0, concat_axis=0, tiled=True
+    ).reshape(number * rank_limit, kvq)
+
+    down_got = swap(features(down, 1 - x, y, 0), "own")
+    down_piece = jnp.concatenate([features(down, x, y, 0), down_got], axis=1)
     ids_row = token_adapter[:, 0].astype(bf16)[None, :]
-    up_here, up_there = cut(up, x * kvq, kvq, 1), cut(up, (1 - x) * kvq, kvq, 1)
-    packet = jnp.concatenate(
-        [
-            cotangent,
-            jnp.concatenate([up_there, jnp.broadcast_to(ids_row, (rank_limit, rows))], axis=1),
-        ],
-        axis=0,
-    )
-    packet = swap(packet, "own")
+    packet = swap(
+        jnp.concatenate(
+            [cotangent, jnp.broadcast_to(jnp.concatenate([ids_row, ids_row], axis=1), (16, kv))]
+        ),
+        "own",
+    )
     dy_half = jnp.concatenate([cotangent, packet[:rows]], axis=0)
-    up_piece = jnp.concatenate([up_here, packet[rows:, :kvq]], axis=0)
-    ids = jnp.concatenate([token_adapter[:, 0], packet[rows, kvq:].astype(jnp.int32)])[:, None]
-    x_here = jnp.concatenate(features(tokens, x, 1), axis=1)
-    x_there = swap(jnp.concatenate(features(tokens, 1 - x, 1), axis=1), "own")
-    x_both = jnp.concatenate([x_here, x_there], axis=0)
-    down_here = features(down, x, 0)
-    down_piece = jnp.concatenate(
-        [down_here[0], swap(cut(down, (1 - x) * quarter + y * eighth, eighth, 0), "own")], axis=1
-    )
+    ids = jnp.concatenate([token_adapter[:, 0], packet[rows, :rows].astype(jnp.int32)])[:, None]
+    def spread(ids, value, order):
+        place = jnp.repeat(jnp.stack([jnp.asarray(a, jnp.int32) for a in order]), rank_limit)
+        tiled = jnp.concatenate([value] * number, axis=1)
+        return jnp.where(ids == place[None, :], tiled, jnp.zeros_like(tiled))
 
     ranks = rank_limit // 8 * rank_step_count
-    number = ranks.shape[0]
-    onehot = ids == jnp.arange(number, dtype=jnp.int32)[None, :]
-    token_rank = jnp.sum(jnp.where(onehot, ranks[None, :], 0), axis=1, keepdims=True)
+    token_rank = jnp.sum(
+        jnp.where(ids == jnp.arange(number, dtype=jnp.int32)[None, :], ranks[None, :], 0),
+        axis=1,
+        keepdims=True,
+    )
     token_scale = 16.0 / token_rank.astype(f32)
     keep = jnp.arange(rank_limit, dtype=jnp.int32)[None, :] < token_rank
 
-    def compact(part):
+    def compact(part, order):
         total = jnp.zeros((2 * rows, rank_limit), f32)
-        for i, a in enumerate(adapters):
+        for i, a in enumerate(order):
             total = total + jnp.where(ids == a, part[:, i * rank_limit : (i + 1) * rank_limit], 0.0)
-        return total
-
-    def expand(value, order):
-        return jnp.concatenate(
-            [jnp.where(ids == a, value, jnp.zeros_like(value)) for a in order], axis=1
-        )
-
-    def sum_features(part):
-        part = compact(part)
-        part = part + swap(part, "tp")
-        return part + jnp.roll(swap(part, "own"), rows, axis=0)
-
-    up_near, up_far = gather_line(up_piece)
-    up_all = jnp.concatenate([up_piece, up_near, up_far[0], up_far[1]], axis=0)
+        return total + swap(total, "tp")
+
+    def sum_own(total):
+        return total + jnp.roll(swap(total, "own"), rows, axis=0)
+
+    def share_tokens(half, *earlier):
+        sent = after(features(tokens, 1 - x, half, 1), *earlier)
+        return jnp.concatenate([features(tokens, x, half, 1), swap(sent, "own")], axis=0)
+
     dy_quarter = cut(dy_half, x * kvq, kvq, 1)
-    back = sum_features(contract_final_axis(dy_quarter, up_all))
+    back_half = compact(contract_final_axis(dy_quarter, up_all), range(number))
+    x_both = [share_tokens(y, up_all), share_tokens(1 - y, back_half)]
+    back = sum_own(back_half)
     back = (token_scale * jnp.where(keep, back, 0.0)).astype(bf16)
-    back_wide = expand(back, adapters)
-
-    wide = 2 * rank_limit
-
-    def partial(i):
-        return contract_first(x_both, back_wide[:, i * wide : (i + 1) * wide])
-
-    to_end, to_middle, to_pair, to_self = partial(3), partial(2), partial(1), partial(0)
-    from_end = along(to_end.astype(bf16), INWARD)
-    from_end_too = along(to_middle.astype(bf16), INWARD)
-    crossed_end = along((to_end + from_end.astype(f32)).astype(bf16), MIDDLE)
-    crossed_middle = along((to_middle + from_end_too.astype(f32)).astype(bf16), MIDDLE)
-    from_pair = along((to_pair + crossed_end.astype(f32)).astype(bf16), NEIGHBOURS)
-    grad = (to_self + from_pair.astype(f32) + crossed_middle.astype(f32)).astype(bf16)
-    grad_here = grad[:, :rank_limit]
-    grad_there = swap(grad[:, rank_limit:], "own")
+    back_wide = spread(ids, back, adapters)
+    back_in = along(
+        jnp.concatenate([back, jnp.broadcast_to(ids.astype(bf16), back.shape)], axis=1), INWARD
+    )
+    back_in_wide = spread(
+        back_in[:, rank_limit : rank_limit + 1].astype(jnp.int32), back_in[:, :rank_limit], adapters
+    )
+
+    def far_pair(piece, near):
+        crossed = along(jnp.concatenate([piece, near], axis=1), MIDDLE)
+        outer = along(crossed, OUTWARD)
+        return jnp.where(is_middle, crossed, outer)
+
+    weight_far = far_pair(weight_here, weight_near)
+    down_piece = after(down_piece, up_all)
+    down_near = along(down_piece, NEIGHBOURS)
+    down_far = far_pair(down_piece, down_near)
+    grad_here, grad_there = [], []
+    for x_half in x_both:
+        x_in = along(x_half, INWARD)
+
+        def total(first, last):
+            span = slice(first * wide, last * wide)
+            return contract_first(x_half, back_wide[:, span])
+
+        def total_in(first, last):
+            span = slice(first * wide, last * wide)
+            return contract_first(x_in, back_in_wide[:, span])
+
+        crossed = along((total(2, 4) + total_in(2, 4)).astype(bf16), MIDDLE)
+        outer = along((total(1, 2) + crossed[:, wide:].astype(f32)).astype(bf16), OUTWARD)
+        grad = total(0, 1) + total_in(0, 1) + crossed[:, :wide].astype(f32) + outer.astype(f32)
+        grad = grad.astype(bf16)
+        grad_here.append(grad[:, :rank_limit])
+        grad_there.append(swap(grad[:, rank_limit:], "own"))
+
+    down_mine = jnp.concatenate([down_piece, down_near, down_far], axis=1)
+    down_other = jnp.concatenate(
+        [swap(jnp.concatenate([down_piece, down_near], axis=1), "rep"), swap(down_far, "rep")],
+        axis=1,
+    )
+    low = sum_own(
+        compact(matmul(x_both[0], down_mine) + matmul(x_both[1], down_other), adapters)
+    )
+    low = jnp.where(keep, low, 0.0).astype(bf16)
+    low_wide = spread(ids, low, range(number))
+    delta = (token_scale * matmul(low_wide, up_all)).astype(bf16)
+    up_part = contract_first(low_wide, dy_quarter).astype(bf16)
+    up_got = lax.all_to_all(
+        up_part.reshape(4, 2, rank_limit, kvq), "fsdp", split_axis=0, concat_axis=0, tiled=True
+    )
+    up_sum = jnp.sum(up_got.astype(f32), axis=0)
+    own_ranks = cut(ranks, 2 * z, 2, 0).astype(f32)
+    up_sum = ((16.0 / own_ranks)[:, None, None] * up_sum).astype(bf16)
+    up_mine = cut(up_sum, x, 1, 0)
+    up_theirs = swap(cut(up_sum, 1 - x, 1, 0), "own")
+    up_gradient = jnp.where(
+        x == 0,
+        jnp.concatenate([up_mine, up_theirs], axis=2),
+        jnp.concatenate([up_theirs, up_mine], axis=2),
+    )
 
     def in_place(here, there, axis):
         blocks = jnp.concatenate(here + there, axis=axis)
@@ -156,31 +201,7 @@
             axis=axis,
         )
 
-    down_gradient = in_place([grad_here], [grad_there], 0)[None]
-
-    down_near, down_far = gather_line(down_piece)
-    down_mine = jnp.concatenate([down_piece, down_near, down_far[0], down_far[1]], axis=1)
-    down_other = swap(down_mine, "rep")
-    low = sum_features(
-        matmul(x_both[:, :eighth], down_mine) + matmul(x_both[:, eighth:], down_other)
-    )
-    low = jnp.where(keep, low, 0.0).astype(bf16)
-    delta = (token_scale * matmul(expand(low, adapters), up_all)).astype(bf16)
-    natural = [2 * (i // 2) + i % 2 for i in range(number)]
-    up_part = contract_first(expand(low, natural), dy_quarter).astype(bf16)
-    up_sent = lax.all_to_all(
-        up_part.reshape(4, 2, rank_limit, kvq), "fsdp", split_axis=0, concat_axis=0, tiled=True
-    )
-    up_sum = jnp.sum(up_sent.astype(f32), axis=0)
-    own_ranks = cut(ranks, 2 * z, 2, 0).astype(f32)
-    up_sum = ((16.0 / own_ranks)[:, None, None] * up_sum).astype(bf16)
-    up_mine = cut(up_sum, x, 1, 0)
-    up_theirs = swap(cut(up_sum, 1 - x, 1, 0), "own")
-    up_gradient = jnp.where(
-        x == 0,
-        jnp.concatenate([up_mine, up_theirs], axis=2),
-        jnp.concatenate([up_theirs, up_mine], axis=2),
-    )
+    down_gradient = in_place(grad_here, grad_there, 0)[None]
 
     dy_tp = swap(dy_half, "tp")
     dy_full = jnp.where(
@@ -190,11 +211,15 @@
     )
     dy_line = jnp.concatenate([cut(dy_full, t * cols, cols, 1) for t in line], axis=1)
 
-    weight_here = features(frozen_value_weight, x, 0)
-    weight_near, weight_far = gather_line(weight_here[0])
-    got = jnp.concatenate([weight_near, weight_far[0], weight_far[1]], axis=1)
-    weight_mine = jnp.concatenate([weight_here[0], got], axis=1)
-    weight_other = jnp.concatenate([weight_here[1], swap(got, "rep")], axis=1)
+    weight_mine = jnp.concatenate([weight_here, weight_near, weight_far], axis=1)
+    weight_other = jnp.concatenate(
+        [
+            features(frozen_value_weight, x, 1 - y, 0),
+            swap(weight_near, "rep"),
+            swap(weight_far, "rep"),
+        ],
+        axis=1,
+    )
 
     def input_grad_of(weight, adapter):
         lora = contract_final_axis(back_wide, adapter).astype(bf16)
@@ -206,7 +231,7 @@
     back_other = swap(dx_other[rows:], "own")
     input_grad = in_place([dx_mine[:rows], dx_other[:rows]], [back_mine, back_other], 1)
 
-    part = matmul(x_both[:, :eighth], weight_mine) + matmul(x_both[:, eighth:], weight_other)
+    part = matmul(x_both[0], weight_mine) + matmul(x_both[1], weight_other)
     first, second = part[:, :kv], part[:, kv:]
     own_first = (c == 0) == first_pair
     half = jnp.where(own_first, first, second) + swap(jnp.where(own_first, second, first), "tp")

time: 322 us -> 269 us (0.84)
  waiting for transfers between devices: 213 us -> 123 us
  starting transfers between devices: 46.5 us -> 73.9 us
  matrix products: 22.5 us -> 29 us
  local copies, waits for them, and re-layouts: 13 us -> 18.9 us
  other arithmetic: 25.4 us -> 20.9 us
    ppermute x14 -> x13, waiting for transfers between devices: 124 us -> 54.7 us  [along(): return lax.ppermute(value, 'fsdp', pairs)]
    ppermute x16 -> x20, waiting for transfers between devices: 88.1 us -> 68.5 us  [swap(): return lax.ppermute(value, axis, PAIR)]
    all_to_all x1, starting transfers between devices: 4.2 us -> 15.6 us  [body_line(): lax.all_to_all(up_part.reshape(4, 2, rank_limit, kvq), 'fsdp', split_axis...]
    ppermute x14 -> x13, starting transfers between devices: 24.3 us -> 33.3 us  [along(): return lax.ppermute(value, 'fsdp', pairs)]
    all_to_all x0 -> x1, starting transfers between devices: none -> 5.01 us  [body_line(): lax.all_to_all(up_sent, ('fsdp', 'own'), split_axis=0, concat_axis=0, til...]
    unnamed x8 -> x1, other arithmetic: 4.87 us -> 0.21 us
    dot_general x5 -> x11, matrix products: 11.4 us -> 14.7 us  [contract_first(): lax.dot_general(left, right, (((0,), (0,)), ((), ())), preferred_element_...]
    ppermute x16 -> x20, starting transfers between devices: 18 us -> 20 us  [swap(): return lax.ppermute(value, axis, PAIR)]
  transfers between devices with their start and end apart: 31 -> 35, of which waited for: 11 -> 15; matrix products, arithmetic and copies ran while one was open for 14% -> 23% of each run, Pallas kernels for 0% -> 0%
where the time goes in v2:
time: 269 us; the launch traced here: 268 us
  waiting for transfers between devices  123 us (46%)
  starting transfers between devices  73.9 us (27%)
  matrix products  29 us (11%)
  other arithmetic  20.9 us (8%)
  local copies, waits for them, and re-layouts  18.9 us (7%)
    ppermute x20, waiting for transfers between devices, swap(): return lax.ppermute(value, axis, PAIR)  68.5 us
    ppermute x13, waiting for transfers between devices, along(): return lax.ppermute(value, 'fsdp', pairs)  54.7 us
    ppermute x13, starting transfers between devices, along(): return lax.ppermute(value, 'fsdp', pairs)  33.3 us
    ppermute x20, starting transfers between devices, swap(): return lax.ppermute(value, axis, PAIR)  20 us
    all_to_all x1, starting transfers between devices, body_line(): lax.all_to_all(up_part.reshape(4, 2, rank_limit, kvq), 'fsdp', split_axis...  15.6 us
    dot_general x11, matrix products, contract_first(): lax.dot_general(left, right, (((0,), (0,)), ((), ())), preferred_element_...  14.7 us
    dot_general x5, matrix products, matmul(): return jnp.dot(left, right, preferred_element_type=f32)  7.48 us
    dynamic_slice x7, local copies, waits for them, and re-layouts, cut(): return lax.dynamic_slice_in_dim(value, start, size, axis)  6.87 us
  transfers between devices with their start and end apart: 35, of which 15 were waited for; matrix products, arithmetic and copies ran while one was open for 23% of the time, Pallas kernels for 0%

profile of v2, /device:TPU:0, one launch (start us, length us, event | category | flops | bytes accessed | tf_op | source)
XLA Modules:
  0.0 267.7 jit_solution(223374568631418106)
XLA Ops:
  2.5 2.9 %collective-permute-start.10 = (bf16[1024,128]{1,0:T(8,128)(2,1)S(1)}, bf16[1024,128]{1,0:T(8,128)(2,1)S(1)}, u32[]{:S(2)}, u32[]{:S(2)}) collective-permute-start(bf16[1024,128]{1,0:T(8,128)(2,1)S(1)} %get-tuple-element.37), channel_id=1, source_target_pairs={{0,2},{2,0},{1,3},{3,1},{4,6},{6,4},{5,7},{7,5},{8,10},{10,8},{9,1... | collective-permute-start | bytes 786440 | tf_op jit(solution)/shard_map/ppermute | solution.py:34
  7.2 5.0 %all-to-all-start = ((bf16[8,128,256]{2,1,0:T(8,128)(2,1)}), bf16[8,128,256]{2,1,0:T(8,128)(2,1)S(1)}, u32[]{:S(2)}, u32[]{:S(2)}) async-start(bf16[8,128,256]{2,1,0:T(8,128)(2,1)} %bitcast.1), calls=%async_computation | async-start | bytes 1048576 | tf_op jit(solution)/shard_map/all_to_all | solution.py:83
  13.0 2.0 collective-permute-start.4
  15.1 2.3 constant_dynamic-slice_fusion.14
  22.7 3.4 %collective-permute-done.4 = bf16[272,512]{1,0:T(8,128)(2,1)} collective-permute-done((bf16[272,512]{1,0:T(8,128)(2,1)}, bf16[272,512]{1,0:T(8,128)(2,1)}, u32[]{:S(2)}, u32[]{:S(2)}) %collective-permute-start.4) | collective-permute-done | bytes 278560 | tf_op jit(solution)/shard_map/ppermute | solution.py:34
  28.6 5.8 %collective-permute-done.1 = bf16[1024,256]{1,0:T(8,128)(2,1)} collective-permute-done((bf16[1024,256]{1,0:T(8,128)(2,1)}, bf16[1024,256]{1,0:T(8,128)(2,1)}, u32[]{:S(2)}, u32[]{:S(2)}) %collective-permute-start.1) | collective-permute-done | bytes 524320 | tf_op jit(solution)/shard_map/ppermute | solution.py:38
  37.4 3.0 %collective-permute-start.11 = (bf16[1024,256]{1,0:T(8,128)(2,1)S(1)}, bf16[1024,256]{1,0:T(8,128)(2,1)S(1)}, u32[]{:S(2)}, u32[]{:S(2)}) collective-permute-start(bf16[1024,256]{1,0:T(8,128)(2,1)S(1)} %pad_maximum_fusion.19), channel_id=1, source_target_pairs={{0,4},{4,0},{8,12},{12,8},{1,5},{5,1},{9,13},{13,9},{2,6},{6,2},{1... | collective-permute-start | bytes 1572872 | tf_op jit(solution)/shard_map/ppermute | solution.py:38
  40.6 12.4 %collective-permute-done.11 = bf16[1024,256]{1,0:T(8,128)(2,1)S(1)} collective-permute-done((bf16[1024,256]{1,0:T(8,128)(2,1)S(1)}, bf16[1024,256]{1,0:T(8,128)(2,1)S(1)}, u32[]{:S(2)}, u32[]{:S(2)}) %collective-permute-start.11) | collective-permute-done | bytes 524320 | tf_op jit(solution)/shard_map/ppermute | solution.py:38
  63.9 9.0 %collective-permute-done = bf16[256,1024]{1,0:T(8,128)(2,1)S(1)} collective-permute-done((bf16[256,1024]{1,0:T(8,128)(2,1)S(1)}, bf16[256,1024]{1,0:T(8,128)(2,1)S(1)}, u32[]{:S(2)}, u32[]{:S(2)}) %collective-permute-start) | collective-permute-done | bytes 524320 | tf_op jit(solution)/shard_map/ppermute | solution.py:34
  74.5 10.3 %collective-permute-done.3 = bf16[1024,512]{1,0:T(8,128)(2,1)S(1)} collective-permute-done((bf16[1024,512]{1,0:T(8,128)(2,1)}, bf16[1024,512]{1,0:T(8,128)(2,1)S(1)}, u32[]{:S(2)}, u32[]{:S(2)}) %collective-permute-start.3) | collective-permute-done | bytes 1048608 | tf_op jit(solution)/shard_map/ppermute | solution.py:38
  88.0 5.9 %collective-permute-done.6 = bf16[256,1024]{1,0:T(8,128)(2,1)S(1)} collective-permute-done((bf16[256,1024]{1,0:T(8,128)(2,1)S(1)}, bf16[256,1024]{1,0:T(8,128)(2,1)S(1)}, u32[]{:S(2)}, u32[]{:S(2)}) %collective-permute-start.6) | collective-permute-done | bytes 524320 | tf_op jit(solution)/shard_map/ppermute | solution.py:34
  94.0 12.2 %collective-permute-start.23 = (bf16[512,1024]{1,0:T(8,128)(2,1)}, bf16[512,1024]{1,0:T(8,128)(2,1)S(1)}, u32[]{:S(2)}, u32[]{:S(2)}) collective-permute-start(bf16[512,1024]{1,0:T(8,128)(2,1)} %pad_maximum_fusion.5), channel_id=1, source_target_pairs={{0,4},{12,8},{1,5},{13,9},{2,6},{14,10},{3,7},{15,11},{16,20},{28,... | collective-permute-start | bytes 3145736 | tf_op jit(solution)/shard_map/ppermute | solution.py:38
  110.6 2.5 fusion.12
  113.1 8.3 %collective-permute-done.8 = bf16[1024,512]{1,0:T(8,128)(2,1)S(1)} collective-permute-done((bf16[1024,512]{1,0:T(8,128)(2,1)S(1)}, bf16[1024,512]{1,0:T(8,128)(2,1)S(1)}, u32[]{:S(2)}, u32[]{:S(2)}) %collective-permute-start.8) | collective-permute-done | bytes 1048608 | tf_op jit(solution)/shard_map/ppermute | solution.py:34
  123.0 19.0 %collective-permute-done.15 = bf16[1024,512]{1,0:T(8,128)(2,1)S(1)} collective-permute-done((bf16[1024,512]{1,0:T(8,128)(2,1)S(1)}, bf16[1024,512]{1,0:T(8,128)(2,1)S(1)}, u32[]{:S(2)}, u32[]{:S(2)}) %collective-permute-start.15) | collective-permute-done | bytes 1048608 | tf_op jit(solution)/shard_map/ppermute | solution.py:34
  150.6 5.8 %collective-permute-done.17 = f32[512,128]{1,0:T(8,128)S(1)} collective-permute-done((f32[512,128]{1,0:T(8,128)S(1)}, f32[512,128]{1,0:T(8,128)S(1)}, u32[]{:S(2)}, u32[]{:S(2)}) %collective-permute-start.17) | collective-permute-done | bytes 262176 | tf_op jit(solution)/shard_map/ppermute | solution.py:34
  160.9 15.6 %all-to-all-start.1 = ((bf16[4,2,128,256]{3,2,1,0:T(8,128)(2,1)}), bf16[4,2,128,256]{3,2,1,0:T(8,128)(2,1)}, u32[]{:S(2)}, u32[]{:S(2)}) async-start(bf16[4,2,128,256]{3,2,1,0:T(8,128)(2,1)} %bitcast.38), calls=%async_computation.1 | async-start | bytes 1048576 | tf_op jit(solution)/shard_map/all_to_all | solution.py:178
  176.7 3.9 %collective-permute-start.24 = (bf16[512,256]{1,0:T(8,128)(2,1)S(1)}, bf16[512,256]{1,0:T(8,128)(2,1)S(1)}, u32[]{:S(2)}, u32[]{:S(2)}) collective-permute-start(bf16[512,256]{1,0:T(8,128)(2,1)S(1)} %pad_maximum_fusion.21), channel_id=1, source_target_pairs={{0,4},{12,8},{1,5},{13,9},{2,6},{14,10},{3,7},{15,11},{16,20},{28,... | collective-permute-start | bytes 786440 | tf_op jit(solution)/shard_map/ppermute | solution.py:38
  182.9 7.3 %collective-permute-done.24 = bf16[512,256]{1,0:T(8,128)(2,1)S(1)} collective-permute-done((bf16[512,256]{1,0:T(8,128)(2,1)S(1)}, bf16[512,256]{1,0:T(8,128)(2,1)S(1)}, u32[]{:S(2)}, u32[]{:S(2)}) %collective-permute-start.24) | collective-permute-done | bytes 262176 | tf_op jit(solution)/shard_map/ppermute | solution.py:38
  203.7 2.5 add_convert_fusion.3
  219.5 2.9 %collective-permute-done.21 = bf16[256,1024]{1,0:T(8,128)(2,1)} collective-permute-done((bf16[256,1024]{1,0:T(8,128)(2,1)}, bf16[256,1024]{1,0:T(8,128)(2,1)}, u32[]{:S(2)}, u32[]{:S(2)}) %collective-permute-start.21) | collective-permute-done | bytes 524320 | tf_op jit(solution)/shard_map/ppermute | solution.py:34
  222.4 9.3 %collective-permute-done.22 = bf16[256,1024]{1,0:T(8,128)(2,1)} collective-permute-done((bf16[256,1024]{1,0:T(8,128)(2,1)}, bf16[256,1024]{1,0:T(8,128)(2,1)}, u32[]{:S(2)}, u32[]{:S(2)}) %collective-permute-start.22) | collective-permute-done | bytes 524320 | tf_op jit(solution)/shard_map/ppermute | solution.py:34
  239.5 18.9 %collective-permute-done.29 = bf16[1024,256]{1,0:T(8,128)(2,1)S(1)} collective-permute-done((bf16[1024,256]{1,0:T(8,128)(2,1)S(1)}, bf16[1024,256]{1,0:T(8,128)(2,1)S(1)}, u32[]{:S(2)}, u32[]{:S(2)}) %collective-permute-start.29) | collective-permute-done | bytes 524320 | tf_op jit(solution)/shard_map/ppermute | solution.py:38
  262.8 3.7 %collective-permute-done.31 = bf16[1024,128]{1,0:T(8,128)(2,1)S(1)} collective-permute-done((bf16[1024,128]{1,0:T(8,128)(2,1)S(1)}, bf16[1024,128]{1,0:T(8,128)(2,1)S(1)}, u32[]{:S(2)}, u32[]{:S(2)}) %collective-permute-start.31) | collective-permute-done | bytes 262176 | tf_op jit(solution)/shard_map/ppermute | solution.py:34
  (259 shorter events, 91.7 us)
Async XLA Ops:
  2.5 18.5 %collective-permute-start.10 = (bf16[1024,128]{1,0:T(8,128)(2,1)S(1)}, bf16[1024,128]{1,0:T(8,128)(2,1)S(1)}, u32[]{:S(2)}, u32[]{:S(2)}) collective-permute-start(bf16[1024,128]{1,0:T(8,128)(2,1)S(1)} %get-tuple-element.37), channel_id=1, source_target_pairs={{0,2},{2,0},{1,3},{3,1},{4,6},{6,4},{5,7},{7,5},{8,10},{10,8},{9,1... | collective-permute-start | bytes 786440 | tf_op jit(solution)/shard_map/ppermute | solution.py:34
  7.2 30.2 %all-to-all-start = ((bf16[8,128,256]{2,1,0:T(8,128)(2,1)}), bf16[8,128,256]{2,1,0:T(8,128)(2,1)S(1)}, u32[]{:S(2)}, u32[]{:S(2)}) async-start(bf16[8,128,256]{2,1,0:T(8,128)(2,1)} %bitcast.1), calls=%async_computation | async-start | bytes 1048576 | tf_op jit(solution)/shard_map/all_to_all | solution.py:83
  17.4 17.0 %collective-permute-start.1 = (bf16[1024,256]{1,0:T(8,128)(2,1)}, bf16[1024,256]{1,0:T(8,128)(2,1)}, u32[]{:S(2)}, u32[]{:S(2)}) collective-permute-start(bf16[1024,256]{1,0:T(8,128)(2,1)} %get-tuple-element.23), channel_id=1, source_target_pairs={{0,4},{4,0},{8,12},{12,8},{1,5},{5,1},{9,13},{13,9},{2,6},{6,2},{1... | collective-permute-start | bytes 1572872 | tf_op jit(solution)/shard_map/ppermute | solution.py:38
  35.7 19.8 %collective-permute-start.2 = (bf16[1024,512]{1,0:T(8,128)(2,1)S(1)}, bf16[1024,512]{1,0:T(8,128)(2,1)}, u32[]{:S(2)}, u32[]{:S(2)}) collective-permute-start(bf16[1024,512]{1,0:T(8,128)(2,1)S(1)} %pad_maximum_fusion.6), channel_id=1, source_target_pairs={{4,8},{8,4},{5,9},{9,5},{6,10},{10,6},{7,11},{11,7},{20,24},{24,20... | collective-permute-start | bytes 3145736 | tf_op jit(solution)/shard_map/ppermute | solution.py:38
  37.3 20.8 %collective-permute-start.19 = (bf16[512,512]{1,0:T(8,128)(2,1)}, bf16[512,512]{1,0:T(8,128)(2,1)S(1)}, u32[]{:S(2)}, u32[]{:S(2)}) collective-permute-start(bf16[512,512]{1,0:T(8,128)(2,1)} %pad_maximum_fusion.18), channel_id=1, source_target_pairs={{0,1},{1,0},{2,3},{3,2},{4,5},{5,4},{6,7},{7,6},{8,9},{9,8},{10,11... | collective-permute-start | bytes 1572872 | tf_op jit(solution)/shard_map/ppermute | solution.py:34
  53.8 59.3 %collective-permute-start.7 = (bf16[1024,256]{1,0:T(8,128)(2,1)}, bf16[1024,256]{1,0:T(8,128)(2,1)S(1)}, u32[]{:S(2)}, u32[]{:S(2)}) collective-permute-start(bf16[1024,256]{1,0:T(8,128)(2,1)} %collective-permute-done.1), channel_id=1, source_target_pairs={{0,16},{16,0},{1,17},{17,1},{2,18},{18,2},{3,19},{19,3},{4,20},{20... | collective-permute-start | bytes 1572872 | tf_op jit(solution)/shard_map/ppermute | solution.py:34
  55.4 29.3 %collective-permute-start.3 = (bf16[1024,512]{1,0:T(8,128)(2,1)}, bf16[1024,512]{1,0:T(8,128)(2,1)S(1)}, u32[]{:S(2)}, u32[]{:S(2)}) collective-permute-start(bf16[1024,512]{1,0:T(8,128)(2,1)} %collective-permute-done.2), channel_id=1, source_target_pairs={{4,0},{8,12},{5,1},{9,13},{6,2},{10,14},{7,3},{11,15},{20,16},{24,... | collective-permute-start | bytes 3145736 | tf_op jit(solution)/shard_map/ppermute | solution.py:38
  61.1 46.2 %collective-permute-start.13 = (bf16[1024,512]{1,0:T(8,128)(2,1)S(1)}, bf16[1024,512]{1,0:T(8,128)(2,1)S(1)}, u32[]{:S(2)}, u32[]{:S(2)}) collective-permute-start(bf16[1024,512]{1,0:T(8,128)(2,1)S(1)} %collective-permute-done.12), channel_id=1, source_target_pairs={{4,0},{8,12},{5,1},{9,13},{6,2},{10,14},{7,3},{11,15},{20,16},{24,... | collective-permute-start | bytes 3145736 | tf_op jit(solution)/shard_map/ppermute | solution.py:38
  63.3 23.2 %collective-permute-start.20 = (f32[512,128]{1,0:T(8,128)S(1)}, f32[512,128]{1,0:T(8,128)S(1)}, u32[]{:S(2)}, u32[]{:S(2)}) collective-permute-start(f32[512,128]{1,0:T(8,128)S(1)} %fusion.81), channel_id=1, source_target_pairs={{0,2},{2,0},{1,3},{3,1},{4,6},{6,4},{5,7},{7,5},{8,10},{10,8},{9,1... | collective-permute-start | bytes 786440 | tf_op jit(solution)/shard_map/ppermute | solution.py:34
  72.9 36.0 %collective-permute-start.14 = (bf16[1024,512]{1,0:T(8,128)(2,1)S(1)}, bf16[1024,512]{1,0:T(8,128)(2,1)S(1)}, u32[]{:S(2)}, u32[]{:S(2)}) collective-permute-start(bf16[1024,512]{1,0:T(8,128)(2,1)S(1)} %constant_dynamic-update-slice_fusion), channel_id=1, source_target_pairs={{0,16},{16,0},{1,17},{17,1},{2,18},{18,2},{3,19},{19,3},{4,20},{20... | collective-permute-start | bytes 3145736 | tf_op jit(solution)/shard_map/ppermute | solution.py:34
  86.4 35.0 %collective-permute-start.8 = (bf16[1024,512]{1,0:T(8,128)(2,1)S(1)}, bf16[1024,512]{1,0:T(8,128)(2,1)S(1)}, u32[]{:S(2)}, u32[]{:S(2)}) collective-permute-start(bf16[1024,512]{1,0:T(8,128)(2,1)S(1)} %broadcast_select_fusion.1), channel_id=1, source_target_pairs={{0,16},{16,0},{1,17},{17,1},{2,18},{18,2},{3,19},{19,3},{4,20},{20... | collective-permute-start | bytes 3145736 | tf_op jit(solution)/shard_map/ppermute | solution.py:34
  94.0 97.4 %collective-permute-start.23 = (bf16[512,1024]{1,0:T(8,128)(2,1)}, bf16[512,1024]{1,0:T(8,128)(2,1)S(1)}, u32[]{:S(2)}, u32[]{:S(2)}) collective-permute-start(bf16[512,1024]{1,0:T(8,128)(2,1)} %pad_maximum_fusion.5), channel_id=1, source_target_pairs={{0,4},{12,8},{1,5},{13,9},{2,6},{14,10},{3,7},{15,11},{16,20},{28,... | collective-permute-start | bytes 3145736 | tf_op jit(solution)/shard_map/ppermute | solution.py:38
  107.2 90.4 %collective-permute-start.27 = (bf16[512,1024]{1,0:T(8,128)(2,1)}, bf16[512,1024]{1,0:T(8,128)(2,1)S(1)}, u32[]{:S(2)}, u32[]{:S(2)}) collective-permute-start(bf16[512,1024]{1,0:T(8,128)(2,1)} %pad_maximum_fusion.7), channel_id=1, source_target_pairs={{0,4},{12,8},{1,5},{13,9},{2,6},{14,10},{3,7},{15,11},{16,20},{28,... | collective-permute-start | bytes 3145736 | tf_op jit(solution)/shard_map/ppermute | solution.py:38
  108.9 33.1 %collective-permute-start.15 = (bf16[1024,512]{1,0:T(8,128)(2,1)S(1)}, bf16[1024,512]{1,0:T(8,128)(2,1)S(1)}, u32[]{:S(2)}, u32[]{:S(2)}) collective-permute-start(bf16[1024,512]{1,0:T(8,128)(2,1)S(1)} %broadcast_select_fusion), channel_id=1, source_target_pairs={{0,16},{16,0},{1,17},{17,1},{2,18},{18,2},{3,19},{19,3},{4,20},{20... | collective-permute-start | bytes 3145736 | tf_op jit(solution)/shard_map/ppermute | solution.py:34
  123.0 22.7 %collective-permute-start.9 = (f32[512,512]{1,0:T(8,128)S(1)}, f32[512,512]{1,0:T(8,128)S(1)}, u32[]{:S(2)}, u32[]{:S(2)}) collective-permute-start(f32[512,512]{1,0:T(8,128)S(1)} %slice_select_fusion), channel_id=1, source_target_pairs={{0,1},{1,0},{2,3},{3,2},{4,5},{5,4},{6,7},{7,6},{8,9},{9,8},{10,11... | collective-permute-start | bytes 3145736 | tf_op jit(solution)/shard_map/ppermute | solution.py:34
  160.9 53.5 %all-to-all-start.1 = ((bf16[4,2,128,256]{3,2,1,0:T(8,128)(2,1)}), bf16[4,2,128,256]{3,2,1,0:T(8,128)(2,1)}, u32[]{:S(2)}, u32[]{:S(2)}) async-start(bf16[4,2,128,256]{3,2,1,0:T(8,128)(2,1)} %bitcast.38), calls=%async_computation.1 | async-start | bytes 1048576 | tf_op jit(solution)/shard_map/all_to_all | solution.py:178
  182.3 31.3 %collective-permute-start.18 = (f32[256,512]{1,0:T(8,128)S(1)}, f32[256,512]{1,0:T(8,128)S(1)}, u32[]{:S(2)}, u32[]{:S(2)}) collective-permute-start(f32[256,512]{1,0:T(8,128)S(1)} %slice.222), channel_id=1, source_target_pairs={{0,2},{2,0},{1,3},{3,1},{4,6},{6,4},{5,7},{7,5},{8,10},{10,8},{9,1... | collective-permute-start | bytes 1572872 | tf_op jit(solution)/shard_map/ppermute | solution.py:34
  194.6 22.0 %collective-permute-start.25 = (bf16[1024,512]{1,0:T(8,128)(2,1)}, bf16[1024,512]{1,0:T(8,128)(2,1)}, u32[]{:S(2)}, u32[]{:S(2)}) collective-permute-start(bf16[1024,512]{1,0:T(8,128)(2,1)} %add_convert_fusion.1), channel_id=1, source_target_pairs={{4,8},{8,4},{5,9},{9,5},{6,10},{10,6},{7,11},{11,7},{20,24},{24,20... | collective-permute-start | bytes 3145736 | tf_op jit(solution)/shard_map/ppermute | solution.py:38
  200.6 32.8 %collective-permute-start.28 = (bf16[1024,512]{1,0:T(8,128)(2,1)}, bf16[1024,512]{1,0:T(8,128)(2,1)}, u32[]{:S(2)}, u32[]{:S(2)}) collective-permute-start(bf16[1024,512]{1,0:T(8,128)(2,1)} %add_convert_fusion), channel_id=1, source_target_pairs={{4,8},{8,4},{5,9},{9,5},{6,10},{10,6},{7,11},{11,7},{20,24},{24,20... | collective-permute-start | bytes 3145736 | tf_op jit(solution)/shard_map/ppermute | solution.py:38
  210.5 21.3 %collective-permute-start.22 = (bf16[256,1024]{1,0:T(8,128)(2,1)}, bf16[256,1024]{1,0:T(8,128)(2,1)}, u32[]{:S(2)}, u32[]{:S(2)}) collective-permute-start(bf16[256,1024]{1,0:T(8,128)(2,1)} %get-tuple-element.31), channel_id=1, source_target_pairs={{0,2},{2,0},{1,3},{3,1},{4,6},{6,4},{5,7},{7,5},{8,10},{10,8},{9,1... | collective-permute-start | bytes 1572872 | tf_op jit(solution)/shard_map/ppermute | solution.py:34
  215.7 46.4 %collective-permute-start.32 = (bf16[1,128,256]{2,1,0:T(8,128)(2,1)S(1)}, bf16[1,128,256]{2,1,0:T(8,128)(2,1)S(1)}, u32[]{:S(2)}, u32[]{:S(2)}) collective-permute-start(bf16[1,128,256]{2,1,0:T(8,128)(2,1)S(1)} %get-tuple-element.49), channel_id=1, source_target_pairs={{0,2},{2,0},{1,3},{3,1},{4,6},{6,4},{5,7},{7,5},{8,10},{10,8},{9,1... | collective-permute-start | bytes 196616 | tf_op jit(solution)/shard_map/ppermute | solution.py:34
  218.2 19.1 %collective-permute-start.26 = (bf16[1024,256]{1,0:T(8,128)(2,1)S(1)}, bf16[1024,256]{1,0:T(8,128)(2,1)S(1)}, u32[]{:S(2)}, u32[]{:S(2)}) collective-permute-start(bf16[1024,256]{1,0:T(8,128)(2,1)S(1)} %fusion.5), channel_id=1, source_target_pairs={{4,0},{8,12},{5,1},{9,13},{6,2},{10,14},{7,3},{11,15},{20,16},{24,... | collective-permute-start | bytes 1572872 | tf_op jit(solution)/shard_map/ppermute | solution.py:38
  236.0 22.4 %collective-permute-start.29 = (bf16[1024,256]{1,0:T(8,128)(2,1)S(1)}, bf16[1024,256]{1,0:T(8,128)(2,1)S(1)}, u32[]{:S(2)}, u32[]{:S(2)}) collective-permute-start(bf16[1024,256]{1,0:T(8,128)(2,1)S(1)} %fusion.7), channel_id=1, source_target_pairs={{4,0},{8,12},{5,1},{9,13},{6,2},{10,14},{7,3},{11,15},{20,16},{24,... | collective-permute-start | bytes 1572872 | tf_op jit(solution)/shard_map/ppermute | solution.py:38
  239.0 23.8 %collective-permute-start.30 = (bf16[1024,128]{1,0:T(8,128)(2,1)S(1)}, bf16[1024,128]{1,0:T(8,128)(2,1)S(1)}, u32[]{:S(2)}, u32[]{:S(2)}) collective-permute-start(bf16[1024,128]{1,0:T(8,128)(2,1)S(1)} %get-tuple-element.41), channel_id=1, source_target_pairs={{0,2},{2,0},{1,3},{3,1},{4,6},{6,4},{5,7},{7,5},{8,10},{10,8},{9,1... | collective-permute-start | bytes 786440 | tf_op jit(solution)/shard_map/ppermute | solution.py:34
  (62 other events, 809.5 us)

commit v3 on v0

v3 whole, which is shorter than its diff:
```python
import jax
import jax.numpy as jnp
from jax import lax
from jax.experimental import pallas as pl
from jax.experimental.pallas import tpu as pltpu
from jax.sharding import PartitionSpec as P

bf16 = jnp.bfloat16
f32 = jnp.float32


def contract_first(left, right):
    return lax.dot_general(
        left, right, (((0,), (0,)), ((), ())), preferred_element_type=f32
    )


def contract_final_axis(left, right):
    return lax.dot_general(
        left, right, (((1,), (1,)), ((), ())), preferred_element_type=f32
    )


def matmul(left, right):
    return jnp.dot(left, right, preferred_element_type=f32)


PAIR = [(0, 1), (1, 0)]
NEIGHBOURS = [(0, 1), (1, 0), (2, 3), (3, 2)]
MIDDLE = [(1, 2), (2, 1)]
OUTWARD = [(1, 0), (2, 3)]
INWARD = [(0, 1), (3, 2)]


def swap(value, axis):
    return lax.ppermute(value, axis, PAIR)


def along(value, pairs):
    return lax.ppermute(value, "fsdp", pairs)


def kernel_call(body, outs, *operands, scalars=None):
    specs = [pl.BlockSpec(memory_space=pltpu.VMEM)] * len(operands)
    if scalars is not None:
        operands = (scalars, *operands)
        specs = [pl.BlockSpec(memory_space=pltpu.SMEM), *specs]
    return pl.pallas_call(
        body,
        out_shape=list(outs),
        in_specs=specs,
        out_specs=[pl.BlockSpec(memory_space=pltpu.VMEM)] * len(outs),
        compiler_params=pltpu.CompilerParams(vmem_limit_bytes=28 * 2**20),
        cost_estimate=pl.CostEstimate(flops=0, bytes_accessed=0, transcendentals=0),
    )(*operands)


def spread_kernel(order, ids, value, out):
    size = value.shape[1]
    rows = value[...].astype(f32)
    for i in range(out.shape[1] // size):
        out[:, i * size : (i + 1) * size] = jnp.where(ids[...] == order[i], rows, 0.0).astype(bf16)


def back_kernel(ids, dy, up, out):
    size = out.shape[1]
    for i in range(0, up.shape[0] // size, 2):
        both = contract_final_axis(dy[...], up[i * size : (i + 2) * size, :])
        for j in (0, 1):
            part = jnp.where(ids[...] == i + j, both[:, j * size : (j + 1) * size], 0.0)
            out[...] = part if i + j == 0 else out[...] + part


def low_kernel(order, ids, x_mine, x_other, own, near, far, own_near_other, far_other, out):
    size = out.shape[1]
    wide = 2 * size
    mine = [own[...], near[...], far[:, :wide], far[:, wide:]]
    other = [
        own_near_other[:, :wide],
        own_near_other[:, wide:],
        far_other[:, :wide],
        far_other[:, wide:],
    ]
    for i in range(4):
        both = matmul(x_mine[...], mine[i]) + matmul(x_other[...], other[i])
        for j in (0, 1):
            part = jnp.where(ids[...] == order[2 * i + j], both[:, j * size : (j + 1) * size], 0.0)
            out[...] = part if i + j == 0 else out[...] + part


def dx_kernel(dy, back, own, near, far_a, far_b, *rest):
    *adapter, here, there = rest
    rows, width = here.shape
    cols = own.shape[1]
    tile = far_a.shape[0] // 2
    for t in range(width // tile):
        span = slice(t * tile, (t + 1) * tile)
        far = (far_a, far_b)[t // 2]
        part = slice((t % 2) * tile, (t % 2 + 1) * tile)
        base = contract_final_axis(dy[:, :cols], own[span, :])
        base += contract_final_axis(dy[:, cols : 2 * cols], near[span, :])
        base += contract_final_axis(dy[:, 2 * cols :], far[part, :])
        lora, start = 0.0, 0
        for piece in adapter:
            stop = start + piece.shape[1]
            lora += contract_final_axis(back[:, start:stop], piece[span, :])
            start = stop
        total = (base + lora.astype(bf16).astype(f32)).astype(bf16)
        here[:, span] = total[:rows]
        there[:, span] = total[rows:]


def y_kernel(flags, x_mine, x_other, *rest):
    mine, other, (keep, send) = rest[:4], rest[4:8], rest[8:]
    cols = mine[0].shape[1]
    half = mine[2].shape[0]

    def store(block, pair, place):
        kept = flags[0] == (1 if pair else 0)

        @pl.when(kept)
        def _():
            keep[place] = block

        @pl.when(jnp.logical_not(kept))
        def _():
            send[place] = block

    for i in (0, 1):
        block = matmul(x_mine[...], mine[i][...]) + matmul(x_other[...], other[i][...])
        store(block, True, (flags[1] + i) % 2)
    for i in (0, 1):
        span = slice(i * cols, (i + 1) * cols)
        block = 0.0
        for tokens, parts in ((x_mine, mine), (x_other, other)):
            block += matmul(tokens[:, :half], parts[2][:, span])
            block += matmul(tokens[:, half:], parts[3][:, span])
        store(block, False, (flags[2] + i) % 2)


def body_line(
    tokens,
    cotangent,
    frozen_value_weight,
    adapter_down_weight,
    adapter_up_weight,
    token_adapter,
    rank_step_count,
):
    rows, width = tokens.shape
    kv = cotangent.shape[1]
    cols = frozen_value_weight.shape[1]
    down = adapter_down_weight[0]
    up = adapter_up_weight[0]
    rank_limit = down.shape[1]
    wide = 2 * rank_limit
    quarter = width // 2
    eighth = quarter // 2
    part = eighth // 2
    kvq = kv // 2
    z, x = lax.axis_index("fsdp"), lax.axis_index("own")
    y, c = lax.axis_index("rep"), lax.axis_index("tp")
    first_pair = z < 2
    is_middle = (z == 1) | (z == 2)
    line = [z, z + 1 - 2 * (z % 2), jnp.where(first_pair, 2, 1), jnp.where(first_pair, 3, 0)]
    adapters = jnp.stack([2 * t + o for t in line for o in (x, 1 - x)]).astype(jnp.int32)
    number = adapters.shape[0]
    natural = jnp.arange(number, dtype=jnp.int32)

    latest = []

    def step(*values):
        if latest:
            values = lax.optimization_barrier((*values, latest[0]))[: len(values)]
        return values[0] if len(values) == 1 else values

    def done(value):
        latest[:] = [value]
        return value

    def cut(value, start, size, axis):
        return lax.dynamic_slice_in_dim(value, start, size, axis)

    def features(value, side, half, axis):
        return cut(value, side * quarter + half * eighth, eighth, axis)

    def spread(ids, value, order):
        out = jax.ShapeDtypeStruct((value.shape[0], number * rank_limit), bf16)
        return kernel_call(spread_kernel, [out], ids, value, scalars=order)[0]

    def join(*values):
        return jnp.concatenate(values, axis=1)

    weight_here = done(features(frozen_value_weight, x, y, 0))
    weight_near = along(weight_here, NEIGHBOURS)
    down_got = swap(done(features(step(down), 1 - x, y, 0)), "own")
    ids_row = token_adapter[:, 0].astype(bf16)[None, :]
    packet = done(
        jnp.concatenate(
            [step(cotangent), jnp.broadcast_to(jnp.concatenate([ids_row, ids_row], axis=1), (16, kv))]
        )
    )
    packet = swap(packet, "own")
    up_sent = jnp.broadcast_to(
        step(up).reshape(rank_limit, 2, kvq).transpose(1, 0, 2)[None], (4, 2, rank_limit, kvq)
    ).reshape(number, rank_limit, kvq)
    up_all = lax.all_to_all(
        done(up_sent), ("fsdp", "own"), split_axis=0, concat_axis=0, tiled=True
    ).reshape(number * rank_limit, kvq)
    sent = done(features(step(tokens), 1 - x, y, 1))
    x_there = [swap(sent, "own")]
    sent = done(features(step(tokens), 1 - x, 1 - y, 1))
    x_there.append(swap(sent, "own"))
    down_piece = done(join(features(down, x, y, 0), step(down_got)))
    down_near = along(down_piece, NEIGHBOURS)
    weight_near = step(weight_near)
    crossing = done(join(weight_here[:part], weight_near[:part]))
    crossed_a = along(crossing, MIDDLE)
    weight_near_other = swap(weight_near, "rep")

    packet = step(packet)
    dy_half = jnp.concatenate([cotangent, packet[:rows]], axis=0)
    ids = jnp.concatenate([token_adapter[:, 0], packet[rows, :rows].astype(jnp.int32)])[:, None]
    ranks = rank_limit // 8 * rank_step_count
    token_rank = jnp.sum(
        jnp.where(ids == natural[None, :], ranks[None, :], 0), axis=1, keepdims=True
    )
    token_scale = 16.0 / token_rank.astype(f32)
    keep = jnp.arange(rank_limit, dtype=jnp.int32)[None, :] < token_rank
    dy_quarter = cut(dy_half, x * kvq, kvq, 1)
    dy_tp = swap(done(dy_half), "tp")

    compact = jax.ShapeDtypeStruct((2 * rows, rank_limit), f32)

    def sum_own(total):
        return jnp.roll(swap(total, "own"), rows, axis=0)

    up_all, dy_quarter = step(up_all, dy_quarter)
    back_part = done(kernel_call(back_kernel, [compact], ids, dy_quarter, up_all)[0])
    back_tp = swap(back_part, "tp")
    near = step(down_near)
    down_near = near
    crossing = done(join(down_piece, near))
    down_crossed = along(crossing, MIDDLE)
    down_other = swap(crossing, "rep")
    back_part = done(back_part + step(back_tp))
    back_own = sum_own(back_part)
    crossing = done(join(step(weight_here)[part:], weight_near[part:]))
    crossed_b = along(crossing, MIDDLE)
    x_mine = done(jnp.concatenate([features(tokens, x, y, 1), step(x_there[0])], axis=0))
    x_in = [along(x_mine, INWARD)]
    back = back_part + step(back_own)
    back = (token_scale * jnp.where(keep, back, 0.0)).astype(bf16)
    back_in = done(join(back, jnp.broadcast_to(ids.astype(bf16), back.shape)))
    back_in = along(back_in, INWARD)
    x_other = done(
        jnp.concatenate([features(tokens, x, 1 - y, 1), step(x_there[1])], axis=0)
    )
    x_in.append(along(x_other, INWARD))
    x_both = [x_mine, x_other]
    outer_a = along(step(crossed_a), OUTWARD)
    back_wide = done(spread(ids, step(back), adapters))

    dy_tp = step(dy_tp)
    dy_full = jnp.where(c == 0, join(dy_half, dy_tp), join(dy_tp, dy_half))
    dy_line = done(join(*[cut(dy_full, t * cols, cols, 1) for t in line]))

    down_outer = along(step(down_crossed), OUTWARD)
    back_in, down_other = step(back_in, down_other)
    in_ids = back_in[:, rank_limit : rank_limit + 1].astype(jnp.int32)
    back_in_wide = done(spread(in_ids, back_in[:, :rank_limit], adapters))

    outer_a, crossed_a, weight_near_other = step(outer_a, crossed_a, weight_near_other)
    far_a = done(jnp.where(is_middle, crossed_a, outer_a))
    far_a_other = swap(far_a, "rep")

    def total(half, first, last):
        span = slice(first * wide, last * wide)
        return contract_first(x_both[half], back_wide[:, span])

    def total_in(half, first, last):
        span = slice(first * wide, last * wide)
        return contract_first(x_in[half], back_in_wide[:, span])

    def to_middle(half):
        x_in[half] = step(x_in[half])
        return along(
            done((total(half, 2, 4) + total_in(half, 2, 4)).astype(bf16)), MIDDLE
        )

    def to_end(half, crossed):
        crossed = step(crossed)
        sums = total(half, 1, 2) + crossed[:, wide:].astype(f32)
        return along(done(sums.astype(bf16)), OUTWARD)

    def finish(half, crossed, outer):
        outer = step(outer)
        grad = total(half, 0, 1) + total_in(half, 0, 1)
        grad = (grad + crossed[:, :wide].astype(f32) + outer.astype(f32)).astype(bf16)
        here, there = grad[:, :rank_limit], grad[:, rank_limit:]
        done(here)
        return here, swap(there, "own")

    middle = [to_middle(0)]
    outer_b = along(step(crossed_b), OUTWARD)
    down_outer, down_crossed, far_a_other = step(down_outer, down_crossed, far_a_other)
    down_far = done(jnp.where(is_middle, down_crossed, down_outer))
    down_far_other = swap(down_far, "rep")
    middle.append(to_middle(1))
    outer_b, crossed_b = step(outer_b, crossed_b)
    far_b = done(jnp.where(is_middle, crossed_b, outer_b))
    far_b_other = swap(far_b, "rep")

    half_grad = [jax.ShapeDtypeStruct((rows, eighth), bf16)] * 2
    dx_mine, dx_sent = kernel_call(
        dx_kernel,
        half_grad,
        step(dy_line),
        back_wide,
        weight_here,
        weight_near,
        far_a,
        far_b,
        down_piece,
        down_near,
        down_far,
    )
    dx_mine_got = swap(done(dx_sent), "own")
    outward = [to_end(0, middle[0])]

    down_far_other, dx_mine_got = step(down_far_other, dx_mine_got)
    low_part = done(
        kernel_call(
            low_kernel,
            [compact],
            ids,
            x_mine,
            x_other,
            down_piece,
            down_near,
            down_far,
            down_other,
            down_far_other,
            scalars=adapters,
        )[0]
    )
    low_tp = swap(low_part, "tp")
    low_part = done(low_part + step(low_tp))
    low_own = sum_own(low_part)
    weight_other = features(frozen_value_weight, x, 1 - y, 0)
    grads = [finish(0, middle[0], outward[0])]

    far_b_other = step(far_b_other)
    dx_other, dx_sent = kernel_call(
        dx_kernel,
        half_grad,
        step(dy_line),
        back_wide,
        weight_other,
        weight_near_other,
        far_a_other,
        far_b_other,
        down_other,
        down_far_other,
    )
    dx_other_got = swap(done(dx_sent), "own")
    outward.append(to_end(1, middle[1]))

    low_own, grad_got = step(low_own, grads[0][1])
    low = jnp.where(keep, low_part + low_own, 0.0).astype(bf16)
    low_wide = done(spread(ids, low, natural))
    up_part = done(contract_first(step(low_wide), dy_quarter).astype(bf16))
    up_got = lax.all_to_all(
        up_part.reshape(4, 2, rank_limit, kvq), "fsdp", split_axis=0, concat_axis=0, tiled=True
    )
    delta = done((token_scale * matmul(step(low_wide), up_all)).astype(bf16))

    flags = jnp.stack([(c == 0) == first_pair, z % 2 == 1, z >= 2]).astype(jnp.int32)
    y_keep, y_sent = kernel_call(
        y_kernel,
        [jax.ShapeDtypeStruct((2, 2 * rows, cols), f32)] * 2,
        step(x_mine),
        x_other,
        weight_here,
        weight_near,
        far_a,
        far_b,
        weight_other,
        weight_near_other,
        far_a_other,
        far_b_other,
        scalars=flags,
    )
    y_got = swap(done(y_sent), "tp")
    chosen = jnp.arange(2)[:, None, None] == x
    y_got, dx_other_got = step(y_got, dx_other_got)
    y_sum = y_keep + y_got + jnp.where(chosen, delta[None].astype(f32), 0.0)
    y_got = swap(done(y_sum[:, rows:].astype(bf16)), "own")
    grads.append(finish(1, middle[1], outward[1]))

    up_sum = jnp.sum(step(up_got).astype(f32), axis=0)
    own_ranks = cut(ranks, 2 * z, 2, 0).astype(f32)
    up_sum = done(((16.0 / own_ranks)[:, None, None] * up_sum).astype(bf16))
    up_mine = cut(up_sum, x, 1, 0)
    up_theirs = swap(cut(up_sum, 1 - x, 1, 0), "own")

    def in_place(here, there, axis):
        blocks = jnp.concatenate(here + there, axis=axis)
        size = blocks.shape[axis] // 4
        return jnp.concatenate(
            [
                cut(blocks, (2 * ((i + x) % 2) + (j + y) % 2) * size, size, axis)
                for i in (0, 1)
                for j in (0, 1)
            ],
            axis=axis,
        )

    input_grad = done(in_place([step(dx_mine), dx_other], [dx_mine_got, dx_other_got], 1))
    y_sum = y_sum[:, :rows] + step(y_got).astype(f32)
    projected = done(join(y_sum[0], y_sum[1]).astype(bf16))
    second = step(grads[1][1])
    down_gradient = done(in_place([grads[0][0], grads[1][0]], [grad_got, second], 0)[None])
    up_theirs = step(up_theirs)
    up_gradient = jnp.where(
        x == 0,
        jnp.concatenate([up_mine, up_theirs], axis=2),
        jnp.concatenate([up_theirs, up_mine], axis=2),
    )
    return (projected, input_grad, down_gradient, up_gradient)


def body_routed(
    tokens,
    cotangent,
    frozen_value_weight,
    adapter_down_weight,
    adapter_up_weight,
    token_adapter,
    rank_step_count,
):
    rows, width_halved = tokens.shape
    half_kv = cotangent.shape[1]
    owning_adapters = lax.axis_size(("fsdp", "own"))
    greatest_rank = 3 * rows // (2 * owning_adapters)
    ids = token_adapter[:, 0]
    table = (ids[:, None] == jnp.arange(owning_adapters, dtype=jnp.int32)[None, :]).astype(
        f32
    )
    order = jnp.arange(rows, dtype=jnp.int32)
    earlier = (order[:, None] > order[None, :]).astype(f32)
    before = jnp.dot(earlier, table, precision=lax.Precision.HIGHEST)
    place = jnp.sum(before * table, axis=1).astype(jnp.int32)
    slot = ids * greatest_rank + place
    source_rows = jnp.full((owning_adapters * greatest_rank,), rows, jnp.int32).at[slot].set(order)
    padded_x = jnp.concatenate([tokens, jnp.zeros((1, width_halved), bf16)], axis=0)
    padded_dy = jnp.concatenate([cotangent, jnp.zeros((1, half_kv), bf16)], axis=0)
    send_x = jnp.take(padded_x, source_rows, axis=0)
    send_dy = jnp.take(padded_dy, source_rows, axis=0)
    recv_x, recv_dy = (
        lax.all_to_all(
            send_x.reshape(owning_adapters, greatest_rank, width_halved),
            ("fsdp", "own"),
            split_axis=0,
            concat_axis=0,
            tiled=True,
        ),
        lax.all_to_all(
            send_dy.reshape(owning_adapters, greatest_rank, half_kv),
            ("fsdp", "own"),
            split_axis=0,
            concat_axis=0,
            tiled=True,
        ),
    )
    flat_x = recv_x.reshape(owning_adapters * greatest_rank, width_halved)
    flat_dy = recv_dy.reshape(owning_adapters * greatest_rank, half_kv)
    dy_full = lax.all_gather(cotangent, "tp", axis=1, tiled=True)
    whole = lax.all_gather(frozen_value_weight, "fsdp", axis=1, tiled=True)
    partial_y = jnp.dot(tokens, whole, preferred_element_type=f32)
    base_dx = contract_final_axis(dy_full, whole)
    base_y = lax.psum_scatter(partial_y, "tp", scatter_dimension=1, tiled=True)
    down_matrix = adapter_down_weight[0]
    up_matrix = adapter_up_weight[0]
    part_low = jnp.dot(flat_x, down_matrix, preferred_element_type=f32)
    part_back = contract_final_axis(flat_dy, up_matrix)
    low_sum, back_sum = lax.psum((part_low, part_back), "tp")
    width_rank = down_matrix.shape[1]
    rank = width_rank // 8 * rank_step_count[lax.axis_index(("fsdp", "own"))]
    keep = jnp.arange(width_rank, dtype=jnp.int32)[None, :] < rank
    scale = 16.0 / rank.astype(f32)
    low = jnp.where(keep, low_sum, 0.0).astype(bf16)
    backward_pass = (scale * jnp.where(keep, back_sum, 0.0)).astype(bf16)
    delta = (scale * jnp.dot(low, up_matrix, preferred_element_type=f32)).astype(
        bf16
    )
    adapter_input_gradient = contract_final_axis(backward_pass, down_matrix).astype(bf16)
    down_gradient = contract_first(flat_x, backward_pass).astype(bf16)[None]
    up_gradient = (scale * contract_first(low, flat_dy)).astype(bf16)[None]
    home_delta, home_dx = (
        lax.all_to_all(
            delta.reshape(owning_adapters, greatest_rank, half_kv),
            ("fsdp", "own"),
            split_axis=0,
            concat_axis=0,
            tiled=True,
        ),
        lax.all_to_all(
            adapter_input_gradient.reshape(owning_adapters, greatest_rank, width_halved),
            ("fsdp", "own"),
            split_axis=0,
            concat_axis=0,
            tiled=True,
        ),
    )
    adapter_delta_rows = jnp.take(
        home_delta.reshape(owning_adapters * greatest_rank, half_kv), slot, axis=0
    )
    input_gradient_rows = jnp.take(
        home_dx.reshape(owning_adapters * greatest_rank, width_halved), slot, axis=0
    )
    projected = (base_y + adapter_delta_rows.astype(f32)).astype(bf16)
    input_grad = (base_dx + input_gradient_rows.astype(f32)).astype(bf16)
    return (projected, input_grad, down_gradient, up_gradient)


def solution(mesh):
    placed = (
        P(("rep", "fsdp", "own"), "tp"),
        P(("rep", "fsdp", "own"), "tp"),
        P("tp", "fsdp"),
        P(("fsdp", "own"), "tp", None),
        P(("fsdp", "own"), None, "tp"),
        P(("rep", "fsdp", "own"), None),
        P(),
    )
    line = mesh.shape["fsdp"] == 4 and mesh.shape["own"] == 2 and mesh.shape["rep"] == 2
    return jax.shard_map(
        body_line if line else body_routed,
        mesh=mesh,
        in_specs=placed,
        out_specs=(
            P(("rep", "fsdp", "own"), "tp"),
            P(("rep", "fsdp", "own"), "tp"),
            P(("rep", "fsdp", "own"), "tp", None),
            P(("rep", "fsdp", "own"), None, "tp"),
        ),
        check_vma=False,
    )
```

time: 352 us -> 241 us (0.68)
  waiting for transfers between devices: 240 us -> 89.2 us
  starting transfers between devices: 13.9 us -> 61.3 us
  blocking collectives: 25.6 us -> 0 us
  Pallas kernels: 0 us -> 24.6 us
  between operations: 16.4 us -> 1.74 us
  other arithmetic: 7.14 us -> 16 us
  matrix products: 28.8 us -> 21.5 us
  local copies, waits for them, and re-layouts: 19 us -> 24.9 us
    all_to_all x3 -> x2, waiting for transfers between devices: 190 us -> 1.25 us  [the longest x1 1.25 us: body_line(): lax.all_to_all(up_part.reshape(4, 2, rank_limit, kvq), 'fsdp', split_axis...]
    ppermute x0 -> x36, waiting for transfers between devices: none -> 88 us  [the longest x15 53 us: along(): return lax.ppermute(value, 'fsdp', pairs)]
    ppermute x0 -> x36, starting transfers between devices: none -> 51.5 us  [the longest x15 30.1 us: along(): return lax.ppermute(value, 'fsdp', pairs)]
    all_gather x1 -> x0, waiting for transfers between devices: 49.2 us -> none  [body(): whole = lax.all_gather(frozen_value_weight, 'fsdp', axis=1, tiled=True)]
    pallas_call x0 -> x8, Pallas kernels: none -> 24.6 us  [kernel_call(): pl.pallas_call(body, out_shape=list(outs), in_specs=specs, out_specs=[pl....]
    dot_general x7 -> x1, matrix products: 24 us -> 1.24 us  [matmul(): return jnp.dot(left, right, preferred_element_type=f32)]
    all_to_all x1 -> x0, blocking collectives: 19.1 us -> none  [body(): lax.all_to_all(send_dy.reshape(owning_adapters, greatest_rank, half_kv),...]
    dot_general x2 -> x11, matrix products: 4.79 us -> 20.3 us  [contract_first(): lax.dot_general(left, right, (((0,), (0,)), ((), ())), preferred_element_...]
  transfers between devices with their start and end apart: 6 -> 38, of which waited for: 4 -> 14; matrix products, arithmetic and copies ran while one was open for 13% -> 20% of each run, Pallas kernels for 0% -> 7%
where the time goes in v3:
time: 241 us; the launch traced here: 239 us
  waiting for transfers between devices  89.2 us (37%)
  starting transfers between devices  61.3 us (25%)
  local copies, waits for them, and re-layouts  24.9 us (10%)
  Pallas kernels  24.6 us (10%)
  matrix products  21.5 us (9%)
  other arithmetic  16 us (7%)
    ppermute x15, waiting for transfers between devices, along(): return lax.ppermute(value, 'fsdp', pairs)  53 us
    ppermute x21, waiting for transfers between devices, swap(): return lax.ppermute(value, axis, PAIR)  35 us
    ppermute x15, starting transfers between devices, along(): return lax.ppermute(value, 'fsdp', pairs)  30.1 us
    pallas_call x8, Pallas kernels, kernel_call(): pl.pallas_call(body, out_shape=list(outs), in_specs=specs, out_specs=[pl....  24.6 us
    ppermute x21, starting transfers between devices, swap(): return lax.ppermute(value, axis, PAIR)  21.3 us
    dot_general x11, matrix products, contract_first(): lax.dot_general(left, right, (((0,), (0,)), ((), ())), preferred_element_...  20.3 us
    unnamed x123, local copies, waits for them, and re-layouts  9.26 us
    dynamic_slice x10, local copies, waits for them, and re-layouts, cut(): return lax.dynamic_slice_in_dim(value, start, size, axis)  8.66 us
  transfers between devices with their start and end apart: 38, of which 14 were waited for; matrix products, arithmetic and copies ran while one was open for 20% of the time, Pallas kernels for 7%

profile of v3, /device:TPU:0, one launch (start us, length us, event | category | flops | bytes accessed | tf_op | source)
XLA Modules:
  0.0 239.2 jit_solution(6280529400800856483)
XLA Ops:
  2.9 3.0 %collective-permute-start.2 = (bf16[1024,256]{1,0:T(8,128)(2,1)S(1)}, bf16[1024,256]{1,0:T(8,128)(2,1)}, u32[]{:S(2)}, u32[]{:S(2)}) collective-permute-start(bf16[1024,256]{1,0:T(8,128)(2,1)S(1)} %get-tuple-element.77.own.rest_0_), channel_id=1, source_target_pairs={{0,4},{4,0},{8,12},{12,8},{1,5},{5,1},{9,13},{13,9},{2,6},{6,2},{1... | collective-permute-start | bytes 1572872 | tf_op jit(solution)/shard_map/ppermute | solution.py:40
  9.7 4.8 %all-to-all-start = ((bf16[8,128,256]{2,1,0:T(8,128)(2,1)}), bf16[8,128,256]{2,1,0:T(8,128)(2,1)S(1)}, u32[]{:S(2)}, u32[]{:S(2)}) async-start(bf16[8,128,256]{2,1,0:T(8,128)(2,1)} %bitcast.7), calls=%async_computation | async-start | bytes 1048576 | tf_op jit(solution)/shard_map/all_to_all | solution.py:207
  31.9 5.6 %collective-permute-done.5.rest_1_.near = bf16[1024,256]{1,0:T(8,128)(2,1)S(1)} collective-permute-done((bf16[1024,256]{1,0:T(8,128)(2,1)S(1)}, bf16[1024,256]{1,0:T(8,128)(2,1)S(1)}, u32[]{:S(2)}, u32[]{:S(2)}) %collective-permute-start.5) | collective-permute-done | bytes 524320 | tf_op jit(solution)/shard_map/ppermute | solution.py:40
  44.2 9.2 %collective-permute-done.7 = f32[512,128]{1,0:T(8,128)S(1)} collective-permute-done((f32[512,128]{1,0:T(8,128)S(1)}, f32[512,128]{1,0:T(8,128)S(1)}, u32[]{:S(2)}, u32[]{:S(2)}) %collective-permute-start.7) | collective-permute-done | bytes 262176 | tf_op jit(solution)/shard_map/ppermute | solution.py:36
  58.5 6.3 %collective-permute-start.17 = (bf16[512,1024]{1,0:T(8,128)(2,1)S(1)}, bf16[512,1024]{1,0:T(8,128)(2,1)S(1)}, u32[]{:S(2)}, u32[]{:S(2)}) collective-permute-start(bf16[512,1024]{1,0:T(8,128)(2,1)S(1)} %pad_maximum_fusion.2.x_mine), channel_id=1, source_target_pairs={{0,4},{12,8},{1,5},{13,9},{2,6},{14,10},{3,7},{15,11},{16,20},{28,... | collective-permute-start | bytes 3145736 | tf_op jit(solution)/shard_map/ppermute | solution.py:40
  68.0 23.0 %collective-permute-done.14 = bf16[512,256]{1,0:T(8,128)(2,1)S(1)} collective-permute-done((bf16[512,256]{1,0:T(8,128)(2,1)S(1)}, bf16[512,256]{1,0:T(8,128)(2,1)S(1)}, u32[]{:S(2)}, u32[]{:S(2)}) %collective-permute-start.14) | collective-permute-done | bytes 262176 | tf_op jit(solution)/shard_map/ppermute | solution.py:40
  98.3 6.2 %collective-permute-start.21 = (bf16[512,1024]{1,0:T(8,128)(2,1)S(1)}, bf16[512,1024]{1,0:T(8,128)(2,1)S(1)}, u32[]{:S(2)}, u32[]{:S(2)}) collective-permute-start(bf16[512,1024]{1,0:T(8,128)(2,1)S(1)} %pad_maximum_fusion.3.x_other), channel_id=1, source_target_pairs={{0,4},{12,8},{1,5},{13,9},{2,6},{14,10},{3,7},{15,11},{16,20},{28,... | collective-permute-start | bytes 3145736 | tf_op jit(solution)/shard_map/ppermute | solution.py:40
  104.5 3.2 %collective-permute-done.12 = bf16[512,512]{1,0:T(8,128)(2,1)S(1)} collective-permute-done((bf16[512,512]{1,0:T(8,128)(2,1)S(1)}, bf16[512,512]{1,0:T(8,128)(2,1)S(1)}, u32[]{:S(2)}, u32[]{:S(2)}) %collective-permute-start.12) | collective-permute-done | bytes 524320 | tf_op jit(solution)/shard_map/ppermute | solution.py:40
  113.5 3.6 %collective-permute-done.16.far_a.rest_6_ = bf16[512,512]{1,0:T(8,128)(2,1)S(1)} collective-permute-done((bf16[512,512]{1,0:T(8,128)(2,1)S(1)}, bf16[512,512]{1,0:T(8,128)(2,1)S(1)}, u32[]{:S(2)}, u32[]{:S(2)}) %collective-permute-start.16) | collective-permute-done | bytes 524320 | tf_op jit(solution)/shard_map/ppermute | solution.py:36
  117.9 12.4 %collective-permute-done.10 = bf16[1024,512]{1,0:T(8,128)(2,1)S(1)} collective-permute-done((bf16[1024,512]{1,0:T(8,128)(2,1)S(1)}, bf16[1024,512]{1,0:T(8,128)(2,1)S(1)}, u32[]{:S(2)}, u32[]{:S(2)}) %collective-permute-start.10) | collective-permute-done | bytes 1048608 | tf_op jit(solution)/shard_map/ppermute | solution.py:40
  133.6 4.2 %collective-permute-done.20 = bf16[512,512]{1,0:T(8,128)(2,1)S(1)} collective-permute-done((bf16[512,512]{1,0:T(8,128)(2,1)S(1)}, bf16[512,512]{1,0:T(8,128)(2,1)S(1)}, u32[]{:S(2)}, u32[]{:S(2)}) %collective-permute-start.20) | collective-permute-done | bytes 524320 | tf_op jit(solution)/shard_map/ppermute | solution.py:40
  137.8 4.8 %shard_map.105 = (bf16[256,1024]{1,0:T(8,128)(2,1)S(1)}, bf16[256,1024]{1,0:T(8,128)(2,1)}) custom-call(bf16[512,1024]{1,0:T(8,128)(2,1)S(1)} %pad_maximum_fusion.4.dy, bf16[512,1024]{1,0:T(8,128)(2,1)S(1)} %shard_map.103.back, bf16[1024,256]{1,0:T(8,128)(2,1)S(1)} %copy-done.6, bf16[1024,256]{1,0:T(8,128)(2,1)} %collective-permute-done.2.near.rest_1_, ...), custom_call_target="tpu_custom_call" | custom-call | tf_op jit(solution)/shard_map/pallas_call | solution.py:48
  144.9 2.7 %add_convert_fusion.3 = bf16[1024,256]{1,0:T(8,128)(2,1)} fusion(bf16[1024,512]{1,0:T(8,128)(2,1)S(1)} %collective-permute-done.23, bf16[512,1024]{1,0:T(8,128)(2,1)S(1)} %shard_map.103.back, bf16[256,1024]{1,0:T(8,128)(2,1)} %collective-permute-done, bf16[256,1024]{1,0:T(8,128)(2,1)S(1)} %copy-done.47), kind=kOutput, calls=%fused_computation.24 | convolution fusion | flops 271319040 | bytes 2359296 | tf_op jit(solution)/shard_map/dot_general | solution.py:13
  150.5 3.4 %collective-permute-done.22 = bf16[256,1024]{1,0:T(8,128)(2,1)} collective-permute-done((bf16[256,1024]{1,0:T(8,128)(2,1)}, bf16[256,1024]{1,0:T(8,128)(2,1)}, u32[]{:S(2)}, u32[]{:S(2)}) %collective-permute-start.22) | collective-permute-done | bytes 524320 | tf_op jit(solution)/shard_map/ppermute | solution.py:36
  157.2 4.0 %shard_map.106 = f32[512,128]{1,0:T(8,128)S(1)} custom-call(s32[8]{0:T(128)S(1)} %stack.51.order, s32[512,1]{1,0:T(8,128)S(1)} %copy.18.ids, bf16[512,1024]{1,0:T(8,128)(2,1)S(1)} %pad_maximum_fusion.2.x_mine, bf16[512,1024]{1,0:T(8,128)(2,1)S(1)} %pad_maximum_fusion.3.x_other, bf16[1024,256]{1,0:T(8,128)(2,1)S(1)} %copy-done.17, ...), custom_call_target="tpu_custom_call" | custom-call | tf_op jit(solution)/shard_map/pallas_call | solution.py:48
  167.7 9.6 %collective-permute-done.29.far_b.rest_7_ = bf16[512,512]{1,0:T(8,128)(2,1)S(1)} collective-permute-done((bf16[512,512]{1,0:T(8,128)(2,1)S(1)}, bf16[512,512]{1,0:T(8,128)(2,1)S(1)}, u32[]{:S(2)}, u32[]{:S(2)}) %collective-permute-start.29) | collective-permute-done | bytes 524320 | tf_op jit(solution)/shard_map/ppermute | solution.py:36
  177.4 4.5 %shard_map.107 = (bf16[256,1024]{1,0:T(8,128)(2,1)S(1)}, bf16[256,1024]{1,0:T(8,128)(2,1)}) custom-call(bf16[512,1024]{1,0:T(8,128)(2,1)S(1)} %copy-done.3, bf16[512,1024]{1,0:T(8,128)(2,1)S(1)} %shard_map.103.back, bf16[1024,256]{1,0:T(8,128)(2,1)S(1)} %copy-done.12, bf16[1024,256]{1,0:T(8,128)(2,1)S(1)} %copy-done.25, bf16[512,512]{1,0:T(8,128)(2,1)S(1)} %copy-done.27, ...), custom_call_target="tpu_custom_call" | custom-call | tf_op jit(solution)/shard_map/pallas_call | solution.py:48
  183.3 2.5 %add_convert_fusion.2 = bf16[1024,256]{1,0:T(8,128)(2,1)} fusion(bf16[1024,512]{1,0:T(8,128)(2,1)} %collective-permute-done.28, bf16[512,1024]{1,0:T(8,128)(2,1)S(1)} %shard_map.103.back, bf16[256,1024]{1,0:T(8,128)(2,1)} %collective-permute-done.6, bf16[256,1024]{1,0:T(8,128)(2,1)S(1)} %copy-done.46), kind=kOutput, calls=%fused_computation.23 | convolution fusion | flops 271319040 | bytes 2359296 | tf_op jit(solution)/shard_map/dot_general | solution.py:13
  185.9 3.7 %collective-permute-done.27 = bf16[1024,128]{1,0:T(8,128)(2,1)S(1)} collective-permute-done((bf16[1024,128]{1,0:T(8,128)(2,1)S(1)}, bf16[1024,128]{1,0:T(8,128)(2,1)S(1)}, u32[]{:S(2)}, u32[]{:S(2)}) %collective-permute-start.27) | collective-permute-done | bytes 262176 | tf_op jit(solution)/shard_map/ppermute | solution.py:36
  193.5 7.3 %shard_map.109 = (f32[2,512,256]{2,1,0:T(8,128)S(1)}, f32[2,512,256]{2,1,0:T(8,128)}) custom-call(s32[3]{0:T(128)S(1)} %add_convert_fusion.4.flags, bf16[512,1024]{1,0:T(8,128)(2,1)S(1)} %pad_maximum_fusion.2.x_mine, bf16[512,1024]{1,0:T(8,128)(2,1)S(1)} %pad_maximum_fusion.3.x_other, bf16[1024,256]{1,0:T(8,128)(2,1)S(1)} %copy-done.7, ...), custom_call_target="tpu_custom_call" | custom-call | tf_op jit(solution)/shard_map/pallas_call | solution.py:48
  204.7 2.7 %fusion.17 = f32[1024,256]{1,0:T(8,128)} fusion(bf16[512,1024]{1,0:T(8,128)(2,1)S(1)} %shard_map.103.back, bf16[256,1024]{1,0:T(8,128)(2,1)} %collective-permute-done.6, bf16[256,1024]{1,0:T(8,128)(2,1)} %get-tuple-element.132), kind=kOutput, calls=%fused_computation.56 | convolution fusion | flops 270532608 | bytes 2359296 | tf_op jit(solution)/shard_map/dot_general | solution.py:13
  207.4 5.0 %all-to-all-start.1 = ((bf16[4,2,128,256]{3,2,1,0:T(8,128)(2,1)}), bf16[4,2,128,256]{3,2,1,0:T(8,128)(2,1)S(1)}, u32[]{:S(2)}, u32[]{:S(2)}) async-start(bf16[4,2,128,256]{3,2,1,0:T(8,128)(2,1)} %bitcast.41), calls=%async_computation.1 | async-start | bytes 1048576 | tf_op jit(solution)/shard_map/all_to_all | solution.py:373
  212.4 4.0 %collective-permute-done.31 = bf16[256,1024]{1,0:T(8,128)(2,1)} collective-permute-done((bf16[256,1024]{1,0:T(8,128)(2,1)}, bf16[256,1024]{1,0:T(8,128)(2,1)}, u32[]{:S(2)}, u32[]{:S(2)}) %collective-permute-start.31) | collective-permute-done | bytes 524320 | tf_op jit(solution)/shard_map/ppermute | solution.py:36
  219.6 4.6 %collective-permute-done.33 = bf16[1024,256]{1,0:T(8,128)(2,1)} collective-permute-done((bf16[1024,256]{1,0:T(8,128)(2,1)}, bf16[1024,256]{1,0:T(8,128)(2,1)}, u32[]{:S(2)}, u32[]{:S(2)}) %collective-permute-start.33) | collective-permute-done | bytes 524320 | tf_op jit(solution)/shard_map/ppermute | solution.py:40
  (266 shorter events, 97.4 us)
Async XLA Ops:
  2.9 23.0 %collective-permute-start.2 = (bf16[1024,256]{1,0:T(8,128)(2,1)S(1)}, bf16[1024,256]{1,0:T(8,128)(2,1)}, u32[]{:S(2)}, u32[]{:S(2)}) collective-permute-start(bf16[1024,256]{1,0:T(8,128)(2,1)S(1)} %get-tuple-element.77.own.rest_0_), channel_id=1, source_target_pairs={{0,4},{4,0},{8,12},{12,8},{1,5},{5,1},{9,13},{13,9},{2,6},{6,2},{1... | collective-permute-start | bytes 1572872 | tf_op jit(solution)/shard_map/ppermute | solution.py:40
  5.9 17.8 %collective-permute-start.3 = (bf16[1024,128]{1,0:T(8,128)(2,1)S(1)}, bf16[1024,128]{1,0:T(8,128)(2,1)S(1)}, u32[]{:S(2)}, u32[]{:S(2)}) collective-permute-start(bf16[1024,128]{1,0:T(8,128)(2,1)S(1)} %constant_dynamic-slice_fusion.19), channel_id=1, source_target_pairs={{0,2},{2,0},{1,3},{3,1},{4,6},{6,4},{5,7},{7,5},{8,10},{10,8},{9,1... | collective-permute-start | bytes 786440 | tf_op jit(solution)/shard_map/ppermute | solution.py:36
  8.3 19.5 %collective-permute-start.1 = (bf16[272,512]{1,0:T(8,128)(2,1)}, bf16[272,512]{1,0:T(8,128)(2,1)}, u32[]{:S(2)}, u32[]{:S(2)}) collective-permute-start(bf16[272,512]{1,0:T(8,128)(2,1)} %pad_maximum_fusion.10), channel_id=1, source_target_pairs={{0,2},{2,0},{1,3},{3,1},{4,6},{6,4},{5,7},{7,5},{8,10},{10,8},{9,1... | collective-permute-start | bytes 835592 | tf_op jit(solution)/shard_map/ppermute | solution.py:36
  9.7 21.0 %all-to-all-start = ((bf16[8,128,256]{2,1,0:T(8,128)(2,1)}), bf16[8,128,256]{2,1,0:T(8,128)(2,1)S(1)}, u32[]{:S(2)}, u32[]{:S(2)}) async-start(bf16[8,128,256]{2,1,0:T(8,128)(2,1)} %bitcast.7), calls=%async_computation | async-start | bytes 1048576 | tf_op jit(solution)/shard_map/all_to_all | solution.py:207
  16.4 25.0 %collective-permute-start = (bf16[256,1024]{1,0:T(8,128)(2,1)}, bf16[256,1024]{1,0:T(8,128)(2,1)}, u32[]{:S(2)}, u32[]{:S(2)}) collective-permute-start(bf16[256,1024]{1,0:T(8,128)(2,1)} %constant_dynamic-slice_fusion.18), channel_id=1, source_target_pairs={{0,2},{2,0},{1,3},{3,1},{4,6},{6,4},{5,7},{7,5},{8,10},{10,8},{9,1... | collective-permute-start | bytes 1572872 | tf_op jit(solution)/shard_map/ppermute | solution.py:36
  20.3 34.3 %collective-permute-start.6 = (bf16[256,1024]{1,0:T(8,128)(2,1)}, bf16[256,1024]{1,0:T(8,128)(2,1)}, u32[]{:S(2)}, u32[]{:S(2)}) collective-permute-start(bf16[256,1024]{1,0:T(8,128)(2,1)} %constant_dynamic-slice_fusion.17), channel_id=1, source_target_pairs={{0,2},{2,0},{1,3},{3,1},{4,6},{6,4},{5,7},{7,5},{8,10},{10,8},{9,1... | collective-permute-start | bytes 1572872 | tf_op jit(solution)/shard_map/ppermute | solution.py:36
  30.6 27.9 %collective-permute-start.9 = (bf16[512,512]{1,0:T(8,128)(2,1)}, bf16[512,512]{1,0:T(8,128)(2,1)}, u32[]{:S(2)}, u32[]{:S(2)}) collective-permute-start(bf16[512,512]{1,0:T(8,128)(2,1)} %pad_maximum_fusion.6), channel_id=1, source_target_pairs={{0,1},{1,0},{2,3},{3,2},{4,5},{5,4},{6,7},{7,6},{8,9},{9,8},{10,11... | collective-permute-start | bytes 1572872 | tf_op jit(solution)/shard_map/ppermute | solution.py:36
  37.5 27.3 %collective-permute-start.11 = (bf16[512,512]{1,0:T(8,128)(2,1)}, bf16[512,512]{1,0:T(8,128)(2,1)S(1)}, u32[]{:S(2)}, u32[]{:S(2)}) collective-permute-start(bf16[512,512]{1,0:T(8,128)(2,1)} %pad_maximum_fusion.8), channel_id=1, source_target_pairs={{4,8},{8,4},{5,9},{9,5},{6,10},{10,6},{7,11},{11,7},{20,24},{24,20... | collective-permute-start | bytes 1572872 | tf_op jit(solution)/shard_map/ppermute | solution.py:40
  41.4 52.7 %collective-permute-start.15 = (bf16[1024,512]{1,0:T(8,128)(2,1)S(1)}, bf16[1024,512]{1,0:T(8,128)(2,1)S(1)}, u32[]{:S(2)}, u32[]{:S(2)}) collective-permute-start(bf16[1024,512]{1,0:T(8,128)(2,1)S(1)} %pad_maximum_fusion.1), channel_id=1, source_target_pairs={{0,16},{16,0},{1,17},{17,1},{2,18},{18,2},{3,19},{19,3},{4,20},{20... | collective-permute-start | bytes 3145736 | tf_op jit(solution)/shard_map/ppermute | solution.py:36
  53.4 42.3 %collective-permute-start.8 = (bf16[1024,512]{1,0:T(8,128)(2,1)S(1)}, bf16[1024,512]{1,0:T(8,128)(2,1)S(1)}, u32[]{:S(2)}, u32[]{:S(2)}) collective-permute-start(bf16[1024,512]{1,0:T(8,128)(2,1)S(1)} %pad_maximum_fusion.1), channel_id=1, source_target_pairs={{4,8},{8,4},{5,9},{9,5},{6,10},{10,6},{7,11},{11,7},{20,24},{24,20... | collective-permute-start | bytes 3145736 | tf_op jit(solution)/shard_map/ppermute | solution.py:40
  54.6 43.7 %collective-permute-start.13 = (bf16[1024,256]{1,0:T(8,128)(2,1)}, bf16[1024,256]{1,0:T(8,128)(2,1)S(1)}, u32[]{:S(2)}, u32[]{:S(2)}) collective-permute-start(bf16[1024,256]{1,0:T(8,128)(2,1)} %collective-permute-done.2.near.rest_1_), channel_id=1, source_target_pairs={{0,16},{16,0},{1,17},{17,1},{2,18},{18,2},{3,19},{19,3},{4,20},{20... | collective-permute-start | bytes 1572872 | tf_op jit(solution)/shard_map/ppermute | solution.py:36
  58.5 49.9 %collective-permute-start.17 = (bf16[512,1024]{1,0:T(8,128)(2,1)S(1)}, bf16[512,1024]{1,0:T(8,128)(2,1)S(1)}, u32[]{:S(2)}, u32[]{:S(2)}) collective-permute-start(bf16[512,1024]{1,0:T(8,128)(2,1)S(1)} %pad_maximum_fusion.2.x_mine), channel_id=1, source_target_pairs={{0,4},{12,8},{1,5},{13,9},{2,6},{14,10},{3,7},{15,11},{16,20},{28,... | collective-permute-start | bytes 3145736 | tf_op jit(solution)/shard_map/ppermute | solution.py:40
  64.8 26.2 %collective-permute-start.14 = (bf16[512,256]{1,0:T(8,128)(2,1)S(1)}, bf16[512,256]{1,0:T(8,128)(2,1)S(1)}, u32[]{:S(2)}, u32[]{:S(2)}) collective-permute-start(bf16[512,256]{1,0:T(8,128)(2,1)S(1)} %pad_maximum_fusion.12), channel_id=1, source_target_pairs={{0,4},{12,8},{1,5},{13,9},{2,6},{14,10},{3,7},{15,11},{16,20},{28,... | collective-permute-start | bytes 786440 | tf_op jit(solution)/shard_map/ppermute | solution.py:40
  95.8 34.4 %collective-permute-start.10 = (bf16[1024,512]{1,0:T(8,128)(2,1)S(1)}, bf16[1024,512]{1,0:T(8,128)(2,1)S(1)}, u32[]{:S(2)}, u32[]{:S(2)}) collective-permute-start(bf16[1024,512]{1,0:T(8,128)(2,1)S(1)} %collective-permute-done.8), channel_id=1, source_target_pairs={{4,0},{8,12},{5,1},{9,13},{6,2},{10,14},{7,3},{11,15},{20,16},{24,... | collective-permute-start | bytes 3145736 | tf_op jit(solution)/shard_map/ppermute | solution.py:40
  98.3 33.5 %collective-permute-start.21 = (bf16[512,1024]{1,0:T(8,128)(2,1)S(1)}, bf16[512,1024]{1,0:T(8,128)(2,1)S(1)}, u32[]{:S(2)}, u32[]{:S(2)}) collective-permute-start(bf16[512,1024]{1,0:T(8,128)(2,1)S(1)} %pad_maximum_fusion.3.x_other), channel_id=1, source_target_pairs={{0,4},{12,8},{1,5},{13,9},{2,6},{14,10},{3,7},{15,11},{16,20},{28,... | collective-permute-start | bytes 3145736 | tf_op jit(solution)/shard_map/ppermute | solution.py:40
  109.5 35.4 %collective-permute-start.23 = (bf16[1024,512]{1,0:T(8,128)(2,1)S(1)}, bf16[1024,512]{1,0:T(8,128)(2,1)S(1)}, u32[]{:S(2)}, u32[]{:S(2)}) collective-permute-start(bf16[1024,512]{1,0:T(8,128)(2,1)S(1)} %add_convert_fusion.1), channel_id=1, source_target_pairs={{4,8},{8,4},{5,9},{9,5},{6,10},{10,6},{7,11},{11,7},{20,24},{24,20... | collective-permute-start | bytes 3145736 | tf_op jit(solution)/shard_map/ppermute | solution.py:40
  112.0 25.7 %collective-permute-start.20 = (bf16[512,512]{1,0:T(8,128)(2,1)S(1)}, bf16[512,512]{1,0:T(8,128)(2,1)S(1)}, u32[]{:S(2)}, u32[]{:S(2)}) collective-permute-start(bf16[512,512]{1,0:T(8,128)(2,1)S(1)} %collective-permute-done.19), channel_id=1, source_target_pairs={{4,0},{8,12},{5,1},{9,13},{6,2},{10,14},{7,3},{11,15},{20,16},{24,... | collective-permute-start | bytes 1572872 | tf_op jit(solution)/shard_map/ppermute | solution.py:40
  131.3 22.6 %collective-permute-start.18 = (bf16[1024,512]{1,0:T(8,128)(2,1)}, bf16[1024,512]{1,0:T(8,128)(2,1)}, u32[]{:S(2)}, u32[]{:S(2)}) collective-permute-start(bf16[1024,512]{1,0:T(8,128)(2,1)} %broadcast_select_fusion.rest_2_.far), channel_id=1, source_target_pairs={{0,16},{16,0},{1,17},{17,1},{2,18},{18,2},{3,19},{19,3},{4,20},{20... | collective-permute-start | bytes 3145736 | tf_op jit(solution)/shard_map/ppermute | solution.py:36
  147.6 17.7 %collective-permute-start.26 = (bf16[1024,256]{1,0:T(8,128)(2,1)}, bf16[1024,256]{1,0:T(8,128)(2,1)}, u32[]{:S(2)}, u32[]{:S(2)}) collective-permute-start(bf16[1024,256]{1,0:T(8,128)(2,1)} %add_convert_fusion.3), channel_id=1, source_target_pairs={{4,0},{8,12},{5,1},{9,13},{6,2},{10,14},{7,3},{11,15},{20,16},{24,... | collective-permute-start | bytes 1572872 | tf_op jit(solution)/shard_map/ppermute | solution.py:40
  148.9 33.0 %collective-permute-start.28 = (bf16[1024,512]{1,0:T(8,128)(2,1)}, bf16[1024,512]{1,0:T(8,128)(2,1)}, u32[]{:S(2)}, u32[]{:S(2)}) collective-permute-start(bf16[1024,512]{1,0:T(8,128)(2,1)} %add_convert_fusion), channel_id=1, source_target_pairs={{4,8},{8,4},{5,9},{9,5},{6,10},{10,6},{7,11},{11,7},{20,24},{24,20... | collective-permute-start | bytes 3145736 | tf_op jit(solution)/shard_map/ppermute | solution.py:40
  163.7 22.1 %collective-permute-start.25 = (f32[512,128]{1,0:T(8,128)S(1)}, f32[512,128]{1,0:T(8,128)S(1)}, u32[]{:S(2)}, u32[]{:S(2)}) collective-permute-start(f32[512,128]{1,0:T(8,128)S(1)} %add.236), channel_id=1, source_target_pairs={{0,2},{2,0},{1,3},{3,1},{4,6},{6,4},{5,7},{7,5},{8,10},{10,8},{9,1... | collective-permute-start | bytes 786440 | tf_op jit(solution)/shard_map/ppermute | solution.py:36
  203.3 20.9 %collective-permute-start.33 = (bf16[1024,256]{1,0:T(8,128)(2,1)}, bf16[1024,256]{1,0:T(8,128)(2,1)}, u32[]{:S(2)}, u32[]{:S(2)}) collective-permute-start(bf16[1024,256]{1,0:T(8,128)(2,1)} %add_convert_fusion.2), channel_id=1, source_target_pairs={{4,0},{8,12},{5,1},{9,13},{6,2},{10,14},{7,3},{11,15},{20,16},{24,... | collective-permute-start | bytes 1572872 | tf_op jit(solution)/shard_map/ppermute | solution.py:40
  207.4 20.6 %all-to-all-start.1 = ((bf16[4,2,128,256]{3,2,1,0:T(8,128)(2,1)}), bf16[4,2,128,256]{3,2,1,0:T(8,128)(2,1)S(1)}, u32[]{:S(2)}, u32[]{:S(2)}) async-start(bf16[4,2,128,256]{3,2,1,0:T(8,128)(2,1)} %bitcast.41), calls=%async_computation.1 | async-start | bytes 1048576 | tf_op jit(solution)/shard_map/all_to_all | solution.py:373
  218.0 17.0 %collective-permute-start.32 = (bf16[2,256,256]{2,1,0:T(8,128)(2,1)S(1)}, bf16[2,256,256]{2,1,0:T(8,128)(2,1)S(1)}, u32[]{:S(2)}, u32[]{:S(2)}) collective-permute-start(bf16[2,256,256]{2,1,0:T(8,128)(2,1)S(1)} %slice.181), channel_id=1, source_target_pairs={{0,2},{2,0},{1,3},{3,1},{4,6},{6,4},{5,7},{7,5},{8,10},{10,8},{9,1... | collective-permute-start | bytes 786440 | tf_op jit(solution)/shard_map/ppermute | solution.py:36
  (74 other events, 671.6 us)

commit v4 on v3

v4 whole, which is shorter than its diff:
```python
import jax
import jax.numpy as jnp
from jax import lax
from jax.experimental import pallas as pl
from jax.experimental.pallas import tpu as pltpu
from jax.sharding import PartitionSpec as P

bf16 = jnp.bfloat16
f32 = jnp.float32


def contract_first(left, right):
    return lax.dot_general(
        left, right, (((0,), (0,)), ((), ())), preferred_element_type=f32
    )


def contract_final_axis(left, right):
    return lax.dot_general(
        left, right, (((1,), (1,)), ((), ())), preferred_element_type=f32
    )


def matmul(left, right):
    return jnp.dot(left, right, preferred_element_type=f32)


PAIR = [(0, 1), (1, 0)]
NEIGHBOURS = [(0, 1), (1, 0), (2, 3), (3, 2)]
MIDDLE = [(1, 2), (2, 1)]
OUTWARD = [(1, 0), (2, 3)]
INWARD = [(0, 1), (3, 2)]


def swap(value, axis):
    return lax.ppermute(value, axis, PAIR)


def along(value, pairs):
    return lax.ppermute(value, "fsdp", pairs)


def kernel_call(body, outs, *operands, scalars=None, scratch=(), space=pltpu.VMEM):
    specs = [pl.BlockSpec(memory_space=space)] * len(operands)
    if scalars is not None:
        operands = (scalars, *operands)
        specs = [pl.BlockSpec(memory_space=pltpu.SMEM), *specs]
    return pl.pallas_call(
        body,
        out_shape=list(outs),
        in_specs=specs,
        out_specs=[pl.BlockSpec(memory_space=space)] * len(outs),
        scratch_shapes=list(scratch),
        compiler_params=pltpu.CompilerParams(vmem_limit_bytes=28 * 2**20),
        cost_estimate=pl.CostEstimate(flops=0, bytes_accessed=0, transcendentals=0),
    )(*operands)


def copy_call(plan, outs, scalars, *operands):
    count = len(plan(None, [None] * len(operands), [None] * len(outs)))

    def body(numbers, *refs):
        sems = refs[-1]
        pairs = plan(numbers, refs[: len(operands)], refs[len(operands) : -1])
        copies = [pltpu.make_async_copy(a, b, sems.at[i]) for i, (a, b) in enumerate(pairs)]
        for copy in copies:
            copy.start()
        for copy in copies:
            copy.wait()

    return kernel_call(
        body,
        outs,
        *operands,
        scalars=scalars,
        scratch=[pltpu.SemaphoreType.DMA((count,))],
        space=pl.ANY,
    )


def view(ref, *spans):
    if ref is None:
        return None
    index = tuple(
        pl.ds(start if isinstance(start, int) else pl.multiple_of(start, 128), size)
        for start, size in spans
    )
    return ref.at[index]


def at(numbers, i):
    return None if numbers is None else numbers[i]


def ranks_of(ranks, ids):
    total = jnp.zeros(ids.shape, f32)
    for a in range(ranks.shape[0]):
        total = jnp.where(ids == a, ranks[a].astype(f32), total)
    return total


def kept(ids, ranks, value):
    rank = ranks_of(ranks, ids)
    column = lax.broadcasted_iota(jnp.int32, value.shape, 1).astype(f32)
    return jnp.where(column < rank, value, 0.0), 16.0 / rank


def roll_rows(value):
    half = value.shape[0] // 2
    return jnp.concatenate([value[half:], value[:half]], axis=0)


def back_kernel(ids, dy, up, out):
    size = out.shape[1]
    token = ids[...].astype(f32)
    for i in range(0, up.shape[0] // size, 2):
        both = contract_final_axis(dy[...], up[i * size : (i + 2) * size, :])
        for j in (0, 1):
            part = jnp.where(token == i + j, both[:, j * size : (j + 1) * size], 0.0)
            out[...] = part if i + j == 0 else out[...] + part


def spread_into(out, token, value, order):
    size = value.shape[1]
    for i in range(out.shape[1] // size):
        a = order[i].astype(f32)
        out[:, i * size : (i + 1) * size] = jnp.where(token == a, value, 0.0).astype(bf16)


def back_end_kernel(numbers, ids, part, got, wide, sent):
    token = ids[...].astype(f32)
    count = numbers.shape[0] // 2
    ranks, order = [numbers[i] for i in range(count)], [numbers[count + i] for i in range(count)]
    value, scale = kept(token, jnp.stack(ranks), part[...] + roll_rows(got[...]))
    value = (scale * value).astype(bf16)
    size = value.shape[1]
    sent[:, :size] = value
    sent[:, size:] = ids[...]
    spread_into(wide, token, value.astype(f32), order)


def spread_in_kernel(numbers, packet, wide):
    size = packet.shape[1] // 2
    count = numbers.shape[0] // 2
    order = [numbers[count + i] for i in range(count)]
    spread_into(wide, packet[:, size:].astype(f32), packet[:, :size].astype(f32), order)


def low_kernel(numbers, ids, x_mine, x_other, own, near, far, own_near_other, far_other, out):
    size = out.shape[1]
    wide = 2 * size
    token = ids[...].astype(f32)
    mine = [own[...], near[...], far[:, :wide], far[:, wide:]]
    other = [
        own_near_other[:, :wide],
        own_near_other[:, wide:],
        far_other[:, :wide],
        far_other[:, wide:],
    ]
    for i in range(4):
        both = matmul(x_mine[...], mine[i]) + matmul(x_other[...], other[i])
        for j in (0, 1):
            place = numbers[numbers.shape[0] // 2 + 2 * i + j].astype(f32)
            part = jnp.where(token == place, both[:, j * size : (j + 1) * size], 0.0)
            out[...] = part if i + j == 0 else out[...] + part


def low_end_kernel(numbers, ids, part, got, up, wide, delta):
    token = ids[...].astype(f32)
    count = numbers.shape[0] // 2
    ranks = jnp.stack([numbers[i] for i in range(count)])
    value, scale = kept(token, ranks, part[...] + roll_rows(got[...]))
    value = value.astype(bf16).astype(f32)
    spread_into(wide, token, value, [jnp.int32(i) for i in range(count)])
    delta[...] = (scale[:, :1] * matmul(wide[...], up[...])).astype(bf16)


def dx_kernel(dy, back, own, near, far, *rest):
    *adapter, here, there = rest
    rows, width = here.shape
    cols = own.shape[1]
    tile = min(cols, width)
    for t in range(width // tile):
        span = slice(t * tile, (t + 1) * tile)
        base = contract_final_axis(dy[:, :cols], own[span, :])
        base += contract_final_axis(dy[:, cols : 2 * cols], near[span, :])
        base += contract_final_axis(dy[:, 2 * cols :], far[span, :])
        lora, start = 0.0, 0
        for piece in adapter:
            stop = start + piece.shape[1]
            lora += contract_final_axis(back[:, start:stop], piece[span, :])
            start = stop
        total = (base + lora.astype(bf16).astype(f32)).astype(bf16)
        here[:, span] = total[:rows]
        there[:, span] = total[rows:]


def y_kernel(flags, tokens, own, near, far, *rest):
    *before, keep, send = rest
    cols = own.shape[1]

    def store(pair, first, part):
        mine = flags[0] == (1 if pair else 0)
        for i in (0, 1):
            place = (first + i) % 2
            block = matmul(tokens[...], part(i))

            @pl.when(mine)
            def _():
                keep[place] = block + before[0][place] if before else block

            @pl.when(jnp.logical_not(mine))
            def _():
                send[place] = block + before[1][place] if before else block

    store(True, flags[1], lambda i: (own, near)[i][...])
    store(False, flags[2], lambda i: far[:, i * cols : (i + 1) * cols])


def y_sum_kernel(flags, keep, got, delta, here, there):
    rows = here.shape[1]
    for i in (0, 1):
        added = jnp.where(flags[3] == i, delta[...].astype(f32), 0.0)
        total = keep[i] + got[i] + added
        here[i] = total[:rows]
        there[i] = total[rows:].astype(bf16)


def y_end_kernel(here, got, out):
    cols = here.shape[2]
    for i in (0, 1):
        out[:, i * cols : (i + 1) * cols] = (here[i] + got[i].astype(f32)).astype(bf16)


def body_line(
    tokens,
    cotangent,
    frozen_value_weight,
    adapter_down_weight,
    adapter_up_weight,
    token_adapter,
    rank_step_count,
):
    rows, width = tokens.shape
    kv = cotangent.shape[1]
    cols = frozen_value_weight.shape[1]
    down = adapter_down_weight[0]
    up = adapter_up_weight[0]
    size = down.shape[1]
    wide = 2 * size
    quarter = width // 2
    eighth = quarter // 2
    kvq = kv // 2
    both = 2 * rows
    z, x = lax.axis_index("fsdp"), lax.axis_index("own")
    y, c = lax.axis_index("rep"), lax.axis_index("tp")
    first_pair = z < 2
    is_middle = (z == 1) | (z == 2)
    line = [z, z + 1 - 2 * (z % 2), jnp.where(first_pair, 2, 1), jnp.where(first_pair, 3, 0)]
    adapters = jnp.stack([2 * t + o for t in line for o in (x, 1 - x)]).astype(jnp.int32)
    number = adapters.shape[0]
    starts = jnp.stack(
        [side * quarter + half * eighth for side in (x, 1 - x) for half in (y, 1 - y)]
    ).astype(jnp.int32)
    ranks = size // 8 * rank_step_count
    numbers = jnp.concatenate([ranks, adapters])
    flags = jnp.stack([(c == 0) == first_pair, z % 2 == 1, z >= 2, x == 1]).astype(jnp.int32)

    latest = []

    def step(*values):
        if latest:
            values = lax.optimization_barrier((*values, latest[0]))[: len(values)]
        return values[0] if len(values) == 1 else values

    def done(value):
        latest[:] = [value]
        return value

    def like(*shape, kind=bf16):
        return jax.ShapeDtypeStruct(shape, kind)

    def cut(value, start, length, axis):
        return lax.dynamic_slice_in_dim(value, start, length, axis)

    def join(*values):
        return jnp.concatenate(values, axis=1)

    def rows_at(i, value, length):
        out = like(length, value.shape[1])
        return copy_call(
            lambda n, a, o: [(view(a[0], (at(n, i), length), (0, value.shape[1])), o[0])],
            [out],
            starts,
            value,
        )[0]

    def columns_at(i, value):
        out = like(value.shape[0], eighth)
        return copy_call(
            lambda n, a, o: [(view(a[0], (0, value.shape[0]), (at(n, i), eighth)), o[0])],
            [out],
            starts,
            value,
        )[0]

    def side_by_side(*values):
        widths = [v.shape[1] for v in values]
        length = values[0].shape[0]
        return copy_call(
            lambda n, a, o: [
                (a[i], view(o[0], (0, length), (sum(widths[:i]), widths[i])))
                for i in range(len(values))
            ],
            [like(length, sum(widths))],
            starts,
            *values,
        )[0]

    def tokens_of(i, value, got):
        return copy_call(
            lambda n, a, o: [
                (view(a[0], (0, rows), (at(n, i), eighth)), view(o[0], (0, rows), (0, eighth))),
                (a[1], view(o[0], (rows, rows), (0, eighth))),
            ],
            [like(both, eighth)],
            starts,
            value,
            got,
        )[0]

    down_got = swap(done(rows_at(2, down, eighth)), "own")
    ids_here = jnp.broadcast_to(token_adapter.astype(bf16), (rows, size))
    packet = swap(done(join(step(cotangent), ids_here)), "own")
    x_got = [swap(done(columns_at(2, step(tokens))), "own")]
    x_got.append(swap(done(columns_at(3, step(tokens))), "own"))
    down_piece = done(
        copy_call(
            lambda n, a, o: [
                (view(a[0], (at(n, 0), eighth), (0, size)), view(o[0], (0, eighth), (0, size))),
                (a[1], view(o[0], (0, eighth), (size, size))),
            ],
            [like(eighth, wide)],
            starts,
            down,
            step(down_got),
        )[0]
    )
    down_near = along(down_piece, NEIGHBOURS)
    up_sent = jnp.broadcast_to(
        step(up).reshape(size, 2, kvq).transpose(1, 0, 2)[None], (4, 2, size, kvq)
    ).reshape(number, size, kvq)
    up_all = lax.all_to_all(
        done(up_sent), ("fsdp", "own"), split_axis=0, concat_axis=0, tiled=True
    ).reshape(number * size, kvq)
    weight_here = done(rows_at(0, step(frozen_value_weight), eighth))
    weight_near = along(weight_here, NEIGHBOURS)

    packet = step(packet)
    dy_half = jnp.concatenate([cotangent, packet[:, :kv]], axis=0)
    ids = jnp.concatenate([ids_here, packet[:, kv:]], axis=0)
    dy_quarter = cut(dy_half, x * kvq, kvq, 1)
    dy_tp = swap(done(dy_half), "tp")

    down_near = step(down_near)
    crossing = done(side_by_side(down_piece, down_near))
    down_crossed = along(crossing, MIDDLE)
    down_other = swap(crossing, "rep")

    compact = like(both, size, kind=f32)
    up_all, dy_quarter = step(up_all, dy_quarter)
    back_part = done(kernel_call(back_kernel, [compact], ids, dy_quarter, up_all)[0])
    back_tp = swap(back_part, "tp")
    x_mine = done(tokens_of(0, tokens, step(x_got[0])))
    back_part = done(back_part + step(back_tp))
    back_got = swap(back_part, "own")
    x_in = [along(x_mine, INWARD)]
    weight_near = step(weight_near)
    crossing = done(side_by_side(weight_here, weight_near))
    weight_crossed = along(crossing, MIDDLE)
    weight_near_other = swap(weight_near, "rep")
    back_wide, back_sent = kernel_call(
        back_end_kernel,
        [like(both, number * size), like(both, wide)],
        ids,
        back_part,
        step(back_got),
        scalars=numbers,
    )
    back_in = along(done(back_sent), INWARD)
    x_other = done(tokens_of(1, tokens, step(x_got[1])))
    x_in.append(along(x_other, INWARD))
    x_both = [x_mine, x_other]

    dy_tp = step(dy_tp)
    dy_full = jnp.where(c == 0, join(dy_half, dy_tp), join(dy_tp, dy_half))
    dy_line = done(join(*[cut(dy_full, t * cols, cols, 1) for t in line]))
    weight_other = done(rows_at(1, step(frozen_value_weight), eighth))

    def total(half, first, last):
        return contract_first(x_both[half], back_wide[:, first * wide : last * wide])

    def total_in(half, first, last):
        return contract_first(x_in[half], back_in_wide[:, first * wide : last * wide])

    def to_middle(half, *others):
        x_in[half], *_ = step(x_in[half], back_in_wide, *others)
        sums = total(half, 2, 4) + total_in(half, 2, 4)
        return along(done(sums.astype(bf16)), MIDDLE)

    def to_end(half, crossed):
        crossed = step(crossed)
        sums = total(half, 1, 2) + crossed[:, wide:].astype(f32)
        return along(done(sums.astype(bf16)), OUTWARD)

    def finish(half, crossed, outer, *others):
        outer, *_ = step(outer, x_mine, *others)
        grad = total(half, 0, 1) + total_in(half, 0, 1)
        grad = (grad + crossed[:, :wide].astype(f32) + outer.astype(f32)).astype(bf16)
        here, there = grad[:, :size], grad[:, size:]
        done(here)
        return here, swap(there, "own")

    down_crossed, back_in, down_other = step(down_crossed, back_in, down_other)
    down_outer = along(down_crossed, OUTWARD)
    back_in_wide = done(
        kernel_call(
            spread_in_kernel, [like(both, number * size)], back_in, scalars=numbers
        )[0]
    )
    middle = [to_middle(0)]
    weight_crossed, weight_near_other = step(weight_crossed, weight_near_other)
    weight_outer = along(weight_crossed, OUTWARD)
    down_outer = step(down_outer)
    down_far = done(jnp.where(is_middle, down_crossed, down_outer))
    down_far_other = swap(down_far, "rep")
    middle.append(to_middle(1))
    outward = [to_end(0, middle[0])]
    weight_outer = step(weight_outer)
    weight_far = done(jnp.where(is_middle, weight_crossed, weight_outer))
    weight_far_other = swap(weight_far, "rep")

    low_part = done(
        kernel_call(
            low_kernel,
            [compact],
            ids,
            x_mine,
            x_other,
            down_piece,
            down_near,
            down_far,
            down_other,
            step(down_far_other),
            scalars=numbers,
        )[0]
    )
    low_tp = swap(low_part, "tp")
    half_grad = [like(rows, eighth)] * 2
    dx_mine, dx_sent = kernel_call(
        dx_kernel,
        half_grad,
        step(dy_line),
        back_wide,
        weight_here,
        weight_near,
        weight_far,
        down_piece,
        down_near,
        down_far,
    )
    done(dx_mine)
    low_part = done(low_part + step(low_tp))
    low_got = swap(low_part, "own")
    dx_mine_got = swap(dx_sent, "own")
    grads = [finish(0, middle[0], outward[0])]
    blocks = [like(2, both, cols, kind=f32)] * 2
    y_first = kernel_call(
        y_kernel, blocks, step(x_mine), weight_here, weight_near, weight_far, scalars=flags
    )
    done(y_first[0])
    low_wide, delta = kernel_call(
        low_end_kernel,
        [like(both, number * size), like(both, kvq)],
        ids,
        low_part,
        step(low_got),
        up_all,
        scalars=numbers,
    )
    up_part = done(contract_first(low_wide, dy_quarter).astype(bf16))
    up_got = lax.all_to_all(
        up_part.reshape(4, 2, size, kvq), "fsdp", split_axis=0, concat_axis=0, tiled=True
    )
    outward.append(to_end(1, middle[1]))

    weight_far_other, dx_mine_got = step(weight_far_other, dx_mine_got)
    y_keep, y_sent = kernel_call(
        y_kernel,
        blocks,
        x_other,
        weight_other,
        weight_near_other,
        weight_far_other,
        *y_first,
        scalars=flags,
    )
    y_got = swap(done(y_sent), "tp")
    dx_other, dx_sent = kernel_call(
        dx_kernel,
        half_grad,
        step(dy_line),
        back_wide,
        weight_other,
        weight_near_other,
        weight_far_other,
        down_other,
        down_far_other,
    )
    dx_other_got = swap(done(dx_sent), "own")
    y_here, y_sent = kernel_call(
        y_sum_kernel,
        [like(2, rows, cols, kind=f32), like(2, rows, cols)],
        y_keep,
        step(y_got),
        delta,
        scalars=flags,
    )
    y_got = swap(done(y_sent), "own")
    grads.append(finish(1, middle[1], outward[1], grads[0][1]))

    up_sum = jnp.sum(step(up_got).astype(f32), axis=0)
    own_ranks = cut(ranks, 2 * z, 2, 0).astype(f32)
    up_sum = done(((16.0 / own_ranks)[:, None, None] * up_sum).astype(bf16))
    up_mine = cut(up_sum, x, 1, 0)
    up_theirs = swap(cut(up_sum, 1 - x, 1, 0), "own")

    def in_place(axis, out, *pieces):
        def plan(n, a, o):
            spans = [[(0, length) for length in out.shape] for _ in range(4)]
            for i in range(4):
                spans[i][axis] = (at(n, i), eighth)
            return [(a[i], view(o[0], *spans[i])) for i in range(4)]

        return copy_call(plan, [out], starts, *pieces)[0]

    dx_other_got, _ = step(dx_other_got, dx_mine)
    input_grad = done(
        in_place(1, like(rows, width), dx_mine, dx_other, dx_mine_got, dx_other_got)
    )
    projected = done(kernel_call(y_end_kernel, [like(rows, kv)], y_here, step(y_got))[0])
    down_gradient = done(
        in_place(
            0, like(width, size), grads[0][0], grads[1][0], grads[0][1], step(grads[1][1])
        )[None]
    )
    up_theirs = step(up_theirs)
    up_gradient = jnp.where(
        x == 0,
        jnp.concatenate([up_mine, up_theirs], axis=2),
        jnp.concatenate([up_theirs, up_mine], axis=2),
    )
    return (projected, input_grad, down_gradient, up_gradient)


def body_routed(
    tokens,
    cotangent,
    frozen_value_weight,
    adapter_down_weight,
    adapter_up_weight,
    token_adapter,
    rank_step_count,
):
    rows, width_halved = tokens.shape
    half_kv = cotangent.shape[1]
    owning_adapters = lax.axis_size(("fsdp", "own"))
    greatest_rank = 3 * rows // (2 * owning_adapters)
    ids = token_adapter[:, 0]
    table = (ids[:, None] == jnp.arange(owning_adapters, dtype=jnp.int32)[None, :]).astype(
        f32
    )
    order = jnp.arange(rows, dtype=jnp.int32)
    earlier = (order[:, None] > order[None, :]).astype(f32)
    before = jnp.dot(earlier, table, precision=lax.Precision.HIGHEST)
    place = jnp.sum(before * table, axis=1).astype(jnp.int32)
    slot = ids * greatest_rank + place
    source_rows = jnp.full((owning_adapters * greatest_rank,), rows, jnp.int32).at[slot].set(order)
    padded_x = jnp.concatenate([tokens, jnp.zeros((1, width_halved), bf16)], axis=0)
    padded_dy = jnp.concatenate([cotangent, jnp.zeros((1, half_kv), bf16)], axis=0)
    send_x = jnp.take(padded_x, source_rows, axis=0)
    send_dy = jnp.take(padded_dy, source_rows, axis=0)
    recv_x, recv_dy = (
        lax.all_to_all(
            send_x.reshape(owning_adapters, greatest_rank, width_halved),
            ("fsdp", "own"),
            split_axis=0,
            concat_axis=0,
            tiled=True,
        ),
        lax.all_to_all(
            send_dy.reshape(owning_adapters, greatest_rank, half_kv),
            ("fsdp", "own"),
            split_axis=0,
            concat_axis=0,
            tiled=True,
        ),
    )
    flat_x = recv_x.reshape(owning_adapters * greatest_rank, width_halved)
    flat_dy = recv_dy.reshape(owning_adapters * greatest_rank, half_kv)
    dy_full = lax.all_gather(cotangent, "tp", axis=1, tiled=True)
    whole = lax.all_gather(frozen_value_weight, "fsdp", axis=1, tiled=True)
    partial_y = jnp.dot(tokens, whole, preferred_element_type=f32)
    base_dx = contract_final_axis(dy_full, whole)
    base_y = lax.psum_scatter(partial_y, "tp", scatter_dimension=1, tiled=True)
    down_matrix = adapter_down_weight[0]
    up_matrix = adapter_up_weight[0]
    part_low = jnp.dot(flat_x, down_matrix, preferred_element_type=f32)
    part_back = contract_final_axis(flat_dy, up_matrix)
    low_sum, back_sum = lax.psum((part_low, part_back), "tp")
    width_rank = down_matrix.shape[1]
    rank = width_rank // 8 * rank_step_count[lax.axis_index(("fsdp", "own"))]
    keep = jnp.arange(width_rank, dtype=jnp.int32)[None, :] < rank
    scale = 16.0 / rank.astype(f32)
    low = jnp.where(keep, low_sum, 0.0).astype(bf16)
    backward_pass = (scale * jnp.where(keep, back_sum, 0.0)).astype(bf16)
    delta = (scale * jnp.dot(low, up_matrix, preferred_element_type=f32)).astype(
        bf16
    )
    adapter_input_gradient = contract_final_axis(backward_pass, down_matrix).astype(bf16)
    down_gradient = contract_first(flat_x, backward_pass).astype(bf16)[None]
    up_gradient = (scale * contract_first(low, flat_dy)).astype(bf16)[None]
    home_delta, home_dx = (
        lax.all_to_all(
            delta.reshape(owning_adapters, greatest_rank, half_kv),
            ("fsdp", "own"),
            split_axis=0,
            concat_axis=0,
            tiled=True,
        ),
        lax.all_to_all(
            adapter_input_gradient.reshape(owning_adapters, greatest_rank, width_halved),
            ("fsdp", "own"),
            split_axis=0,
            concat_axis=0,
            tiled=True,
        ),
    )
    adapter_delta_rows = jnp.take(
        home_delta.reshape(owning_adapters * greatest_rank, half_kv), slot, axis=0
    )
    input_gradient_rows = jnp.take(
        home_dx.reshape(owning_adapters * greatest_rank, width_halved), slot, axis=0
    )
    projected = (base_y + adapter_delta_rows.astype(f32)).astype(bf16)
    input_grad = (base_dx + input_gradient_rows.astype(f32)).astype(bf16)
    return (projected, input_grad, down_gradient, up_gradient)


def solution(mesh):
    placed = (
        P(("rep", "fsdp", "own"), "tp"),
        P(("rep", "fsdp", "own"), "tp"),
        P("tp", "fsdp"),
        P(("fsdp", "own"), "tp", None),
        P(("fsdp", "own"), None, "tp"),
        P(("rep", "fsdp", "own"), None),
        P(),
    )
    line = mesh.shape["fsdp"] == 4 and mesh.shape["own"] == 2 and mesh.shape["rep"] == 2
    return jax.shard_map(
        body_line if line else body_routed,
        mesh=mesh,
        in_specs=placed,
        out_specs=(
            P(("rep", "fsdp", "own"), "tp"),
            P(("rep", "fsdp", "own"), "tp"),
            P(("rep", "fsdp", "own"), "tp", None),
            P(("rep", "fsdp", "own"), None, "tp"),
        ),
        check_vma=False,
    )
```

time: 241 us -> 270 us (1.12)
  Pallas kernels: 24.6 us -> 102 us
  waiting for transfers between devices: 89.2 us -> 70.8 us
  local copies, waits for them, and re-layouts: 24.9 us -> 15.2 us
  matrix products: 21.5 us -> 13.4 us
  other arithmetic: 16 us -> 9.79 us
  starting transfers between devices: 61.3 us -> 55.5 us
    pallas_call x8 -> x23, Pallas kernels: 24.6 us -> 102 us  [kernel_call(): pl.pallas_call(body, out_shape=list(outs), in_specs=specs, out_specs=[pl....]
    ppermute x15 -> x13, waiting for transfers between devices: 53 us -> 34.6 us  [along(): return lax.ppermute(value, 'fsdp', pairs)]
    dynamic_slice x10 -> x2, local copies, waits for them, and re-layouts: 8.66 us -> 0.17 us  [cut(): return lax.dynamic_slice_in_dim(value, start, length, axis)]
    dot_general x11, matrix products: 20.3 us -> 13.4 us  [contract_first(): lax.dot_general(left, right, (((0,), (0,)), ((), ())), preferred_element_...]
    ppermute x15 -> x13, starting transfers between devices: 30.1 us -> 25 us  [along(): return lax.ppermute(value, 'fsdp', pairs)]
    concatenate x10 -> x3, other arithmetic: 5.5 us -> 0.88 us  [the longest x2 0.87 us: body_line(): dy_half = jnp.concatenate([cotangent, packet[:, :kv]], axis=0)]
    ppermute x21 -> x20, starting transfers between devices: 21.3 us -> 18.8 us  [swap(): return lax.ppermute(value, axis, PAIR)]
    unnamed x123 -> x100, local copies, waits for them, and re-layouts: 9.26 us -> 10.5 us
  transfers between devices with their start and end apart: 38 -> 35, of which waited for: 14 -> 10; matrix products, arithmetic and copies ran while one was open for 20% -> 9% of each run, Pallas kernels for 7% -> 36%
where the time goes in v4:
time: 270 us; the launch traced here: 268 us
  Pallas kernels  102 us (38%)
  waiting for transfers between devices  70.8 us (26%)
  starting transfers between devices  55.5 us (21%)
  local copies, waits for them, and re-layouts  15.2 us (6%)
  matrix products  13.4 us (5%)
  other arithmetic  9.79 us (4%)
    pallas_call x23, Pallas kernels, kernel_call(): pl.pallas_call(body, out_shape=list(outs), in_specs=specs, out_specs=[pl....  102 us
    ppermute x13, waiting for transfers between devices, along(): return lax.ppermute(value, 'fsdp', pairs)  34.6 us
    ppermute x20, waiting for transfers between devices, swap(): return lax.ppermute(value, axis, PAIR)  33.9 us
    ppermute x13, starting transfers between devices, along(): return lax.ppermute(value, 'fsdp', pairs)  25 us
    ppermute x20, starting transfers between devices, swap(): return lax.ppermute(value, axis, PAIR)  18.8 us
    dot_general x11, matrix products, contract_first(): lax.dot_general(left, right, (((0,), (0,)), ((), ())), preferred_element_...  13.4 us
    unnamed x100, local copies, waits for them, and re-layouts  10.5 us
    all_to_all x1, starting transfers between devices, body_line(): lax.all_to_all(done(up_sent), ('fsdp', 'own'), split_axis=0, concat_axis=...  6.19 us
  transfers between devices with their start and end apart: 35, of which 10 were waited for; matrix products, arithmetic and copies ran while one was open for 9% of the time, Pallas kernels for 36%

profile of v4, /device:TPU:0, one launch (start us, length us, event | category | flops | bytes accessed | tf_op | source)
XLA Modules:
  0.0 267.9 jit_solution(12379956718427136806)
XLA Ops:
  2.5 3.0 %collective-permute-start.2 = (bf16[1024,128]{1,0:T(8,128)(2,1)S(1)}, bf16[1024,128]{1,0:T(8,128)(2,1)S(1)}, u32[]{:S(2)}, u32[]{:S(2)}) collective-permute-start(bf16[1024,128]{1,0:T(8,128)(2,1)S(1)} %shard_map.102), channel_id=1, source_target_pairs={{0,2},{2,0},{1,3},{3,1},{4,6},{6,4},{5,7},{7,5},{8,10},{10,8},{9,1... | collective-permute-start | bytes 786440 | tf_op jit(solution)/shard_map/ppermute | solution.py:36
  13.5 6.2 %all-to-all-start = ((bf16[8,128,256]{2,1,0:T(8,128)(2,1)}), bf16[8,128,256]{2,1,0:T(8,128)(2,1)}, u32[]{:S(2)}, u32[]{:S(2)}) async-start(bf16[8,128,256]{2,1,0:T(8,128)(2,1)} %bitcast.19), calls=%async_computation | async-start | bytes 1048576 | tf_op jit(solution)/shard_map/all_to_all | solution.py:353
  19.7 2.0 collective-permute-start.1
  25.2 10.5 %collective-permute-done.1 = bf16[256,640]{1,0:T(8,128)(2,1)} collective-permute-done((bf16[256,640]{1,0:T(8,128)(2,1)S(1)}, bf16[256,640]{1,0:T(8,128)(2,1)}, u32[]{:S(2)}, u32[]{:S(2)}) %collective-permute-start.1) | collective-permute-done | bytes 327712 | tf_op jit(solution)/shard_map/ppermute | solution.py:36
  38.5 4.8 %collective-permute-done.3.refs_1_.near.rest_1_ = bf16[1024,256]{1,0:T(8,128)(2,1)} collective-permute-done((bf16[1024,256]{1,0:T(8,128)(2,1)S(1)}, bf16[1024,256]{1,0:T(8,128)(2,1)}, u32[]{:S(2)}, u32[]{:S(2)}) %collective-permute-start.3) | collective-permute-done | bytes 524320 | tf_op jit(solution)/shard_map/ppermute | solution.py:40
  54.5 7.1 %collective-permute-done.6.got = f32[512,128]{1,0:T(8,128)S(1)} collective-permute-done((f32[512,128]{1,0:T(8,128)S(1)}, f32[512,128]{1,0:T(8,128)S(1)}, u32[]{:S(2)}, u32[]{:S(2)}) %collective-permute-start.6) | collective-permute-done | bytes 262176 | tf_op jit(solution)/shard_map/ppermute | solution.py:36
  62.4 6.2 %collective-permute-start.11 = (bf16[512,1024]{1,0:T(8,128)(2,1)S(1)}, bf16[512,1024]{1,0:T(8,128)(2,1)}, u32[]{:S(2)}, u32[]{:S(2)}) collective-permute-start(bf16[512,1024]{1,0:T(8,128)(2,1)S(1)} %shard_map.109.x_mine.tokens), channel_id=1, source_target_pairs={{0,4},{12,8},{1,5},{13,9},{2,6},{14,10},{3,7},{15,11},{16,20},{28,... | collective-permute-start | bytes 3145736 | tf_op jit(solution)/shard_map/ppermute | solution.py:40
  68.7 33.4 %shard_map.110 = bf16[1024,512]{1,0:T(8,128)(2,1)} custom-call(s32[4]{0:T(128)S(1)} %pad_add_fusion.numbers, bf16[1024,256]{1,0:T(8,128)(2,1)} %shard_map.106.refs_0_.own, bf16[1024,256]{1,0:T(8,128)(2,1)} %collective-permute-done.7.refs_1_.near), custom_call_target="tpu_custom_call" | custom-call | tf_op jit(solution)/shard_map/pallas_call | solution.py:48
  116.0 5.6 %collective-permute-start.17 = (bf16[512,1024]{1,0:T(8,128)(2,1)S(1)}, bf16[512,1024]{1,0:T(8,128)(2,1)S(1)}, u32[]{:S(2)}, u32[]{:S(2)}) collective-permute-start(bf16[512,1024]{1,0:T(8,128)(2,1)S(1)} %copy-done.3), channel_id=1, source_target_pairs={{0,4},{12,8},{1,5},{13,9},{2,6},{14,10},{3,7},{15,11},{16,20},{28,... | collective-permute-start | bytes 3145736 | tf_op jit(solution)/shard_map/ppermute | solution.py:40
  122.5 2.4 fusion.10
  128.7 13.8 %collective-permute-done.18 = bf16[1024,512]{1,0:T(8,128)(2,1)} collective-permute-done((bf16[1024,512]{1,0:T(8,128)(2,1)}, bf16[1024,512]{1,0:T(8,128)(2,1)}, u32[]{:S(2)}, u32[]{:S(2)}) %collective-permute-start.18) | collective-permute-done | bytes 1048608 | tf_op jit(solution)/shard_map/ppermute | solution.py:40
  148.7 16.1 %collective-permute-done.15 = bf16[1024,512]{1,0:T(8,128)(2,1)S(1)} collective-permute-done((bf16[1024,512]{1,0:T(8,128)(2,1)}, bf16[1024,512]{1,0:T(8,128)(2,1)S(1)}, u32[]{:S(2)}, u32[]{:S(2)}) %collective-permute-start.15) | collective-permute-done | bytes 1048608 | tf_op jit(solution)/shard_map/ppermute | solution.py:40
  164.9 4.1 %shard_map.115 = f32[512,128]{1,0:T(8,128)S(1)} custom-call(s32[16]{0:T(128)S(1)} %concatenate.44.numbers, bf16[512,128]{1,0:T(8,128)(2,1)S(1)} %pad_maximum_fusion.3.ids, bf16[512,1024]{1,0:T(8,128)(2,1)S(1)} %shard_map.109.x_mine.tokens, bf16[512,1024]{1,0:T(8,128)(2,1)S(1)} %copy-done.3, bf16[1024,256]{1,0:T(8,128)(2,1)S(1)} %copy-done.11, ...), custom_call_target="tpu_custom_call" | custom-call | tf_op jit(solution)/shard_map/pallas_call | solution.py:48
  171.6 3.7 %shard_map.116 = (bf16[256,1024]{1,0:T(8,128)(2,1)S(1)}, bf16[256,1024]{1,0:T(8,128)(2,1)S(1)}) custom-call(bf16[512,1024]{1,0:T(8,128)(2,1)S(1)} %copy-done.6, bf16[512,1024]{1,0:T(8,128)(2,1)S(1)} %copy-done.5, bf16[1024,256]{1,0:T(8,128)(2,1)} %shard_map.106.refs_0_.own, bf16[1024,256]{1,0:T(8,128)(2,1)} %collective-permute-done.7.refs_1_.near, ...), custom_call_target="tpu_custom_call" | custom-call | tf_op jit(solution)/shard_map/pallas_call | solution.py:48
  178.8 4.1 %shard_map.117 = (f32[2,512,256]{2,1,0:T(8,128)S(1)}, f32[2,512,256]{2,1,0:T(8,128)S(1)}) custom-call(s32[4]{0:T(128)S(1)} %add_convert_fusion.2.flags, bf16[512,1024]{1,0:T(8,128)(2,1)S(1)} %shard_map.109.x_mine.tokens, bf16[1024,256]{1,0:T(8,128)(2,1)} %shard_map.106.refs_0_.own, bf16[1024,256]{1,0:T(8,128)(2,1)} %collective-permute-done.7.refs_1_.near, ...), custom_call_target="tpu_custom_call" | custom-call | tf_op jit(solution)/shard_map/pallas_call | solution.py:48
  182.9 12.1 %collective-permute-done.24.got = f32[512,128]{1,0:T(8,128)S(1)} collective-permute-done((f32[512,128]{1,0:T(8,128)S(1)}, f32[512,128]{1,0:T(8,128)S(1)}, u32[]{:S(2)}, u32[]{:S(2)}) %collective-permute-start.24) | collective-permute-done | bytes 262176 | tf_op jit(solution)/shard_map/ppermute | solution.py:36
  199.5 4.5 %shard_map.119 = (f32[2,512,256]{2,1,0:T(8,128)S(1)}, f32[2,512,256]{2,1,0:T(8,128)}) custom-call(s32[4]{0:T(128)S(1)} %add_convert_fusion.2.flags, bf16[512,1024]{1,0:T(8,128)(2,1)S(1)} %copy-done.3, bf16[1024,256]{1,0:T(8,128)(2,1)S(1)} %copy-done.14, bf16[1024,256]{1,0:T(8,128)(2,1)S(1)} %collective-permute-done.10.near, ...), custom_call_target="tpu_custom_call" | custom-call | tf_op jit(solution)/shard_map/pallas_call | solution.py:48
  207.9 5.5 %all-to-all-start.1 = ((bf16[4,2,128,256]{3,2,1,0:T(8,128)(2,1)}), bf16[4,2,128,256]{3,2,1,0:T(8,128)(2,1)}, u32[]{:S(2)}, u32[]{:S(2)}) async-start(bf16[4,2,128,256]{3,2,1,0:T(8,128)(2,1)} %bitcast.38), calls=%async_computation.1 | async-start | bytes 1048576 | tf_op jit(solution)/shard_map/all_to_all | solution.py:492
  216.6 4.5 %shard_map.120 = (bf16[256,1024]{1,0:T(8,128)(2,1)S(1)}, bf16[256,1024]{1,0:T(8,128)(2,1)}) custom-call(bf16[512,1024]{1,0:T(8,128)(2,1)S(1)} %copy-done.7, bf16[512,1024]{1,0:T(8,128)(2,1)S(1)} %copy-done.5, bf16[1024,256]{1,0:T(8,128)(2,1)S(1)} %copy-done.15, bf16[1024,256]{1,0:T(8,128)(2,1)S(1)} %copy-done.23, bf16[1024,512]{1,0:T(8,128)(2,1)S(1)} %copy-done.21, ...), custom_call_target="tpu_custom_call" | custom-call | tf_op jit(solution)/shard_map/pallas_call | solution.py:48
  221.7 2.1 shard_map.121
  227.7 2.3 all-to-all-done.1
  233.3 3.0 %collective-permute-done.28.refs_3_ = bf16[256,1024]{1,0:T(8,128)(2,1)} collective-permute-done((bf16[256,1024]{1,0:T(8,128)(2,1)}, bf16[256,1024]{1,0:T(8,128)(2,1)}, u32[]{:S(2)}, u32[]{:S(2)}) %collective-permute-start.28) | collective-permute-done | bytes 524320 | tf_op jit(solution)/shard_map/ppermute | solution.py:36
  237.4 17.6 %shard_map.122 = bf16[256,4096]{1,0:T(8,128)(2,1)} custom-call(s32[4]{0:T(128)S(1)} %pad_add_fusion.numbers, bf16[256,1024]{1,0:T(8,128)(2,1)S(1)} %copy-done.30, bf16[256,1024]{1,0:T(8,128)(2,1)S(1)} %copy-done.34, bf16[256,1024]{1,0:T(8,128)(2,1)S(1)} %copy-done.32, bf16[256,1024]{1,0:T(8,128)(2,1)} %collective-permute-done.28.refs_3_), custom_call_target="tpu_custom_call" | custom-call | tf_op jit(solution)/shard_map/pallas_call | solution.py:48
  256.7 9.6 %shard_map.124 = bf16[4096,128]{1,0:T(8,128)(2,1)} custom-call(s32[4]{0:T(128)S(1)} %pad_add_fusion.numbers, bf16[1024,128]{1,0:T(8,128)(2,1)S(1)} %get-tuple-element.127.refs_0_, bf16[1024,128]{1,0:T(8,128)(2,1)S(1)} %get-tuple-element.125.refs_1_, bf16[1024,128]{1,0:T(8,128)(2,1)} %collective-permute-done.30.refs_2_, ...), custom_call_target="tpu_custom_call" | custom-call | tf_op jit(solution)/shard_map/pallas_call | solution.py:48
  (209 shorter events, 82.3 us)
Async XLA Ops:
  13.5 32.4 %all-to-all-start = ((bf16[8,128,256]{2,1,0:T(8,128)(2,1)}), bf16[8,128,256]{2,1,0:T(8,128)(2,1)}, u32[]{:S(2)}, u32[]{:S(2)}) async-start(bf16[8,128,256]{2,1,0:T(8,128)(2,1)} %bitcast.19), calls=%async_computation | async-start | bytes 1048576 | tf_op jit(solution)/shard_map/all_to_all | solution.py:353
  21.7 21.6 %collective-permute-start.3 = (bf16[1024,256]{1,0:T(8,128)(2,1)S(1)}, bf16[1024,256]{1,0:T(8,128)(2,1)}, u32[]{:S(2)}, u32[]{:S(2)}) collective-permute-start(bf16[1024,256]{1,0:T(8,128)(2,1)S(1)} %shard_map.105.refs_0_.own.rest_0_), channel_id=1, source_target_pairs={{0,4},{4,0},{8,12},{12,8},{1,5},{5,1},{9,13},{13,9},{2,6},{6,2},{1... | collective-permute-start | bytes 1572872 | tf_op jit(solution)/shard_map/ppermute | solution.py:40
  23.2 27.5 %collective-permute-start.5 = (bf16[256,1024]{1,0:T(8,128)(2,1)}, bf16[256,1024]{1,0:T(8,128)(2,1)}, u32[]{:S(2)}, u32[]{:S(2)}) collective-permute-start(bf16[256,1024]{1,0:T(8,128)(2,1)} %shard_map.103), channel_id=1, source_target_pairs={{0,2},{2,0},{1,3},{3,1},{4,6},{6,4},{5,7},{7,5},{8,10},{10,8},{9,1... | collective-permute-start | bytes 1572872 | tf_op jit(solution)/shard_map/ppermute | solution.py:36
  25.1 29.4 %collective-permute-start.7 = (bf16[1024,256]{1,0:T(8,128)(2,1)}, bf16[1024,256]{1,0:T(8,128)(2,1)}, u32[]{:S(2)}, u32[]{:S(2)}) collective-permute-start(bf16[1024,256]{1,0:T(8,128)(2,1)} %shard_map.106.refs_0_.own), channel_id=1, source_target_pairs={{0,4},{4,0},{8,12},{12,8},{1,5},{5,1},{9,13},{13,9},{2,6},{6,2},{1... | collective-permute-start | bytes 1572872 | tf_op jit(solution)/shard_map/ppermute | solution.py:40
  47.5 66.6 %collective-permute-start.12 = (bf16[1024,512]{1,0:T(8,128)(2,1)}, bf16[1024,512]{1,0:T(8,128)(2,1)}, u32[]{:S(2)}, u32[]{:S(2)}) collective-permute-start(bf16[1024,512]{1,0:T(8,128)(2,1)} %copy-done.24), channel_id=1, source_target_pairs={{4,8},{8,4},{5,9},{9,5},{6,10},{10,6},{7,11},{11,7},{20,24},{24,20... | collective-permute-start | bytes 3145736 | tf_op jit(solution)/shard_map/ppermute | solution.py:40
  49.2 64.9 %collective-permute-start.14 = (bf16[1024,512]{1,0:T(8,128)(2,1)}, bf16[1024,512]{1,0:T(8,128)(2,1)}, u32[]{:S(2)}, u32[]{:S(2)}) collective-permute-start(bf16[1024,512]{1,0:T(8,128)(2,1)} %copy-done.24), channel_id=1, source_target_pairs={{0,16},{16,0},{1,17},{17,1},{2,18},{18,2},{3,19},{19,3},{4,20},{20... | collective-permute-start | bytes 3145736 | tf_op jit(solution)/shard_map/ppermute | solution.py:36
  53.3 51.3 %collective-permute-start = (bf16[256,1024]{1,0:T(8,128)(2,1)}, bf16[256,1024]{1,0:T(8,128)(2,1)}, u32[]{:S(2)}, u32[]{:S(2)}) collective-permute-start(bf16[256,1024]{1,0:T(8,128)(2,1)} %shard_map.104), channel_id=1, source_target_pairs={{0,2},{2,0},{1,3},{3,1},{4,6},{6,4},{5,7},{7,5},{8,10},{10,8},{9,1... | collective-permute-start | bytes 1572872 | tf_op jit(solution)/shard_map/ppermute | solution.py:36
  54.5 53.3 %collective-permute-start.8 = (bf16[512,512]{1,0:T(8,128)(2,1)}, bf16[512,512]{1,0:T(8,128)(2,1)}, u32[]{:S(2)}, u32[]{:S(2)}) collective-permute-start(bf16[512,512]{1,0:T(8,128)(2,1)} %pad_maximum_fusion.1), channel_id=1, source_target_pairs={{0,1},{1,0},{2,3},{3,2},{4,5},{5,4},{6,7},{7,6},{8,9},{9,8},{10,11... | collective-permute-start | bytes 1572872 | tf_op jit(solution)/shard_map/ppermute | solution.py:36
  62.4 60.1 %collective-permute-start.11 = (bf16[512,1024]{1,0:T(8,128)(2,1)S(1)}, bf16[512,1024]{1,0:T(8,128)(2,1)}, u32[]{:S(2)}, u32[]{:S(2)}) collective-permute-start(bf16[512,1024]{1,0:T(8,128)(2,1)S(1)} %shard_map.109.x_mine.tokens), channel_id=1, source_target_pairs={{0,4},{12,8},{1,5},{13,9},{2,6},{14,10},{3,7},{15,11},{16,20},{28,... | collective-permute-start | bytes 3145736 | tf_op jit(solution)/shard_map/ppermute | solution.py:40
  104.5 22.9 %collective-permute-start.9 = (bf16[1024,512]{1,0:T(8,128)(2,1)}, bf16[1024,512]{1,0:T(8,128)(2,1)}, u32[]{:S(2)}, u32[]{:S(2)}) collective-permute-start(bf16[1024,512]{1,0:T(8,128)(2,1)} %shard_map.110), channel_id=1, source_target_pairs={{4,8},{8,4},{5,9},{9,5},{6,10},{10,6},{7,11},{11,7},{20,24},{24,20... | collective-permute-start | bytes 3145736 | tf_op jit(solution)/shard_map/ppermute | solution.py:40
  114.1 28.3 %collective-permute-start.18 = (bf16[1024,512]{1,0:T(8,128)(2,1)}, bf16[1024,512]{1,0:T(8,128)(2,1)}, u32[]{:S(2)}, u32[]{:S(2)}) collective-permute-start(bf16[1024,512]{1,0:T(8,128)(2,1)} %collective-permute-done.12), channel_id=1, source_target_pairs={{4,0},{8,12},{5,1},{9,13},{6,2},{10,14},{7,3},{11,15},{20,16},{24,... | collective-permute-start | bytes 3145736 | tf_op jit(solution)/shard_map/ppermute | solution.py:40
  116.0 28.3 %collective-permute-start.17 = (bf16[512,1024]{1,0:T(8,128)(2,1)S(1)}, bf16[512,1024]{1,0:T(8,128)(2,1)S(1)}, u32[]{:S(2)}, u32[]{:S(2)}) collective-permute-start(bf16[512,1024]{1,0:T(8,128)(2,1)S(1)} %copy-done.3), channel_id=1, source_target_pairs={{0,4},{12,8},{1,5},{13,9},{2,6},{14,10},{3,7},{15,11},{16,20},{28,... | collective-permute-start | bytes 3145736 | tf_op jit(solution)/shard_map/ppermute | solution.py:40
  125.6 21.0 %collective-permute-start.16 = (bf16[1024,512]{1,0:T(8,128)(2,1)S(1)}, bf16[1024,512]{1,0:T(8,128)(2,1)S(1)}, u32[]{:S(2)}, u32[]{:S(2)}) collective-permute-start(bf16[1024,512]{1,0:T(8,128)(2,1)S(1)} %add_convert_fusion.1), channel_id=1, source_target_pairs={{4,8},{8,4},{5,9},{9,5},{6,10},{10,6},{7,11},{11,7},{20,24},{24,20... | collective-permute-start | bytes 3145736 | tf_op jit(solution)/shard_map/ppermute | solution.py:40
  127.4 37.4 %collective-permute-start.15 = (bf16[1024,512]{1,0:T(8,128)(2,1)}, bf16[1024,512]{1,0:T(8,128)(2,1)S(1)}, u32[]{:S(2)}, u32[]{:S(2)}) collective-permute-start(bf16[1024,512]{1,0:T(8,128)(2,1)} %collective-permute-done.9), channel_id=1, source_target_pairs={{4,0},{8,12},{5,1},{9,13},{6,2},{10,14},{7,3},{11,15},{20,16},{24,... | collective-permute-start | bytes 3145736 | tf_op jit(solution)/shard_map/ppermute | solution.py:40
  143.8 21.1 %collective-permute-start.20 = (bf16[1024,512]{1,0:T(8,128)(2,1)S(1)}, bf16[1024,512]{1,0:T(8,128)(2,1)S(1)}, u32[]{:S(2)}, u32[]{:S(2)}) collective-permute-start(bf16[1024,512]{1,0:T(8,128)(2,1)S(1)} %broadcast_select_fusion.1.far.rest_2_), channel_id=1, source_target_pairs={{0,16},{16,0},{1,17},{17,1},{2,18},{18,2},{3,19},{19,3},{4,20},{20... | collective-permute-start | bytes 3145736 | tf_op jit(solution)/shard_map/ppermute | solution.py:36
  145.8 52.3 %collective-permute-start.22 = (bf16[1024,512]{1,0:T(8,128)(2,1)S(1)}, bf16[1024,512]{1,0:T(8,128)(2,1)S(1)}, u32[]{:S(2)}, u32[]{:S(2)}) collective-permute-start(bf16[1024,512]{1,0:T(8,128)(2,1)S(1)} %add_convert_fusion), channel_id=1, source_target_pairs={{4,8},{8,4},{5,9},{9,5},{6,10},{10,6},{7,11},{11,7},{20,24},{24,20... | collective-permute-start | bytes 3145736 | tf_op jit(solution)/shard_map/ppermute | solution.py:40
  147.1 30.4 %collective-permute-start.25 = (bf16[1024,256]{1,0:T(8,128)(2,1)S(1)}, bf16[1024,256]{1,0:T(8,128)(2,1)S(1)}, u32[]{:S(2)}, u32[]{:S(2)}) collective-permute-start(bf16[1024,256]{1,0:T(8,128)(2,1)S(1)} %fusion.4), channel_id=1, source_target_pairs={{4,0},{8,12},{5,1},{9,13},{6,2},{10,14},{7,3},{11,15},{20,16},{24,... | collective-permute-start | bytes 1572872 | tf_op jit(solution)/shard_map/ppermute | solution.py:40
  171.0 28.5 %collective-permute-start.19 = (bf16[1024,512]{1,0:T(8,128)(2,1)S(1)}, bf16[1024,512]{1,0:T(8,128)(2,1)S(1)}, u32[]{:S(2)}, u32[]{:S(2)}) collective-permute-start(bf16[1024,512]{1,0:T(8,128)(2,1)S(1)} %broadcast_select_fusion.far), channel_id=1, source_target_pairs={{0,16},{16,0},{1,17},{17,1},{2,18},{18,2},{3,19},{19,3},{4,20},{20... | collective-permute-start | bytes 3145736 | tf_op jit(solution)/shard_map/ppermute | solution.py:36
  175.3 24.1 %collective-permute-start.21 = (bf16[256,1024]{1,0:T(8,128)(2,1)S(1)}, bf16[256,1024]{1,0:T(8,128)(2,1)S(1)}, u32[]{:S(2)}, u32[]{:S(2)}) collective-permute-start(bf16[256,1024]{1,0:T(8,128)(2,1)S(1)} %get-tuple-element.93), channel_id=1, source_target_pairs={{0,2},{2,0},{1,3},{3,1},{4,6},{6,4},{5,7},{7,5},{8,10},{10,8},{9,1... | collective-permute-start | bytes 1572872 | tf_op jit(solution)/shard_map/ppermute | solution.py:36
  205.0 20.3 %collective-permute-start.29 = (bf16[1024,256]{1,0:T(8,128)(2,1)}, bf16[1024,256]{1,0:T(8,128)(2,1)}, u32[]{:S(2)}, u32[]{:S(2)}) collective-permute-start(bf16[1024,256]{1,0:T(8,128)(2,1)} %fusion.5), channel_id=1, source_target_pairs={{4,0},{8,12},{5,1},{9,13},{6,2},{10,14},{7,3},{11,15},{20,16},{24,... | collective-permute-start | bytes 1572872 | tf_op jit(solution)/shard_map/ppermute | solution.py:40
  207.9 22.0 %all-to-all-start.1 = ((bf16[4,2,128,256]{3,2,1,0:T(8,128)(2,1)}), bf16[4,2,128,256]{3,2,1,0:T(8,128)(2,1)}, u32[]{:S(2)}, u32[]{:S(2)}) async-start(bf16[4,2,128,256]{3,2,1,0:T(8,128)(2,1)} %bitcast.38), calls=%async_computation.1 | async-start | bytes 1048576 | tf_op jit(solution)/shard_map/all_to_all | solution.py:492
  223.8 31.1 %collective-permute-start.27 = (bf16[2,256,256]{2,1,0:T(8,128)(2,1)}, bf16[2,256,256]{2,1,0:T(8,128)(2,1)}, u32[]{:S(2)}, u32[]{:S(2)}) collective-permute-start(bf16[2,256,256]{2,1,0:T(8,128)(2,1)} %get-tuple-element.111), channel_id=1, source_target_pairs={{0,2},{2,0},{1,3},{3,1},{4,6},{6,4},{5,7},{7,5},{8,10},{10,8},{9,1... | collective-permute-start | bytes 786440 | tf_op jit(solution)/shard_map/ppermute | solution.py:36
  229.9 26.8 %collective-permute-start.31 = (bf16[1024,128]{1,0:T(8,128)(2,1)}, bf16[1024,128]{1,0:T(8,128)(2,1)S(1)}, u32[]{:S(2)}, u32[]{:S(2)}) collective-permute-start(bf16[1024,128]{1,0:T(8,128)(2,1)} %get-tuple-element.124), channel_id=1, source_target_pairs={{0,2},{2,0},{1,3},{3,1},{4,6},{6,4},{5,7},{7,5},{8,10},{10,8},{9,1... | collective-permute-start | bytes 786440 | tf_op jit(solution)/shard_map/ppermute | solution.py:36
  232.6 33.7 %collective-permute-start.32 = (bf16[1,128,256]{2,1,0:T(8,128)(2,1)S(1)}, bf16[1,128,256]{2,1,0:T(8,128)(2,1)}, u32[]{:S(2)}, u32[]{:S(2)}) collective-permute-start(bf16[1,128,256]{2,1,0:T(8,128)(2,1)S(1)} %get-tuple-element.129), channel_id=1, source_target_pairs={{0,2},{2,0},{1,3},{3,1},{4,6},{6,4},{5,7},{7,5},{8,10},{10,8},{9,1... | collective-permute-start | bytes 196616 | tf_op jit(solution)/shard_map/ppermute | solution.py:36
  (61 other events, 588.6 us)

commit v5 on v4

--- a/solution.py
+++ b/solution.py
@@ -49,7 +49,7 @@
         body,
         out_shape=list(outs),
         in_specs=specs,
-        out_specs=[pl.BlockSpec(memory_space=space)] * len(outs),
+        out_specs=[pl.BlockSpec(memory_space=pltpu.VMEM)] * len(outs),
         scratch_shapes=list(scratch),
         compiler_params=pltpu.CompilerParams(vmem_limit_bytes=28 * 2**20),
         cost_estimate=pl.CostEstimate(flops=0, bytes_accessed=0, transcendentals=0),
@@ -330,10 +330,12 @@
         )[0]
 
     down_got = swap(done(rows_at(2, down, eighth)), "own")
-    ids_here = jnp.broadcast_to(token_adapter.astype(bf16), (rows, size))
-    packet = swap(done(join(step(cotangent), ids_here)), "own")
-    x_got = [swap(done(columns_at(2, step(tokens))), "own")]
-    x_got.append(swap(done(columns_at(3, step(tokens))), "own"))
+    up_sent = jnp.broadcast_to(
+        step(up).reshape(size, 2, kvq).transpose(1, 0, 2)[None], (4, 2, size, kvq)
+    ).reshape(number, size, kvq)
+    up_all = lax.all_to_all(
+        done(up_sent), ("fsdp", "own"), split_axis=0, concat_axis=0, tiled=True
+    ).reshape(number * size, kvq)
     down_piece = done(
         copy_call(
             lambda n, a, o: [
@@ -347,12 +349,9 @@
         )[0]
     )
     down_near = along(down_piece, NEIGHBOURS)
-    up_sent = jnp.broadcast_to(
-        step(up).reshape(size, 2, kvq).transpose(1, 0, 2)[None], (4, 2, size, kvq)
-    ).reshape(number, size, kvq)
-    up_all = lax.all_to_all(
-        done(up_sent), ("fsdp", "own"), split_axis=0, concat_axis=0, tiled=True
-    ).reshape(number * size, kvq)
+    ids_here = jnp.broadcast_to(token_adapter.astype(bf16), (rows, size))
+    packet = swap(done(join(step(cotangent), ids_here)), "own")
+    x_got = [swap(done(columns_at(2, step(tokens))), "own")]
     weight_here = done(rows_at(0, step(frozen_value_weight), eighth))
     weight_near = along(weight_here, NEIGHBOURS)
 
@@ -374,6 +373,7 @@
     x_mine = done(tokens_of(0, tokens, step(x_got[0])))
     back_part = done(back_part + step(back_tp))
     back_got = swap(back_part, "own")
+    x_got.append(swap(done(columns_at(3, step(tokens))), "own"))
     x_in = [along(x_mine, INWARD)]
     weight_near = step(weight_near)
     crossing = done(side_by_side(weight_here, weight_near))
@@ -456,6 +456,13 @@
         )[0]
     )
     low_tp = swap(low_part, "tp")
+    blocks = [like(2, both, cols, kind=f32)] * 2
+    y_first = kernel_call(
+        y_kernel, blocks, step(x_mine), weight_here, weight_near, weight_far, scalars=flags
+    )
+    done(y_first[0])
+    low_part = done(low_part + step(low_tp))
+    low_got = swap(low_part, "own")
     half_grad = [like(rows, eighth)] * 2
     dx_mine, dx_sent = kernel_call(
         dx_kernel,
@@ -470,15 +477,8 @@
         down_far,
     )
     done(dx_mine)
-    low_part = done(low_part + step(low_tp))
-    low_got = swap(low_part, "own")
     dx_mine_got = swap(dx_sent, "own")
     grads = [finish(0, middle[0], outward[0])]
-    blocks = [like(2, both, cols, kind=f32)] * 2
-    y_first = kernel_call(
-        y_kernel, blocks, step(x_mine), weight_here, weight_near, weight_far, scalars=flags
-    )
-    done(y_first[0])
     low_wide, delta = kernel_call(
         low_end_kernel,
         [like(both, number * size), like(both, kvq)],

time: 270 us -> 220 us (0.81)
  Pallas kernels: 102 us -> 49.6 us
  waiting for transfers between devices: 70.8 us -> 74 us
    pallas_call x23, Pallas kernels: 102 us -> 49.6 us  [kernel_call(): pl.pallas_call(body, out_shape=list(outs), in_specs=specs, out_specs=[pl....]
    ppermute x13, waiting for transfers between devices: 34.6 us -> 43.1 us  [along(): return lax.ppermute(value, 'fsdp', pairs)]
    ppermute x20, waiting for transfers between devices: 33.9 us -> 28 us  [swap(): return lax.ppermute(value, axis, PAIR)]
    ppermute x13, starting transfers between devices: 25 us -> 28.7 us  [along(): return lax.ppermute(value, 'fsdp', pairs)]
    unnamed x100 -> x106, local copies, waits for them, and re-layouts: 10.5 us -> 10.7 us
  transfers between devices with their start and end apart: 35 -> 35, of which waited for: 10 -> 14; matrix products, arithmetic and copies ran while one was open for 9% -> 11% of each run, Pallas kernels for 36% -> 20%
where the time goes in v5:
time: 220 us; the launch traced here: 218 us
  waiting for transfers between devices  74 us (34%)
  starting transfers between devices  57.3 us (26%)
  Pallas kernels  49.6 us (23%)
  local copies, waits for them, and re-layouts  14.6 us (7%)
  matrix products  13.4 us (6%)
  other arithmetic  8.01 us (4%)
    pallas_call x23, Pallas kernels, kernel_call(): pl.pallas_call(body, out_shape=list(outs), in_specs=specs, out_specs=[pl....  49.6 us
    ppermute x13, waiting for transfers between devices, along(): return lax.ppermute(value, 'fsdp', pairs)  43.1 us
    ppermute x13, starting transfers between devices, along(): return lax.ppermute(value, 'fsdp', pairs)  28.7 us
    ppermute x20, waiting for transfers between devices, swap(): return lax.ppermute(value, axis, PAIR)  28 us
    ppermute x20, starting transfers between devices, swap(): return lax.ppermute(value, axis, PAIR)  19.1 us
    dot_general x11, matrix products, contract_first(): lax.dot_general(left, right, (((0,), (0,)), ((), ())), preferred_element_...  13.4 us
    unnamed x106, local copies, waits for them, and re-layouts  10.7 us
    all_to_all x1, starting transfers between devices, body_line(): lax.all_to_all(done(up_sent), ('fsdp', 'own'), split_axis=0, concat_axis=...  4.88 us
  transfers between devices with their start and end apart: 35, of which 14 were waited for; matrix products, arithmetic and copies ran while one was open for 11% of the time, Pallas kernels for 20%

profile of v5, /device:TPU:0, one launch (start us, length us, event | category | flops | bytes accessed | tf_op | source)
XLA Modules:
  0.0 218.4 jit_solution(9511614057958605798)
XLA Ops:
  2.6 3.0 %collective-permute-start = (bf16[1024,128]{1,0:T(8,128)(2,1)S(1)}, bf16[1024,128]{1,0:T(8,128)(2,1)S(1)}, u32[]{:S(2)}, u32[]{:S(2)}) collective-permute-start(bf16[1024,128]{1,0:T(8,128)(2,1)S(1)} %shard_map.102), channel_id=1, source_target_pairs={{0,2},{2,0},{1,3},{3,1},{4,6},{6,4},{5,7},{7,5},{8,10},{10,8},{9,1... | collective-permute-start | bytes 786440 | tf_op jit(solution)/shard_map/ppermute | solution.py:36
  7.4 4.9 %all-to-all-start = ((bf16[8,128,256]{2,1,0:T(8,128)(2,1)}), bf16[8,128,256]{2,1,0:T(8,128)(2,1)}, u32[]{:S(2)}, u32[]{:S(2)}) async-start(bf16[8,128,256]{2,1,0:T(8,128)(2,1)} %bitcast.37), calls=%async_computation | async-start | bytes 1048576 | tf_op jit(solution)/shard_map/all_to_all | solution.py:336
  22.2 6.2 %collective-permute-done.1 = bf16[256,640]{1,0:T(8,128)(2,1)S(1)} collective-permute-done((bf16[256,640]{1,0:T(8,128)(2,1)}, bf16[256,640]{1,0:T(8,128)(2,1)S(1)}, u32[]{:S(2)}, u32[]{:S(2)}) %collective-permute-start.1) | collective-permute-done | bytes 327712 | tf_op jit(solution)/shard_map/ppermute | solution.py:36
  31.1 3.6 %collective-permute-done.2.refs_1_.near.rest_1_ = bf16[1024,256]{1,0:T(8,128)(2,1)} collective-permute-done((bf16[1024,256]{1,0:T(8,128)(2,1)S(1)}, bf16[1024,256]{1,0:T(8,128)(2,1)}, u32[]{:S(2)}, u32[]{:S(2)}) %collective-permute-start.2) | collective-permute-done | bytes 524320 | tf_op jit(solution)/shard_map/ppermute | solution.py:40
  47.5 5.7 %collective-permute-done.6.got = f32[512,128]{1,0:T(8,128)S(1)} collective-permute-done((f32[512,128]{1,0:T(8,128)S(1)}, f32[512,128]{1,0:T(8,128)S(1)}, u32[]{:S(2)}, u32[]{:S(2)}) %collective-permute-start.6) | collective-permute-done | bytes 262176 | tf_op jit(solution)/shard_map/ppermute | solution.py:36
  53.9 7.3 %collective-permute-start.11 = (bf16[512,1024]{1,0:T(8,128)(2,1)S(1)}, bf16[512,1024]{1,0:T(8,128)(2,1)}, u32[]{:S(2)}, u32[]{:S(2)}) collective-permute-start(bf16[512,1024]{1,0:T(8,128)(2,1)S(1)} %shard_map.108.x_mine.tokens), channel_id=1, source_target_pairs={{0,4},{12,8},{1,5},{13,9},{2,6},{14,10},{3,7},{15,11},{16,20},{28,... | collective-permute-start | bytes 3145736 | tf_op jit(solution)/shard_map/ppermute | solution.py:40
  61.2 2.7 %shard_map.110 = bf16[1024,512]{1,0:T(8,128)(2,1)} custom-call(s32[4]{0:T(128)S(1)} %pad_add_fusion.numbers, bf16[1024,256]{1,0:T(8,128)(2,1)} %shard_map.105.refs_0_.own, bf16[1024,256]{1,0:T(8,128)(2,1)} %collective-permute-done.7.refs_1_.near), custom_call_target="tpu_custom_call" | custom-call | tf_op jit(solution)/shard_map/pallas_call | solution.py:48
  69.7 3.9 %collective-permute-start.13 = (bf16[512,256]{1,0:T(8,128)(2,1)S(1)}, bf16[512,256]{1,0:T(8,128)(2,1)S(1)}, u32[]{:S(2)}, u32[]{:S(2)}) collective-permute-start(bf16[512,256]{1,0:T(8,128)(2,1)S(1)} %get-tuple-element.76), channel_id=1, source_target_pairs={{0,4},{12,8},{1,5},{13,9},{2,6},{14,10},{3,7},{15,11},{16,20},{28,... | collective-permute-start | bytes 786440 | tf_op jit(solution)/shard_map/ppermute | solution.py:40
  78.5 7.8 %collective-permute-done.13.packet = bf16[512,256]{1,0:T(8,128)(2,1)S(1)} collective-permute-done((bf16[512,256]{1,0:T(8,128)(2,1)S(1)}, bf16[512,256]{1,0:T(8,128)(2,1)S(1)}, u32[]{:S(2)}, u32[]{:S(2)}) %collective-permute-start.13) | collective-permute-done | bytes 262176 | tf_op jit(solution)/shard_map/ppermute | solution.py:40
  88.3 5.5 %collective-permute-start.17 = (bf16[512,1024]{1,0:T(8,128)(2,1)S(1)}, bf16[512,1024]{1,0:T(8,128)(2,1)S(1)}, u32[]{:S(2)}, u32[]{:S(2)}) collective-permute-start(bf16[512,1024]{1,0:T(8,128)(2,1)S(1)} %copy-done.2), channel_id=1, source_target_pairs={{0,4},{12,8},{1,5},{13,9},{2,6},{14,10},{3,7},{15,11},{16,20},{28,... | collective-permute-start | bytes 3145736 | tf_op jit(solution)/shard_map/ppermute | solution.py:40
  94.7 2.4 %fusion.10 = f32[1024,512]{1,0:T(8,128)S(1)} fusion(bf16[512,1024]{1,0:T(8,128)(2,1)} %collective-permute-done.11, bf16[512,1024]{1,0:T(8,128)(2,1)S(1)} %shard_map.114), kind=kOutput, calls=%fused_computation.25 | convolution fusion | flops 536870912 | bytes 3670016 | tf_op jit(solution)/shard_map/dot_general | solution.py:13
  100.2 14.5 %collective-permute-done.18 = bf16[1024,512]{1,0:T(8,128)(2,1)} collective-permute-done((bf16[1024,512]{1,0:T(8,128)(2,1)}, bf16[1024,512]{1,0:T(8,128)(2,1)}, u32[]{:S(2)}, u32[]{:S(2)}) %collective-permute-start.18) | collective-permute-done | bytes 1048608 | tf_op jit(solution)/shard_map/ppermute | solution.py:40
  120.8 16.2 %collective-permute-done.15 = bf16[1024,512]{1,0:T(8,128)(2,1)S(1)} collective-permute-done((bf16[1024,512]{1,0:T(8,128)(2,1)}, bf16[1024,512]{1,0:T(8,128)(2,1)S(1)}, u32[]{:S(2)}, u32[]{:S(2)}) %collective-permute-start.15) | collective-permute-done | bytes 1048608 | tf_op jit(solution)/shard_map/ppermute | solution.py:40
  137.2 4.1 %shard_map.115 = f32[512,128]{1,0:T(8,128)S(1)} custom-call(s32[16]{0:T(128)S(1)} %concatenate.46.numbers, bf16[512,128]{1,0:T(8,128)(2,1)S(1)} %pad_maximum_fusion.3.ids, bf16[512,1024]{1,0:T(8,128)(2,1)S(1)} %shard_map.108.x_mine.tokens, bf16[512,1024]{1,0:T(8,128)(2,1)S(1)} %copy-done.2, bf16[1024,256]{1,0:T(8,128)(2,1)S(1)} %copy-done.10, ...), custom_call_target="tpu_custom_call" | custom-call | tf_op jit(solution)/shard_map/pallas_call | solution.py:48
  143.7 4.3 %shard_map.116 = (f32[2,512,256]{2,1,0:T(8,128)S(1)}, f32[2,512,256]{2,1,0:T(8,128)S(1)}) custom-call(s32[4]{0:T(128)S(1)} %add_convert_fusion.2.flags, bf16[512,1024]{1,0:T(8,128)(2,1)S(1)} %shard_map.108.x_mine.tokens, bf16[1024,256]{1,0:T(8,128)(2,1)} %shard_map.105.refs_0_.own, bf16[1024,256]{1,0:T(8,128)(2,1)} %collective-permute-done.7.refs_1_.near, ...), custom_call_target="tpu_custom_call" | custom-call | tf_op jit(solution)/shard_map/pallas_call | solution.py:48
  149.6 3.7 %shard_map.117 = (bf16[256,1024]{1,0:T(8,128)(2,1)S(1)}, bf16[256,1024]{1,0:T(8,128)(2,1)S(1)}) custom-call(bf16[512,1024]{1,0:T(8,128)(2,1)S(1)} %copy-done.5, bf16[512,1024]{1,0:T(8,128)(2,1)S(1)} %copy-done.4, bf16[1024,256]{1,0:T(8,128)(2,1)} %shard_map.105.refs_0_.own, bf16[1024,256]{1,0:T(8,128)(2,1)} %collective-permute-done.7.refs_1_.near, ...), custom_call_target="tpu_custom_call" | custom-call | tf_op jit(solution)/shard_map/pallas_call | solution.py:48
  161.5 7.3 %collective-permute-done.19.far = bf16[1024,512]{1,0:T(8,128)(2,1)S(1)} collective-permute-done((bf16[1024,512]{1,0:T(8,128)(2,1)S(1)}, bf16[1024,512]{1,0:T(8,128)(2,1)S(1)}, u32[]{:S(2)}, u32[]{:S(2)}) %collective-permute-start.19) | collective-permute-done | bytes 1048608 | tf_op jit(solution)/shard_map/ppermute | solution.py:36
  168.8 4.5 %shard_map.119 = (f32[2,512,256]{2,1,0:T(8,128)S(1)}, f32[2,512,256]{2,1,0:T(8,128)}) custom-call(s32[4]{0:T(128)S(1)} %add_convert_fusion.2.flags, bf16[512,1024]{1,0:T(8,128)(2,1)S(1)} %copy-done.2, bf16[1024,256]{1,0:T(8,128)(2,1)S(1)} %copy-done.13, bf16[1024,256]{1,0:T(8,128)(2,1)S(1)} %collective-permute-done.10.near, ...), custom_call_target="tpu_custom_call" | custom-call | tf_op jit(solution)/shard_map/pallas_call | solution.py:48
  177.3 4.7 %all-to-all-start.1 = ((bf16[4,2,128,256]{3,2,1,0:T(8,128)(2,1)}), bf16[4,2,128,256]{3,2,1,0:T(8,128)(2,1)}, u32[]{:S(2)}, u32[]{:S(2)}) async-start(bf16[4,2,128,256]{3,2,1,0:T(8,128)(2,1)} %bitcast.39), calls=%async_computation.1 | async-start | bytes 1048576 | tf_op jit(solution)/shard_map/all_to_all | solution.py:492
  185.2 4.5 %shard_map.120 = (bf16[256,1024]{1,0:T(8,128)(2,1)S(1)}, bf16[256,1024]{1,0:T(8,128)(2,1)}) custom-call(bf16[512,1024]{1,0:T(8,128)(2,1)S(1)} %copy-done.6, bf16[512,1024]{1,0:T(8,128)(2,1)S(1)} %copy-done.4, bf16[1024,256]{1,0:T(8,128)(2,1)S(1)} %copy-done.14, bf16[1024,256]{1,0:T(8,128)(2,1)S(1)} %copy-done.22, bf16[1024,512]{1,0:T(8,128)(2,1)S(1)} %copy-done.20, ...), custom_call_target="tpu_custom_call" | custom-call | tf_op jit(solution)/shard_map/pallas_call | solution.py:48
  196.2 2.9 %all-to-all-done.1 = bf16[4,2,128,256]{3,2,1,0:T(8,128)(2,1)} async-done(((bf16[4,2,128,256]{3,2,1,0:T(8,128)(2,1)}), bf16[4,2,128,256]{3,2,1,0:T(8,128)(2,1)}, u32[]{:S(2)}, u32[]{:S(2)}) %all-to-all-start.1) | async-done | bytes 524320 | tf_op jit(solution)/shard_map/all_to_all | solution.py:492
  205.9 3.1 %shard_map.122 = bf16[256,4096]{1,0:T(8,128)(2,1)} custom-call(s32[4]{0:T(128)S(1)} %pad_add_fusion.numbers, bf16[256,1024]{1,0:T(8,128)(2,1)S(1)} %copy-done.29, bf16[256,1024]{1,0:T(8,128)(2,1)S(1)} %copy-done.33, bf16[256,1024]{1,0:T(8,128)(2,1)S(1)} %copy-done.31, bf16[256,1024]{1,0:T(8,128)(2,1)} %collective-permute-done.28.refs_3_), custom_call_target="tpu_custom_call" | custom-call | tf_op jit(solution)/shard_map/pallas_call | solution.py:48
  212.2 3.0 %collective-permute-done.31.refs_3_ = bf16[1024,128]{1,0:T(8,128)(2,1)S(1)} collective-permute-done((bf16[1024,128]{1,0:T(8,128)(2,1)S(1)}, bf16[1024,128]{1,0:T(8,128)(2,1)S(1)}, u32[]{:S(2)}, u32[]{:S(2)}) %collective-permute-start.31) | collective-permute-done | bytes 262176 | tf_op jit(solution)/shard_map/ppermute | solution.py:36
  215.2 2.5 %shard_map.124 = bf16[4096,128]{1,0:T(8,128)(2,1)} custom-call(s32[4]{0:T(128)S(1)} %pad_add_fusion.numbers, bf16[1024,128]{1,0:T(8,128)(2,1)S(1)} %get-tuple-element.127.refs_0_, bf16[1024,128]{1,0:T(8,128)(2,1)S(1)} %get-tuple-element.125.refs_1_, bf16[1024,128]{1,0:T(8,128)(2,1)} %collective-permute-done.30.refs_2_, ...), custom_call_target="tpu_custom_call" | custom-call | tf_op jit(solution)/shard_map/pallas_call | solution.py:48
  (215 shorter events, 88.5 us)
Async XLA Ops:
  7.4 30.0 %all-to-all-start = ((bf16[8,128,256]{2,1,0:T(8,128)(2,1)}), bf16[8,128,256]{2,1,0:T(8,128)(2,1)}, u32[]{:S(2)}, u32[]{:S(2)}) async-start(bf16[8,128,256]{2,1,0:T(8,128)(2,1)} %bitcast.37), calls=%async_computation | async-start | bytes 1048576 | tf_op jit(solution)/shard_map/all_to_all | solution.py:336
  17.1 17.6 %collective-permute-start.2 = (bf16[1024,256]{1,0:T(8,128)(2,1)S(1)}, bf16[1024,256]{1,0:T(8,128)(2,1)}, u32[]{:S(2)}, u32[]{:S(2)}) collective-permute-start(bf16[1024,256]{1,0:T(8,128)(2,1)S(1)} %shard_map.103.refs_0_.own.rest_0_), channel_id=1, source_target_pairs={{0,4},{4,0},{8,12},{12,8},{1,5},{5,1},{9,13},{13,9},{2,6},{6,2},{1... | collective-permute-start | bytes 1572872 | tf_op jit(solution)/shard_map/ppermute | solution.py:40
  20.0 22.2 %collective-permute-start.4 = (bf16[256,1024]{1,0:T(8,128)(2,1)}, bf16[256,1024]{1,0:T(8,128)(2,1)}, u32[]{:S(2)}, u32[]{:S(2)}) collective-permute-start(bf16[256,1024]{1,0:T(8,128)(2,1)} %shard_map.104), channel_id=1, source_target_pairs={{0,2},{2,0},{1,3},{3,1},{4,6},{6,4},{5,7},{7,5},{8,10},{10,8},{9,1... | collective-permute-start | bytes 1572872 | tf_op jit(solution)/shard_map/ppermute | solution.py:36
  22.0 25.5 %collective-permute-start.7 = (bf16[1024,256]{1,0:T(8,128)(2,1)}, bf16[1024,256]{1,0:T(8,128)(2,1)}, u32[]{:S(2)}, u32[]{:S(2)}) collective-permute-start(bf16[1024,256]{1,0:T(8,128)(2,1)} %shard_map.105.refs_0_.own), channel_id=1, source_target_pairs={{0,4},{4,0},{8,12},{12,8},{1,5},{5,1},{9,13},{13,9},{2,6},{6,2},{1... | collective-permute-start | bytes 1572872 | tf_op jit(solution)/shard_map/ppermute | solution.py:40
  39.0 47.4 %collective-permute-start.14 = (bf16[1024,512]{1,0:T(8,128)(2,1)}, bf16[1024,512]{1,0:T(8,128)(2,1)}, u32[]{:S(2)}, u32[]{:S(2)}) collective-permute-start(bf16[1024,512]{1,0:T(8,128)(2,1)} %copy-done.23), channel_id=1, source_target_pairs={{0,16},{16,0},{1,17},{17,1},{2,18},{18,2},{3,19},{19,3},{4,20},{20... | collective-permute-start | bytes 3145736 | tf_op jit(solution)/shard_map/ppermute | solution.py:36
  40.5 45.8 %collective-permute-start.12 = (bf16[1024,512]{1,0:T(8,128)(2,1)}, bf16[1024,512]{1,0:T(8,128)(2,1)}, u32[]{:S(2)}, u32[]{:S(2)}) collective-permute-start(bf16[1024,512]{1,0:T(8,128)(2,1)} %copy-done.23), channel_id=1, source_target_pairs={{4,8},{8,4},{5,9},{9,5},{6,10},{10,6},{7,11},{11,7},{20,24},{24,20... | collective-permute-start | bytes 3145736 | tf_op jit(solution)/shard_map/ppermute | solution.py:40
  46.9 19.3 %collective-permute-start.5 = (bf16[256,1024]{1,0:T(8,128)(2,1)}, bf16[256,1024]{1,0:T(8,128)(2,1)}, u32[]{:S(2)}, u32[]{:S(2)}) collective-permute-start(bf16[256,1024]{1,0:T(8,128)(2,1)} %shard_map.109), channel_id=1, source_target_pairs={{0,2},{2,0},{1,3},{3,1},{4,6},{6,4},{5,7},{7,5},{8,10},{10,8},{9,1... | collective-permute-start | bytes 1572872 | tf_op jit(solution)/shard_map/ppermute | solution.py:36
  47.5 22.2 %collective-permute-start.8 = (bf16[512,512]{1,0:T(8,128)(2,1)}, bf16[512,512]{1,0:T(8,128)(2,1)}, u32[]{:S(2)}, u32[]{:S(2)}) collective-permute-start(bf16[512,512]{1,0:T(8,128)(2,1)} %pad_maximum_fusion.1), channel_id=1, source_target_pairs={{0,1},{1,0},{2,3},{3,2},{4,5},{5,4},{6,7},{7,6},{8,9},{9,8},{10,11... | collective-permute-start | bytes 1572872 | tf_op jit(solution)/shard_map/ppermute | solution.py:36
  53.9 40.8 %collective-permute-start.11 = (bf16[512,1024]{1,0:T(8,128)(2,1)S(1)}, bf16[512,1024]{1,0:T(8,128)(2,1)}, u32[]{:S(2)}, u32[]{:S(2)}) collective-permute-start(bf16[512,1024]{1,0:T(8,128)(2,1)S(1)} %shard_map.108.x_mine.tokens), channel_id=1, source_target_pairs={{0,4},{12,8},{1,5},{13,9},{2,6},{14,10},{3,7},{15,11},{16,20},{28,... | collective-permute-start | bytes 3145736 | tf_op jit(solution)/shard_map/ppermute | solution.py:40
  66.2 32.7 %collective-permute-start.9 = (bf16[1024,512]{1,0:T(8,128)(2,1)}, bf16[1024,512]{1,0:T(8,128)(2,1)}, u32[]{:S(2)}, u32[]{:S(2)}) collective-permute-start(bf16[1024,512]{1,0:T(8,128)(2,1)} %shard_map.110), channel_id=1, source_target_pairs={{4,8},{8,4},{5,9},{9,5},{6,10},{10,6},{7,11},{11,7},{20,24},{24,20... | collective-permute-start | bytes 3145736 | tf_op jit(solution)/shard_map/ppermute | solution.py:40
  69.7 16.7 %collective-permute-start.13 = (bf16[512,256]{1,0:T(8,128)(2,1)S(1)}, bf16[512,256]{1,0:T(8,128)(2,1)S(1)}, u32[]{:S(2)}, u32[]{:S(2)}) collective-permute-start(bf16[512,256]{1,0:T(8,128)(2,1)S(1)} %get-tuple-element.76), channel_id=1, source_target_pairs={{0,4},{12,8},{1,5},{13,9},{2,6},{14,10},{3,7},{15,11},{16,20},{28,... | collective-permute-start | bytes 786440 | tf_op jit(solution)/shard_map/ppermute | solution.py:40
  86.4 28.3 %collective-permute-start.18 = (bf16[1024,512]{1,0:T(8,128)(2,1)}, bf16[1024,512]{1,0:T(8,128)(2,1)}, u32[]{:S(2)}, u32[]{:S(2)}) collective-permute-start(bf16[1024,512]{1,0:T(8,128)(2,1)} %collective-permute-done.12), channel_id=1, source_target_pairs={{4,0},{8,12},{5,1},{9,13},{6,2},{10,14},{7,3},{11,15},{20,16},{24,... | collective-permute-start | bytes 3145736 | tf_op jit(solution)/shard_map/ppermute | solution.py:40
  88.3 28.3 %collective-permute-start.17 = (bf16[512,1024]{1,0:T(8,128)(2,1)S(1)}, bf16[512,1024]{1,0:T(8,128)(2,1)S(1)}, u32[]{:S(2)}, u32[]{:S(2)}) collective-permute-start(bf16[512,1024]{1,0:T(8,128)(2,1)S(1)} %copy-done.2), channel_id=1, source_target_pairs={{0,4},{12,8},{1,5},{13,9},{2,6},{14,10},{3,7},{15,11},{16,20},{28,... | collective-permute-start | bytes 3145736 | tf_op jit(solution)/shard_map/ppermute | solution.py:40
  97.8 21.0 %collective-permute-start.16 = (bf16[1024,512]{1,0:T(8,128)(2,1)S(1)}, bf16[1024,512]{1,0:T(8,128)(2,1)S(1)}, u32[]{:S(2)}, u32[]{:S(2)}) collective-permute-start(bf16[1024,512]{1,0:T(8,128)(2,1)S(1)} %add_convert_fusion.1), channel_id=1, source_target_pairs={{4,8},{8,4},{5,9},{9,5},{6,10},{10,6},{7,11},{11,7},{20,24},{24,20... | collective-permute-start | bytes 3145736 | tf_op jit(solution)/shard_map/ppermute | solution.py:40
  98.9 38.1 %collective-permute-start.15 = (bf16[1024,512]{1,0:T(8,128)(2,1)}, bf16[1024,512]{1,0:T(8,128)(2,1)S(1)}, u32[]{:S(2)}, u32[]{:S(2)}) collective-permute-start(bf16[1024,512]{1,0:T(8,128)(2,1)} %collective-permute-done.9), channel_id=1, source_target_pairs={{4,0},{8,12},{5,1},{9,13},{6,2},{10,14},{7,3},{11,15},{20,16},{24,... | collective-permute-start | bytes 3145736 | tf_op jit(solution)/shard_map/ppermute | solution.py:40
  116.0 21.1 %collective-permute-start.20 = (bf16[1024,512]{1,0:T(8,128)(2,1)S(1)}, bf16[1024,512]{1,0:T(8,128)(2,1)S(1)}, u32[]{:S(2)}, u32[]{:S(2)}) collective-permute-start(bf16[1024,512]{1,0:T(8,128)(2,1)S(1)} %broadcast_select_fusion.1.far.rest_2_), channel_id=1, source_target_pairs={{0,16},{16,0},{1,17},{17,1},{2,18},{18,2},{3,19},{19,3},{4,20},{20... | collective-permute-start | bytes 3145736 | tf_op jit(solution)/shard_map/ppermute | solution.py:36
  118.1 42.1 %collective-permute-start.23 = (bf16[1024,512]{1,0:T(8,128)(2,1)S(1)}, bf16[1024,512]{1,0:T(8,128)(2,1)S(1)}, u32[]{:S(2)}, u32[]{:S(2)}) collective-permute-start(bf16[1024,512]{1,0:T(8,128)(2,1)S(1)} %add_convert_fusion), channel_id=1, source_target_pairs={{4,8},{8,4},{5,9},{9,5},{6,10},{10,6},{7,11},{11,7},{20,24},{24,20... | collective-permute-start | bytes 3145736 | tf_op jit(solution)/shard_map/ppermute | solution.py:40
  119.3 34.0 %collective-permute-start.25 = (bf16[1024,256]{1,0:T(8,128)(2,1)S(1)}, bf16[1024,256]{1,0:T(8,128)(2,1)S(1)}, u32[]{:S(2)}, u32[]{:S(2)}) collective-permute-start(bf16[1024,256]{1,0:T(8,128)(2,1)S(1)} %fusion.4), channel_id=1, source_target_pairs={{4,0},{8,12},{5,1},{9,13},{6,2},{10,14},{7,3},{11,15},{20,16},{24,... | collective-permute-start | bytes 1572872 | tf_op jit(solution)/shard_map/ppermute | solution.py:40
  143.1 25.6 %collective-permute-start.19 = (bf16[1024,512]{1,0:T(8,128)(2,1)S(1)}, bf16[1024,512]{1,0:T(8,128)(2,1)S(1)}, u32[]{:S(2)}, u32[]{:S(2)}) collective-permute-start(bf16[1024,512]{1,0:T(8,128)(2,1)S(1)} %broadcast_select_fusion.far), channel_id=1, source_target_pairs={{0,16},{16,0},{1,17},{17,1},{2,18},{18,2},{3,19},{19,3},{4,20},{20... | collective-permute-start | bytes 3145736 | tf_op jit(solution)/shard_map/ppermute | solution.py:36
  174.2 20.4 %collective-permute-start.29 = (bf16[1024,256]{1,0:T(8,128)(2,1)}, bf16[1024,256]{1,0:T(8,128)(2,1)}, u32[]{:S(2)}, u32[]{:S(2)}) collective-permute-start(bf16[1024,256]{1,0:T(8,128)(2,1)} %fusion.5), channel_id=1, source_target_pairs={{4,0},{8,12},{5,1},{9,13},{6,2},{10,14},{7,3},{11,15},{20,16},{24,... | collective-permute-start | bytes 1572872 | tf_op jit(solution)/shard_map/ppermute | solution.py:40
  175.7 18.0 %collective-permute-start.30 = (bf16[1024,128]{1,0:T(8,128)(2,1)}, bf16[1024,128]{1,0:T(8,128)(2,1)}, u32[]{:S(2)}, u32[]{:S(2)}) collective-permute-start(bf16[1024,128]{1,0:T(8,128)(2,1)} %get-tuple-element.126), channel_id=1, source_target_pairs={{0,2},{2,0},{1,3},{3,1},{4,6},{6,4},{5,7},{7,5},{8,10},{10,8},{9,1... | collective-permute-start | bytes 786440 | tf_op jit(solution)/shard_map/ppermute | solution.py:36
  177.3 21.9 %all-to-all-start.1 = ((bf16[4,2,128,256]{3,2,1,0:T(8,128)(2,1)}), bf16[4,2,128,256]{3,2,1,0:T(8,128)(2,1)}, u32[]{:S(2)}, u32[]{:S(2)}) async-start(bf16[4,2,128,256]{3,2,1,0:T(8,128)(2,1)} %bitcast.39), calls=%async_computation.1 | async-start | bytes 1048576 | tf_op jit(solution)/shard_map/all_to_all | solution.py:492
  192.2 18.2 %collective-permute-start.27 = (bf16[2,256,256]{2,1,0:T(8,128)(2,1)}, bf16[2,256,256]{2,1,0:T(8,128)(2,1)}, u32[]{:S(2)}, u32[]{:S(2)}) collective-permute-start(bf16[2,256,256]{2,1,0:T(8,128)(2,1)} %get-tuple-element.111), channel_id=1, source_target_pairs={{0,2},{2,0},{1,3},{3,1},{4,6},{6,4},{5,7},{7,5},{8,10},{10,8},{9,1... | collective-permute-start | bytes 786440 | tf_op jit(solution)/shard_map/ppermute | solution.py:36
  199.2 16.0 %collective-permute-start.31 = (bf16[1024,128]{1,0:T(8,128)(2,1)S(1)}, bf16[1024,128]{1,0:T(8,128)(2,1)S(1)}, u32[]{:S(2)}, u32[]{:S(2)}) collective-permute-start(bf16[1024,128]{1,0:T(8,128)(2,1)S(1)} %get-tuple-element.124), channel_id=1, source_target_pairs={{0,2},{2,0},{1,3},{3,1},{4,6},{6,4},{5,7},{7,5},{8,10},{10,8},{9,1... | collective-permute-start | bytes 786440 | tf_op jit(solution)/shard_map/ppermute | solution.py:36
  (64 other events, 543.3 us)

commit v6 on v5

--- a/solution.py
+++ b/solution.py
@@ -165,14 +165,104 @@
             out[...] = part if i + j == 0 else out[...] + part
 
 
-def low_end_kernel(numbers, ids, part, got, up, wide, delta):
+def low_end_kernel(numbers, ids, part, got, up, dy, wide, delta, grad):
     token = ids[...].astype(f32)
     count = numbers.shape[0] // 2
     ranks = jnp.stack([numbers[i] for i in range(count)])
     value, scale = kept(token, ranks, part[...] + roll_rows(got[...]))
     value = value.astype(bf16).astype(f32)
     spread_into(wide, token, value, [jnp.int32(i) for i in range(count)])
+    grad[...] = contract_first(wide[...], dy[...]).astype(bf16)
     delta[...] = (scale[:, :1] * matmul(wide[...], up[...])).astype(bf16)
+
+
+def to_middle_kernel(x_here, back, x_in, back_in, out):
+    half = back.shape[1] // 2
+    sums = contract_first(x_here[...], back[:, half:])
+    out[...] = (sums + contract_first(x_in[...], back_in[:, half:])).astype(bf16)
+
+
+def to_end_kernel(x_here, back, crossed, out):
+    wide = out.shape[1]
+    sums = contract_first(x_here[...], back[:, wide : 2 * wide])
+    out[...] = (sums + crossed[:, wide:].astype(f32)).astype(bf16)
+
+
+def finish_kernel(x_here, back, x_in, back_in, crossed, outer, here, there):
+    size = here.shape[1]
+    wide = 2 * size
+    sums = contract_first(x_here[...], back[:, :wide])
+    sums += contract_first(x_in[...], back_in[:, :wide])
+    sums += crossed[:, :wide].astype(f32) + outer[...].astype(f32)
+    here[...] = sums[:, :size].astype(bf16)
+    there[...] = sums[:, size:].astype(bf16)
+
+
+def up_sent_kernel(up, out):
+    cols = out.shape[2]
+    for i in range(out.shape[0]):
+        out[i] = up[:, (i % 2) * cols : (i % 2 + 1) * cols]
+
+
+def packet_kernel(flags, here, ids_here, packet, half, ids, quarter):
+    rows, kv = here.shape
+    half[:rows] = here[...]
+    half[rows:] = packet[:, :kv]
+    ids[:rows] = ids_here[...]
+    ids[rows:] = packet[:, kv:]
+    cols = quarter.shape[1]
+    span = pl.ds(pl.multiple_of(flags[3] * cols, 128), cols)
+    quarter[:rows] = here[:, span]
+    quarter[rows:] = packet[:, span]
+
+
+def dy_line_kernel(places, here, got, out):
+    cols = out.shape[1] // 4
+    for i in range(4):
+        place = places[i]
+        span = pl.ds(pl.multiple_of((place % 2) * cols, 128), cols)
+        own = place // 2 == places[4]
+
+        @pl.when(own)
+        def _():
+            out[:, i * cols : (i + 1) * cols] = here[:, span]
+
+        @pl.when(jnp.logical_not(own))
+        def _():
+            out[:, i * cols : (i + 1) * cols] = got[:, span]
+
+
+def far_kernel(flags, crossed, outer, out):
+    @pl.when(flags[4] == 1)
+    def _():
+        out[...] = crossed[...]
+
+    @pl.when(flags[4] == 0)
+    def _():
+        out[...] = outer[...]
+
+
+def up_sum_kernel(numbers, got, here, there):
+    count = numbers.shape[0] // 2
+    for i, out in enumerate((here, there)):
+        adapter = numbers[count + i]
+        rank = jnp.float32(1.0)
+        for a in range(count):
+            rank = jnp.where(adapter == a, numbers[a].astype(f32), rank)
+        part = got[0, adapter % 2].astype(f32)
+        for source in range(1, got.shape[0]):
+            part += got[source, adapter % 2].astype(f32)
+        out[...] = (jnp.full(part.shape, 16.0, f32) / rank * part).astype(bf16)
+
+
+def up_place_kernel(flags, here, there, out):
+    cols = here.shape[1]
+    out[:, pl.ds(pl.multiple_of(flags[3] * cols, 128), cols)] = here[...]
+    out[:, pl.ds(pl.multiple_of((1 - flags[3]) * cols, 128), cols)] = there[...]
+
+
+def add_kernel(left, right, out):
+    out[...] = left[...] + right[...]
 
 
 def dx_kernel(dy, back, own, near, far, *rest):
@@ -264,7 +354,9 @@
     ).astype(jnp.int32)
     ranks = size // 8 * rank_step_count
     numbers = jnp.concatenate([ranks, adapters])
-    flags = jnp.stack([(c == 0) == first_pair, z % 2 == 1, z >= 2, x == 1]).astype(jnp.int32)
+    flags = jnp.stack([(c == 0) == first_pair, z % 2 == 1, z >= 2, x == 1, is_middle])
+    flags = flags.astype(jnp.int32)
+    places = jnp.stack([*line, c]).astype(jnp.int32)
 
     latest = []
 
@@ -279,9 +371,6 @@
 
     def like(*shape, kind=bf16):
         return jax.ShapeDtypeStruct(shape, kind)
-
-    def cut(value, start, length, axis):
-        return lax.dynamic_slice_in_dim(value, start, length, axis)
 
     def join(*values):
         return jnp.concatenate(values, axis=1)
@@ -330,12 +419,9 @@
         )[0]
 
     down_got = swap(done(rows_at(2, down, eighth)), "own")
-    up_sent = jnp.broadcast_to(
-        step(up).reshape(size, 2, kvq).transpose(1, 0, 2)[None], (4, 2, size, kvq)
-    ).reshape(number, size, kvq)
-    up_all = lax.all_to_all(
-        done(up_sent), ("fsdp", "own"), split_axis=0, concat_axis=0, tiled=True
-    ).reshape(number * size, kvq)
+    ids_here = jnp.broadcast_to(token_adapter.astype(bf16), (rows, size))
+    packet = swap(done(join(step(cotangent), ids_here)), "own")
+    x_got = [swap(done(columns_at(2, step(tokens))), "own")]
     down_piece = done(
         copy_call(
             lambda n, a, o: [
@@ -349,36 +435,49 @@
         )[0]
     )
     down_near = along(down_piece, NEIGHBOURS)
-    ids_here = jnp.broadcast_to(token_adapter.astype(bf16), (rows, size))
-    packet = swap(done(join(step(cotangent), ids_here)), "own")
-    x_got = [swap(done(columns_at(2, step(tokens))), "own")]
+    up, packet = step(up, packet)
+    up_sent = kernel_call(up_sent_kernel, [like(number, size, kvq)], up)[0]
+    up_all = lax.all_to_all(
+        done(up_sent), ("fsdp", "own"), split_axis=0, concat_axis=0, tiled=True
+    ).reshape(number * size, kvq)
     weight_here = done(rows_at(0, step(frozen_value_weight), eighth))
     weight_near = along(weight_here, NEIGHBOURS)
 
-    packet = step(packet)
-    dy_half = jnp.concatenate([cotangent, packet[:, :kv]], axis=0)
-    ids = jnp.concatenate([ids_here, packet[:, kv:]], axis=0)
-    dy_quarter = cut(dy_half, x * kvq, kvq, 1)
-    dy_tp = swap(done(dy_half), "tp")
-
-    down_near = step(down_near)
+    dy_half, ids, dy_quarter = kernel_call(
+        packet_kernel,
+        [like(both, kv), like(both, size), like(both, kvq)],
+        cotangent,
+        ids_here,
+        step(packet),
+        scalars=flags,
+    )
+    done(dy_quarter)
+    dy_tp = swap(dy_half, "tp")
+
+    down_near, x_got[0] = step(down_near, x_got[0])
     crossing = done(side_by_side(down_piece, down_near))
     down_crossed = along(crossing, MIDDLE)
     down_other = swap(crossing, "rep")
+    x_mine = done(tokens_of(0, tokens, step(x_got[0])))
+    x_in = [along(x_mine, INWARD)]
+    dy_line = done(
+        kernel_call(
+            dy_line_kernel, [like(both, 2 * kv)], dy_half, step(dy_tp), scalars=places
+        )[0]
+    )
 
     compact = like(both, size, kind=f32)
-    up_all, dy_quarter = step(up_all, dy_quarter)
+    up_all = step(up_all)
     back_part = done(kernel_call(back_kernel, [compact], ids, dy_quarter, up_all)[0])
     back_tp = swap(back_part, "tp")
-    x_mine = done(tokens_of(0, tokens, step(x_got[0])))
-    back_part = done(back_part + step(back_tp))
-    back_got = swap(back_part, "own")
-    x_got.append(swap(done(columns_at(3, step(tokens))), "own"))
-    x_in = [along(x_mine, INWARD)]
     weight_near = step(weight_near)
     crossing = done(side_by_side(weight_here, weight_near))
     weight_crossed = along(crossing, MIDDLE)
-    weight_near_other = swap(weight_near, "rep")
+    back_part = done(kernel_call(add_kernel, [compact], back_part, step(back_tp))[0])
+    back_got = swap(back_part, "own")
+    sent, down_other = step(tokens, down_other)
+    x_got.append(swap(done(columns_at(3, sent)), "own"))
+    weight_other = done(rows_at(1, step(frozen_value_weight), eighth))
     back_wide, back_sent = kernel_call(
         back_end_kernel,
         [like(both, number * size), like(both, wide)],
@@ -388,56 +487,64 @@
         scalars=numbers,
     )
     back_in = along(done(back_sent), INWARD)
+    down_crossed = done(step(down_crossed))
+    down_outer = along(down_crossed, OUTWARD)
     x_other = done(tokens_of(1, tokens, step(x_got[1])))
     x_in.append(along(x_other, INWARD))
     x_both = [x_mine, x_other]
 
-    dy_tp = step(dy_tp)
-    dy_full = jnp.where(c == 0, join(dy_half, dy_tp), join(dy_tp, dy_half))
-    dy_line = done(join(*[cut(dy_full, t * cols, cols, 1) for t in line]))
-    weight_other = done(rows_at(1, step(frozen_value_weight), eighth))
-
-    def total(half, first, last):
-        return contract_first(x_both[half], back_wide[:, first * wide : last * wide])
-
-    def total_in(half, first, last):
-        return contract_first(x_in[half], back_in_wide[:, first * wide : last * wide])
-
-    def to_middle(half, *others):
-        x_in[half], *_ = step(x_in[half], back_in_wide, *others)
-        sums = total(half, 2, 4) + total_in(half, 2, 4)
-        return along(done(sums.astype(bf16)), MIDDLE)
+    def to_middle(half):
+        x_in[half] = step(x_in[half])
+        sums = kernel_call(
+            to_middle_kernel,
+            [like(eighth, 2 * wide)],
+            x_both[half],
+            back_wide,
+            x_in[half],
+            back_in_wide,
+        )[0]
+        return along(done(sums), MIDDLE)
 
     def to_end(half, crossed):
-        crossed = step(crossed)
-        sums = total(half, 1, 2) + crossed[:, wide:].astype(f32)
-        return along(done(sums.astype(bf16)), OUTWARD)
+        sums = kernel_call(
+            to_end_kernel, [like(eighth, wide)], x_both[half], back_wide, step(crossed)
+        )[0]
+        return along(done(sums), OUTWARD)
 
     def finish(half, crossed, outer, *others):
         outer, *_ = step(outer, x_mine, *others)
-        grad = total(half, 0, 1) + total_in(half, 0, 1)
-        grad = (grad + crossed[:, :wide].astype(f32) + outer.astype(f32)).astype(bf16)
-        here, there = grad[:, :size], grad[:, size:]
+        here, there = kernel_call(
+            finish_kernel,
+            [like(eighth, size)] * 2,
+            x_both[half],
+            back_wide,
+            x_in[half],
+            back_in_wide,
+            crossed,
+            outer,
+        )
         done(here)
         return here, swap(there, "own")
 
-    down_crossed, back_in, down_other = step(down_crossed, back_in, down_other)
-    down_outer = along(down_crossed, OUTWARD)
+    def far_of(crossed, outer):
+        out = like(*crossed.shape)
+        return kernel_call(far_kernel, [out], crossed, outer, scalars=flags)[0]
+
     back_in_wide = done(
         kernel_call(
-            spread_in_kernel, [like(both, number * size)], back_in, scalars=numbers
+            spread_in_kernel, [like(both, number * size)], step(back_in), scalars=numbers
         )[0]
     )
     middle = [to_middle(0)]
-    weight_crossed, weight_near_other = step(weight_crossed, weight_near_other)
+    weight_near_other = swap(step(weight_near), "rep")
+    weight_crossed = done(step(weight_crossed))
     weight_outer = along(weight_crossed, OUTWARD)
-    down_outer = step(down_outer)
-    down_far = done(jnp.where(is_middle, down_crossed, down_outer))
+    down_outer, weight_near_other = step(down_outer, weight_near_other)
+    down_far = done(far_of(down_crossed, down_outer))
     down_far_other = swap(down_far, "rep")
     middle.append(to_middle(1))
     outward = [to_end(0, middle[0])]
-    weight_outer = step(weight_outer)
-    weight_far = done(jnp.where(is_middle, weight_crossed, weight_outer))
+    weight_far = done(far_of(weight_crossed, step(weight_outer)))
     weight_far_other = swap(weight_far, "rep")
 
     low_part = done(
@@ -479,37 +586,25 @@
     done(dx_mine)
     dx_mine_got = swap(dx_sent, "own")
     grads = [finish(0, middle[0], outward[0])]
-    low_wide, delta = kernel_call(
+    _, delta, up_part = kernel_call(
         low_end_kernel,
-        [like(both, number * size), like(both, kvq)],
+        [like(both, number * size), like(both, kvq), like(number * size, kvq)],
         ids,
         low_part,
         step(low_got),
         up_all,
+        dy_quarter,
         scalars=numbers,
     )
-    up_part = done(contract_first(low_wide, dy_quarter).astype(bf16))
     up_got = lax.all_to_all(
-        up_part.reshape(4, 2, size, kvq), "fsdp", split_axis=0, concat_axis=0, tiled=True
+        done(up_part).reshape(4, 2, size, kvq), "fsdp", split_axis=0, concat_axis=0, tiled=True
     )
     outward.append(to_end(1, middle[1]))
-
-    weight_far_other, dx_mine_got = step(weight_far_other, dx_mine_got)
-    y_keep, y_sent = kernel_call(
-        y_kernel,
-        blocks,
-        x_other,
-        weight_other,
-        weight_near_other,
-        weight_far_other,
-        *y_first,
-        scalars=flags,
-    )
-    y_got = swap(done(y_sent), "tp")
+    weight_far_other, dx_mine_got, grad_got = step(weight_far_other, dx_mine_got, grads[0][1])
     dx_other, dx_sent = kernel_call(
         dx_kernel,
         half_grad,
-        step(dy_line),
+        dy_line,
         back_wide,
         weight_other,
         weight_near_other,
@@ -518,6 +613,17 @@
         down_far_other,
     )
     dx_other_got = swap(done(dx_sent), "own")
+    y_keep, y_sent = kernel_call(
+        y_kernel,
+        blocks,
+        step(x_other),
+        weight_other,
+        weight_near_other,
+        weight_far_other,
+        *y_first,
+        scalars=flags,
+    )
+    y_got = swap(done(y_sent), "tp")
     y_here, y_sent = kernel_call(
         y_sum_kernel,
         [like(2, rows, cols, kind=f32), like(2, rows, cols)],
@@ -527,13 +633,11 @@
         scalars=flags,
     )
     y_got = swap(done(y_sent), "own")
-    grads.append(finish(1, middle[1], outward[1], grads[0][1]))
-
-    up_sum = jnp.sum(step(up_got).astype(f32), axis=0)
-    own_ranks = cut(ranks, 2 * z, 2, 0).astype(f32)
-    up_sum = done(((16.0 / own_ranks)[:, None, None] * up_sum).astype(bf16))
-    up_mine = cut(up_sum, x, 1, 0)
-    up_theirs = swap(cut(up_sum, 1 - x, 1, 0), "own")
+    up_mine, up_theirs = kernel_call(
+        up_sum_kernel, [like(size, kvq)] * 2, step(up_got), scalars=numbers
+    )
+    up_theirs = swap(done(up_theirs), "own")
+    grads.append(finish(1, middle[1], outward[1]))
 
     def in_place(axis, out, *pieces):
         def plan(n, a, o):
@@ -551,15 +655,12 @@
     projected = done(kernel_call(y_end_kernel, [like(rows, kv)], y_here, step(y_got))[0])
     down_gradient = done(
         in_place(
-            0, like(width, size), grads[0][0], grads[1][0], grads[0][1], step(grads[1][1])
+            0, like(width, size), grads[0][0], grads[1][0], grad_got, step(grads[1][1])
         )[None]
     )
-    up_theirs = step(up_theirs)
-    up_gradient = jnp.where(
-        x == 0,
-        jnp.concatenate([up_mine, up_theirs], axis=2),
-        jnp.concatenate([up_theirs, up_mine], axis=2),
-    )
+    up_gradient = kernel_call(
+        up_place_kernel, [like(size, kv)], up_mine, step(up_theirs), scalars=flags
+    )[0][None]
     return (projected, input_grad, down_gradient, up_gradient)
 
 

time: 220 us -> 223 us (1.014)
  matrix products: 13.4 us -> 0 us
  Pallas kernels: 49.6 us -> 62.8 us
  local copies, waits for them, and re-layouts: 14.6 us -> 24.2 us
  other arithmetic: 8.01 us -> 1.82 us
  waiting for transfers between devices: 74 us -> 69.6 us
  starting transfers between devices: 57.3 us -> 61.2 us
    dot_general x11 -> x0, matrix products: 13.4 us -> none  [contract_first(): lax.dot_general(left, right, (((0,), (0,)), ((), ())), preferred_element_...]
    pallas_call x23 -> x37, Pallas kernels: 49.6 us -> 62.8 us  [kernel_call(): pl.pallas_call(body, out_shape=list(outs), in_specs=specs, out_specs=[pl....]
    unnamed x106 -> x104, local copies, waits for them, and re-layouts: 10.7 us -> 23.8 us
    ppermute x13, waiting for transfers between devices: 43.1 us -> 30.2 us  [along(): return lax.ppermute(value, 'fsdp', pairs)]
    ppermute x20, waiting for transfers between devices: 28 us -> 32.4 us  [swap(): return lax.ppermute(value, axis, PAIR)]
    all_to_all x1, waiting for transfers between devices: 2.94 us -> 7.06 us  [body_line(): lax.all_to_all(done(up_part).reshape(4, 2, size, kvq), 'fsdp', split_axis...]
    select_n x4 -> x0, other arithmetic: 3.66 us -> none  [the longest x1 1.52 us: body_line(): dy_full = jnp.where(c == 0, join(dy_half, dy_tp), join(dy_tp, dy_half))]
  transfers between devices with their start and end apart: 35 -> 35, of which waited for: 14 -> 17; matrix products, arithmetic and copies ran while one was open for 11% -> 1% of each run, Pallas kernels for 20% -> 24%
where the time goes in v6:
time: 223 us; the launch traced here: 221 us
  waiting for transfers between devices  69.6 us (31%)
  Pallas kernels  62.8 us (28%)
  starting transfers between devices  61.2 us (27%)
  local copies, waits for them, and re-layouts  24.2 us (11%)
    pallas_call x37, Pallas kernels, kernel_call(): pl.pallas_call(body, out_shape=list(outs), in_specs=specs, out_specs=[pl....  62.8 us
    ppermute x20, waiting for transfers between devices, swap(): return lax.ppermute(value, axis, PAIR)  32.4 us
    ppermute x13, waiting for transfers between devices, along(): return lax.ppermute(value, 'fsdp', pairs)  30.2 us
    ppermute x13, starting transfers between devices, along(): return lax.ppermute(value, 'fsdp', pairs)  29.4 us
    unnamed x104, local copies, waits for them, and re-layouts  23.8 us
    ppermute x20, starting transfers between devices, swap(): return lax.ppermute(value, axis, PAIR)  21.2 us
    all_to_all x1, waiting for transfers between devices, body_line(): lax.all_to_all(done(up_part).reshape(4, 2, size, kvq), 'fsdp', split_axis...  7.06 us
    all_to_all x1, starting transfers between devices, body_line(): lax.all_to_all(done(up_sent), ('fsdp', 'own'), split_axis=0, concat_axis=...  6.37 us
  transfers between devices with their start and end apart: 35, of which 17 were waited for; matrix products, arithmetic and copies ran while one was open for 1% of the time, Pallas kernels for 24%

profile of v6, /device:TPU:0, one launch (start us, length us, event | category | flops | bytes accessed | tf_op | source)
XLA Modules:
  0.0 221.0 jit_solution(10809940899148383894)
XLA Ops:
  2.5 3.0 %collective-permute-start = (bf16[1024,128]{1,0:T(8,128)(2,1)S(1)}, bf16[1024,128]{1,0:T(8,128)(2,1)S(1)}, u32[]{:S(2)}, u32[]{:S(2)}) collective-permute-start(bf16[1024,128]{1,0:T(8,128)(2,1)S(1)} %shard_map.102), channel_id=1, source_target_pairs={{0,2},{2,0},{1,3},{3,1},{4,6},{6,4},{5,7},{7,5},{8,10},{10,8},{9,1... | collective-permute-start | bytes 786440 | tf_op jit(solution)/shard_map/ppermute | solution.py:36
  15.6 4.1 %collective-permute-done.3.packet = bf16[256,640]{1,0:T(8,128)(2,1)S(1)} collective-permute-done((bf16[256,640]{1,0:T(8,128)(2,1)S(1)}, bf16[256,640]{1,0:T(8,128)(2,1)S(1)}, u32[]{:S(2)}, u32[]{:S(2)}) %collective-permute-start.3) | collective-permute-done | bytes 327712 | tf_op jit(solution)/shard_map/ppermute | solution.py:36
  21.3 6.4 %all-to-all-start = ((bf16[8,128,256]{2,1,0:T(8,128)(2,1)}), bf16[8,128,256]{2,1,0:T(8,128)(2,1)}, u32[]{:S(2)}, u32[]{:S(2)}) async-start(bf16[8,128,256]{2,1,0:T(8,128)(2,1)} %shard_map.105), calls=%async_computation | async-start | bytes 1048576 | tf_op jit(solution)/shard_map/all_to_all | solution.py:440
  33.0 2.6 %shard_map.108 = bf16[1024,512]{1,0:T(8,128)(2,1)} custom-call(s32[4]{0:T(128)S(1)} %pad_add_fusion.numbers, bf16[1024,256]{1,0:T(8,128)(2,1)S(1)} %shard_map.104.refs_0_.own.rest_0_, bf16[1024,256]{1,0:T(8,128)(2,1)} %collective-permute-done.1.refs_1_.near.rest_1_), custom_call_target="tpu_custom_call" | custom-call | tf_op jit(solution)/shard_map/pallas_call | solution.py:48
  38.9 5.0 %collective-permute-start.7 = (bf16[1024,256]{1,0:T(8,128)(2,1)S(1)}, bf16[1024,256]{1,0:T(8,128)(2,1)S(1)}, u32[]{:S(2)}, u32[]{:S(2)}) collective-permute-start(bf16[1024,256]{1,0:T(8,128)(2,1)S(1)} %shard_map.106.refs_0_.own), channel_id=1, source_target_pairs={{0,4},{4,0},{8,12},{12,8},{1,5},{5,1},{9,13},{13,9},{2,6},{6,2},{1... | collective-permute-start | bytes 1572872 | tf_op jit(solution)/shard_map/ppermute | solution.py:40
  51.2 3.1 %collective-permute-start.12 = (bf16[512,1024]{1,0:T(8,128)(2,1)S(1)}, bf16[512,1024]{1,0:T(8,128)(2,1)}, u32[]{:S(2)}, u32[]{:S(2)}) collective-permute-start(bf16[512,1024]{1,0:T(8,128)(2,1)S(1)} %shard_map.109.x_here.x_mine.tokens), channel_id=1, source_target_pairs={{0,4},{12,8},{1,5},{13,9},{2,6},{14,10},{3,7},{15,11},{16,20},{28,... | collective-permute-start | bytes 3145736 | tf_op jit(solution)/shard_map/ppermute | solution.py:40
  71.2 4.6 %collective-permute-start.13 = (bf16[512,256]{1,0:T(8,128)(2,1)S(1)}, bf16[512,256]{1,0:T(8,128)(2,1)S(1)}, u32[]{:S(2)}, u32[]{:S(2)}) collective-permute-start(bf16[512,256]{1,0:T(8,128)(2,1)S(1)} %get-tuple-element.94), channel_id=1, source_target_pairs={{0,4},{12,8},{1,5},{13,9},{2,6},{14,10},{3,7},{15,11},{16,20},{28,... | collective-permute-start | bytes 786440 | tf_op jit(solution)/shard_map/ppermute | solution.py:40
  84.4 2.9 %shard_map.119 = bf16[1024,512]{1,0:T(8,128)(2,1)S(1)} custom-call(bf16[512,1024]{1,0:T(8,128)(2,1)S(1)} %shard_map.109.x_here.x_mine.tokens, bf16[512,1024]{1,0:T(8,128)(2,1)S(1)} %get-tuple-element.97.back, bf16[512,1024]{1,0:T(8,128)(2,1)} %collective-permute-done.12.x_in, bf16[512,1024]{1,0:T(8,128)(2,1)S(1)} %shard_map.118.back_in), custom_call_target="tpu_custom_call" | custom-call | tf_op jit(solution)/shard_map/pallas_call | solution.py:48
  87.9 4.4 %collective-permute-start.18 = (bf16[512,1024]{1,0:T(8,128)(2,1)S(1)}, bf16[512,1024]{1,0:T(8,128)(2,1)S(1)}, u32[]{:S(2)}, u32[]{:S(2)}) collective-permute-start(bf16[512,1024]{1,0:T(8,128)(2,1)S(1)} %shard_map.117.x_here.x_other.tokens), channel_id=1, source_target_pairs={{0,4},{12,8},{1,5},{13,9},{2,6},{14,10},{3,7},{15,11},{16,20},{28,... | collective-permute-start | bytes 3145736 | tf_op jit(solution)/shard_map/ppermute | solution.py:40
  94.4 6.2 %collective-permute-done.14.near = bf16[1024,256]{1,0:T(8,128)(2,1)S(1)} collective-permute-done((bf16[1024,256]{1,0:T(8,128)(2,1)S(1)}, bf16[1024,256]{1,0:T(8,128)(2,1)S(1)}, u32[]{:S(2)}, u32[]{:S(2)}) %collective-permute-start.14) | collective-permute-done | bytes 524320 | tf_op jit(solution)/shard_map/ppermute | solution.py:36
  102.5 11.6 %collective-permute-done.18.x_in = bf16[512,1024]{1,0:T(8,128)(2,1)S(1)} collective-permute-done((bf16[512,1024]{1,0:T(8,128)(2,1)S(1)}, bf16[512,1024]{1,0:T(8,128)(2,1)S(1)}, u32[]{:S(2)}, u32[]{:S(2)}) %collective-permute-start.18) | collective-permute-done | bytes 1048608 | tf_op jit(solution)/shard_map/ppermute | solution.py:40
  122.1 6.0 %collective-permute-done.20.far_other.rest_1_ = bf16[1024,512]{1,0:T(8,128)(2,1)S(1)} collective-permute-done((bf16[1024,512]{1,0:T(8,128)(2,1)S(1)}, bf16[1024,512]{1,0:T(8,128)(2,1)S(1)}, u32[]{:S(2)}, u32[]{:S(2)}) %collective-permute-start.20) | collective-permute-done | bytes 1048608 | tf_op jit(solution)/shard_map/ppermute | solution.py:36
  128.1 3.8 %shard_map.124 = f32[512,128]{1,0:T(8,128)S(1)} custom-call(s32[16]{0:T(128)S(1)} %concatenate.7.numbers, bf16[512,128]{1,0:T(8,128)(2,1)S(1)} %get-tuple-element.83.ids, bf16[512,1024]{1,0:T(8,128)(2,1)S(1)} %shard_map.109.x_here.x_mine.tokens, bf16[512,1024]{1,0:T(8,128)(2,1)S(1)} %shard_map.117.x_here.x_other.tokens, bf16[1024,256]{1,0:T(8,128)(2,1)S(1)} %copy-done.13, ...), custom_call_target="tpu_custom_call" | custom-call | tf_op jit(solution)/shard_map/pallas_call | solution.py:48
  133.4 3.6 %shard_map.125 = (f32[2,512,256]{2,1,0:T(8,128)S(1)}, f32[2,512,256]{2,1,0:T(8,128)S(1)}) custom-call(s32[5]{0:T(128)S(1)} %convert_element_type.6.flags, bf16[512,1024]{1,0:T(8,128)(2,1)S(1)} %shard_map.109.x_here.x_mine.tokens, bf16[1024,256]{1,0:T(8,128)(2,1)S(1)} %copy-done.11, bf16[1024,256]{1,0:T(8,128)(2,1)S(1)} %copy-done.15, ...), custom_call_target="tpu_custom_call" | custom-call | tf_op jit(solution)/shard_map/pallas_call | solution.py:48
  137.1 3.4 %shard_map.126 = (bf16[256,1024]{1,0:T(8,128)(2,1)S(1)}, bf16[256,1024]{1,0:T(8,128)(2,1)S(1)}) custom-call(bf16[512,1024]{1,0:T(8,128)(2,1)S(1)} %copy-done.7, bf16[512,1024]{1,0:T(8,128)(2,1)S(1)} %get-tuple-element.97.back, bf16[1024,256]{1,0:T(8,128)(2,1)S(1)} %copy-done.11, bf16[1024,256]{1,0:T(8,128)(2,1)S(1)} %copy-done.15, ...), custom_call_target="tpu_custom_call" | custom-call | tf_op jit(solution)/shard_map/pallas_call | solution.py:48
  143.0 5.4 %collective-permute-done.23.outer = bf16[1024,256]{1,0:T(8,128)(2,1)S(1)} collective-permute-done((bf16[1024,256]{1,0:T(8,128)(2,1)S(1)}, bf16[1024,256]{1,0:T(8,128)(2,1)S(1)}, u32[]{:S(2)}, u32[]{:S(2)}) %collective-permute-start.23) | collective-permute-done | bytes 524320 | tf_op jit(solution)/shard_map/ppermute | solution.py:40
  152.9 8.4 %collective-permute-done.26.got = f32[512,128]{1,0:T(8,128)S(1)} collective-permute-done((f32[512,128]{1,0:T(8,128)S(1)}, f32[512,128]{1,0:T(8,128)S(1)}, u32[]{:S(2)}, u32[]{:S(2)}) %collective-permute-start.26) | collective-permute-done | bytes 262176 | tf_op jit(solution)/shard_map/ppermute | solution.py:36
  161.3 2.6 %shard_map.128 = (bf16[512,1024]{1,0:T(8,128)(2,1)}, bf16[512,256]{1,0:T(8,128)(2,1)S(1)}, bf16[1024,256]{1,0:T(8,128)(2,1)S(1)}) custom-call(s32[16]{0:T(128)S(1)} %concatenate.7.numbers, bf16[512,128]{1,0:T(8,128)(2,1)S(1)} %get-tuple-element.83.ids, f32[512,128]{1,0:T(8,128)S(1)} %add.61.part, f32[512,128]{1,0:T(8,128)S(1)} %collective-permute-done.26.got, ...), custom_call_target="tpu_custom_call" | custom-call | tf_op jit(solution)/shard_map/pallas_call | solution.py:48
  166.6 3.9 %shard_map.130 = (bf16[256,1024]{1,0:T(8,128)(2,1)S(1)}, bf16[256,1024]{1,0:T(8,128)(2,1)S(1)}) custom-call(bf16[512,1024]{1,0:T(8,128)(2,1)S(1)} %copy-done.7, bf16[512,1024]{1,0:T(8,128)(2,1)S(1)} %get-tuple-element.97.back, bf16[1024,256]{1,0:T(8,128)(2,1)S(1)} %shard_map.115.own, bf16[1024,256]{1,0:T(8,128)(2,1)S(1)} %collective-permute-done.14.near, ...), custom_call_target="tpu_custom_call" | custom-call | tf_op jit(solution)/shard_map/pallas_call | solution.py:48
  171.3 4.5 %shard_map.131 = (f32[2,512,256]{2,1,0:T(8,128)S(1)}, f32[2,512,256]{2,1,0:T(8,128)}) custom-call(s32[5]{0:T(128)S(1)} %convert_element_type.6.flags, bf16[512,1024]{1,0:T(8,128)(2,1)S(1)} %shard_map.117.x_here.x_other.tokens, bf16[1024,256]{1,0:T(8,128)(2,1)S(1)} %shard_map.115.own, bf16[1024,256]{1,0:T(8,128)(2,1)S(1)} %collective-permute-done.14.near, ...), custom_call_target="tpu_custom_call" | custom-call | tf_op jit(solution)/shard_map/pallas_call | solution.py:48
  176.8 4.3 %all-to-all-start.1 = ((bf16[4,2,128,256]{3,2,1,0:T(8,128)(2,1)}), bf16[4,2,128,256]{3,2,1,0:T(8,128)(2,1)}, u32[]{:S(2)}, u32[]{:S(2)}) async-start(bf16[4,2,128,256]{3,2,1,0:T(8,128)(2,1)} %bitcast.30), calls=%async_computation.1 | async-start | bytes 1048576 | tf_op jit(solution)/shard_map/all_to_all | solution.py:599
  189.6 7.1 %all-to-all-done.1.got = bf16[4,2,128,256]{3,2,1,0:T(8,128)(2,1)} async-done(((bf16[4,2,128,256]{3,2,1,0:T(8,128)(2,1)}), bf16[4,2,128,256]{3,2,1,0:T(8,128)(2,1)}, u32[]{:S(2)}, u32[]{:S(2)}) %all-to-all-start.1) | async-done | bytes 524320 | tf_op jit(solution)/shard_map/all_to_all | solution.py:599
  197.8 7.1 %collective-permute-done.30.outer = bf16[1024,256]{1,0:T(8,128)(2,1)} collective-permute-done((bf16[1024,256]{1,0:T(8,128)(2,1)}, bf16[1024,256]{1,0:T(8,128)(2,1)}, u32[]{:S(2)}, u32[]{:S(2)}) %collective-permute-start.30) | collective-permute-done | bytes 524320 | tf_op jit(solution)/shard_map/ppermute | solution.py:40
  211.5 3.1 %shard_map.135 = bf16[256,4096]{1,0:T(8,128)(2,1)} custom-call(s32[4]{0:T(128)S(1)} %pad_add_fusion.numbers, bf16[256,1024]{1,0:T(8,128)(2,1)S(1)} %copy-done.30, bf16[256,1024]{1,0:T(8,128)(2,1)S(1)} %copy-done.34, bf16[256,1024]{1,0:T(8,128)(2,1)S(1)} %copy-done.32, bf16[256,1024]{1,0:T(8,128)(2,1)} %collective-permute-done.29.refs_3_), custom_call_target="tpu_custom_call" | custom-call | tf_op jit(solution)/shard_map/pallas_call | solution.py:48
  (197 shorter events, 102.6 us)
Async XLA Ops:
  10.5 22.5 %collective-permute-start.2 = (bf16[256,1024]{1,0:T(8,128)(2,1)}, bf16[256,1024]{1,0:T(8,128)(2,1)}, u32[]{:S(2)}, u32[]{:S(2)}) collective-permute-start(bf16[256,1024]{1,0:T(8,128)(2,1)} %shard_map.103), channel_id=1, source_target_pairs={{0,2},{2,0},{1,3},{3,1},{4,6},{6,4},{5,7},{7,5},{8,10},{10,8},{9,1... | collective-permute-start | bytes 1572872 | tf_op jit(solution)/shard_map/ppermute | solution.py:36
  13.3 19.7 %collective-permute-start.1 = (bf16[1024,256]{1,0:T(8,128)(2,1)S(1)}, bf16[1024,256]{1,0:T(8,128)(2,1)}, u32[]{:S(2)}, u32[]{:S(2)}) collective-permute-start(bf16[1024,256]{1,0:T(8,128)(2,1)S(1)} %shard_map.104.refs_0_.own.rest_0_), channel_id=1, source_target_pairs={{0,4},{4,0},{8,12},{12,8},{1,5},{5,1},{9,13},{13,9},{2,6},{6,2},{1... | collective-permute-start | bytes 1572872 | tf_op jit(solution)/shard_map/ppermute | solution.py:40
  21.3 28.4 %all-to-all-start = ((bf16[8,128,256]{2,1,0:T(8,128)(2,1)}), bf16[8,128,256]{2,1,0:T(8,128)(2,1)}, u32[]{:S(2)}, u32[]{:S(2)}) async-start(bf16[8,128,256]{2,1,0:T(8,128)(2,1)} %shard_map.105), calls=%async_computation | async-start | bytes 1048576 | tf_op jit(solution)/shard_map/all_to_all | solution.py:440
  35.6 26.2 %collective-permute-start.4 = (bf16[1024,512]{1,0:T(8,128)(2,1)}, bf16[1024,512]{1,0:T(8,128)(2,1)}, u32[]{:S(2)}, u32[]{:S(2)}) collective-permute-start(bf16[1024,512]{1,0:T(8,128)(2,1)} %shard_map.108), channel_id=1, source_target_pairs={{0,16},{16,0},{1,17},{17,1},{2,18},{18,2},{3,19},{19,3},{4,20},{20... | collective-permute-start | bytes 3145736 | tf_op jit(solution)/shard_map/ppermute | solution.py:36
  37.2 32.7 %collective-permute-start.9 = (bf16[1024,512]{1,0:T(8,128)(2,1)}, bf16[1024,512]{1,0:T(8,128)(2,1)}, u32[]{:S(2)}, u32[]{:S(2)}) collective-permute-start(bf16[1024,512]{1,0:T(8,128)(2,1)} %shard_map.108), channel_id=1, source_target_pairs={{4,8},{8,4},{5,9},{9,5},{6,10},{10,6},{7,11},{11,7},{20,24},{24,20... | collective-permute-start | bytes 3145736 | tf_op jit(solution)/shard_map/ppermute | solution.py:40
  38.9 17.3 %collective-permute-start.7 = (bf16[1024,256]{1,0:T(8,128)(2,1)S(1)}, bf16[1024,256]{1,0:T(8,128)(2,1)S(1)}, u32[]{:S(2)}, u32[]{:S(2)}) collective-permute-start(bf16[1024,256]{1,0:T(8,128)(2,1)S(1)} %shard_map.106.refs_0_.own), channel_id=1, source_target_pairs={{0,4},{4,0},{8,12},{12,8},{1,5},{5,1},{9,13},{13,9},{2,6},{6,2},{1... | collective-permute-start | bytes 1572872 | tf_op jit(solution)/shard_map/ppermute | solution.py:40
  51.2 33.2 %collective-permute-start.12 = (bf16[512,1024]{1,0:T(8,128)(2,1)S(1)}, bf16[512,1024]{1,0:T(8,128)(2,1)}, u32[]{:S(2)}, u32[]{:S(2)}) collective-permute-start(bf16[512,1024]{1,0:T(8,128)(2,1)S(1)} %shard_map.109.x_here.x_mine.tokens), channel_id=1, source_target_pairs={{0,4},{12,8},{1,5},{13,9},{2,6},{14,10},{3,7},{15,11},{16,20},{28,... | collective-permute-start | bytes 3145736 | tf_op jit(solution)/shard_map/ppermute | solution.py:40
  60.3 32.8 %collective-permute-start.15 = (bf16[1024,512]{1,0:T(8,128)(2,1)}, bf16[1024,512]{1,0:T(8,128)(2,1)}, u32[]{:S(2)}, u32[]{:S(2)}) collective-permute-start(bf16[1024,512]{1,0:T(8,128)(2,1)} %shard_map.112), channel_id=1, source_target_pairs={{4,8},{8,4},{5,9},{9,5},{6,10},{10,6},{7,11},{11,7},{20,24},{24,20... | collective-permute-start | bytes 3145736 | tf_op jit(solution)/shard_map/ppermute | solution.py:40
  64.1 13.7 %collective-permute-start.8 = (bf16[256,1024]{1,0:T(8,128)(2,1)S(1)}, bf16[256,1024]{1,0:T(8,128)(2,1)S(1)}, u32[]{:S(2)}, u32[]{:S(2)}) collective-permute-start(bf16[256,1024]{1,0:T(8,128)(2,1)S(1)} %shard_map.114), channel_id=1, source_target_pairs={{0,2},{2,0},{1,3},{3,1},{4,6},{6,4},{5,7},{7,5},{8,10},{10,8},{9,1... | collective-permute-start | bytes 1572872 | tf_op jit(solution)/shard_map/ppermute | solution.py:36
  69.9 30.7 %collective-permute-start.11 = (bf16[1024,512]{1,0:T(8,128)(2,1)}, bf16[1024,512]{1,0:T(8,128)(2,1)S(1)}, u32[]{:S(2)}, u32[]{:S(2)}) collective-permute-start(bf16[1024,512]{1,0:T(8,128)(2,1)} %collective-permute-done.9.crossed), channel_id=1, source_target_pairs={{4,0},{8,12},{5,1},{9,13},{6,2},{10,14},{7,3},{11,15},{20,16},{24,... | collective-permute-start | bytes 3145736 | tf_op jit(solution)/shard_map/ppermute | solution.py:40
  87.9 26.2 %collective-permute-start.18 = (bf16[512,1024]{1,0:T(8,128)(2,1)S(1)}, bf16[512,1024]{1,0:T(8,128)(2,1)S(1)}, u32[]{:S(2)}, u32[]{:S(2)}) collective-permute-start(bf16[512,1024]{1,0:T(8,128)(2,1)S(1)} %shard_map.117.x_here.x_other.tokens), channel_id=1, source_target_pairs={{0,4},{12,8},{1,5},{13,9},{2,6},{14,10},{3,7},{15,11},{16,20},{28,... | collective-permute-start | bytes 3145736 | tf_op jit(solution)/shard_map/ppermute | solution.py:40
  92.3 23.8 %collective-permute-start.17 = (bf16[1024,512]{1,0:T(8,128)(2,1)S(1)}, bf16[1024,512]{1,0:T(8,128)(2,1)S(1)}, u32[]{:S(2)}, u32[]{:S(2)}) collective-permute-start(bf16[1024,512]{1,0:T(8,128)(2,1)S(1)} %shard_map.119), channel_id=1, source_target_pairs={{4,8},{8,4},{5,9},{9,5},{6,10},{10,6},{7,11},{11,7},{20,24},{24,20... | collective-permute-start | bytes 3145736 | tf_op jit(solution)/shard_map/ppermute | solution.py:40
  93.1 26.1 %collective-permute-start.16 = (bf16[1024,512]{1,0:T(8,128)(2,1)}, bf16[1024,512]{1,0:T(8,128)(2,1)S(1)}, u32[]{:S(2)}, u32[]{:S(2)}) collective-permute-start(bf16[1024,512]{1,0:T(8,128)(2,1)} %collective-permute-done.15.crossed), channel_id=1, source_target_pairs={{4,0},{8,12},{5,1},{9,13},{6,2},{10,14},{7,3},{11,15},{20,16},{24,... | collective-permute-start | bytes 3145736 | tf_op jit(solution)/shard_map/ppermute | solution.py:40
  102.0 26.2 %collective-permute-start.20 = (bf16[1024,512]{1,0:T(8,128)(2,1)S(1)}, bf16[1024,512]{1,0:T(8,128)(2,1)S(1)}, u32[]{:S(2)}, u32[]{:S(2)}) collective-permute-start(bf16[1024,512]{1,0:T(8,128)(2,1)S(1)} %shard_map.120.far.rest_2_), channel_id=1, source_target_pairs={{0,16},{16,0},{1,17},{17,1},{2,18},{18,2},{3,19},{19,3},{4,20},{20... | collective-permute-start | bytes 3145736 | tf_op jit(solution)/shard_map/ppermute | solution.py:36
  115.4 48.6 %collective-permute-start.25 = (bf16[1024,512]{1,0:T(8,128)(2,1)S(1)}, bf16[1024,512]{1,0:T(8,128)(2,1)S(1)}, u32[]{:S(2)}, u32[]{:S(2)}) collective-permute-start(bf16[1024,512]{1,0:T(8,128)(2,1)S(1)} %shard_map.121), channel_id=1, source_target_pairs={{4,8},{8,4},{5,9},{9,5},{6,10},{10,6},{7,11},{11,7},{20,24},{24,20... | collective-permute-start | bytes 3145736 | tf_op jit(solution)/shard_map/ppermute | solution.py:40
  120.6 44.8 %collective-permute-start.19 = (bf16[1024,512]{1,0:T(8,128)(2,1)S(1)}, bf16[1024,512]{1,0:T(8,128)(2,1)S(1)}, u32[]{:S(2)}, u32[]{:S(2)}) collective-permute-start(bf16[1024,512]{1,0:T(8,128)(2,1)S(1)} %shard_map.123.far), channel_id=1, source_target_pairs={{0,16},{16,0},{1,17},{17,1},{2,18},{18,2},{3,19},{19,3},{4,20},{20... | collective-permute-start | bytes 3145736 | tf_op jit(solution)/shard_map/ppermute | solution.py:36
  132.0 16.4 %collective-permute-start.23 = (bf16[1024,256]{1,0:T(8,128)(2,1)S(1)}, bf16[1024,256]{1,0:T(8,128)(2,1)S(1)}, u32[]{:S(2)}, u32[]{:S(2)}) collective-permute-start(bf16[1024,256]{1,0:T(8,128)(2,1)S(1)} %shard_map.122), channel_id=1, source_target_pairs={{4,0},{8,12},{5,1},{9,13},{6,2},{10,14},{7,3},{11,15},{20,16},{24,... | collective-permute-start | bytes 1572872 | tf_op jit(solution)/shard_map/ppermute | solution.py:40
  140.5 26.1 %collective-permute-start.22 = (bf16[256,1024]{1,0:T(8,128)(2,1)S(1)}, bf16[256,1024]{1,0:T(8,128)(2,1)S(1)}, u32[]{:S(2)}, u32[]{:S(2)}) collective-permute-start(bf16[256,1024]{1,0:T(8,128)(2,1)S(1)} %get-tuple-element.113), channel_id=1, source_target_pairs={{0,2},{2,0},{1,3},{3,1},{4,6},{6,4},{5,7},{7,5},{8,10},{10,8},{9,1... | collective-permute-start | bytes 1572872 | tf_op jit(solution)/shard_map/ppermute | solution.py:36
  142.9 18.4 %collective-permute-start.26 = (f32[512,128]{1,0:T(8,128)S(1)}, f32[512,128]{1,0:T(8,128)S(1)}, u32[]{:S(2)}, u32[]{:S(2)}) collective-permute-start(f32[512,128]{1,0:T(8,128)S(1)} %add.61.part), channel_id=1, source_target_pairs={{0,2},{2,0},{1,3},{3,1},{4,6},{6,4},{5,7},{7,5},{8,10},{10,8},{9,1... | collective-permute-start | bytes 786440 | tf_op jit(solution)/shard_map/ppermute | solution.py:36
  150.5 16.1 %collective-permute-start.24 = (bf16[1024,128]{1,0:T(8,128)(2,1)S(1)}, bf16[1024,128]{1,0:T(8,128)(2,1)S(1)}, u32[]{:S(2)}, u32[]{:S(2)}) collective-permute-start(bf16[1024,128]{1,0:T(8,128)(2,1)S(1)} %get-tuple-element.116), channel_id=1, source_target_pairs={{0,2},{2,0},{1,3},{3,1},{4,6},{6,4},{5,7},{7,5},{8,10},{10,8},{9,1... | collective-permute-start | bytes 786440 | tf_op jit(solution)/shard_map/ppermute | solution.py:36
  176.8 19.8 %all-to-all-start.1 = ((bf16[4,2,128,256]{3,2,1,0:T(8,128)(2,1)}), bf16[4,2,128,256]{3,2,1,0:T(8,128)(2,1)}, u32[]{:S(2)}, u32[]{:S(2)}) async-start(bf16[4,2,128,256]{3,2,1,0:T(8,128)(2,1)} %bitcast.30), calls=%async_computation.1 | async-start | bytes 1048576 | tf_op jit(solution)/shard_map/all_to_all | solution.py:599
  181.1 23.8 %collective-permute-start.30 = (bf16[1024,256]{1,0:T(8,128)(2,1)}, bf16[1024,256]{1,0:T(8,128)(2,1)}, u32[]{:S(2)}, u32[]{:S(2)}) collective-permute-start(bf16[1024,256]{1,0:T(8,128)(2,1)} %copy-done.35), channel_id=1, source_target_pairs={{4,0},{8,12},{5,1},{9,13},{6,2},{10,14},{7,3},{11,15},{20,16},{24,... | collective-permute-start | bytes 1572872 | tf_op jit(solution)/shard_map/ppermute | solution.py:40
  182.4 29.1 %collective-permute-start.29 = (bf16[256,1024]{1,0:T(8,128)(2,1)}, bf16[256,1024]{1,0:T(8,128)(2,1)}, u32[]{:S(2)}, u32[]{:S(2)}) collective-permute-start(bf16[256,1024]{1,0:T(8,128)(2,1)} %copy-done.50), channel_id=1, source_target_pairs={{0,2},{2,0},{1,3},{3,1},{4,6},{6,4},{5,7},{7,5},{8,10},{10,8},{9,1... | collective-permute-start | bytes 1572872 | tf_op jit(solution)/shard_map/ppermute | solution.py:36
  189.3 25.3 %collective-permute-start.28 = (bf16[2,256,256]{2,1,0:T(8,128)(2,1)}, bf16[2,256,256]{2,1,0:T(8,128)(2,1)}, u32[]{:S(2)}, u32[]{:S(2)}) collective-permute-start(bf16[2,256,256]{2,1,0:T(8,128)(2,1)} %get-tuple-element.130), channel_id=1, source_target_pairs={{0,2},{2,0},{1,3},{3,1},{4,6},{6,4},{5,7},{7,5},{8,10},{10,8},{9,1... | collective-permute-start | bytes 786440 | tf_op jit(solution)/shard_map/ppermute | solution.py:36
  (63 other events, 464.4 us)

commit v7 on v6

--- a/solution.py
+++ b/solution.py
@@ -110,13 +110,16 @@
     return jnp.concatenate([value[half:], value[:half]], axis=0)
 
 
-def back_kernel(ids, dy, up, out):
+def back_kernel(numbers, ids, dy, *rest):
+    *ups, out = rest
     size = out.shape[1]
     token = ids[...].astype(f32)
-    for i in range(0, up.shape[0] // size, 2):
-        both = contract_final_axis(dy[...], up[i * size : (i + 2) * size, :])
+    first = 2 * (numbers.shape[0] // 3)
+    for i, up in enumerate(ups):
+        both = contract_final_axis(dy[...], up[...])
         for j in (0, 1):
-            part = jnp.where(token == i + j, both[:, j * size : (j + 1) * size], 0.0)
+            place = numbers[first + 2 * i + j].astype(f32)
+            part = jnp.where(token == place, both[:, j * size : (j + 1) * size], 0.0)
             out[...] = part if i + j == 0 else out[...] + part
 
 
@@ -129,7 +132,7 @@
 
 def back_end_kernel(numbers, ids, part, got, wide, sent):
     token = ids[...].astype(f32)
-    count = numbers.shape[0] // 2
+    count = numbers.shape[0] // 3
     ranks, order = [numbers[i] for i in range(count)], [numbers[count + i] for i in range(count)]
     value, scale = kept(token, jnp.stack(ranks), part[...] + roll_rows(got[...]))
     value = (scale * value).astype(bf16)
@@ -141,7 +144,7 @@
 
 def spread_in_kernel(numbers, packet, wide):
     size = packet.shape[1] // 2
-    count = numbers.shape[0] // 2
+    count = numbers.shape[0] // 3
     order = [numbers[count + i] for i in range(count)]
     spread_into(wide, packet[:, size:].astype(f32), packet[:, :size].astype(f32), order)
 
@@ -160,20 +163,31 @@
     for i in range(4):
         both = matmul(x_mine[...], mine[i]) + matmul(x_other[...], other[i])
         for j in (0, 1):
-            place = numbers[numbers.shape[0] // 2 + 2 * i + j].astype(f32)
+            place = numbers[numbers.shape[0] // 3 + 2 * i + j].astype(f32)
             part = jnp.where(token == place, both[:, j * size : (j + 1) * size], 0.0)
             out[...] = part if i + j == 0 else out[...] + part
 
 
-def low_end_kernel(numbers, ids, part, got, up, dy, wide, delta, grad):
+def low_end_kernel(numbers, ids, part, got, dy, *rest):
+    *ups, delta, first, second, third, fourth = rest
     token = ids[...].astype(f32)
-    count = numbers.shape[0] // 2
+    count = numbers.shape[0] // 3
+    size = part.shape[1]
     ranks = jnp.stack([numbers[i] for i in range(count)])
     value, scale = kept(token, ranks, part[...] + roll_rows(got[...]))
     value = value.astype(bf16).astype(f32)
-    spread_into(wide, token, value, [jnp.int32(i) for i in range(count)])
-    grad[...] = contract_first(wide[...], dy[...]).astype(bf16)
-    delta[...] = (scale[:, :1] * matmul(wide[...], up[...])).astype(bf16)
+    total = 0.0
+    for i, out in enumerate((first, second, third, fourth)):
+        wide = jnp.concatenate(
+            [
+                jnp.where(token == numbers[2 * count + 2 * i + j].astype(f32), value, 0.0)
+                for j in (0, 1)
+            ],
+            axis=1,
+        ).astype(bf16)
+        out[...] = contract_first(wide, dy[...]).astype(bf16)
+        total += matmul(wide, ups[i][...])
+    delta[...] = (scale[:, :1] * total).astype(bf16)
 
 
 def to_middle_kernel(x_here, back, x_in, back_in, out):
@@ -198,22 +212,35 @@
     there[...] = sums[:, size:].astype(bf16)
 
 
-def up_sent_kernel(up, out):
-    cols = out.shape[2]
-    for i in range(out.shape[0]):
-        out[i] = up[:, (i % 2) * cols : (i % 2 + 1) * cols]
-
-
-def packet_kernel(flags, here, ids_here, packet, half, ids, quarter):
+def packet_kernel(flags, cotangent, adapters, up, out):
+    rows, kv = cotangent.shape
+    size = up.shape[0]
+    half = up.shape[1] // 2
+    count = rows // size
+    cols = half // count
+    out[:, :kv] = cotangent[...]
+    numbers = jnp.broadcast_to(adapters[...].astype(f32), (rows, size))
+    out[:, kv : kv + size] = numbers.astype(bf16)
+    for i in range(count):
+        start = pl.multiple_of((1 - flags[3]) * half + i * cols, 128)
+        out[i * size : (i + 1) * size, kv + size :] = up[:, pl.ds(start, cols)]
+
+
+def unpack_kernel(flags, here, ids_here, up_here, packet, half, ids, quarter, up):
     rows, kv = here.shape
+    size = up_here.shape[0]
     half[:rows] = here[...]
     half[rows:] = packet[:, :kv]
-    ids[:rows] = ids_here[...]
-    ids[rows:] = packet[:, kv:]
+    ids[:rows] = ids_here[:, kv : kv + size]
+    ids[rows:] = packet[:, kv : kv + size]
     cols = quarter.shape[1]
     span = pl.ds(pl.multiple_of(flags[3] * cols, 128), cols)
     quarter[:rows] = here[:, span]
     quarter[rows:] = packet[:, span]
+    up[:size] = up_here[:, span]
+    part = cols * size // rows
+    for i in range(rows // size):
+        up[size:, i * part : (i + 1) * part] = packet[i * size : (i + 1) * size, kv + size :]
 
 
 def dy_line_kernel(places, here, got, out):
@@ -242,16 +269,16 @@
         out[...] = outer[...]
 
 
-def up_sum_kernel(numbers, got, here, there):
-    count = numbers.shape[0] // 2
+def up_sum_kernel(numbers, first, second, third, fourth, here, there):
+    count = numbers.shape[0] // 3
+    size = here.shape[0]
     for i, out in enumerate((here, there)):
         adapter = numbers[count + i]
         rank = jnp.float32(1.0)
         for a in range(count):
             rank = jnp.where(adapter == a, numbers[a].astype(f32), rank)
-        part = got[0, adapter % 2].astype(f32)
-        for source in range(1, got.shape[0]):
-            part += got[source, adapter % 2].astype(f32)
+        span = slice(i * size, (i + 1) * size)
+        part = sum(v[span, :].astype(f32) for v in (first, second, third, fourth))
         out[...] = (jnp.full(part.shape, 16.0, f32) / rank * part).astype(bf16)
 
 
@@ -353,7 +380,8 @@
         [side * quarter + half * eighth for side in (x, 1 - x) for half in (y, 1 - y)]
     ).astype(jnp.int32)
     ranks = size // 8 * rank_step_count
-    numbers = jnp.concatenate([ranks, adapters])
+    ring = jnp.stack([2 * ((z + k) % 4) + o for k in range(4) for o in (x, 1 - x)])
+    numbers = jnp.concatenate([ranks, adapters, ring.astype(jnp.int32)])
     flags = jnp.stack([(c == 0) == first_pair, z % 2 == 1, z >= 2, x == 1, is_middle])
     flags = flags.astype(jnp.int32)
     places = jnp.stack([*line, c]).astype(jnp.int32)
@@ -372,8 +400,8 @@
     def like(*shape, kind=bf16):
         return jax.ShapeDtypeStruct(shape, kind)
 
-    def join(*values):
-        return jnp.concatenate(values, axis=1)
+    def around(value, shift):
+        return along(value, [(i, (i + shift) % 4) for i in range(4)])
 
     def rows_at(i, value, length):
         out = like(length, value.shape[1])
@@ -419,9 +447,17 @@
         )[0]
 
     down_got = swap(done(rows_at(2, down, eighth)), "own")
-    ids_here = jnp.broadcast_to(token_adapter.astype(bf16), (rows, size))
-    packet = swap(done(join(step(cotangent), ids_here)), "own")
-    x_got = [swap(done(columns_at(2, step(tokens))), "own")]
+    packet_here = done(
+        kernel_call(
+            packet_kernel,
+            [like(rows, kv + size + kvq * size // rows)],
+            step(cotangent),
+            token_adapter,
+            up,
+            scalars=flags,
+        )[0]
+    )
+    packet = swap(packet_here, "own")
     down_piece = done(
         copy_call(
             lambda n, a, o: [
@@ -435,49 +471,36 @@
         )[0]
     )
     down_near = along(down_piece, NEIGHBOURS)
-    up, packet = step(up, packet)
-    up_sent = kernel_call(up_sent_kernel, [like(number, size, kvq)], up)[0]
-    up_all = lax.all_to_all(
-        done(up_sent), ("fsdp", "own"), split_axis=0, concat_axis=0, tiled=True
-    ).reshape(number * size, kvq)
+    x_got = [swap(done(columns_at(2, step(tokens))), "own")]
+    dy_half, ids, dy_quarter, up_piece = kernel_call(
+        unpack_kernel,
+        [like(both, kv), like(both, size), like(both, kvq), like(wide, kvq)],
+        cotangent,
+        packet_here,
+        up,
+        step(packet),
+        scalars=flags,
+    )
+    ups = [done(up_piece)] + [around(up_piece, 4 - k) for k in (1, 2, 3)]
+
+    crossing = done(side_by_side(down_piece, step(down_near)))
+    down_crossed = along(crossing, MIDDLE)
+    x_mine = done(tokens_of(0, tokens, step(x_got[0])))
+    x_in = [along(x_mine, INWARD)]
+    compact = like(both, size, kind=f32)
+    dy_quarter, *ups = step(dy_quarter, *ups)
+    back_part = done(
+        kernel_call(back_kernel, [compact], ids, dy_quarter, *ups, scalars=numbers)[0]
+    )
+    back_tp = swap(back_part, "tp")
     weight_here = done(rows_at(0, step(frozen_value_weight), eighth))
     weight_near = along(weight_here, NEIGHBOURS)
-
-    dy_half, ids, dy_quarter = kernel_call(
-        packet_kernel,
-        [like(both, kv), like(both, size), like(both, kvq)],
-        cotangent,
-        ids_here,
-        step(packet),
-        scalars=flags,
-    )
-    done(dy_quarter)
-    dy_tp = swap(dy_half, "tp")
-
-    down_near, x_got[0] = step(down_near, x_got[0])
-    crossing = done(side_by_side(down_piece, down_near))
-    down_crossed = along(crossing, MIDDLE)
-    down_other = swap(crossing, "rep")
-    x_mine = done(tokens_of(0, tokens, step(x_got[0])))
-    x_in = [along(x_mine, INWARD)]
-    dy_line = done(
-        kernel_call(
-            dy_line_kernel, [like(both, 2 * kv)], dy_half, step(dy_tp), scalars=places
-        )[0]
-    )
-
-    compact = like(both, size, kind=f32)
-    up_all = step(up_all)
-    back_part = done(kernel_call(back_kernel, [compact], ids, dy_quarter, up_all)[0])
-    back_tp = swap(back_part, "tp")
-    weight_near = step(weight_near)
-    crossing = done(side_by_side(weight_here, weight_near))
-    weight_crossed = along(crossing, MIDDLE)
     back_part = done(kernel_call(add_kernel, [compact], back_part, step(back_tp))[0])
     back_got = swap(back_part, "own")
-    sent, down_other = step(tokens, down_other)
-    x_got.append(swap(done(columns_at(3, sent)), "own"))
+    dy_tp = swap(step(dy_half), "tp")
     weight_other = done(rows_at(1, step(frozen_value_weight), eighth))
+    weight_near = step(weight_near)
+    weight_crossed = along(done(side_by_side(weight_here, weight_near)), MIDDLE)
     back_wide, back_sent = kernel_call(
         back_end_kernel,
         [like(both, number * size), like(both, wide)],
@@ -487,6 +510,12 @@
         scalars=numbers,
     )
     back_in = along(done(back_sent), INWARD)
+    x_got.append(swap(done(columns_at(3, step(tokens))), "own"))
+    dy_line = done(
+        kernel_call(
+            dy_line_kernel, [like(both, 2 * kv)], dy_half, step(dy_tp), scalars=places
+        )[0]
+    )
     down_crossed = done(step(down_crossed))
     down_outer = along(down_crossed, OUTWARD)
     x_other = done(tokens_of(1, tokens, step(x_got[1])))
@@ -536,16 +565,33 @@
         )[0]
     )
     middle = [to_middle(0)]
-    weight_near_other = swap(step(weight_near), "rep")
+    down_other = swap(step(crossing), "rep")
+    down_outer = step(down_outer)
+    down_far = done(far_of(down_crossed, down_outer))
+    down_far_other = swap(down_far, "rep")
     weight_crossed = done(step(weight_crossed))
     weight_outer = along(weight_crossed, OUTWARD)
-    down_outer, weight_near_other = step(down_outer, weight_near_other)
-    down_far = done(far_of(down_crossed, down_outer))
-    down_far_other = swap(down_far, "rep")
     middle.append(to_middle(1))
+    middle[0], down_other = step(middle[0], down_other)
     outward = [to_end(0, middle[0])]
+    weight_near_other = swap(step(weight_near), "rep")
     weight_far = done(far_of(weight_crossed, step(weight_outer)))
     weight_far_other = swap(weight_far, "rep")
+    half_grad = [like(rows, eighth)] * 2
+    dy_line, weight_near_other = step(dy_line, weight_near_other)
+    dx_mine, dx_sent = kernel_call(
+        dx_kernel,
+        half_grad,
+        dy_line,
+        back_wide,
+        weight_here,
+        weight_near,
+        weight_far,
+        down_piece,
+        down_near,
+        down_far,
+    )
+    dx_mine_got = swap(done(dx_sent), "own")
 
     low_part = done(
         kernel_call(
@@ -568,39 +614,23 @@
         y_kernel, blocks, step(x_mine), weight_here, weight_near, weight_far, scalars=flags
     )
     done(y_first[0])
-    low_part = done(low_part + step(low_tp))
+    low_part = done(kernel_call(add_kernel, [compact], low_part, step(low_tp))[0])
     low_got = swap(low_part, "own")
-    half_grad = [like(rows, eighth)] * 2
-    dx_mine, dx_sent = kernel_call(
-        dx_kernel,
-        half_grad,
-        step(dy_line),
-        back_wide,
-        weight_here,
-        weight_near,
-        weight_far,
-        down_piece,
-        down_near,
-        down_far,
-    )
-    done(dx_mine)
-    dx_mine_got = swap(dx_sent, "own")
-    grads = [finish(0, middle[0], outward[0])]
-    _, delta, up_part = kernel_call(
+    outward.append(to_end(1, middle[1]))
+    low_got, dx_mine_got = step(low_got, dx_mine_got)
+    delta, *up_parts = kernel_call(
         low_end_kernel,
-        [like(both, number * size), like(both, kvq), like(number * size, kvq)],
+        [like(both, kvq)] + [like(wide, kvq)] * 4,
         ids,
         low_part,
-        step(low_got),
-        up_all,
+        low_got,
         dy_quarter,
+        *ups,
         scalars=numbers,
     )
-    up_got = lax.all_to_all(
-        done(up_part).reshape(4, 2, size, kvq), "fsdp", split_axis=0, concat_axis=0, tiled=True
-    )
-    outward.append(to_end(1, middle[1]))
-    weight_far_other, dx_mine_got, grad_got = step(weight_far_other, dx_mine_got, grads[0][1])
+    done(delta)
+    up_got = [around(up_parts[k], k) for k in (1, 2, 3)]
+    grads = [finish(0, middle[0], outward[0])]
     dx_other, dx_sent = kernel_call(
         dx_kernel,
         half_grad,
@@ -608,7 +638,7 @@
         back_wide,
         weight_other,
         weight_near_other,
-        weight_far_other,
+        step(weight_far_other),
         down_other,
         down_far_other,
     )
@@ -624,6 +654,11 @@
         scalars=flags,
     )
     y_got = swap(done(y_sent), "tp")
+    grads.append(finish(1, middle[1], outward[1], *up_got))
+    up_mine, up_theirs = kernel_call(
+        up_sum_kernel, [like(size, kvq)] * 2, step(up_parts[0]), *up_got, scalars=numbers
+    )
+    up_theirs = swap(done(up_theirs), "own")
     y_here, y_sent = kernel_call(
         y_sum_kernel,
         [like(2, rows, cols, kind=f32), like(2, rows, cols)],
@@ -633,11 +668,7 @@
         scalars=flags,
     )
     y_got = swap(done(y_sent), "own")
-    up_mine, up_theirs = kernel_call(
-        up_sum_kernel, [like(size, kvq)] * 2, step(up_got), scalars=numbers
-    )
-    up_theirs = swap(done(up_theirs), "own")
-    grads.append(finish(1, middle[1], outward[1]))
+    grad_got = grads[0][1]
 
     def in_place(axis, out, *pieces):
         def plan(n, a, o):

time: 223 us -> 264 us (1.18)
  waiting for transfers between devices: 69.6 us -> 128 us
  local copies, waits for them, and re-layouts: 24.2 us -> 9.68 us
  starting transfers between devices: 61.2 us -> 72.4 us
  Pallas kernels: 62.8 us -> 51.8 us
    ppermute x20, waiting for transfers between devices: 32.4 us -> 77.3 us  [swap(): return lax.ppermute(value, axis, PAIR)]
    ppermute x13 -> x19, starting transfers between devices: 29.4 us -> 51.4 us  [along(): return lax.ppermute(value, 'fsdp', pairs)]
    ppermute x13 -> x19, waiting for transfers between devices: 30.2 us -> 50.7 us  [along(): return lax.ppermute(value, 'fsdp', pairs)]
    unnamed x104 -> x43, local copies, waits for them, and re-layouts: 23.8 us -> 9.4 us
    pallas_call x37 -> x38, Pallas kernels: 62.8 us -> 51.8 us  [kernel_call(): pl.pallas_call(body, out_shape=list(outs), in_specs=specs, out_specs=[pl....]
    all_to_all x2 -> x0, starting transfers between devices: 10.6 us -> none  [the longest x1 6.37 us: body_line(): lax.all_to_all(done(up_sent), ('fsdp', 'own'), split_axis=0, concat_axis=...]
    all_to_all x2 -> x0, waiting for transfers between devices: 7.07 us -> none  [the longest x1 7.06 us: body_line(): lax.all_to_all(done(up_part).reshape(4, 2, size, kvq), 'fsdp', split_axis...]
  transfers between devices with their start and end apart: 35 -> 39, of which waited for: 17 -> 16; matrix products, arithmetic and copies ran while one was open for 1% -> 0% of each run, Pallas kernels for 24% -> 17%
where the time goes in v7:
time: 264 us; the launch traced here: 263 us
  waiting for transfers between devices  128 us (48%)
  starting transfers between devices  72.4 us (27%)
  Pallas kernels  51.8 us (20%)
  local copies, waits for them, and re-layouts  9.68 us (4%)
    ppermute x20, waiting for transfers between devices, swap(): return lax.ppermute(value, axis, PAIR)  77.3 us
    pallas_call x38, Pallas kernels, kernel_call(): pl.pallas_call(body, out_shape=list(outs), in_specs=specs, out_specs=[pl....  51.8 us
    ppermute x19, starting transfers between devices, along(): return lax.ppermute(value, 'fsdp', pairs)  51.4 us
    ppermute x19, waiting for transfers between devices, along(): return lax.ppermute(value, 'fsdp', pairs)  50.7 us
    ppermute x20, starting transfers between devices, swap(): return lax.ppermute(value, axis, PAIR)  21 us
    unnamed x43, local copies, waits for them, and re-layouts  9.4 us
  transfers between devices with their start and end apart: 39, of which 16 were waited for; matrix products, arithmetic and copies ran while one was open for 0% of the time, Pallas kernels for 17%

profile of v7, /device:TPU:0, one launch (start us, length us, event | category | flops | bytes accessed | tf_op | source)
XLA Modules:
  0.0 263.1 jit_solution(7910371828619882432)
XLA Ops:
  2.5 3.0 %collective-permute-start.1 = (bf16[1024,128]{1,0:T(8,128)(2,1)S(1)}, bf16[1024,128]{1,0:T(8,128)(2,1)S(1)}, u32[]{:S(2)}, u32[]{:S(2)}) collective-permute-start(bf16[1024,128]{1,0:T(8,128)(2,1)S(1)} %shard_map.102), channel_id=1, source_target_pairs={{0,2},{2,0},{1,3},{3,1},{4,6},{6,4},{5,7},{7,5},{8,10},{10,8},{9,1... | collective-permute-start | bytes 786440 | tf_op jit(solution)/shard_map/ppermute | solution.py:36
  9.0 2.9 %collective-permute-done.1.refs_1_ = bf16[1024,128]{1,0:T(8,128)(2,1)S(1)} collective-permute-done((bf16[1024,128]{1,0:T(8,128)(2,1)S(1)}, bf16[1024,128]{1,0:T(8,128)(2,1)S(1)}, u32[]{:S(2)}, u32[]{:S(2)}) %collective-permute-start.1) | collective-permute-done | bytes 262176 | tf_op jit(solution)/shard_map/ppermute | solution.py:36
  18.4 9.3 %collective-permute-done.packet = bf16[256,768]{1,0:T(8,128)(2,1)S(1)} collective-permute-done((bf16[256,768]{1,0:T(8,128)(2,1)S(1)}, bf16[256,768]{1,0:T(8,128)(2,1)S(1)}, u32[]{:S(2)}, u32[]{:S(2)}) %collective-permute-start) | collective-permute-done | bytes 393248 | tf_op jit(solution)/shard_map/ppermute | solution.py:36
  40.9 25.9 %collective-permute-done.3.rest_2_ = bf16[256,256]{1,0:T(8,128)(2,1)} collective-permute-done((bf16[256,256]{1,0:T(8,128)(2,1)}, bf16[256,256]{1,0:T(8,128)(2,1)}, u32[]{:S(2)}, u32[]{:S(2)}) %collective-permute-start.3) | collective-permute-done | bytes 131104 | tf_op jit(solution)/shard_map/ppermute | solution.py:40
  72.0 4.6 %collective-permute-start.13 = (bf16[512,1024]{1,0:T(8,128)(2,1)S(1)}, bf16[512,1024]{1,0:T(8,128)(2,1)}, u32[]{:S(2)}, u32[]{:S(2)}) collective-permute-start(bf16[512,1024]{1,0:T(8,128)(2,1)S(1)} %shard_map.108.x_here.x_mine.tokens), channel_id=1, source_target_pairs={{0,4},{12,8},{1,5},{13,9},{2,6},{14,10},{3,7},{15,11},{16,20},{28,... | collective-permute-start | bytes 3145736 | tf_op jit(solution)/shard_map/ppermute | solution.py:40
  78.9 5.6 %collective-permute-done.9.refs_1_.near = bf16[1024,256]{1,0:T(8,128)(2,1)} collective-permute-done((bf16[1024,256]{1,0:T(8,128)(2,1)}, bf16[1024,256]{1,0:T(8,128)(2,1)}, u32[]{:S(2)}, u32[]{:S(2)}) %collective-permute-start.9) | collective-permute-done | bytes 524320 | tf_op jit(solution)/shard_map/ppermute | solution.py:40
  93.6 6.2 %collective-permute-start.14 = (bf16[512,256]{1,0:T(8,128)(2,1)S(1)}, bf16[512,256]{1,0:T(8,128)(2,1)S(1)}, u32[]{:S(2)}, u32[]{:S(2)}) collective-permute-start(bf16[512,256]{1,0:T(8,128)(2,1)S(1)} %get-tuple-element.100), channel_id=1, source_target_pairs={{0,4},{12,8},{1,5},{13,9},{2,6},{14,10},{3,7},{15,11},{16,20},{28,... | collective-permute-start | bytes 786440 | tf_op jit(solution)/shard_map/ppermute | solution.py:40
  99.8 5.9 %collective-permute-done.10.refs_1_ = bf16[256,1024]{1,0:T(8,128)(2,1)S(1)} collective-permute-done((bf16[256,1024]{1,0:T(8,128)(2,1)S(1)}, bf16[256,1024]{1,0:T(8,128)(2,1)S(1)}, u32[]{:S(2)}, u32[]{:S(2)}) %collective-permute-start.10) | collective-permute-done | bytes 524320 | tf_op jit(solution)/shard_map/ppermute | solution.py:36
  106.4 5.8 %collective-permute-start.17 = (bf16[512,1024]{1,0:T(8,128)(2,1)S(1)}, bf16[512,1024]{1,0:T(8,128)(2,1)S(1)}, u32[]{:S(2)}, u32[]{:S(2)}) collective-permute-start(bf16[512,1024]{1,0:T(8,128)(2,1)S(1)} %shard_map.117.x_here.x_other.tokens), channel_id=1, source_target_pairs={{0,4},{12,8},{1,5},{13,9},{2,6},{14,10},{3,7},{15,11},{16,20},{28,... | collective-permute-start | bytes 3145736 | tf_op jit(solution)/shard_map/ppermute | solution.py:40
  121.2 11.9 %collective-permute-done.17.x_in = bf16[512,1024]{1,0:T(8,128)(2,1)S(1)} collective-permute-done((bf16[512,1024]{1,0:T(8,128)(2,1)S(1)}, bf16[512,1024]{1,0:T(8,128)(2,1)S(1)}, u32[]{:S(2)}, u32[]{:S(2)}) %collective-permute-start.17) | collective-permute-done | bytes 1048608 | tf_op jit(solution)/shard_map/ppermute | solution.py:40
  134.3 7.6 %collective-permute-done.16.own_near_other.rest_0_ = bf16[1024,512]{1,0:T(8,128)(2,1)S(1)} collective-permute-done((bf16[1024,512]{1,0:T(8,128)(2,1)}, bf16[1024,512]{1,0:T(8,128)(2,1)S(1)}, u32[]{:S(2)}, u32[]{:S(2)}) %collective-permute-start.16) | collective-permute-done | bytes 1048608 | tf_op jit(solution)/shard_map/ppermute | solution.py:36
  147.8 27.8 %collective-permute-done.20.near = bf16[1024,256]{1,0:T(8,128)(2,1)S(1)} collective-permute-done((bf16[1024,256]{1,0:T(8,128)(2,1)}, bf16[1024,256]{1,0:T(8,128)(2,1)S(1)}, u32[]{:S(2)}, u32[]{:S(2)}) %collective-permute-start.20) | collective-permute-done | bytes 524320 | tf_op jit(solution)/shard_map/ppermute | solution.py:36
  175.7 3.6 %shard_map.124 = (bf16[256,1024]{1,0:T(8,128)(2,1)S(1)}, bf16[256,1024]{1,0:T(8,128)(2,1)S(1)}) custom-call(bf16[512,1024]{1,0:T(8,128)(2,1)S(1)} %shard_map.116.dy, bf16[512,1024]{1,0:T(8,128)(2,1)S(1)} %get-tuple-element.107.back, bf16[1024,256]{1,0:T(8,128)(2,1)} %shard_map.110.refs_0_.own, bf16[1024,256]{1,0:T(8,128)(2,1)} %collective-permute-done.9.refs_1_.near, ...), custom_call_target="tpu_custom_call" | custom-call | tf_op jit(solution)/shard_map/pallas_call | solution.py:48
  179.2 2.9 %shard_map.125.left = f32[512,128]{1,0:T(8,128)S(1)} custom-call(s32[24]{0:T(128)S(1)} %concatenate.3.numbers, bf16[512,128]{1,0:T(8,128)(2,1)S(1)} %get-tuple-element.85.ids, bf16[512,1024]{1,0:T(8,128)(2,1)S(1)} %shard_map.108.x_here.x_mine.tokens, bf16[512,1024]{1,0:T(8,128)(2,1)S(1)} %shard_map.117.x_here.x_other.tokens, ...), custom_call_target="tpu_custom_call" | custom-call | tf_op jit(solution)/shard_map/pallas_call | solution.py:48
  185.0 4.3 %shard_map.126 = (f32[2,512,256]{2,1,0:T(8,128)S(1)}, f32[2,512,256]{2,1,0:T(8,128)S(1)}) custom-call(s32[5]{0:T(128)S(1)} %convert_element_type.3.flags, bf16[512,1024]{1,0:T(8,128)(2,1)S(1)} %shard_map.108.x_here.x_mine.tokens, bf16[1024,256]{1,0:T(8,128)(2,1)} %shard_map.110.refs_0_.own, bf16[1024,256]{1,0:T(8,128)(2,1)} %collective-permute-done.9.refs_1_.near, ...), custom_call_target="tpu_custom_call" | custom-call | tf_op jit(solution)/shard_map/pallas_call | solution.py:48
  190.5 6.5 %collective-permute-done.27.refs_2_ = bf16[256,1024]{1,0:T(8,128)(2,1)S(1)} collective-permute-done((bf16[256,1024]{1,0:T(8,128)(2,1)S(1)}, bf16[256,1024]{1,0:T(8,128)(2,1)S(1)}, u32[]{:S(2)}, u32[]{:S(2)}) %collective-permute-start.27) | collective-permute-done | bytes 524320 | tf_op jit(solution)/shard_map/ppermute | solution.py:36
  197.0 5.2 %collective-permute-done.26.got = f32[512,128]{1,0:T(8,128)S(1)} collective-permute-done((f32[512,128]{1,0:T(8,128)S(1)}, f32[512,128]{1,0:T(8,128)S(1)}, u32[]{:S(2)}, u32[]{:S(2)}) %collective-permute-start.26) | collective-permute-done | bytes 262176 | tf_op jit(solution)/shard_map/ppermute | solution.py:36
  208.6 3.5 %shard_map.132 = (f32[2,512,256]{2,1,0:T(8,128)S(1)}, f32[2,512,256]{2,1,0:T(8,128)S(1)}) custom-call(s32[5]{0:T(128)S(1)} %convert_element_type.3.flags, bf16[512,1024]{1,0:T(8,128)(2,1)S(1)} %shard_map.117.x_here.x_other.tokens, bf16[1024,256]{1,0:T(8,128)(2,1)S(1)} %shard_map.112.own, bf16[1024,256]{1,0:T(8,128)(2,1)S(1)} %collective-permute-done.20.near, ...), custom_call_target="tpu_custom_call" | custom-call | tf_op jit(solution)/shard_map/pallas_call | solution.py:48
  213.5 2.7 %collective-permute-start.31 = (bf16[256,256]{1,0:T(8,128)(2,1)S(1)}, bf16[256,256]{1,0:T(8,128)(2,1)S(1)}, u32[]{:S(2)}, u32[]{:S(2)}) collective-permute-start(bf16[256,256]{1,0:T(8,128)(2,1)S(1)} %get-tuple-element.138), channel_id=1, source_target_pairs={{0,4},{4,8},{8,12},{12,0},{1,5},{5,9},{9,13},{13,1},{2,6},{6,10},{... | collective-permute-start | bytes 393224 | tf_op jit(solution)/shard_map/ppermute | solution.py:40
  221.4 15.1 %collective-permute-start.33 = (bf16[256,256]{1,0:T(8,128)(2,1)S(1)}, bf16[256,256]{1,0:T(8,128)(2,1)S(1)}, u32[]{:S(2)}, u32[]{:S(2)}) collective-permute-start(bf16[256,256]{1,0:T(8,128)(2,1)S(1)} %get-tuple-element.140), channel_id=1, source_target_pairs={{0,12},{4,0},{8,4},{12,8},{1,13},{5,1},{9,5},{13,9},{2,14},{6,2},{... | collective-permute-start | bytes 393224 | tf_op jit(solution)/shard_map/ppermute | solution.py:40
  236.5 2.6 %collective-permute-done.33.fourth = bf16[256,256]{1,0:T(8,128)(2,1)S(1)} collective-permute-done((bf16[256,256]{1,0:T(8,128)(2,1)S(1)}, bf16[256,256]{1,0:T(8,128)(2,1)S(1)}, u32[]{:S(2)}, u32[]{:S(2)}) %collective-permute-start.33) | collective-permute-done | bytes 131104 | tf_op jit(solution)/shard_map/ppermute | solution.py:40
  247.5 3.1 %collective-permute-done.34.got = bf16[2,256,256]{2,1,0:T(8,128)(2,1)S(1)} collective-permute-done((bf16[2,256,256]{2,1,0:T(8,128)(2,1)S(1)}, bf16[2,256,256]{2,1,0:T(8,128)(2,1)S(1)}, u32[]{:S(2)}, u32[]{:S(2)}) %collective-permute-start.34) | collective-permute-done | bytes 262176 | tf_op jit(solution)/shard_map/ppermute | solution.py:36
  251.4 4.9 %collective-permute-done.37.refs_3_ = bf16[1024,128]{1,0:T(8,128)(2,1)S(1)} collective-permute-done((bf16[1024,128]{1,0:T(8,128)(2,1)S(1)}, bf16[1024,128]{1,0:T(8,128)(2,1)S(1)}, u32[]{:S(2)}, u32[]{:S(2)}) %collective-permute-start.37) | collective-permute-done | bytes 262176 | tf_op jit(solution)/shard_map/ppermute | solution.py:36
  256.2 4.0 %collective-permute-done.36.refs_2_ = bf16[1024,128]{1,0:T(8,128)(2,1)S(1)} collective-permute-done((bf16[1024,128]{1,0:T(8,128)(2,1)S(1)}, bf16[1024,128]{1,0:T(8,128)(2,1)S(1)}, u32[]{:S(2)}, u32[]{:S(2)}) %collective-permute-start.36) | collective-permute-done | bytes 262176 | tf_op jit(solution)/shard_map/ppermute | solution.py:36
  (141 shorter events, 87.0 us)
Async XLA Ops:
  17.8 20.6 %collective-permute-start.5 = (bf16[256,1024]{1,0:T(8,128)(2,1)S(1)}, bf16[256,1024]{1,0:T(8,128)(2,1)S(1)}, u32[]{:S(2)}, u32[]{:S(2)}) collective-permute-start(bf16[256,1024]{1,0:T(8,128)(2,1)S(1)} %shard_map.105), channel_id=1, source_target_pairs={{0,2},{2,0},{1,3},{3,1},{4,6},{6,4},{5,7},{7,5},{8,10},{10,8},{9,1... | collective-permute-start | bytes 1572872 | tf_op jit(solution)/shard_map/ppermute | solution.py:36
  31.6 58.5 %collective-permute-start.11 = (bf16[1024,512]{1,0:T(8,128)(2,1)}, bf16[1024,512]{1,0:T(8,128)(2,1)}, u32[]{:S(2)}, u32[]{:S(2)}) collective-permute-start(bf16[1024,512]{1,0:T(8,128)(2,1)} %shard_map.107), channel_id=1, source_target_pairs={{4,8},{8,4},{5,9},{9,5},{6,10},{10,6},{7,11},{11,7},{20,24},{24,20... | collective-permute-start | bytes 3145736 | tf_op jit(solution)/shard_map/ppermute | solution.py:40
  35.7 31.1 %collective-permute-start.3 = (bf16[256,256]{1,0:T(8,128)(2,1)}, bf16[256,256]{1,0:T(8,128)(2,1)}, u32[]{:S(2)}, u32[]{:S(2)}) collective-permute-start(bf16[256,256]{1,0:T(8,128)(2,1)} %copy-done.17), channel_id=1, source_target_pairs={{0,8},{4,12},{8,0},{12,4},{1,9},{5,13},{9,1},{13,5},{2,10},{6,14},... | collective-permute-start | bytes 393224 | tf_op jit(solution)/shard_map/ppermute | solution.py:40
  38.2 28.6 %collective-permute-start.4 = (bf16[256,256]{1,0:T(8,128)(2,1)}, bf16[256,256]{1,0:T(8,128)(2,1)}, u32[]{:S(2)}, u32[]{:S(2)}) collective-permute-start(bf16[256,256]{1,0:T(8,128)(2,1)} %copy-done.17), channel_id=1, source_target_pairs={{0,4},{4,8},{8,12},{12,0},{1,5},{5,9},{9,13},{13,1},{2,6},{6,10},{... | collective-permute-start | bytes 393224 | tf_op jit(solution)/shard_map/ppermute | solution.py:40
  70.0 18.6 %collective-permute-start.12 = (bf16[512,512]{1,0:T(8,128)(2,1)}, bf16[512,512]{1,0:T(8,128)(2,1)}, u32[]{:S(2)}, u32[]{:S(2)}) collective-permute-start(bf16[512,512]{1,0:T(8,128)(2,1)} %get-tuple-element.103.here), channel_id=1, source_target_pairs={{0,1},{1,0},{2,3},{3,2},{4,5},{5,4},{6,7},{7,6},{8,9},{9,8},{10,11... | collective-permute-start | bytes 1572872 | tf_op jit(solution)/shard_map/ppermute | solution.py:36
  72.0 41.0 %collective-permute-start.13 = (bf16[512,1024]{1,0:T(8,128)(2,1)S(1)}, bf16[512,1024]{1,0:T(8,128)(2,1)}, u32[]{:S(2)}, u32[]{:S(2)}) collective-permute-start(bf16[512,1024]{1,0:T(8,128)(2,1)S(1)} %shard_map.108.x_here.x_mine.tokens), channel_id=1, source_target_pairs={{0,4},{12,8},{1,5},{13,9},{2,6},{14,10},{3,7},{15,11},{16,20},{28,... | collective-permute-start | bytes 3145736 | tf_op jit(solution)/shard_map/ppermute | solution.py:40
  90.1 27.8 %collective-permute-start.19 = (bf16[1024,512]{1,0:T(8,128)(2,1)}, bf16[1024,512]{1,0:T(8,128)(2,1)S(1)}, u32[]{:S(2)}, u32[]{:S(2)}) collective-permute-start(bf16[1024,512]{1,0:T(8,128)(2,1)} %collective-permute-done.11.crossed), channel_id=1, source_target_pairs={{4,0},{8,12},{5,1},{9,13},{6,2},{10,14},{7,3},{11,15},{20,16},{24,... | collective-permute-start | bytes 3145736 | tf_op jit(solution)/shard_map/ppermute | solution.py:40
  91.4 27.9 %collective-permute-start.18 = (bf16[1024,512]{1,0:T(8,128)(2,1)S(1)}, bf16[1024,512]{1,0:T(8,128)(2,1)S(1)}, u32[]{:S(2)}, u32[]{:S(2)}) collective-permute-start(bf16[1024,512]{1,0:T(8,128)(2,1)S(1)} %shard_map.113), channel_id=1, source_target_pairs={{4,8},{8,4},{5,9},{9,5},{6,10},{10,6},{7,11},{11,7},{20,24},{24,20... | collective-permute-start | bytes 3145736 | tf_op jit(solution)/shard_map/ppermute | solution.py:40
  93.6 18.5 %collective-permute-start.14 = (bf16[512,256]{1,0:T(8,128)(2,1)S(1)}, bf16[512,256]{1,0:T(8,128)(2,1)S(1)}, u32[]{:S(2)}, u32[]{:S(2)}) collective-permute-start(bf16[512,256]{1,0:T(8,128)(2,1)S(1)} %get-tuple-element.100), channel_id=1, source_target_pairs={{0,4},{12,8},{1,5},{13,9},{2,6},{14,10},{3,7},{15,11},{16,20},{28,... | collective-permute-start | bytes 786440 | tf_op jit(solution)/shard_map/ppermute | solution.py:40
  106.4 26.7 %collective-permute-start.17 = (bf16[512,1024]{1,0:T(8,128)(2,1)S(1)}, bf16[512,1024]{1,0:T(8,128)(2,1)S(1)}, u32[]{:S(2)}, u32[]{:S(2)}) collective-permute-start(bf16[512,1024]{1,0:T(8,128)(2,1)S(1)} %shard_map.117.x_here.x_other.tokens), channel_id=1, source_target_pairs={{0,4},{12,8},{1,5},{13,9},{2,6},{14,10},{3,7},{15,11},{16,20},{28,... | collective-permute-start | bytes 3145736 | tf_op jit(solution)/shard_map/ppermute | solution.py:40
  115.6 26.4 %collective-permute-start.16 = (bf16[1024,512]{1,0:T(8,128)(2,1)}, bf16[1024,512]{1,0:T(8,128)(2,1)S(1)}, u32[]{:S(2)}, u32[]{:S(2)}) collective-permute-start(bf16[1024,512]{1,0:T(8,128)(2,1)} %shard_map.107), channel_id=1, source_target_pairs={{0,16},{16,0},{1,17},{17,1},{2,18},{18,2},{3,19},{19,3},{4,20},{20... | collective-permute-start | bytes 3145736 | tf_op jit(solution)/shard_map/ppermute | solution.py:36
  117.2 24.8 %collective-permute-start.15 = (bf16[1024,512]{1,0:T(8,128)(2,1)S(1)}, bf16[1024,512]{1,0:T(8,128)(2,1)S(1)}, u32[]{:S(2)}, u32[]{:S(2)}) collective-permute-start(bf16[1024,512]{1,0:T(8,128)(2,1)S(1)} %shard_map.119), channel_id=1, source_target_pairs={{4,8},{8,4},{5,9},{9,5},{6,10},{10,6},{7,11},{11,7},{20,24},{24,20... | collective-permute-start | bytes 3145736 | tf_op jit(solution)/shard_map/ppermute | solution.py:40
  119.2 27.4 %collective-permute-start.21 = (bf16[1024,512]{1,0:T(8,128)(2,1)S(1)}, bf16[1024,512]{1,0:T(8,128)(2,1)S(1)}, u32[]{:S(2)}, u32[]{:S(2)}) collective-permute-start(bf16[1024,512]{1,0:T(8,128)(2,1)S(1)} %collective-permute-done.18.crossed), channel_id=1, source_target_pairs={{4,0},{8,12},{5,1},{9,13},{6,2},{10,14},{7,3},{11,15},{20,16},{24,... | collective-permute-start | bytes 3145736 | tf_op jit(solution)/shard_map/ppermute | solution.py:40
  120.5 58.7 %collective-permute-start.24 = (bf16[1024,512]{1,0:T(8,128)(2,1)S(1)}, bf16[1024,512]{1,0:T(8,128)(2,1)S(1)}, u32[]{:S(2)}, u32[]{:S(2)}) collective-permute-start(bf16[1024,512]{1,0:T(8,128)(2,1)S(1)} %shard_map.120.rest_2_.far), channel_id=1, source_target_pairs={{0,16},{16,0},{1,17},{17,1},{2,18},{18,2},{3,19},{19,3},{4,20},{20... | collective-permute-start | bytes 3145736 | tf_op jit(solution)/shard_map/ppermute | solution.py:36
  142.5 33.2 %collective-permute-start.20 = (bf16[1024,256]{1,0:T(8,128)(2,1)}, bf16[1024,256]{1,0:T(8,128)(2,1)S(1)}, u32[]{:S(2)}, u32[]{:S(2)}) collective-permute-start(bf16[1024,256]{1,0:T(8,128)(2,1)} %collective-permute-done.9.refs_1_.near), channel_id=1, source_target_pairs={{0,16},{16,0},{1,17},{17,1},{2,18},{18,2},{3,19},{19,3},{4,20},{20... | collective-permute-start | bytes 1572872 | tf_op jit(solution)/shard_map/ppermute | solution.py:36
  144.0 46.0 %collective-permute-start.28 = (bf16[1024,512]{1,0:T(8,128)(2,1)S(1)}, bf16[1024,512]{1,0:T(8,128)(2,1)S(1)}, u32[]{:S(2)}, u32[]{:S(2)}) collective-permute-start(bf16[1024,512]{1,0:T(8,128)(2,1)S(1)} %shard_map.121), channel_id=1, source_target_pairs={{4,8},{8,4},{5,9},{9,5},{6,10},{10,6},{7,11},{11,7},{20,24},{24,20... | collective-permute-start | bytes 3145736 | tf_op jit(solution)/shard_map/ppermute | solution.py:40
  147.3 59.0 %collective-permute-start.22 = (bf16[1024,512]{1,0:T(8,128)(2,1)S(1)}, bf16[1024,512]{1,0:T(8,128)(2,1)S(1)}, u32[]{:S(2)}, u32[]{:S(2)}) collective-permute-start(bf16[1024,512]{1,0:T(8,128)(2,1)S(1)} %shard_map.123.far), channel_id=1, source_target_pairs={{0,16},{16,0},{1,17},{17,1},{2,18},{18,2},{3,19},{19,3},{4,20},{20... | collective-permute-start | bytes 3145736 | tf_op jit(solution)/shard_map/ppermute | solution.py:36
  183.8 20.5 %collective-permute-start.23 = (bf16[1024,256]{1,0:T(8,128)(2,1)S(1)}, bf16[1024,256]{1,0:T(8,128)(2,1)S(1)}, u32[]{:S(2)}, u32[]{:S(2)}) collective-permute-start(bf16[1024,256]{1,0:T(8,128)(2,1)S(1)} %shard_map.122), channel_id=1, source_target_pairs={{4,0},{8,12},{5,1},{9,13},{6,2},{10,14},{7,3},{11,15},{20,16},{24,... | collective-permute-start | bytes 1572872 | tf_op jit(solution)/shard_map/ppermute | solution.py:40
  212.1 28.4 %collective-permute-start.29 = (f32[2,512,256]{2,1,0:T(8,128)S(1)}, f32[2,512,256]{2,1,0:T(8,128)S(1)}, u32[]{:S(2)}, u32[]{:S(2)}) collective-permute-start(f32[2,512,256]{2,1,0:T(8,128)S(1)} %get-tuple-element.136), channel_id=1, source_target_pairs={{0,1},{1,0},{2,3},{3,2},{4,5},{5,4},{6,7},{7,6},{8,9},{9,8},{10,11... | collective-permute-start | bytes 3145736 | tf_op jit(solution)/shard_map/ppermute | solution.py:36
  212.2 26.9 %collective-permute-start.30 = (bf16[1024,256]{1,0:T(8,128)(2,1)S(1)}, bf16[1024,256]{1,0:T(8,128)(2,1)S(1)}, u32[]{:S(2)}, u32[]{:S(2)}) collective-permute-start(bf16[1024,256]{1,0:T(8,128)(2,1)S(1)} %shard_map.128), channel_id=1, source_target_pairs={{4,0},{8,12},{5,1},{9,13},{6,2},{10,14},{7,3},{11,15},{20,16},{24,... | collective-permute-start | bytes 1572872 | tf_op jit(solution)/shard_map/ppermute | solution.py:40
  216.2 29.2 %collective-permute-start.35 = (bf16[256,1024]{1,0:T(8,128)(2,1)S(1)}, bf16[256,1024]{1,0:T(8,128)(2,1)S(1)}, u32[]{:S(2)}, u32[]{:S(2)}) collective-permute-start(bf16[256,1024]{1,0:T(8,128)(2,1)S(1)} %get-tuple-element.132), channel_id=1, source_target_pairs={{0,2},{2,0},{1,3},{3,1},{4,6},{6,4},{5,7},{7,5},{8,10},{10,8},{9,1... | collective-permute-start | bytes 1572872 | tf_op jit(solution)/shard_map/ppermute | solution.py:36
  217.7 18.7 %collective-permute-start.32 = (bf16[256,256]{1,0:T(8,128)(2,1)S(1)}, bf16[256,256]{1,0:T(8,128)(2,1)S(1)}, u32[]{:S(2)}, u32[]{:S(2)}) collective-permute-start(bf16[256,256]{1,0:T(8,128)(2,1)S(1)} %get-tuple-element.139), channel_id=1, source_target_pairs={{0,8},{4,12},{8,0},{12,4},{1,9},{5,13},{9,1},{13,5},{2,10},{6,14},... | collective-permute-start | bytes 393224 | tf_op jit(solution)/shard_map/ppermute | solution.py:40
  221.4 17.7 %collective-permute-start.33 = (bf16[256,256]{1,0:T(8,128)(2,1)S(1)}, bf16[256,256]{1,0:T(8,128)(2,1)S(1)}, u32[]{:S(2)}, u32[]{:S(2)}) collective-permute-start(bf16[256,256]{1,0:T(8,128)(2,1)S(1)} %get-tuple-element.140), channel_id=1, source_target_pairs={{0,12},{4,0},{8,4},{12,8},{1,13},{5,1},{9,5},{13,9},{2,14},{6,2},{... | collective-permute-start | bytes 393224 | tf_op jit(solution)/shard_map/ppermute | solution.py:40
  244.9 17.0 %collective-permute-start.38 = (bf16[128,256]{1,0:T(8,128)(2,1)S(1)}, bf16[128,256]{1,0:T(8,128)(2,1)S(1)}, u32[]{:S(2)}, u32[]{:S(2)}) collective-permute-start(bf16[128,256]{1,0:T(8,128)(2,1)S(1)} %get-tuple-element.144), channel_id=1, source_target_pairs={{0,2},{2,0},{1,3},{3,1},{4,6},{6,4},{5,7},{7,5},{8,10},{10,8},{9,1... | collective-permute-start | bytes 196616 | tf_op jit(solution)/shard_map/ppermute | solution.py:36
  (36 other events, 450.9 us)

commit v8 on v6

--- a/solution.py
+++ b/solution.py
@@ -204,16 +204,24 @@
         out[i] = up[:, (i % 2) * cols : (i % 2 + 1) * cols]
 
 
-def packet_kernel(flags, here, ids_here, packet, half, ids, quarter):
-    rows, kv = here.shape
-    half[:rows] = here[...]
-    half[rows:] = packet[:, :kv]
-    ids[:rows] = ids_here[...]
-    ids[rows:] = packet[:, kv:]
+def packet_kernel(cotangent, adapters, out):
+    rows, kv = cotangent.shape
+    size = out.shape[1] - kv
+    out[:, :kv] = cotangent[...]
+    numbers = jnp.broadcast_to(adapters[...].astype(f32), (rows, size))
+    out[:, kv:] = numbers.astype(bf16)
+
+
+def unpack_kernel(flags, here, there, half, ids, quarter):
+    rows = here.shape[0]
+    kv = half.shape[1]
     cols = quarter.shape[1]
     span = pl.ds(pl.multiple_of(flags[3] * cols, 128), cols)
-    quarter[:rows] = here[:, span]
-    quarter[rows:] = packet[:, span]
+    for i, packet in enumerate((here, there)):
+        place = slice(i * rows, (i + 1) * rows)
+        half[place] = packet[:, :kv]
+        ids[place] = packet[:, kv:]
+        quarter[place] = packet[:, span]
 
 
 def dy_line_kernel(places, here, got, out):
@@ -372,9 +380,6 @@
     def like(*shape, kind=bf16):
         return jax.ShapeDtypeStruct(shape, kind)
 
-    def join(*values):
-        return jnp.concatenate(values, axis=1)
-
     def rows_at(i, value, length):
         out = like(length, value.shape[1])
         return copy_call(
@@ -419,9 +424,10 @@
         )[0]
 
     down_got = swap(done(rows_at(2, down, eighth)), "own")
-    ids_here = jnp.broadcast_to(token_adapter.astype(bf16), (rows, size))
-    packet = swap(done(join(step(cotangent), ids_here)), "own")
-    x_got = [swap(done(columns_at(2, step(tokens))), "own")]
+    packet_here = done(
+        kernel_call(packet_kernel, [like(rows, kv + size)], step(cotangent), token_adapter)[0]
+    )
+    packet = swap(packet_here, "own")
     down_piece = done(
         copy_call(
             lambda n, a, o: [
@@ -440,44 +446,34 @@
     up_all = lax.all_to_all(
         done(up_sent), ("fsdp", "own"), split_axis=0, concat_axis=0, tiled=True
     ).reshape(number * size, kvq)
+    x_got = [swap(done(columns_at(2, step(tokens))), "own")]
     weight_here = done(rows_at(0, step(frozen_value_weight), eighth))
     weight_near = along(weight_here, NEIGHBOURS)
-
     dy_half, ids, dy_quarter = kernel_call(
-        packet_kernel,
+        unpack_kernel,
         [like(both, kv), like(both, size), like(both, kvq)],
-        cotangent,
-        ids_here,
-        step(packet),
+        step(packet_here),
+        packet,
         scalars=flags,
     )
     done(dy_quarter)
-    dy_tp = swap(dy_half, "tp")
-
-    down_near, x_got[0] = step(down_near, x_got[0])
-    crossing = done(side_by_side(down_piece, down_near))
+
+    crossing = done(side_by_side(down_piece, step(down_near)))
     down_crossed = along(crossing, MIDDLE)
     down_other = swap(crossing, "rep")
     x_mine = done(tokens_of(0, tokens, step(x_got[0])))
     x_in = [along(x_mine, INWARD)]
-    dy_line = done(
-        kernel_call(
-            dy_line_kernel, [like(both, 2 * kv)], dy_half, step(dy_tp), scalars=places
-        )[0]
-    )
-
     compact = like(both, size, kind=f32)
     up_all = step(up_all)
     back_part = done(kernel_call(back_kernel, [compact], ids, dy_quarter, up_all)[0])
     back_tp = swap(back_part, "tp")
-    weight_near = step(weight_near)
-    crossing = done(side_by_side(weight_here, weight_near))
+    crossing = done(side_by_side(weight_here, step(weight_near)))
     weight_crossed = along(crossing, MIDDLE)
     back_part = done(kernel_call(add_kernel, [compact], back_part, step(back_tp))[0])
     back_got = swap(back_part, "own")
-    sent, down_other = step(tokens, down_other)
-    x_got.append(swap(done(columns_at(3, sent)), "own"))
-    weight_other = done(rows_at(1, step(frozen_value_weight), eighth))
+    sent, down_other = step(frozen_value_weight, down_other)
+    weight_other = done(rows_at(1, sent, eighth))
+    weight_near_other = swap(step(weight_near), "rep")
     back_wide, back_sent = kernel_call(
         back_end_kernel,
         [like(both, number * size), like(both, wide)],
@@ -489,9 +485,12 @@
     back_in = along(done(back_sent), INWARD)
     down_crossed = done(step(down_crossed))
     down_outer = along(down_crossed, OUTWARD)
-    x_other = done(tokens_of(1, tokens, step(x_got[1])))
-    x_in.append(along(x_other, INWARD))
-    x_both = [x_mine, x_other]
+    sent, weight_near_other = step(tokens, weight_near_other)
+    x_got.append(swap(done(columns_at(3, sent)), "own"))
+    dy_tp = swap(step(dy_half), "tp")
+    dy_line = done(
+        kernel_call(dy_line_kernel, [like(both, 2 * kv)], dy_half, dy_tp, scalars=places)[0]
+    )
 
     def to_middle(half):
         x_in[half] = step(x_in[half])
@@ -523,8 +522,7 @@
             crossed,
             outer,
         )
-        done(here)
-        return here, swap(there, "own")
+        return done(here), swap(there, "own")
 
     def far_of(crossed, outer):
         out = like(*crossed.shape)
@@ -535,17 +533,33 @@
             spread_in_kernel, [like(both, number * size)], step(back_in), scalars=numbers
         )[0]
     )
+    x_both = [x_mine]
     middle = [to_middle(0)]
-    weight_near_other = swap(step(weight_near), "rep")
+    x_both.append(done(tokens_of(1, tokens, step(x_got[1]))))
+    x_other = x_both[1]
+    x_in.append(along(x_other, INWARD))
     weight_crossed = done(step(weight_crossed))
     weight_outer = along(weight_crossed, OUTWARD)
-    down_outer, weight_near_other = step(down_outer, weight_near_other)
-    down_far = done(far_of(down_crossed, down_outer))
+    down_far = done(far_of(down_crossed, step(down_outer)))
     down_far_other = swap(down_far, "rep")
     middle.append(to_middle(1))
     outward = [to_end(0, middle[0])]
     weight_far = done(far_of(weight_crossed, step(weight_outer)))
     weight_far_other = swap(weight_far, "rep")
+    half_grad = [like(rows, eighth)] * 2
+    dx_mine, dx_mine_sent = kernel_call(
+        dx_kernel,
+        half_grad,
+        step(dy_line),
+        back_wide,
+        weight_here,
+        weight_near,
+        weight_far,
+        down_piece,
+        down_near,
+        down_far,
+    )
+    done(dx_mine)
 
     low_part = done(
         kernel_call(
@@ -568,30 +582,17 @@
         y_kernel, blocks, step(x_mine), weight_here, weight_near, weight_far, scalars=flags
     )
     done(y_first[0])
-    low_part = done(low_part + step(low_tp))
+    low_part = done(kernel_call(add_kernel, [compact], low_part, step(low_tp))[0])
     low_got = swap(low_part, "own")
-    half_grad = [like(rows, eighth)] * 2
-    dx_mine, dx_sent = kernel_call(
-        dx_kernel,
-        half_grad,
-        step(dy_line),
-        back_wide,
-        weight_here,
-        weight_near,
-        weight_far,
-        down_piece,
-        down_near,
-        down_far,
-    )
-    done(dx_mine)
-    dx_mine_got = swap(dx_sent, "own")
     grads = [finish(0, middle[0], outward[0])]
+    low_got = step(low_got)
+    dx_mine_got = swap(step(dx_mine_sent, low_got)[0], "own")
     _, delta, up_part = kernel_call(
         low_end_kernel,
         [like(both, number * size), like(both, kvq), like(number * size, kvq)],
         ids,
         low_part,
-        step(low_got),
+        low_got,
         up_all,
         dy_quarter,
         scalars=numbers,
@@ -600,7 +601,7 @@
         done(up_part).reshape(4, 2, size, kvq), "fsdp", split_axis=0, concat_axis=0, tiled=True
     )
     outward.append(to_end(1, middle[1]))
-    weight_far_other, dx_mine_got, grad_got = step(weight_far_other, dx_mine_got, grads[0][1])
+    weight_far_other, grad_got = step(weight_far_other, grads[0][1])
     dx_other, dx_sent = kernel_call(
         dx_kernel,
         half_grad,
@@ -613,6 +614,11 @@
         down_far_other,
     )
     dx_other_got = swap(done(dx_sent), "own")
+    up_got, dx_mine_got = step(up_got, dx_mine_got)
+    up_mine, up_theirs = kernel_call(
+        up_sum_kernel, [like(size, kvq)] * 2, up_got, scalars=numbers
+    )
+    up_theirs = swap(done(up_theirs), "own")
     y_keep, y_sent = kernel_call(
         y_kernel,
         blocks,
@@ -624,6 +630,7 @@
         scalars=flags,
     )
     y_got = swap(done(y_sent), "tp")
+    grads.append(finish(1, middle[1], outward[1]))
     y_here, y_sent = kernel_call(
         y_sum_kernel,
         [like(2, rows, cols, kind=f32), like(2, rows, cols)],
@@ -633,11 +640,6 @@
         scalars=flags,
     )
     y_got = swap(done(y_sent), "own")
-    up_mine, up_theirs = kernel_call(
-        up_sum_kernel, [like(size, kvq)] * 2, step(up_got), scalars=numbers
-    )
-    up_theirs = swap(done(up_theirs), "own")
-    grads.append(finish(1, middle[1], outward[1]))
 
     def in_place(axis, out, *pieces):
         def plan(n, a, o):

time: 223 us -> 238 us (1.067)
  waiting for transfers between devices: 69.6 us -> 94.5 us
  local copies, waits for them, and re-layouts: 24.2 us -> 20.3 us
  starting transfers between devices: 61.2 us -> 58.5 us
    ppermute x13, waiting for transfers between devices: 30.2 us -> 49 us  [along(): return lax.ppermute(value, 'fsdp', pairs)]
    ppermute x20, waiting for transfers between devices: 32.4 us -> 45.4 us  [swap(): return lax.ppermute(value, axis, PAIR)]
    all_to_all x1, waiting for transfers between devices: 7.06 us -> 0.01 us  [body_line(): lax.all_to_all(done(up_part).reshape(4, 2, size, kvq), 'fsdp', split_axis...]
    unnamed x104 -> x123, local copies, waits for them, and re-layouts: 23.8 us -> 20 us
    pallas_call x37 -> x39, Pallas kernels: 62.8 us -> 61.6 us  [kernel_call(): pl.pallas_call(body, out_shape=list(outs), in_specs=specs, out_specs=[pl....]
  transfers between devices with their start and end apart: 35 -> 35, of which waited for: 17 -> 14; matrix products, arithmetic and copies ran while one was open for 1% -> 0% of each run, Pallas kernels for 24% -> 21%
where the time goes in v8:
time: 238 us; the launch traced here: 237 us
  waiting for transfers between devices  94.5 us (40%)
  Pallas kernels  61.6 us (26%)
  starting transfers between devices  58.5 us (25%)
  local copies, waits for them, and re-layouts  20.3 us (9%)
    pallas_call x39, Pallas kernels, kernel_call(): pl.pallas_call(body, out_shape=list(outs), in_specs=specs, out_specs=[pl....  61.6 us
    ppermute x13, waiting for transfers between devices, along(): return lax.ppermute(value, 'fsdp', pairs)  49 us
    ppermute x20, waiting for transfers between devices, swap(): return lax.ppermute(value, axis, PAIR)  45.4 us
    ppermute x13, starting transfers between devices, along(): return lax.ppermute(value, 'fsdp', pairs)  30.3 us
    unnamed x123, local copies, waits for them, and re-layouts  20 us
    ppermute x20, starting transfers between devices, swap(): return lax.ppermute(value, axis, PAIR)  19.3 us
    all_to_all x1, starting transfers between devices, body_line(): lax.all_to_all(done(up_sent), ('fsdp', 'own'), split_axis=0, concat_axis=...  4.79 us
  transfers between devices with their start and end apart: 35, of which 14 were waited for; matrix products, arithmetic and copies ran while one was open for 0% of the time, Pallas kernels for 21%

profile of v8, /device:TPU:0, one launch (start us, length us, event | category | flops | bytes accessed | tf_op | source)
XLA Modules:
  0.0 236.6 jit_solution(11509163241489122287)
XLA Ops:
  2.5 3.0 %collective-permute-start.1 = (bf16[1024,128]{1,0:T(8,128)(2,1)S(1)}, bf16[1024,128]{1,0:T(8,128)(2,1)S(1)}, u32[]{:S(2)}, u32[]{:S(2)}) collective-permute-start(bf16[1024,128]{1,0:T(8,128)(2,1)S(1)} %shard_map.102), channel_id=1, source_target_pairs={{0,2},{2,0},{1,3},{3,1},{4,6},{6,4},{5,7},{7,5},{8,10},{10,8},{9,1... | collective-permute-start | bytes 786440 | tf_op jit(solution)/shard_map/ppermute | solution.py:36
  7.4 4.4 %collective-permute-done.1.refs_1_ = bf16[1024,128]{1,0:T(8,128)(2,1)S(1)} collective-permute-done((bf16[1024,128]{1,0:T(8,128)(2,1)S(1)}, bf16[1024,128]{1,0:T(8,128)(2,1)S(1)}, u32[]{:S(2)}, u32[]{:S(2)}) %collective-permute-start.1) | collective-permute-done | bytes 262176 | tf_op jit(solution)/shard_map/ppermute | solution.py:36
  17.1 6.8 %collective-permute-done.there = bf16[256,640]{1,0:T(8,128)(2,1)S(1)} collective-permute-done((bf16[256,640]{1,0:T(8,128)(2,1)S(1)}, bf16[256,640]{1,0:T(8,128)(2,1)S(1)}, u32[]{:S(2)}, u32[]{:S(2)}) %collective-permute-start) | collective-permute-done | bytes 327712 | tf_op jit(solution)/shard_map/ppermute | solution.py:36
  25.5 4.8 %all-to-all-start = ((bf16[8,128,256]{2,1,0:T(8,128)(2,1)}), bf16[8,128,256]{2,1,0:T(8,128)(2,1)S(1)}, u32[]{:S(2)}, u32[]{:S(2)}) async-start(bf16[8,128,256]{2,1,0:T(8,128)(2,1)} %copy-done.27), calls=%async_computation | async-start | bytes 1048576 | tf_op jit(solution)/shard_map/all_to_all | solution.py:446
  41.2 3.2 %collective-permute-start.2 = (bf16[1024,256]{1,0:T(8,128)(2,1)S(1)}, bf16[1024,256]{1,0:T(8,128)(2,1)S(1)}, u32[]{:S(2)}, u32[]{:S(2)}) collective-permute-start(bf16[1024,256]{1,0:T(8,128)(2,1)S(1)} %shard_map.107.refs_0_.own), channel_id=1, source_target_pairs={{0,4},{4,0},{8,12},{12,8},{1,5},{5,1},{9,13},{13,9},{2,6},{6,2},{1... | collective-permute-start | bytes 1572872 | tf_op jit(solution)/shard_map/ppermute | solution.py:40
  44.4 6.0 %collective-permute-done.5.refs_1_ = bf16[256,1024]{1,0:T(8,128)(2,1)S(1)} collective-permute-done((bf16[256,1024]{1,0:T(8,128)(2,1)S(1)}, bf16[256,1024]{1,0:T(8,128)(2,1)S(1)}, u32[]{:S(2)}, u32[]{:S(2)}) %collective-permute-start.5) | collective-permute-done | bytes 524320 | tf_op jit(solution)/shard_map/ppermute | solution.py:36
  55.8 3.2 %collective-permute-done.4.own_near_other.rest_0_ = bf16[1024,512]{1,0:T(8,128)(2,1)} collective-permute-done((bf16[1024,512]{1,0:T(8,128)(2,1)}, bf16[1024,512]{1,0:T(8,128)(2,1)}, u32[]{:S(2)}, u32[]{:S(2)}) %collective-permute-start.4) | collective-permute-done | bytes 1048608 | tf_op jit(solution)/shard_map/ppermute | solution.py:36
  63.7 4.3 %collective-permute-start.11 = (bf16[512,1024]{1,0:T(8,128)(2,1)S(1)}, bf16[512,1024]{1,0:T(8,128)(2,1)}, u32[]{:S(2)}, u32[]{:S(2)}) collective-permute-start(bf16[512,1024]{1,0:T(8,128)(2,1)S(1)} %shard_map.110.x_here.x_mine.tokens), channel_id=1, source_target_pairs={{0,4},{12,8},{1,5},{13,9},{2,6},{14,10},{3,7},{15,11},{16,20},{28,... | collective-permute-start | bytes 3145736 | tf_op jit(solution)/shard_map/ppermute | solution.py:40
  79.3 5.6 %collective-permute-start.12 = (bf16[512,256]{1,0:T(8,128)(2,1)}, bf16[512,256]{1,0:T(8,128)(2,1)S(1)}, u32[]{:S(2)}, u32[]{:S(2)}) collective-permute-start(bf16[512,256]{1,0:T(8,128)(2,1)} %get-tuple-element.91), channel_id=1, source_target_pairs={{0,4},{12,8},{1,5},{13,9},{2,6},{14,10},{3,7},{15,11},{16,20},{28,... | collective-permute-start | bytes 786440 | tf_op jit(solution)/shard_map/ppermute | solution.py:40
  85.7 5.5 %collective-permute-done.12.packet = bf16[512,256]{1,0:T(8,128)(2,1)S(1)} collective-permute-done((bf16[512,256]{1,0:T(8,128)(2,1)}, bf16[512,256]{1,0:T(8,128)(2,1)S(1)}, u32[]{:S(2)}, u32[]{:S(2)}) %collective-permute-start.12) | collective-permute-done | bytes 262176 | tf_op jit(solution)/shard_map/ppermute | solution.py:40
  92.0 2.9 %shard_map.119 = bf16[1024,512]{1,0:T(8,128)(2,1)S(1)} custom-call(bf16[512,1024]{1,0:T(8,128)(2,1)S(1)} %shard_map.110.x_here.x_mine.tokens, bf16[512,1024]{1,0:T(8,128)(2,1)S(1)} %get-tuple-element.94.back, bf16[512,1024]{1,0:T(8,128)(2,1)} %collective-permute-done.11.x_in, bf16[512,1024]{1,0:T(8,128)(2,1)S(1)} %shard_map.118.back_in), custom_call_target="tpu_custom_call" | custom-call | tf_op jit(solution)/shard_map/pallas_call | solution.py:48
  96.6 4.4 %collective-permute-start.19 = (bf16[512,1024]{1,0:T(8,128)(2,1)S(1)}, bf16[512,1024]{1,0:T(8,128)(2,1)S(1)}, u32[]{:S(2)}, u32[]{:S(2)}) collective-permute-start(bf16[512,1024]{1,0:T(8,128)(2,1)S(1)} %shard_map.120.x_here.x_other.tokens), channel_id=1, source_target_pairs={{0,4},{12,8},{1,5},{13,9},{2,6},{14,10},{3,7},{15,11},{16,20},{28,... | collective-permute-start | bytes 3145736 | tf_op jit(solution)/shard_map/ppermute | solution.py:40
  105.3 17.8 %collective-permute-done.19.x_in = bf16[512,1024]{1,0:T(8,128)(2,1)S(1)} collective-permute-done((bf16[512,1024]{1,0:T(8,128)(2,1)S(1)}, bf16[512,1024]{1,0:T(8,128)(2,1)S(1)}, u32[]{:S(2)}, u32[]{:S(2)}) %collective-permute-start.19) | collective-permute-done | bytes 1048608 | tf_op jit(solution)/shard_map/ppermute | solution.py:40
  130.5 3.7 %shard_map.125 = (bf16[256,1024]{1,0:T(8,128)(2,1)S(1)}, bf16[256,1024]{1,0:T(8,128)(2,1)S(1)}) custom-call(bf16[512,1024]{1,0:T(8,128)(2,1)S(1)} %shard_map.117.dy, bf16[512,1024]{1,0:T(8,128)(2,1)S(1)} %get-tuple-element.94.back, bf16[1024,256]{1,0:T(8,128)(2,1)S(1)} %copy-done.11, bf16[1024,256]{1,0:T(8,128)(2,1)S(1)} %copy-done.15, ...), custom_call_target="tpu_custom_call" | custom-call | tf_op jit(solution)/shard_map/pallas_call | solution.py:48
  134.2 4.5 %shard_map.126.left = f32[512,128]{1,0:T(8,128)S(1)} custom-call(s32[16]{0:T(128)S(1)} %concatenate.3.numbers, bf16[512,128]{1,0:T(8,128)(2,1)S(1)} %get-tuple-element.83.ids, bf16[512,1024]{1,0:T(8,128)(2,1)S(1)} %shard_map.110.x_here.x_mine.tokens, bf16[512,1024]{1,0:T(8,128)(2,1)S(1)} %shard_map.120.x_here.x_other.tokens, ...), custom_call_target="tpu_custom_call" | custom-call | tf_op jit(solution)/shard_map/pallas_call | solution.py:48
  141.8 4.3 %shard_map.127 = (f32[2,512,256]{2,1,0:T(8,128)S(1)}, f32[2,512,256]{2,1,0:T(8,128)S(1)}) custom-call(s32[5]{0:T(128)S(1)} %convert_element_type.3.flags, bf16[512,1024]{1,0:T(8,128)(2,1)S(1)} %shard_map.110.x_here.x_mine.tokens, bf16[1024,256]{1,0:T(8,128)(2,1)S(1)} %copy-done.11, bf16[1024,256]{1,0:T(8,128)(2,1)S(1)} %copy-done.15, ...), custom_call_target="tpu_custom_call" | custom-call | tf_op jit(solution)/shard_map/pallas_call | solution.py:48
  148.2 6.8 %collective-permute-done.22.outer = bf16[1024,256]{1,0:T(8,128)(2,1)S(1)} collective-permute-done((bf16[1024,256]{1,0:T(8,128)(2,1)S(1)}, bf16[1024,256]{1,0:T(8,128)(2,1)S(1)}, u32[]{:S(2)}, u32[]{:S(2)}) %collective-permute-start.22) | collective-permute-done | bytes 524320 | tf_op jit(solution)/shard_map/ppermute | solution.py:40
  160.2 4.1 %all-to-all-start.1 = ((bf16[4,2,128,256]{3,2,1,0:T(8,128)(2,1)}), bf16[4,2,128,256]{3,2,1,0:T(8,128)(2,1)}, u32[]{:S(2)}, u32[]{:S(2)}) async-start(bf16[4,2,128,256]{3,2,1,0:T(8,128)(2,1)} %bitcast.25), calls=%async_computation.1 | async-start | bytes 1048576 | tf_op jit(solution)/shard_map/all_to_all | solution.py:600
  169.0 14.9 %collective-permute-done.25.refs_2_ = bf16[1024,128]{1,0:T(8,128)(2,1)S(1)} collective-permute-done((bf16[1024,128]{1,0:T(8,128)(2,1)}, bf16[1024,128]{1,0:T(8,128)(2,1)S(1)}, u32[]{:S(2)}, u32[]{:S(2)}) %collective-permute-start.25) | collective-permute-done | bytes 262176 | tf_op jit(solution)/shard_map/ppermute | solution.py:36
  184.6 4.1 %shard_map.132 = (bf16[256,1024]{1,0:T(8,128)(2,1)S(1)}, bf16[256,1024]{1,0:T(8,128)(2,1)S(1)}) custom-call(bf16[512,1024]{1,0:T(8,128)(2,1)S(1)} %copy-done.7, bf16[512,1024]{1,0:T(8,128)(2,1)S(1)} %get-tuple-element.94.back, bf16[1024,256]{1,0:T(8,128)(2,1)S(1)} %copy-done.19, bf16[1024,256]{1,0:T(8,128)(2,1)} %collective-permute-done.7.near, ...), custom_call_target="tpu_custom_call" | custom-call | tf_op jit(solution)/shard_map/pallas_call | solution.py:48
  195.8 4.5 %shard_map.134 = (f32[2,512,256]{2,1,0:T(8,128)S(1)}, f32[2,512,256]{2,1,0:T(8,128)S(1)}) custom-call(s32[5]{0:T(128)S(1)} %convert_element_type.3.flags, bf16[512,1024]{1,0:T(8,128)(2,1)S(1)} %shard_map.120.x_here.x_other.tokens, bf16[1024,256]{1,0:T(8,128)(2,1)S(1)} %copy-done.20, bf16[1024,256]{1,0:T(8,128)(2,1)} %collective-permute-done.7.near, ...), custom_call_target="tpu_custom_call" | custom-call | tf_op jit(solution)/shard_map/pallas_call | solution.py:48
  202.3 14.3 %collective-permute-done.28.outer = bf16[1024,256]{1,0:T(8,128)(2,1)S(1)} collective-permute-done((bf16[1024,256]{1,0:T(8,128)(2,1)S(1)}, bf16[1024,256]{1,0:T(8,128)(2,1)S(1)}, u32[]{:S(2)}, u32[]{:S(2)}) %collective-permute-start.28) | collective-permute-done | bytes 524320 | tf_op jit(solution)/shard_map/ppermute | solution.py:40
  224.2 4.5 %collective-permute-done.29.got = bf16[2,256,256]{2,1,0:T(8,128)(2,1)S(1)} collective-permute-done((bf16[2,256,256]{2,1,0:T(8,128)(2,1)S(1)}, bf16[2,256,256]{2,1,0:T(8,128)(2,1)S(1)}, u32[]{:S(2)}, u32[]{:S(2)}) %collective-permute-start.29) | collective-permute-done | bytes 262176 | tf_op jit(solution)/shard_map/ppermute | solution.py:36
  229.4 4.3 %collective-permute-done.31.refs_3_ = bf16[1024,128]{1,0:T(8,128)(2,1)S(1)} collective-permute-done((bf16[1024,128]{1,0:T(8,128)(2,1)S(1)}, bf16[1024,128]{1,0:T(8,128)(2,1)S(1)}, u32[]{:S(2)}, u32[]{:S(2)}) %collective-permute-start.31) | collective-permute-done | bytes 262176 | tf_op jit(solution)/shard_map/ppermute | solution.py:36
  (214 shorter events, 93.1 us)
Async XLA Ops:
  13.7 19.5 %collective-permute-start.3 = (bf16[1024,256]{1,0:T(8,128)(2,1)S(1)}, bf16[1024,256]{1,0:T(8,128)(2,1)}, u32[]{:S(2)}, u32[]{:S(2)}) collective-permute-start(bf16[1024,256]{1,0:T(8,128)(2,1)S(1)} %shard_map.104.refs_0_.rest_0_.own), channel_id=1, source_target_pairs={{0,4},{4,0},{8,12},{12,8},{1,5},{5,1},{9,13},{13,9},{2,6},{6,2},{1... | collective-permute-start | bytes 1572872 | tf_op jit(solution)/shard_map/ppermute | solution.py:40
  25.5 25.6 %all-to-all-start = ((bf16[8,128,256]{2,1,0:T(8,128)(2,1)}), bf16[8,128,256]{2,1,0:T(8,128)(2,1)S(1)}, u32[]{:S(2)}, u32[]{:S(2)}) async-start(bf16[8,128,256]{2,1,0:T(8,128)(2,1)} %copy-done.27), calls=%async_computation | async-start | bytes 1048576 | tf_op jit(solution)/shard_map/all_to_all | solution.py:446
  35.9 23.0 %collective-permute-start.4 = (bf16[1024,512]{1,0:T(8,128)(2,1)}, bf16[1024,512]{1,0:T(8,128)(2,1)}, u32[]{:S(2)}, u32[]{:S(2)}) collective-permute-start(bf16[1024,512]{1,0:T(8,128)(2,1)} %shard_map.109), channel_id=1, source_target_pairs={{0,16},{16,0},{1,17},{17,1},{2,18},{18,2},{3,19},{19,3},{4,20},{20... | collective-permute-start | bytes 3145736 | tf_op jit(solution)/shard_map/ppermute | solution.py:36
  39.5 33.5 %collective-permute-start.8 = (bf16[1024,512]{1,0:T(8,128)(2,1)}, bf16[1024,512]{1,0:T(8,128)(2,1)}, u32[]{:S(2)}, u32[]{:S(2)}) collective-permute-start(bf16[1024,512]{1,0:T(8,128)(2,1)} %shard_map.109), channel_id=1, source_target_pairs={{4,8},{8,4},{5,9},{9,5},{6,10},{10,6},{7,11},{11,7},{20,24},{24,20... | collective-permute-start | bytes 3145736 | tf_op jit(solution)/shard_map/ppermute | solution.py:40
  60.4 13.9 %collective-permute-start.7 = (bf16[1024,256]{1,0:T(8,128)(2,1)S(1)}, bf16[1024,256]{1,0:T(8,128)(2,1)}, u32[]{:S(2)}, u32[]{:S(2)}) collective-permute-start(bf16[1024,256]{1,0:T(8,128)(2,1)S(1)} %collective-permute-done.2.refs_1_.near), channel_id=1, source_target_pairs={{0,16},{16,0},{1,17},{17,1},{2,18},{18,2},{3,19},{19,3},{4,20},{20... | collective-permute-start | bytes 1572872 | tf_op jit(solution)/shard_map/ppermute | solution.py:36
  63.7 28.4 %collective-permute-start.11 = (bf16[512,1024]{1,0:T(8,128)(2,1)S(1)}, bf16[512,1024]{1,0:T(8,128)(2,1)}, u32[]{:S(2)}, u32[]{:S(2)}) collective-permute-start(bf16[512,1024]{1,0:T(8,128)(2,1)S(1)} %shard_map.110.x_here.x_mine.tokens), channel_id=1, source_target_pairs={{0,4},{12,8},{1,5},{13,9},{2,6},{14,10},{3,7},{15,11},{16,20},{28,... | collective-permute-start | bytes 3145736 | tf_op jit(solution)/shard_map/ppermute | solution.py:40
  68.1 33.6 %collective-permute-start.15 = (bf16[1024,512]{1,0:T(8,128)(2,1)}, bf16[1024,512]{1,0:T(8,128)(2,1)}, u32[]{:S(2)}, u32[]{:S(2)}) collective-permute-start(bf16[1024,512]{1,0:T(8,128)(2,1)} %shard_map.112), channel_id=1, source_target_pairs={{4,8},{8,4},{5,9},{9,5},{6,10},{10,6},{7,11},{11,7},{20,24},{24,20... | collective-permute-start | bytes 3145736 | tf_op jit(solution)/shard_map/ppermute | solution.py:40
  73.0 30.1 %collective-permute-start.14 = (bf16[1024,512]{1,0:T(8,128)(2,1)}, bf16[1024,512]{1,0:T(8,128)(2,1)}, u32[]{:S(2)}, u32[]{:S(2)}) collective-permute-start(bf16[1024,512]{1,0:T(8,128)(2,1)} %collective-permute-done.8.crossed), channel_id=1, source_target_pairs={{4,0},{8,12},{5,1},{9,13},{6,2},{10,14},{7,3},{11,15},{20,16},{24,... | collective-permute-start | bytes 3145736 | tf_op jit(solution)/shard_map/ppermute | solution.py:40
  77.4 17.6 %collective-permute-start.10 = (bf16[256,1024]{1,0:T(8,128)(2,1)}, bf16[256,1024]{1,0:T(8,128)(2,1)}, u32[]{:S(2)}, u32[]{:S(2)}) collective-permute-start(bf16[256,1024]{1,0:T(8,128)(2,1)} %shard_map.116), channel_id=1, source_target_pairs={{0,2},{2,0},{1,3},{3,1},{4,6},{6,4},{5,7},{7,5},{8,10},{10,8},{9,1... | collective-permute-start | bytes 1572872 | tf_op jit(solution)/shard_map/ppermute | solution.py:36
  96.6 26.4 %collective-permute-start.19 = (bf16[512,1024]{1,0:T(8,128)(2,1)S(1)}, bf16[512,1024]{1,0:T(8,128)(2,1)S(1)}, u32[]{:S(2)}, u32[]{:S(2)}) collective-permute-start(bf16[512,1024]{1,0:T(8,128)(2,1)S(1)} %shard_map.120.x_here.x_other.tokens), channel_id=1, source_target_pairs={{0,4},{12,8},{1,5},{13,9},{2,6},{14,10},{3,7},{15,11},{16,20},{28,... | collective-permute-start | bytes 3145736 | tf_op jit(solution)/shard_map/ppermute | solution.py:40
  101.0 24.3 %collective-permute-start.18 = (bf16[1024,512]{1,0:T(8,128)(2,1)S(1)}, bf16[1024,512]{1,0:T(8,128)(2,1)S(1)}, u32[]{:S(2)}, u32[]{:S(2)}) collective-permute-start(bf16[1024,512]{1,0:T(8,128)(2,1)S(1)} %shard_map.119), channel_id=1, source_target_pairs={{4,8},{8,4},{5,9},{9,5},{6,10},{10,6},{7,11},{11,7},{20,24},{24,20... | collective-permute-start | bytes 3145736 | tf_op jit(solution)/shard_map/ppermute | solution.py:40
  101.7 26.4 %collective-permute-start.17 = (bf16[1024,512]{1,0:T(8,128)(2,1)}, bf16[1024,512]{1,0:T(8,128)(2,1)S(1)}, u32[]{:S(2)}, u32[]{:S(2)}) collective-permute-start(bf16[1024,512]{1,0:T(8,128)(2,1)} %collective-permute-done.15.crossed), channel_id=1, source_target_pairs={{4,0},{8,12},{5,1},{9,13},{6,2},{10,14},{7,3},{11,15},{20,16},{24,... | collective-permute-start | bytes 3145736 | tf_op jit(solution)/shard_map/ppermute | solution.py:40
  104.7 29.5 %collective-permute-start.16 = (bf16[1024,512]{1,0:T(8,128)(2,1)S(1)}, bf16[1024,512]{1,0:T(8,128)(2,1)S(1)}, u32[]{:S(2)}, u32[]{:S(2)}) collective-permute-start(bf16[1024,512]{1,0:T(8,128)(2,1)S(1)} %shard_map.121.rest_2_.far), channel_id=1, source_target_pairs={{0,16},{16,0},{1,17},{17,1},{2,18},{18,2},{3,19},{19,3},{4,20},{20... | collective-permute-start | bytes 3145736 | tf_op jit(solution)/shard_map/ppermute | solution.py:36
  138.8 16.2 %collective-permute-start.22 = (bf16[1024,256]{1,0:T(8,128)(2,1)S(1)}, bf16[1024,256]{1,0:T(8,128)(2,1)S(1)}, u32[]{:S(2)}, u32[]{:S(2)}) collective-permute-start(bf16[1024,256]{1,0:T(8,128)(2,1)S(1)} %shard_map.123), channel_id=1, source_target_pairs={{4,0},{8,12},{5,1},{9,13},{6,2},{10,14},{7,3},{11,15},{20,16},{24,... | collective-permute-start | bytes 1572872 | tf_op jit(solution)/shard_map/ppermute | solution.py:40
  140.1 26.4 %collective-permute-start.26 = (bf16[1024,512]{1,0:T(8,128)(2,1)}, bf16[1024,512]{1,0:T(8,128)(2,1)}, u32[]{:S(2)}, u32[]{:S(2)}) collective-permute-start(bf16[1024,512]{1,0:T(8,128)(2,1)} %shard_map.122), channel_id=1, source_target_pairs={{4,8},{8,4},{5,9},{9,5},{6,10},{10,6},{7,11},{11,7},{20,24},{24,20... | collective-permute-start | bytes 3145736 | tf_op jit(solution)/shard_map/ppermute | solution.py:40
  147.7 36.9 %collective-permute-start.24 = (bf16[1024,512]{1,0:T(8,128)(2,1)}, bf16[1024,512]{1,0:T(8,128)(2,1)}, u32[]{:S(2)}, u32[]{:S(2)}) collective-permute-start(bf16[1024,512]{1,0:T(8,128)(2,1)} %shard_map.124.far), channel_id=1, source_target_pairs={{0,16},{16,0},{1,17},{17,1},{2,18},{18,2},{3,19},{19,3},{4,20},{20... | collective-permute-start | bytes 3145736 | tf_op jit(solution)/shard_map/ppermute | solution.py:36
  160.2 30.9 %all-to-all-start.1 = ((bf16[4,2,128,256]{3,2,1,0:T(8,128)(2,1)}), bf16[4,2,128,256]{3,2,1,0:T(8,128)(2,1)}, u32[]{:S(2)}, u32[]{:S(2)}) async-start(bf16[4,2,128,256]{3,2,1,0:T(8,128)(2,1)} %bitcast.25), calls=%async_computation.1 | async-start | bytes 1048576 | tf_op jit(solution)/shard_map/all_to_all | solution.py:600
  164.4 26.0 %collective-permute-start.23 = (bf16[256,1024]{1,0:T(8,128)(2,1)}, bf16[256,1024]{1,0:T(8,128)(2,1)S(1)}, u32[]{:S(2)}, u32[]{:S(2)}) collective-permute-start(bf16[256,1024]{1,0:T(8,128)(2,1)} %copy-done.56), channel_id=1, source_target_pairs={{0,2},{2,0},{1,3},{3,1},{4,6},{6,4},{5,7},{7,5},{8,10},{10,8},{9,1... | collective-permute-start | bytes 1572872 | tf_op jit(solution)/shard_map/ppermute | solution.py:36
  165.1 18.8 %collective-permute-start.25 = (bf16[1024,128]{1,0:T(8,128)(2,1)}, bf16[1024,128]{1,0:T(8,128)(2,1)S(1)}, u32[]{:S(2)}, u32[]{:S(2)}) collective-permute-start(bf16[1024,128]{1,0:T(8,128)(2,1)} %copy-done.59), channel_id=1, source_target_pairs={{0,2},{2,0},{1,3},{3,1},{4,6},{6,4},{5,7},{7,5},{8,10},{10,8},{9,1... | collective-permute-start | bytes 786440 | tf_op jit(solution)/shard_map/ppermute | solution.py:36
  200.3 18.4 %collective-permute-start.27 = (f32[2,512,256]{2,1,0:T(8,128)S(1)}, f32[2,512,256]{2,1,0:T(8,128)S(1)}, u32[]{:S(2)}, u32[]{:S(2)}) collective-permute-start(f32[2,512,256]{2,1,0:T(8,128)S(1)} %get-tuple-element.128), channel_id=1, source_target_pairs={{0,1},{1,0},{2,3},{3,2},{4,5},{5,4},{6,7},{7,6},{8,9},{9,8},{10,11... | collective-permute-start | bytes 3145736 | tf_op jit(solution)/shard_map/ppermute | solution.py:36
  200.4 16.2 %collective-permute-start.28 = (bf16[1024,256]{1,0:T(8,128)(2,1)S(1)}, bf16[1024,256]{1,0:T(8,128)(2,1)S(1)}, u32[]{:S(2)}, u32[]{:S(2)}) collective-permute-start(bf16[1024,256]{1,0:T(8,128)(2,1)S(1)} %copy-done.45), channel_id=1, source_target_pairs={{4,0},{8,12},{5,1},{9,13},{6,2},{10,14},{7,3},{11,15},{20,16},{24,... | collective-permute-start | bytes 1572872 | tf_op jit(solution)/shard_map/ppermute | solution.py:40
  201.7 20.4 %collective-permute-start.30 = (bf16[256,1024]{1,0:T(8,128)(2,1)S(1)}, bf16[256,1024]{1,0:T(8,128)(2,1)S(1)}, u32[]{:S(2)}, u32[]{:S(2)}) collective-permute-start(bf16[256,1024]{1,0:T(8,128)(2,1)S(1)} %copy-done.58), channel_id=1, source_target_pairs={{0,2},{2,0},{1,3},{3,1},{4,6},{6,4},{5,7},{7,5},{8,10},{10,8},{9,1... | collective-permute-start | bytes 1572872 | tf_op jit(solution)/shard_map/ppermute | solution.py:36
  220.0 13.7 %collective-permute-start.31 = (bf16[1024,128]{1,0:T(8,128)(2,1)S(1)}, bf16[1024,128]{1,0:T(8,128)(2,1)S(1)}, u32[]{:S(2)}, u32[]{:S(2)}) collective-permute-start(bf16[1024,128]{1,0:T(8,128)(2,1)S(1)} %get-tuple-element.140), channel_id=1, source_target_pairs={{0,2},{2,0},{1,3},{3,1},{4,6},{6,4},{5,7},{7,5},{8,10},{10,8},{9,1... | collective-permute-start | bytes 786440 | tf_op jit(solution)/shard_map/ppermute | solution.py:36
  221.5 13.8 %collective-permute-start.32 = (bf16[128,256]{1,0:T(8,128)(2,1)S(1)}, bf16[128,256]{1,0:T(8,128)(2,1)S(1)}, u32[]{:S(2)}, u32[]{:S(2)}) collective-permute-start(bf16[128,256]{1,0:T(8,128)(2,1)S(1)} %get-tuple-element.124), channel_id=1, source_target_pairs={{0,2},{2,0},{1,3},{3,1},{4,6},{6,4},{5,7},{7,5},{8,10},{10,8},{9,1... | collective-permute-start | bytes 196616 | tf_op jit(solution)/shard_map/ppermute | solution.py:36
  (72 other events, 644.5 us)

commit v9 on v8

--- a/solution.py
+++ b/solution.py
@@ -129,7 +129,7 @@
 
 def back_end_kernel(numbers, ids, part, got, wide, sent):
     token = ids[...].astype(f32)
-    count = numbers.shape[0] // 2
+    count = numbers.shape[0] // 3
     ranks, order = [numbers[i] for i in range(count)], [numbers[count + i] for i in range(count)]
     value, scale = kept(token, jnp.stack(ranks), part[...] + roll_rows(got[...]))
     value = (scale * value).astype(bf16)
@@ -141,7 +141,7 @@
 
 def spread_in_kernel(numbers, packet, wide):
     size = packet.shape[1] // 2
-    count = numbers.shape[0] // 2
+    count = numbers.shape[0] // 3
     order = [numbers[count + i] for i in range(count)]
     spread_into(wide, packet[:, size:].astype(f32), packet[:, :size].astype(f32), order)
 
@@ -160,20 +160,30 @@
     for i in range(4):
         both = matmul(x_mine[...], mine[i]) + matmul(x_other[...], other[i])
         for j in (0, 1):
-            place = numbers[numbers.shape[0] // 2 + 2 * i + j].astype(f32)
+            place = numbers[numbers.shape[0] // 3 + 2 * i + j].astype(f32)
             part = jnp.where(token == place, both[:, j * size : (j + 1) * size], 0.0)
             out[...] = part if i + j == 0 else out[...] + part
 
 
-def low_end_kernel(numbers, ids, part, got, up, dy, wide, delta, grad):
+def low_end_kernel(numbers, ids, part, got, up, dy, delta, *grads):
     token = ids[...].astype(f32)
-    count = numbers.shape[0] // 2
+    count = numbers.shape[0] // 3
+    size = part.shape[1]
     ranks = jnp.stack([numbers[i] for i in range(count)])
     value, scale = kept(token, ranks, part[...] + roll_rows(got[...]))
     value = value.astype(bf16).astype(f32)
-    spread_into(wide, token, value, [jnp.int32(i) for i in range(count)])
-    grad[...] = contract_first(wide[...], dy[...]).astype(bf16)
-    delta[...] = (scale[:, :1] * matmul(wide[...], up[...])).astype(bf16)
+
+    def pair(first, second):
+        return jnp.concatenate(
+            [jnp.where(token == a, value, 0.0) for a in (first, second)], axis=1
+        ).astype(bf16)
+
+    total = 0.0
+    for i, out in enumerate(grads):
+        places = [numbers[2 * count + 2 * i + j].astype(f32) for j in (0, 1)]
+        out[...] = contract_first(pair(*places), dy[...]).astype(bf16)
+        total += matmul(pair(2 * i, 2 * i + 1), up[2 * i * size : 2 * (i + 1) * size, :])
+    delta[...] = (scale[:, :1] * total).astype(bf16)
 
 
 def to_middle_kernel(x_here, back, x_in, back_in, out):
@@ -250,16 +260,16 @@
         out[...] = outer[...]
 
 
-def up_sum_kernel(numbers, got, here, there):
-    count = numbers.shape[0] // 2
+def up_sum_kernel(numbers, first, second, third, fourth, here, there):
+    count = numbers.shape[0] // 3
+    size = here.shape[0]
     for i, out in enumerate((here, there)):
         adapter = numbers[count + i]
         rank = jnp.float32(1.0)
         for a in range(count):
             rank = jnp.where(adapter == a, numbers[a].astype(f32), rank)
-        part = got[0, adapter % 2].astype(f32)
-        for source in range(1, got.shape[0]):
-            part += got[source, adapter % 2].astype(f32)
+        span = slice(i * size, (i + 1) * size)
+        part = sum(v[span, :].astype(f32) for v in (first, second, third, fourth))
         out[...] = (jnp.full(part.shape, 16.0, f32) / rank * part).astype(bf16)
 
 
@@ -361,7 +371,8 @@
         [side * quarter + half * eighth for side in (x, 1 - x) for half in (y, 1 - y)]
     ).astype(jnp.int32)
     ranks = size // 8 * rank_step_count
-    numbers = jnp.concatenate([ranks, adapters])
+    ring = jnp.stack([2 * ((z + k) % 4) + o for k in range(4) for o in (x, 1 - x)])
+    numbers = jnp.concatenate([ranks, adapters, ring.astype(jnp.int32)])
     flags = jnp.stack([(c == 0) == first_pair, z % 2 == 1, z >= 2, x == 1, is_middle])
     flags = flags.astype(jnp.int32)
     places = jnp.stack([*line, c]).astype(jnp.int32)
@@ -379,6 +390,9 @@
 
     def like(*shape, kind=bf16):
         return jax.ShapeDtypeStruct(shape, kind)
+
+    def around(value, shift):
+        return along(value, [(i, (i + shift) % 4) for i in range(4)])
 
     def rows_at(i, value, length):
         out = like(length, value.shape[1])
@@ -423,7 +437,11 @@
             got,
         )[0]
 
-    down_got = swap(done(rows_at(2, down, eighth)), "own")
+    up_sent = kernel_call(up_sent_kernel, [like(number, size, kvq)], up)[0]
+    up_all = lax.all_to_all(
+        done(up_sent), ("fsdp", "own"), split_axis=0, concat_axis=0, tiled=True
+    ).reshape(number * size, kvq)
+    down_got = swap(done(rows_at(2, step(down), eighth)), "own")
     packet_here = done(
         kernel_call(packet_kernel, [like(rows, kv + size)], step(cotangent), token_adapter)[0]
     )
@@ -441,24 +459,19 @@
         )[0]
     )
     down_near = along(down_piece, NEIGHBOURS)
-    up, packet = step(up, packet)
-    up_sent = kernel_call(up_sent_kernel, [like(number, size, kvq)], up)[0]
-    up_all = lax.all_to_all(
-        done(up_sent), ("fsdp", "own"), split_axis=0, concat_axis=0, tiled=True
-    ).reshape(number * size, kvq)
     x_got = [swap(done(columns_at(2, step(tokens))), "own")]
     weight_here = done(rows_at(0, step(frozen_value_weight), eighth))
     weight_near = along(weight_here, NEIGHBOURS)
     dy_half, ids, dy_quarter = kernel_call(
         unpack_kernel,
         [like(both, kv), like(both, size), like(both, kvq)],
-        step(packet_here),
-        packet,
+        packet_here,
+        step(packet),
         scalars=flags,
     )
     done(dy_quarter)
-
-    crossing = done(side_by_side(down_piece, step(down_near)))
+    down_near, x_got[0] = step(down_near, x_got[0])
+    crossing = done(side_by_side(down_piece, down_near))
     down_crossed = along(crossing, MIDDLE)
     down_other = swap(crossing, "rep")
     x_mine = done(tokens_of(0, tokens, step(x_got[0])))
@@ -467,10 +480,10 @@
     up_all = step(up_all)
     back_part = done(kernel_call(back_kernel, [compact], ids, dy_quarter, up_all)[0])
     back_tp = swap(back_part, "tp")
+    back_part = done(kernel_call(add_kernel, [compact], back_part, step(back_tp))[0])
+    back_got = swap(back_part, "own")
     crossing = done(side_by_side(weight_here, step(weight_near)))
     weight_crossed = along(crossing, MIDDLE)
-    back_part = done(kernel_call(add_kernel, [compact], back_part, step(back_tp))[0])
-    back_got = swap(back_part, "own")
     sent, down_other = step(frozen_value_weight, down_other)
     weight_other = done(rows_at(1, sent, eighth))
     weight_near_other = swap(step(weight_near), "rep")
@@ -522,7 +535,7 @@
             crossed,
             outer,
         )
-        return done(here), swap(there, "own")
+        return done(here), there
 
     def far_of(crossed, outer):
         out = like(*crossed.shape)
@@ -547,7 +560,7 @@
     weight_far = done(far_of(weight_crossed, step(weight_outer)))
     weight_far_other = swap(weight_far, "rep")
     half_grad = [like(rows, eighth)] * 2
-    dx_mine, dx_mine_sent = kernel_call(
+    dx_mine, dx_sent = kernel_call(
         dx_kernel,
         half_grad,
         step(dy_line),
@@ -559,7 +572,7 @@
         down_near,
         down_far,
     )
-    done(dx_mine)
+    dx_mine_got = swap(done(dx_sent), "own")
 
     low_part = done(
         kernel_call(
@@ -577,19 +590,21 @@
         )[0]
     )
     low_tp = swap(low_part, "tp")
+    grad_here, grad_sent = finish(0, middle[0], outward[0])
     blocks = [like(2, both, cols, kind=f32)] * 2
     y_first = kernel_call(
         y_kernel, blocks, step(x_mine), weight_here, weight_near, weight_far, scalars=flags
     )
     done(y_first[0])
-    low_part = done(kernel_call(add_kernel, [compact], low_part, step(low_tp))[0])
+    low_tp, dx_mine_got = step(low_tp, dx_mine_got)
+    low_part = done(kernel_call(add_kernel, [compact], low_part, low_tp)[0])
     low_got = swap(low_part, "own")
-    grads = [finish(0, middle[0], outward[0])]
+    outward.append(to_end(1, middle[1]))
     low_got = step(low_got)
-    dx_mine_got = swap(step(dx_mine_sent, low_got)[0], "own")
-    _, delta, up_part = kernel_call(
+    grad_got = swap(lax.optimization_barrier((grad_sent, low_got))[0], "own")
+    delta, *up_parts = kernel_call(
         low_end_kernel,
-        [like(both, number * size), like(both, kvq), like(number * size, kvq)],
+        [like(both, kvq)] + [like(wide, kvq)] * 4,
         ids,
         low_part,
         low_got,
@@ -597,11 +612,8 @@
         dy_quarter,
         scalars=numbers,
     )
-    up_got = lax.all_to_all(
-        done(up_part).reshape(4, 2, size, kvq), "fsdp", split_axis=0, concat_axis=0, tiled=True
-    )
-    outward.append(to_end(1, middle[1]))
-    weight_far_other, grad_got = step(weight_far_other, grads[0][1])
+    done(delta)
+    up_got = [around(up_parts[k], k) for k in (1, 2, 3)]
     dx_other, dx_sent = kernel_call(
         dx_kernel,
         half_grad,
@@ -609,14 +621,16 @@
         back_wide,
         weight_other,
         weight_near_other,
-        weight_far_other,
+        step(weight_far_other),
         down_other,
         down_far_other,
     )
     dx_other_got = swap(done(dx_sent), "own")
-    up_got, dx_mine_got = step(up_got, dx_mine_got)
+    grad_last, grad_sent = finish(1, middle[1], outward[1])
+    grad_last_got = swap(grad_sent, "own")
+    up_got = step(*up_got)
     up_mine, up_theirs = kernel_call(
-        up_sum_kernel, [like(size, kvq)] * 2, up_got, scalars=numbers
+        up_sum_kernel, [like(size, kvq)] * 2, up_parts[0], *up_got, scalars=numbers
     )
     up_theirs = swap(done(up_theirs), "own")
     y_keep, y_sent = kernel_call(
@@ -630,7 +644,6 @@
         scalars=flags,
     )
     y_got = swap(done(y_sent), "tp")
-    grads.append(finish(1, middle[1], outward[1]))
     y_here, y_sent = kernel_call(
         y_sum_kernel,
         [like(2, rows, cols, kind=f32), like(2, rows, cols)],
@@ -657,7 +670,7 @@
     projected = done(kernel_call(y_end_kernel, [like(rows, kv)], y_here, step(y_got))[0])
     down_gradient = done(
         in_place(
-            0, like(width, size), grads[0][0], grads[1][0], grad_got, step(grads[1][1])
+            0, like(width, size), grad_here, grad_last, grad_got, step(grad_last_got)
         )[None]
     )
     up_gradient = kernel_call(

time: 238 us -> 228 us (0.958)
  Pallas kernels: 61.6 us -> 56.2 us
  local copies, waits for them, and re-layouts: 20.3 us -> 16.6 us
    ppermute x13 -> x16, waiting for transfers between devices: 49 us -> 35.1 us  [along(): return lax.ppermute(value, 'fsdp', pairs)]
    ppermute x20, waiting for transfers between devices: 45.4 us -> 58.7 us  [swap(): return lax.ppermute(value, axis, PAIR)]
    pallas_call x39, Pallas kernels: 61.6 us -> 56.2 us  [kernel_call(): pl.pallas_call(body, out_shape=list(outs), in_specs=specs, out_specs=[pl....]
    all_to_all x1 -> x0, starting transfers between devices: 4.14 us -> none  [body_line(): lax.all_to_all(done(up_part).reshape(4, 2, size, kvq), 'fsdp', split_axis...]
    unnamed x123 -> x63, local copies, waits for them, and re-layouts: 20 us -> 16.3 us
    ppermute x20, starting transfers between devices: 19.3 us -> 22.2 us  [swap(): return lax.ppermute(value, axis, PAIR)]
    ppermute x13 -> x16, starting transfers between devices: 30.3 us -> 32 us  [along(): return lax.ppermute(value, 'fsdp', pairs)]
  transfers between devices with their start and end apart: 35 -> 37, of which waited for: 14 -> 19; matrix products, arithmetic and copies ran while one was open for 0% -> 0% of each run, Pallas kernels for 21% -> 21%
where the time goes in v9:
time: 228 us; the launch traced here: 227 us
  waiting for transfers between devices  93.8 us (41%)
  starting transfers between devices  59.1 us (26%)
  Pallas kernels  56.2 us (25%)
  local copies, waits for them, and re-layouts  16.6 us (7%)
    ppermute x20, waiting for transfers between devices, swap(): return lax.ppermute(value, axis, PAIR)  58.7 us
    pallas_call x39, Pallas kernels, kernel_call(): pl.pallas_call(body, out_shape=list(outs), in_specs=specs, out_specs=[pl....  56.2 us
    ppermute x16, waiting for transfers between devices, along(): return lax.ppermute(value, 'fsdp', pairs)  35.1 us
    ppermute x16, starting transfers between devices, along(): return lax.ppermute(value, 'fsdp', pairs)  32 us
    ppermute x20, starting transfers between devices, swap(): return lax.ppermute(value, axis, PAIR)  22.2 us
    unnamed x63, local copies, waits for them, and re-layouts  16.3 us
    all_to_all x1, starting transfers between devices, body_line(): lax.all_to_all(done(up_sent), ('fsdp', 'own'), split_axis=0, concat_axis=...  4.92 us
  transfers between devices with their start and end apart: 37, of which 19 were waited for; matrix products, arithmetic and copies ran while one was open for 0% of the time, Pallas kernels for 21%

profile of v9, /device:TPU:0, one launch (start us, length us, event | category | flops | bytes accessed | tf_op | source)
XLA Modules:
  0.0 227.1 jit_solution(8818112824890968001)
XLA Ops:
  4.5 3.0 %collective-permute-start = (bf16[1024,128]{1,0:T(8,128)(2,1)S(1)}, bf16[1024,128]{1,0:T(8,128)(2,1)S(1)}, u32[]{:S(2)}, u32[]{:S(2)}) collective-permute-start(bf16[1024,128]{1,0:T(8,128)(2,1)S(1)} %shard_map.103), channel_id=1, source_target_pairs={{0,2},{2,0},{1,3},{3,1},{4,6},{6,4},{5,7},{7,5},{8,10},{10,8},{9,1... | collective-permute-start | bytes 786440 | tf_op jit(solution)/shard_map/ppermute | solution.py:36
  8.4 5.4 %collective-permute-done.refs_1_ = bf16[1024,128]{1,0:T(8,128)(2,1)S(1)} collective-permute-done((bf16[1024,128]{1,0:T(8,128)(2,1)S(1)}, bf16[1024,128]{1,0:T(8,128)(2,1)S(1)}, u32[]{:S(2)}, u32[]{:S(2)}) %collective-permute-start) | collective-permute-done | bytes 262176 | tf_op jit(solution)/shard_map/ppermute | solution.py:36
  22.6 4.9 %all-to-all-start = ((bf16[8,128,256]{2,1,0:T(8,128)(2,1)}), bf16[8,128,256]{2,1,0:T(8,128)(2,1)S(1)}, u32[]{:S(2)}, u32[]{:S(2)}) async-start(bf16[8,128,256]{2,1,0:T(8,128)(2,1)} %shard_map.102), calls=%async_computation | async-start | bytes 1048576 | tf_op jit(solution)/shard_map/all_to_all | solution.py:441
  29.9 14.2 %collective-permute-done.4.there = bf16[256,640]{1,0:T(8,128)(2,1)S(1)} collective-permute-done((bf16[256,640]{1,0:T(8,128)(2,1)S(1)}, bf16[256,640]{1,0:T(8,128)(2,1)S(1)}, u32[]{:S(2)}, u32[]{:S(2)}) %collective-permute-start.4) | collective-permute-done | bytes 327712 | tf_op jit(solution)/shard_map/ppermute | solution.py:36
  56.6 3.8 %collective-permute-done.1.refs_1_.near = bf16[1024,256]{1,0:T(8,128)(2,1)} collective-permute-done((bf16[1024,256]{1,0:T(8,128)(2,1)S(1)}, bf16[1024,256]{1,0:T(8,128)(2,1)}, u32[]{:S(2)}, u32[]{:S(2)}) %collective-permute-start.1) | collective-permute-done | bytes 524320 | tf_op jit(solution)/shard_map/ppermute | solution.py:40
  63.0 7.4 %collective-permute-done.5.own_near_other.rest_0_ = bf16[1024,512]{1,0:T(8,128)(2,1)} collective-permute-done((bf16[1024,512]{1,0:T(8,128)(2,1)}, bf16[1024,512]{1,0:T(8,128)(2,1)}, u32[]{:S(2)}, u32[]{:S(2)}) %collective-permute-start.5) | collective-permute-done | bytes 1048608 | tf_op jit(solution)/shard_map/ppermute | solution.py:36
  75.2 3.8 %collective-permute-start.11 = (bf16[512,1024]{1,0:T(8,128)(2,1)S(1)}, bf16[512,1024]{1,0:T(8,128)(2,1)}, u32[]{:S(2)}, u32[]{:S(2)}) collective-permute-start(bf16[512,1024]{1,0:T(8,128)(2,1)S(1)} %shard_map.110.x_here.x_mine.tokens), channel_id=1, source_target_pairs={{0,4},{12,8},{1,5},{13,9},{2,6},{14,10},{3,7},{15,11},{16,20},{28,... | collective-permute-start | bytes 3145736 | tf_op jit(solution)/shard_map/ppermute | solution.py:40
  89.6 5.4 %collective-permute-start.12 = (bf16[512,256]{1,0:T(8,128)(2,1)}, bf16[512,256]{1,0:T(8,128)(2,1)S(1)}, u32[]{:S(2)}, u32[]{:S(2)}) collective-permute-start(bf16[512,256]{1,0:T(8,128)(2,1)} %get-tuple-element.95), channel_id=1, source_target_pairs={{0,4},{12,8},{1,5},{13,9},{2,6},{14,10},{3,7},{15,11},{16,20},{28,... | collective-permute-start | bytes 786440 | tf_op jit(solution)/shard_map/ppermute | solution.py:40
  106.9 4.3 %collective-permute-start.19 = (bf16[512,1024]{1,0:T(8,128)(2,1)S(1)}, bf16[512,1024]{1,0:T(8,128)(2,1)S(1)}, u32[]{:S(2)}, u32[]{:S(2)}) collective-permute-start(bf16[512,1024]{1,0:T(8,128)(2,1)S(1)} %shard_map.120.x_here.x_other.tokens), channel_id=1, source_target_pairs={{0,4},{12,8},{1,5},{13,9},{2,6},{14,10},{3,7},{15,11},{16,20},{28,... | collective-permute-start | bytes 3145736 | tf_op jit(solution)/shard_map/ppermute | solution.py:40
  113.3 10.8 %collective-permute-done.14.outer = bf16[1024,512]{1,0:T(8,128)(2,1)} collective-permute-done((bf16[1024,512]{1,0:T(8,128)(2,1)}, bf16[1024,512]{1,0:T(8,128)(2,1)}, u32[]{:S(2)}, u32[]{:S(2)}) %collective-permute-start.14) | collective-permute-done | bytes 1048608 | tf_op jit(solution)/shard_map/ppermute | solution.py:40
  126.7 6.6 %collective-permute-done.19.x_in = bf16[512,1024]{1,0:T(8,128)(2,1)S(1)} collective-permute-done((bf16[512,1024]{1,0:T(8,128)(2,1)S(1)}, bf16[512,1024]{1,0:T(8,128)(2,1)S(1)}, u32[]{:S(2)}, u32[]{:S(2)}) %collective-permute-start.19) | collective-permute-done | bytes 1048608 | tf_op jit(solution)/shard_map/ppermute | solution.py:40
  137.3 9.2 %collective-permute-done.17.outer = bf16[1024,512]{1,0:T(8,128)(2,1)S(1)} collective-permute-done((bf16[1024,512]{1,0:T(8,128)(2,1)}, bf16[1024,512]{1,0:T(8,128)(2,1)S(1)}, u32[]{:S(2)}, u32[]{:S(2)}) %collective-permute-start.17) | collective-permute-done | bytes 1048608 | tf_op jit(solution)/shard_map/ppermute | solution.py:40
  148.0 3.4 %shard_map.125 = (bf16[256,1024]{1,0:T(8,128)(2,1)S(1)}, bf16[256,1024]{1,0:T(8,128)(2,1)S(1)}) custom-call(bf16[512,1024]{1,0:T(8,128)(2,1)S(1)} %shard_map.117.dy, bf16[512,1024]{1,0:T(8,128)(2,1)S(1)} %get-tuple-element.98.back, bf16[1024,256]{1,0:T(8,128)(2,1)S(1)} %shard_map.107.refs_0_.own, bf16[1024,256]{1,0:T(8,128)(2,1)} %collective-permute-done.1.refs_1_.near, ...), custom_call_target="tpu_custom_call" | custom-call | tf_op jit(solution)/shard_map/pallas_call | solution.py:48
  153.0 3.6 %shard_map.126.left = f32[512,128]{1,0:T(8,128)S(1)} custom-call(s32[24]{0:T(128)S(1)} %concatenate.3.numbers, bf16[512,128]{1,0:T(8,128)(2,1)S(1)} %get-tuple-element.86.ids, bf16[512,1024]{1,0:T(8,128)(2,1)S(1)} %shard_map.110.x_here.x_mine.tokens, bf16[512,1024]{1,0:T(8,128)(2,1)S(1)} %shard_map.120.x_here.x_other.tokens, ...), custom_call_target="tpu_custom_call" | custom-call | tf_op jit(solution)/shard_map/pallas_call | solution.py:48
  158.7 3.9 %shard_map.128 = (f32[2,512,256]{2,1,0:T(8,128)S(1)}, f32[2,512,256]{2,1,0:T(8,128)S(1)}) custom-call(s32[5]{0:T(128)S(1)} %convert_element_type.3.flags, bf16[512,1024]{1,0:T(8,128)(2,1)S(1)} %shard_map.110.x_here.x_mine.tokens, bf16[1024,256]{1,0:T(8,128)(2,1)S(1)} %shard_map.107.refs_0_.own, bf16[1024,256]{1,0:T(8,128)(2,1)} %collective-permute-done.1.refs_1_.near, ...), custom_call_target="tpu_custom_call" | custom-call | tf_op jit(solution)/shard_map/pallas_call | solution.py:48
  166.1 7.2 %collective-permute-done.23.got = f32[512,128]{1,0:T(8,128)S(1)} collective-permute-done((f32[512,128]{1,0:T(8,128)S(1)}, f32[512,128]{1,0:T(8,128)S(1)}, u32[]{:S(2)}, u32[]{:S(2)}) %collective-permute-start.23) | collective-permute-done | bytes 262176 | tf_op jit(solution)/shard_map/ppermute | solution.py:36
  177.3 2.8 %collective-permute-start.27 = (bf16[256,256]{1,0:T(8,128)(2,1)S(1)}, bf16[256,256]{1,0:T(8,128)(2,1)S(1)}, u32[]{:S(2)}, u32[]{:S(2)}) collective-permute-start(bf16[256,256]{1,0:T(8,128)(2,1)S(1)} %get-tuple-element.123), channel_id=1, source_target_pairs={{0,12},{4,0},{8,4},{12,8},{1,13},{5,1},{9,5},{13,9},{2,14},{6,2},{... | collective-permute-start | bytes 393224 | tf_op jit(solution)/shard_map/ppermute | solution.py:40
  180.1 3.8 %shard_map.132 = (bf16[256,1024]{1,0:T(8,128)(2,1)S(1)}, bf16[256,1024]{1,0:T(8,128)(2,1)S(1)}) custom-call(bf16[512,1024]{1,0:T(8,128)(2,1)S(1)} %shard_map.117.dy, bf16[512,1024]{1,0:T(8,128)(2,1)S(1)} %get-tuple-element.98.back, bf16[1024,256]{1,0:T(8,128)(2,1)S(1)} %copy-done.11, bf16[1024,256]{1,0:T(8,128)(2,1)} %collective-permute-done.7.near, ...), custom_call_target="tpu_custom_call" | custom-call | tf_op jit(solution)/shard_map/pallas_call | solution.py:48
  184.8 2.7 %collective-permute-done.26.third = bf16[256,256]{1,0:T(8,128)(2,1)S(1)} collective-permute-done((bf16[256,256]{1,0:T(8,128)(2,1)S(1)}, bf16[256,256]{1,0:T(8,128)(2,1)S(1)}, u32[]{:S(2)}, u32[]{:S(2)}) %collective-permute-start.26) | collective-permute-done | bytes 131104 | tf_op jit(solution)/shard_map/ppermute | solution.py:40
  188.5 4.0 %shard_map.135 = (f32[2,512,256]{2,1,0:T(8,128)S(1)}, f32[2,512,256]{2,1,0:T(8,128)S(1)}) custom-call(s32[5]{0:T(128)S(1)} %convert_element_type.3.flags, bf16[512,1024]{1,0:T(8,128)(2,1)S(1)} %shard_map.120.x_here.x_other.tokens, bf16[1024,256]{1,0:T(8,128)(2,1)S(1)} %copy-done.11, bf16[1024,256]{1,0:T(8,128)(2,1)} %collective-permute-done.7.near, ...), custom_call_target="tpu_custom_call" | custom-call | tf_op jit(solution)/shard_map/pallas_call | solution.py:48
  200.1 7.3 %collective-permute-done.32.refs_3_ = bf16[256,1024]{1,0:T(8,128)(2,1)S(1)} collective-permute-done((bf16[256,1024]{1,0:T(8,128)(2,1)S(1)}, bf16[256,1024]{1,0:T(8,128)(2,1)S(1)}, u32[]{:S(2)}, u32[]{:S(2)}) %collective-permute-start.32) | collective-permute-done | bytes 524320 | tf_op jit(solution)/shard_map/ppermute | solution.py:36
  209.5 3.5 %collective-permute-done.31.got = bf16[2,256,256]{2,1,0:T(8,128)(2,1)S(1)} collective-permute-done((bf16[2,256,256]{2,1,0:T(8,128)(2,1)S(1)}, bf16[2,256,256]{2,1,0:T(8,128)(2,1)S(1)}, u32[]{:S(2)}, u32[]{:S(2)}) %collective-permute-start.31) | collective-permute-done | bytes 262176 | tf_op jit(solution)/shard_map/ppermute | solution.py:36
  213.8 4.9 %collective-permute-done.34.refs_3_ = bf16[1024,128]{1,0:T(8,128)(2,1)S(1)} collective-permute-done((bf16[1024,128]{1,0:T(8,128)(2,1)S(1)}, bf16[1024,128]{1,0:T(8,128)(2,1)S(1)}, u32[]{:S(2)}, u32[]{:S(2)}) %collective-permute-start.34) | collective-permute-done | bytes 262176 | tf_op jit(solution)/shard_map/ppermute | solution.py:36
  218.6 5.6 %collective-permute-done.33.refs_2_ = bf16[1024,128]{1,0:T(8,128)(2,1)S(1)} collective-permute-done((bf16[1024,128]{1,0:T(8,128)(2,1)S(1)}, bf16[1024,128]{1,0:T(8,128)(2,1)S(1)}, u32[]{:S(2)}, u32[]{:S(2)}) %collective-permute-start.33) | collective-permute-done | bytes 262176 | tf_op jit(solution)/shard_map/ppermute | solution.py:36
  (158 shorter events, 94.2 us)
Async XLA Ops:
  18.7 27.7 %collective-permute-start.3 = (bf16[256,1024]{1,0:T(8,128)(2,1)}, bf16[256,1024]{1,0:T(8,128)(2,1)}, u32[]{:S(2)}, u32[]{:S(2)}) collective-permute-start(bf16[256,1024]{1,0:T(8,128)(2,1)} %shard_map.106), channel_id=1, source_target_pairs={{0,2},{2,0},{1,3},{3,1},{4,6},{6,4},{5,7},{7,5},{8,10},{10,8},{9,1... | collective-permute-start | bytes 1572872 | tf_op jit(solution)/shard_map/ppermute | solution.py:36
  20.5 25.9 %collective-permute-start.2 = (bf16[1024,256]{1,0:T(8,128)(2,1)S(1)}, bf16[1024,256]{1,0:T(8,128)(2,1)S(1)}, u32[]{:S(2)}, u32[]{:S(2)}) collective-permute-start(bf16[1024,256]{1,0:T(8,128)(2,1)S(1)} %shard_map.105.refs_0_.rest_0_.own), channel_id=1, source_target_pairs={{0,4},{4,0},{8,12},{12,8},{1,5},{5,1},{9,13},{13,9},{2,6},{6,2},{1... | collective-permute-start | bytes 1572872 | tf_op jit(solution)/shard_map/ppermute | solution.py:40
  22.1 21.9 %collective-permute-start.4 = (bf16[256,640]{1,0:T(8,128)(2,1)S(1)}, bf16[256,640]{1,0:T(8,128)(2,1)S(1)}, u32[]{:S(2)}, u32[]{:S(2)}) collective-permute-start(bf16[256,640]{1,0:T(8,128)(2,1)S(1)} %shard_map.104.here), channel_id=1, source_target_pairs={{0,2},{2,0},{1,3},{3,1},{4,6},{6,4},{5,7},{7,5},{8,10},{10,8},{9,1... | collective-permute-start | bytes 983048 | tf_op jit(solution)/shard_map/ppermute | solution.py:36
  22.6 31.8 %all-to-all-start = ((bf16[8,128,256]{2,1,0:T(8,128)(2,1)}), bf16[8,128,256]{2,1,0:T(8,128)(2,1)S(1)}, u32[]{:S(2)}, u32[]{:S(2)}) async-start(bf16[8,128,256]{2,1,0:T(8,128)(2,1)} %shard_map.102), calls=%async_computation | async-start | bytes 1048576 | tf_op jit(solution)/shard_map/all_to_all | solution.py:441
  48.1 22.4 %collective-permute-start.5 = (bf16[1024,512]{1,0:T(8,128)(2,1)}, bf16[1024,512]{1,0:T(8,128)(2,1)}, u32[]{:S(2)}, u32[]{:S(2)}) collective-permute-start(bf16[1024,512]{1,0:T(8,128)(2,1)} %shard_map.109), channel_id=1, source_target_pairs={{0,16},{16,0},{1,17},{17,1},{2,18},{18,2},{3,19},{19,3},{4,20},{20... | collective-permute-start | bytes 3145736 | tf_op jit(solution)/shard_map/ppermute | solution.py:36
  51.2 31.7 %collective-permute-start.8 = (bf16[1024,512]{1,0:T(8,128)(2,1)}, bf16[1024,512]{1,0:T(8,128)(2,1)}, u32[]{:S(2)}, u32[]{:S(2)}) collective-permute-start(bf16[1024,512]{1,0:T(8,128)(2,1)} %shard_map.109), channel_id=1, source_target_pairs={{4,8},{8,4},{5,9},{9,5},{6,10},{10,6},{7,11},{11,7},{20,24},{24,20... | collective-permute-start | bytes 3145736 | tf_op jit(solution)/shard_map/ppermute | solution.py:40
  75.2 27.3 %collective-permute-start.11 = (bf16[512,1024]{1,0:T(8,128)(2,1)S(1)}, bf16[512,1024]{1,0:T(8,128)(2,1)}, u32[]{:S(2)}, u32[]{:S(2)}) collective-permute-start(bf16[512,1024]{1,0:T(8,128)(2,1)S(1)} %shard_map.110.x_here.x_mine.tokens), channel_id=1, source_target_pairs={{0,4},{12,8},{1,5},{13,9},{2,6},{14,10},{3,7},{15,11},{16,20},{28,... | collective-permute-start | bytes 3145736 | tf_op jit(solution)/shard_map/ppermute | solution.py:40
  85.9 26.1 %collective-permute-start.15 = (bf16[1024,512]{1,0:T(8,128)(2,1)}, bf16[1024,512]{1,0:T(8,128)(2,1)}, u32[]{:S(2)}, u32[]{:S(2)}) collective-permute-start(bf16[1024,512]{1,0:T(8,128)(2,1)} %shard_map.113), channel_id=1, source_target_pairs={{4,8},{8,4},{5,9},{9,5},{6,10},{10,6},{7,11},{11,7},{20,24},{24,20... | collective-permute-start | bytes 3145736 | tf_op jit(solution)/shard_map/ppermute | solution.py:40
  87.6 17.7 %collective-permute-start.10 = (bf16[256,1024]{1,0:T(8,128)(2,1)}, bf16[256,1024]{1,0:T(8,128)(2,1)}, u32[]{:S(2)}, u32[]{:S(2)}) collective-permute-start(bf16[256,1024]{1,0:T(8,128)(2,1)} %shard_map.116), channel_id=1, source_target_pairs={{0,2},{2,0},{1,3},{3,1},{4,6},{6,4},{5,7},{7,5},{8,10},{10,8},{9,1... | collective-permute-start | bytes 1572872 | tf_op jit(solution)/shard_map/ppermute | solution.py:36
  89.6 12.1 %collective-permute-start.12 = (bf16[512,256]{1,0:T(8,128)(2,1)}, bf16[512,256]{1,0:T(8,128)(2,1)S(1)}, u32[]{:S(2)}, u32[]{:S(2)}) collective-permute-start(bf16[512,256]{1,0:T(8,128)(2,1)} %get-tuple-element.95), channel_id=1, source_target_pairs={{0,4},{12,8},{1,5},{13,9},{2,6},{14,10},{3,7},{15,11},{16,20},{28,... | collective-permute-start | bytes 786440 | tf_op jit(solution)/shard_map/ppermute | solution.py:40
  95.8 28.3 %collective-permute-start.14 = (bf16[1024,512]{1,0:T(8,128)(2,1)}, bf16[1024,512]{1,0:T(8,128)(2,1)}, u32[]{:S(2)}, u32[]{:S(2)}) collective-permute-start(bf16[1024,512]{1,0:T(8,128)(2,1)} %collective-permute-done.8.crossed), channel_id=1, source_target_pairs={{4,0},{8,12},{5,1},{9,13},{6,2},{10,14},{7,3},{11,15},{20,16},{24,... | collective-permute-start | bytes 3145736 | tf_op jit(solution)/shard_map/ppermute | solution.py:40
  106.9 26.4 %collective-permute-start.19 = (bf16[512,1024]{1,0:T(8,128)(2,1)S(1)}, bf16[512,1024]{1,0:T(8,128)(2,1)S(1)}, u32[]{:S(2)}, u32[]{:S(2)}) collective-permute-start(bf16[512,1024]{1,0:T(8,128)(2,1)S(1)} %shard_map.120.x_here.x_other.tokens), channel_id=1, source_target_pairs={{0,4},{12,8},{1,5},{13,9},{2,6},{14,10},{3,7},{15,11},{16,20},{28,... | collective-permute-start | bytes 3145736 | tf_op jit(solution)/shard_map/ppermute | solution.py:40
  111.3 24.1 %collective-permute-start.18 = (bf16[1024,512]{1,0:T(8,128)(2,1)S(1)}, bf16[1024,512]{1,0:T(8,128)(2,1)S(1)}, u32[]{:S(2)}, u32[]{:S(2)}) collective-permute-start(bf16[1024,512]{1,0:T(8,128)(2,1)S(1)} %shard_map.119), channel_id=1, source_target_pairs={{4,8},{8,4},{5,9},{9,5},{6,10},{10,6},{7,11},{11,7},{20,24},{24,20... | collective-permute-start | bytes 3145736 | tf_op jit(solution)/shard_map/ppermute | solution.py:40
  112.0 34.5 %collective-permute-start.17 = (bf16[1024,512]{1,0:T(8,128)(2,1)}, bf16[1024,512]{1,0:T(8,128)(2,1)S(1)}, u32[]{:S(2)}, u32[]{:S(2)}) collective-permute-start(bf16[1024,512]{1,0:T(8,128)(2,1)} %collective-permute-done.15.crossed), channel_id=1, source_target_pairs={{4,0},{8,12},{5,1},{9,13},{6,2},{10,14},{7,3},{11,15},{20,16},{24,... | collective-permute-start | bytes 3145736 | tf_op jit(solution)/shard_map/ppermute | solution.py:40
  125.7 27.2 %collective-permute-start.16 = (bf16[1024,512]{1,0:T(8,128)(2,1)S(1)}, bf16[1024,512]{1,0:T(8,128)(2,1)S(1)}, u32[]{:S(2)}, u32[]{:S(2)}) collective-permute-start(bf16[1024,512]{1,0:T(8,128)(2,1)S(1)} %shard_map.121.rest_2_.far), channel_id=1, source_target_pairs={{0,16},{16,0},{1,17},{17,1},{2,18},{18,2},{3,19},{19,3},{4,20},{20... | collective-permute-start | bytes 3145736 | tf_op jit(solution)/shard_map/ppermute | solution.py:36
  134.6 28.1 %collective-permute-start.24 = (bf16[1024,512]{1,0:T(8,128)(2,1)S(1)}, bf16[1024,512]{1,0:T(8,128)(2,1)S(1)}, u32[]{:S(2)}, u32[]{:S(2)}) collective-permute-start(bf16[1024,512]{1,0:T(8,128)(2,1)S(1)} %shard_map.122), channel_id=1, source_target_pairs={{4,8},{8,4},{5,9},{9,5},{6,10},{10,6},{7,11},{11,7},{20,24},{24,20... | collective-permute-start | bytes 3145736 | tf_op jit(solution)/shard_map/ppermute | solution.py:40
  135.9 20.8 %collective-permute-start.22 = (bf16[1024,256]{1,0:T(8,128)(2,1)S(1)}, bf16[1024,256]{1,0:T(8,128)(2,1)S(1)}, u32[]{:S(2)}, u32[]{:S(2)}) collective-permute-start(bf16[1024,256]{1,0:T(8,128)(2,1)S(1)} %shard_map.123), channel_id=1, source_target_pairs={{4,0},{8,12},{5,1},{9,13},{6,2},{10,14},{7,3},{11,15},{20,16},{24,... | collective-permute-start | bytes 1572872 | tf_op jit(solution)/shard_map/ppermute | solution.py:40
  152.0 28.1 %collective-permute-start.29 = (bf16[1024,512]{1,0:T(8,128)(2,1)S(1)}, bf16[1024,512]{1,0:T(8,128)(2,1)S(1)}, u32[]{:S(2)}, u32[]{:S(2)}) collective-permute-start(bf16[1024,512]{1,0:T(8,128)(2,1)S(1)} %shard_map.124.far), channel_id=1, source_target_pairs={{0,16},{16,0},{1,17},{17,1},{2,18},{18,2},{3,19},{19,3},{4,20},{20... | collective-permute-start | bytes 3145736 | tf_op jit(solution)/shard_map/ppermute | solution.py:36
  163.3 20.7 %collective-permute-start.28 = (bf16[1024,256]{1,0:T(8,128)(2,1)S(1)}, bf16[1024,256]{1,0:T(8,128)(2,1)S(1)}, u32[]{:S(2)}, u32[]{:S(2)}) collective-permute-start(bf16[1024,256]{1,0:T(8,128)(2,1)S(1)} %shard_map.130), channel_id=1, source_target_pairs={{4,0},{8,12},{5,1},{9,13},{6,2},{10,14},{7,3},{11,15},{20,16},{24,... | collective-permute-start | bytes 1572872 | tf_op jit(solution)/shard_map/ppermute | solution.py:40
  192.6 14.8 %collective-permute-start.32 = (bf16[256,1024]{1,0:T(8,128)(2,1)S(1)}, bf16[256,1024]{1,0:T(8,128)(2,1)S(1)}, u32[]{:S(2)}, u32[]{:S(2)}) collective-permute-start(bf16[256,1024]{1,0:T(8,128)(2,1)S(1)} %get-tuple-element.127), channel_id=1, source_target_pairs={{0,2},{2,0},{1,3},{3,1},{4,6},{6,4},{5,7},{7,5},{8,10},{10,8},{9,1... | collective-permute-start | bytes 1572872 | tf_op jit(solution)/shard_map/ppermute | solution.py:36
  196.0 17.0 %collective-permute-start.31 = (bf16[2,256,256]{2,1,0:T(8,128)(2,1)S(1)}, bf16[2,256,256]{2,1,0:T(8,128)(2,1)S(1)}, u32[]{:S(2)}, u32[]{:S(2)}) collective-permute-start(bf16[2,256,256]{2,1,0:T(8,128)(2,1)S(1)} %get-tuple-element.140), channel_id=1, source_target_pairs={{0,2},{2,0},{1,3},{3,1},{4,6},{6,4},{5,7},{7,5},{8,10},{10,8},{9,1... | collective-permute-start | bytes 786440 | tf_op jit(solution)/shard_map/ppermute | solution.py:36
  197.5 21.1 %collective-permute-start.34 = (bf16[1024,128]{1,0:T(8,128)(2,1)S(1)}, bf16[1024,128]{1,0:T(8,128)(2,1)S(1)}, u32[]{:S(2)}, u32[]{:S(2)}) collective-permute-start(bf16[1024,128]{1,0:T(8,128)(2,1)S(1)} %get-tuple-element.148), channel_id=1, source_target_pairs={{0,2},{2,0},{1,3},{3,1},{4,6},{6,4},{5,7},{7,5},{8,10},{10,8},{9,1... | collective-permute-start | bytes 786440 | tf_op jit(solution)/shard_map/ppermute | solution.py:36
  198.0 26.2 %collective-permute-start.33 = (bf16[1024,128]{1,0:T(8,128)(2,1)S(1)}, bf16[1024,128]{1,0:T(8,128)(2,1)S(1)}, u32[]{:S(2)}, u32[]{:S(2)}) collective-permute-start(bf16[1024,128]{1,0:T(8,128)(2,1)S(1)} %get-tuple-element.147), channel_id=1, source_target_pairs={{0,2},{2,0},{1,3},{3,1},{4,6},{6,4},{5,7},{7,5},{8,10},{10,8},{9,1... | collective-permute-start | bytes 786440 | tf_op jit(solution)/shard_map/ppermute | solution.py:36
  199.5 26.3 %collective-permute-start.35 = (bf16[128,256]{1,0:T(8,128)(2,1)S(1)}, bf16[128,256]{1,0:T(8,128)(2,1)S(1)}, u32[]{:S(2)}, u32[]{:S(2)}) collective-permute-start(bf16[128,256]{1,0:T(8,128)(2,1)S(1)} %get-tuple-element.133), channel_id=1, source_target_pairs={{0,2},{2,0},{1,3},{3,1},{4,6},{6,4},{5,7},{7,5},{8,10},{10,8},{9,1... | collective-permute-start | bytes 196616 | tf_op jit(solution)/shard_map/ppermute | solution.py:36
  (44 other events, 334.7 us)

commit v10 on v9

--- a/solution.py
+++ b/solution.py
@@ -446,6 +446,7 @@
         kernel_call(packet_kernel, [like(rows, kv + size)], step(cotangent), token_adapter)[0]
     )
     packet = swap(packet_here, "own")
+    x_got = [swap(done(columns_at(2, step(tokens))), "own")]
     down_piece = done(
         copy_call(
             lambda n, a, o: [
@@ -459,34 +460,27 @@
         )[0]
     )
     down_near = along(down_piece, NEIGHBOURS)
-    x_got = [swap(done(columns_at(2, step(tokens))), "own")]
-    weight_here = done(rows_at(0, step(frozen_value_weight), eighth))
-    weight_near = along(weight_here, NEIGHBOURS)
+    packet, up_all = step(packet, up_all)
     dy_half, ids, dy_quarter = kernel_call(
         unpack_kernel,
         [like(both, kv), like(both, size), like(both, kvq)],
         packet_here,
-        step(packet),
+        packet,
         scalars=flags,
     )
-    done(dy_quarter)
+    compact = like(both, size, kind=f32)
+    back_part = done(kernel_call(back_kernel, [compact], ids, dy_quarter, up_all)[0])
+    back_tp = swap(back_part, "tp")
+    weight_here = done(rows_at(0, step(frozen_value_weight), eighth))
+    weight_near = along(weight_here, NEIGHBOURS)
+    back_part = done(kernel_call(add_kernel, [compact], back_part, step(back_tp))[0])
+    back_got = swap(back_part, "own")
     down_near, x_got[0] = step(down_near, x_got[0])
     crossing = done(side_by_side(down_piece, down_near))
     down_crossed = along(crossing, MIDDLE)
     down_other = swap(crossing, "rep")
     x_mine = done(tokens_of(0, tokens, step(x_got[0])))
     x_in = [along(x_mine, INWARD)]
-    compact = like(both, size, kind=f32)
-    up_all = step(up_all)
-    back_part = done(kernel_call(back_kernel, [compact], ids, dy_quarter, up_all)[0])
-    back_tp = swap(back_part, "tp")
-    back_part = done(kernel_call(add_kernel, [compact], back_part, step(back_tp))[0])
-    back_got = swap(back_part, "own")
-    crossing = done(side_by_side(weight_here, step(weight_near)))
-    weight_crossed = along(crossing, MIDDLE)
-    sent, down_other = step(frozen_value_weight, down_other)
-    weight_other = done(rows_at(1, sent, eighth))
-    weight_near_other = swap(step(weight_near), "rep")
     back_wide, back_sent = kernel_call(
         back_end_kernel,
         [like(both, number * size), like(both, wide)],
@@ -496,14 +490,22 @@
         scalars=numbers,
     )
     back_in = along(done(back_sent), INWARD)
+    crossing = done(side_by_side(weight_here, step(weight_near)))
+    weight_crossed = along(crossing, MIDDLE)
+    back_in_wide = done(
+        kernel_call(
+            spread_in_kernel, [like(both, number * size)], step(back_in), scalars=numbers
+        )[0]
+    )
+    x_got.append(swap(done(columns_at(3, step(tokens))), "own"))
+    weight_other = done(rows_at(1, step(frozen_value_weight), eighth))
     down_crossed = done(step(down_crossed))
     down_outer = along(down_crossed, OUTWARD)
-    sent, weight_near_other = step(tokens, weight_near_other)
-    x_got.append(swap(done(columns_at(3, sent)), "own"))
-    dy_tp = swap(step(dy_half), "tp")
-    dy_line = done(
-        kernel_call(dy_line_kernel, [like(both, 2 * kv)], dy_half, dy_tp, scalars=places)[0]
-    )
+    weight_near, down_other = step(weight_near, down_other)
+    weight_near_other = swap(done(weight_near), "rep")
+    x_other = done(tokens_of(1, tokens, step(x_got[1])))
+    x_in.append(along(x_other, INWARD))
+    x_both = [x_mine, x_other]
 
     def to_middle(half):
         x_in[half] = step(x_in[half])
@@ -541,18 +543,16 @@
         out = like(*crossed.shape)
         return kernel_call(far_kernel, [out], crossed, outer, scalars=flags)[0]
 
-    back_in_wide = done(
-        kernel_call(
-            spread_in_kernel, [like(both, number * size)], step(back_in), scalars=numbers
-        )[0]
-    )
-    x_both = [x_mine]
     middle = [to_middle(0)]
-    x_both.append(done(tokens_of(1, tokens, step(x_got[1]))))
-    x_other = x_both[1]
-    x_in.append(along(x_other, INWARD))
     weight_crossed = done(step(weight_crossed))
     weight_outer = along(weight_crossed, OUTWARD)
+    dy_half, weight_near_other = step(dy_half, weight_near_other)
+    dy_tp = swap(dy_half, "tp")
+    dy_line = done(
+        kernel_call(
+            dy_line_kernel, [like(both, 2 * kv)], dy_half, step(dy_tp), scalars=places
+        )[0]
+    )
     down_far = done(far_of(down_crossed, step(down_outer)))
     down_far_other = swap(down_far, "rep")
     middle.append(to_middle(1))
@@ -591,6 +591,7 @@
     )
     low_tp = swap(low_part, "tp")
     grad_here, grad_sent = finish(0, middle[0], outward[0])
+    grad_got = swap(grad_sent, "own")
     blocks = [like(2, both, cols, kind=f32)] * 2
     y_first = kernel_call(
         y_kernel, blocks, step(x_mine), weight_here, weight_near, weight_far, scalars=flags
@@ -600,8 +601,7 @@
     low_part = done(kernel_call(add_kernel, [compact], low_part, low_tp)[0])
     low_got = swap(low_part, "own")
     outward.append(to_end(1, middle[1]))
-    low_got = step(low_got)
-    grad_got = swap(lax.optimization_barrier((grad_sent, low_got))[0], "own")
+    low_got, grad_got = step(low_got, grad_got)
     delta, *up_parts = kernel_call(
         low_end_kernel,
         [like(both, kvq)] + [like(wide, kvq)] * 4,
@@ -633,10 +633,11 @@
         up_sum_kernel, [like(size, kvq)] * 2, up_parts[0], *up_got, scalars=numbers
     )
     up_theirs = swap(done(up_theirs), "own")
+    x_other, dx_other_got = step(x_other, dx_other_got)
     y_keep, y_sent = kernel_call(
         y_kernel,
         blocks,
-        step(x_other),
+        x_other,
         weight_other,
         weight_near_other,
         weight_far_other,
@@ -644,11 +645,12 @@
         scalars=flags,
     )
     y_got = swap(done(y_sent), "tp")
+    y_got, grad_last_got = step(y_got, grad_last_got)
     y_here, y_sent = kernel_call(
         y_sum_kernel,
         [like(2, rows, cols, kind=f32), like(2, rows, cols)],
         y_keep,
-        step(y_got),
+        y_got,
         delta,
         scalars=flags,
     )

time: 228 us -> 214 us (0.939)
  waiting for transfers between devices: 93.8 us -> 80.6 us
  local copies, waits for them, and re-layouts: 16.6 us -> 8.99 us
  Pallas kernels: 56.2 us -> 61.4 us
    ppermute x20, waiting for transfers between devices: 58.7 us -> 39.8 us  [swap(): return lax.ppermute(value, axis, PAIR)]
    unnamed x63 -> x51, local copies, waits for them, and re-layouts: 16.3 us -> 8.71 us
    ppermute x16, waiting for transfers between devices: 35.1 us -> 40.8 us  [along(): return lax.ppermute(value, 'fsdp', pairs)]
    pallas_call x39, Pallas kernels: 56.2 us -> 61.4 us  [kernel_call(): pl.pallas_call(body, out_shape=list(outs), in_specs=specs, out_specs=[pl....]
    ppermute x20, starting transfers between devices: 22.2 us -> 18.2 us  [swap(): return lax.ppermute(value, axis, PAIR)]
    ppermute x16, starting transfers between devices: 32 us -> 34.9 us  [along(): return lax.ppermute(value, 'fsdp', pairs)]
    all_to_all x1, starting transfers between devices: 4.92 us -> 7.25 us  [body_line(): lax.all_to_all(done(up_sent), ('fsdp', 'own'), split_axis=0, concat_axis=...]
  transfers between devices with their start and end apart: 37 -> 37, of which waited for: 19 -> 17; matrix products, arithmetic and copies ran while one was open for 0% -> 1% of each run, Pallas kernels for 21% -> 26%
where the time goes in v10:
time: 214 us; the launch traced here: 213 us
  waiting for transfers between devices  80.6 us (38%)
  Pallas kernels  61.4 us (29%)
  starting transfers between devices  60.3 us (28%)
  local copies, waits for them, and re-layouts  8.99 us (4%)
    pallas_call x39, Pallas kernels, kernel_call(): pl.pallas_call(body, out_shape=list(outs), in_specs=specs, out_specs=[pl....  61.4 us
    ppermute x16, waiting for transfers between devices, along(): return lax.ppermute(value, 'fsdp', pairs)  40.8 us
    ppermute x20, waiting for transfers between devices, swap(): return lax.ppermute(value, axis, PAIR)  39.8 us
    ppermute x16, starting transfers between devices, along(): return lax.ppermute(value, 'fsdp', pairs)  34.9 us
    ppermute x20, starting transfers between devices, swap(): return lax.ppermute(value, axis, PAIR)  18.2 us
    unnamed x51, local copies, waits for them, and re-layouts  8.71 us
    all_to_all x1, starting transfers between devices, body_line(): lax.all_to_all(done(up_sent), ('fsdp', 'own'), split_axis=0, concat_axis=...  7.25 us
  transfers between devices with their start and end apart: 37, of which 17 were waited for; matrix products, arithmetic and copies ran while one was open for 1% of the time, Pallas kernels for 26%

profile of v10, /device:TPU:0, one launch (start us, length us, event | category | flops | bytes accessed | tf_op | source)
XLA Modules:
  0.0 212.6 jit_solution(17430049746402328539)
XLA Ops:
  2.5 7.3 %all-to-all-start = ((bf16[8,128,256]{2,1,0:T(8,128)(2,1)}), bf16[8,128,256]{2,1,0:T(8,128)(2,1)S(1)}, u32[]{:S(2)}, u32[]{:S(2)}) async-start(bf16[8,128,256]{2,1,0:T(8,128)(2,1)} %shard_map.102), calls=%async_computation | async-start | bytes 1048576 | tf_op jit(solution)/shard_map/all_to_all | solution.py:441
  19.2 5.4 %collective-permute-done.1.refs_1_ = bf16[1024,128]{1,0:T(8,128)(2,1)} collective-permute-done((bf16[1024,128]{1,0:T(8,128)(2,1)S(1)}, bf16[1024,128]{1,0:T(8,128)(2,1)}, u32[]{:S(2)}, u32[]{:S(2)}) %collective-permute-start.1) | collective-permute-done | bytes 262176 | tf_op jit(solution)/shard_map/ppermute | solution.py:36
  28.2 3.4 %collective-permute-done.there = bf16[256,640]{1,0:T(8,128)(2,1)} collective-permute-done((bf16[256,640]{1,0:T(8,128)(2,1)S(1)}, bf16[256,640]{1,0:T(8,128)(2,1)}, u32[]{:S(2)}, u32[]{:S(2)}) %collective-permute-start) | collective-permute-done | bytes 327712 | tf_op jit(solution)/shard_map/ppermute | solution.py:36
  42.4 2.6 %shard_map.111 = bf16[1024,512]{1,0:T(8,128)(2,1)} custom-call(s32[4]{0:T(128)S(1)} %pad_add_fusion.numbers, bf16[1024,256]{1,0:T(8,128)(2,1)S(1)} %shard_map.106.refs_0_.rest_0_.own, bf16[1024,256]{1,0:T(8,128)(2,1)} %collective-permute-done.4.refs_1_.rest_1_.near), custom_call_target="tpu_custom_call" | custom-call | tf_op jit(solution)/shard_map/pallas_call | solution.py:48
  50.1 5.2 %collective-permute-start.13 = (bf16[512,1024]{1,0:T(8,128)(2,1)S(1)}, bf16[512,1024]{1,0:T(8,128)(2,1)S(1)}, u32[]{:S(2)}, u32[]{:S(2)}) collective-permute-start(bf16[512,1024]{1,0:T(8,128)(2,1)S(1)} %shard_map.112.x_here.x_mine.tokens), channel_id=1, source_target_pairs={{0,4},{12,8},{1,5},{13,9},{2,6},{14,10},{3,7},{15,11},{16,20},{28,... | collective-permute-start | bytes 3145736 | tf_op jit(solution)/shard_map/ppermute | solution.py:40
  61.2 5.4 %collective-permute-start.6 = (bf16[512,256]{1,0:T(8,128)(2,1)S(1)}, bf16[512,256]{1,0:T(8,128)(2,1)S(1)}, u32[]{:S(2)}, u32[]{:S(2)}) collective-permute-start(bf16[512,256]{1,0:T(8,128)(2,1)S(1)} %get-tuple-element.95), channel_id=1, source_target_pairs={{0,4},{12,8},{1,5},{13,9},{2,6},{14,10},{3,7},{15,11},{16,20},{28,... | collective-permute-start | bytes 786440 | tf_op jit(solution)/shard_map/ppermute | solution.py:40
  66.6 15.7 %collective-permute-done.6.packet = bf16[512,256]{1,0:T(8,128)(2,1)S(1)} collective-permute-done((bf16[512,256]{1,0:T(8,128)(2,1)S(1)}, bf16[512,256]{1,0:T(8,128)(2,1)S(1)}, u32[]{:S(2)}, u32[]{:S(2)}) %collective-permute-start.6) | collective-permute-done | bytes 262176 | tf_op jit(solution)/shard_map/ppermute | solution.py:40
  87.9 7.9 %collective-permute-done.8.refs_1_ = bf16[256,1024]{1,0:T(8,128)(2,1)S(1)} collective-permute-done((bf16[256,1024]{1,0:T(8,128)(2,1)S(1)}, bf16[256,1024]{1,0:T(8,128)(2,1)S(1)}, u32[]{:S(2)}, u32[]{:S(2)}) %collective-permute-start.8) | collective-permute-done | bytes 524320 | tf_op jit(solution)/shard_map/ppermute | solution.py:36
  96.5 2.3 %shard_map.119 = bf16[1024,512]{1,0:T(8,128)(2,1)} custom-call(bf16[512,1024]{1,0:T(8,128)(2,1)S(1)} %shard_map.112.x_here.x_mine.tokens, bf16[512,1024]{1,0:T(8,128)(2,1)S(1)} %get-tuple-element.104.back, bf16[512,1024]{1,0:T(8,128)(2,1)S(1)} %collective-permute-done.13.x_in, bf16[512,1024]{1,0:T(8,128)(2,1)S(1)} %shard_map.115.back_in), custom_call_target="tpu_custom_call" | custom-call | tf_op jit(solution)/shard_map/pallas_call | solution.py:48
  99.7 5.5 %collective-permute-start.17 = (bf16[512,1024]{1,0:T(8,128)(2,1)S(1)}, bf16[512,1024]{1,0:T(8,128)(2,1)}, u32[]{:S(2)}, u32[]{:S(2)}) collective-permute-start(bf16[512,1024]{1,0:T(8,128)(2,1)S(1)} %shard_map.118.x_here.x_other.tokens), channel_id=1, source_target_pairs={{0,4},{12,8},{1,5},{13,9},{2,6},{14,10},{3,7},{15,11},{16,20},{28,... | collective-permute-start | bytes 3145736 | tf_op jit(solution)/shard_map/ppermute | solution.py:40
  114.7 12.5 %collective-permute-done.17.x_in = bf16[512,1024]{1,0:T(8,128)(2,1)} collective-permute-done((bf16[512,1024]{1,0:T(8,128)(2,1)S(1)}, bf16[512,1024]{1,0:T(8,128)(2,1)}, u32[]{:S(2)}, u32[]{:S(2)}) %collective-permute-start.17) | collective-permute-done | bytes 1048608 | tf_op jit(solution)/shard_map/ppermute | solution.py:40
  127.2 2.5 %shard_map.122 = bf16[1024,512]{1,0:T(8,128)(2,1)S(1)} custom-call(bf16[512,1024]{1,0:T(8,128)(2,1)S(1)} %shard_map.118.x_here.x_other.tokens, bf16[512,1024]{1,0:T(8,128)(2,1)S(1)} %get-tuple-element.104.back, bf16[512,1024]{1,0:T(8,128)(2,1)} %collective-permute-done.17.x_in, bf16[512,1024]{1,0:T(8,128)(2,1)S(1)} %copy-done.3), custom_call_target="tpu_custom_call" | custom-call | tf_op jit(solution)/shard_map/pallas_call | solution.py:48
  138.3 3.7 %shard_map.125 = (bf16[256,1024]{1,0:T(8,128)(2,1)S(1)}, bf16[256,1024]{1,0:T(8,128)(2,1)S(1)}) custom-call(bf16[512,1024]{1,0:T(8,128)(2,1)S(1)} %shard_map.120.dy, bf16[512,1024]{1,0:T(8,128)(2,1)S(1)} %get-tuple-element.104.back, bf16[1024,256]{1,0:T(8,128)(2,1)} %shard_map.109.refs_0_.own, bf16[1024,256]{1,0:T(8,128)(2,1)} %collective-permute-done.7.refs_1_.near, ...), custom_call_target="tpu_custom_call" | custom-call | tf_op jit(solution)/shard_map/pallas_call | solution.py:48
  143.9 3.7 %shard_map.126.left = f32[512,128]{1,0:T(8,128)S(1)} custom-call(s32[24]{0:T(128)S(1)} %concatenate.3.numbers, bf16[512,128]{1,0:T(8,128)(2,1)S(1)} %get-tuple-element.86.ids, bf16[512,1024]{1,0:T(8,128)(2,1)S(1)} %shard_map.112.x_here.x_mine.tokens, bf16[512,1024]{1,0:T(8,128)(2,1)S(1)} %shard_map.118.x_here.x_other.tokens, ...), custom_call_target="tpu_custom_call" | custom-call | tf_op jit(solution)/shard_map/pallas_call | solution.py:48
  147.7 4.4 %collective-permute-done.23.outer = bf16[1024,256]{1,0:T(8,128)(2,1)S(1)} collective-permute-done((bf16[1024,256]{1,0:T(8,128)(2,1)S(1)}, bf16[1024,256]{1,0:T(8,128)(2,1)S(1)}, u32[]{:S(2)}, u32[]{:S(2)}) %collective-permute-start.23) | collective-permute-done | bytes 524320 | tf_op jit(solution)/shard_map/ppermute | solution.py:40
  154.1 4.1 %shard_map.128 = (f32[2,512,256]{2,1,0:T(8,128)S(1)}, f32[2,512,256]{2,1,0:T(8,128)S(1)}) custom-call(s32[5]{0:T(128)S(1)} %convert_element_type.3.flags, bf16[512,1024]{1,0:T(8,128)(2,1)S(1)} %shard_map.112.x_here.x_mine.tokens, bf16[1024,256]{1,0:T(8,128)(2,1)} %shard_map.109.refs_0_.own, bf16[1024,256]{1,0:T(8,128)(2,1)} %collective-permute-done.7.refs_1_.near, ...), custom_call_target="tpu_custom_call" | custom-call | tf_op jit(solution)/shard_map/pallas_call | solution.py:48
  162.2 5.3 %collective-permute-done.25.refs_2_ = bf16[1024,128]{1,0:T(8,128)(2,1)S(1)} collective-permute-done((bf16[1024,128]{1,0:T(8,128)(2,1)S(1)}, bf16[1024,128]{1,0:T(8,128)(2,1)S(1)}, u32[]{:S(2)}, u32[]{:S(2)}) %collective-permute-start.25) | collective-permute-done | bytes 262176 | tf_op jit(solution)/shard_map/ppermute | solution.py:36
  167.5 3.1 %collective-permute-done.24.got = f32[512,128]{1,0:T(8,128)S(1)} collective-permute-done((f32[512,128]{1,0:T(8,128)S(1)}, f32[512,128]{1,0:T(8,128)S(1)}, u32[]{:S(2)}, u32[]{:S(2)}) %collective-permute-start.24) | collective-permute-done | bytes 262176 | tf_op jit(solution)/shard_map/ppermute | solution.py:36
  172.2 3.6 %shard_map.132 = (bf16[256,1024]{1,0:T(8,128)(2,1)S(1)}, bf16[256,1024]{1,0:T(8,128)(2,1)S(1)}) custom-call(bf16[512,1024]{1,0:T(8,128)(2,1)S(1)} %shard_map.120.dy, bf16[512,1024]{1,0:T(8,128)(2,1)S(1)} %get-tuple-element.104.back, bf16[1024,256]{1,0:T(8,128)(2,1)S(1)} %copy-done.11, bf16[1024,256]{1,0:T(8,128)(2,1)S(1)} %copy-done.17, ...), custom_call_target="tpu_custom_call" | custom-call | tf_op jit(solution)/shard_map/pallas_call | solution.py:48
  176.4 2.4 %collective-permute-start.29 = (bf16[256,256]{1,0:T(8,128)(2,1)S(1)}, bf16[256,256]{1,0:T(8,128)(2,1)S(1)}, u32[]{:S(2)}, u32[]{:S(2)}) collective-permute-start(bf16[256,256]{1,0:T(8,128)(2,1)S(1)} %get-tuple-element.131), channel_id=1, source_target_pairs={{0,8},{4,12},{8,0},{12,4},{1,9},{5,13},{9,1},{13,5},{2,10},{6,14},... | collective-permute-start | bytes 393224 | tf_op jit(solution)/shard_map/ppermute | solution.py:40
  183.9 2.7 %collective-permute-done.29.third = bf16[256,256]{1,0:T(8,128)(2,1)S(1)} collective-permute-done((bf16[256,256]{1,0:T(8,128)(2,1)S(1)}, bf16[256,256]{1,0:T(8,128)(2,1)S(1)}, u32[]{:S(2)}, u32[]{:S(2)}) %collective-permute-start.29) | collective-permute-done | bytes 131104 | tf_op jit(solution)/shard_map/ppermute | solution.py:40
  187.4 3.5 %shard_map.135 = (f32[2,512,256]{2,1,0:T(8,128)S(1)}, f32[2,512,256]{2,1,0:T(8,128)S(1)}) custom-call(s32[5]{0:T(128)S(1)} %convert_element_type.3.flags, bf16[512,1024]{1,0:T(8,128)(2,1)S(1)} %shard_map.118.x_here.x_other.tokens, bf16[1024,256]{1,0:T(8,128)(2,1)S(1)} %copy-done.11, bf16[1024,256]{1,0:T(8,128)(2,1)S(1)} %copy-done.17, ...), custom_call_target="tpu_custom_call" | custom-call | tf_op jit(solution)/shard_map/pallas_call | solution.py:48
  192.6 7.1 %collective-permute-done.33.refs_3_ = bf16[1024,128]{1,0:T(8,128)(2,1)S(1)} collective-permute-done((bf16[1024,128]{1,0:T(8,128)(2,1)S(1)}, bf16[1024,128]{1,0:T(8,128)(2,1)S(1)}, u32[]{:S(2)}, u32[]{:S(2)}) %collective-permute-start.33) | collective-permute-done | bytes 262176 | tf_op jit(solution)/shard_map/ppermute | solution.py:36
  204.6 4.5 %collective-permute-done.34.got = bf16[2,256,256]{2,1,0:T(8,128)(2,1)S(1)} collective-permute-done((bf16[2,256,256]{2,1,0:T(8,128)(2,1)S(1)}, bf16[2,256,256]{2,1,0:T(8,128)(2,1)S(1)}, u32[]{:S(2)}, u32[]{:S(2)}) %collective-permute-start.34) | collective-permute-done | bytes 262176 | tf_op jit(solution)/shard_map/ppermute | solution.py:36
  (146 shorter events, 87.7 us)
Async XLA Ops:
  2.5 29.1 %all-to-all-start = ((bf16[8,128,256]{2,1,0:T(8,128)(2,1)}), bf16[8,128,256]{2,1,0:T(8,128)(2,1)S(1)}, u32[]{:S(2)}, u32[]{:S(2)}) async-start(bf16[8,128,256]{2,1,0:T(8,128)(2,1)} %shard_map.102), calls=%async_computation | async-start | bytes 1048576 | tf_op jit(solution)/shard_map/all_to_all | solution.py:441
  11.7 12.9 %collective-permute-start.1 = (bf16[1024,128]{1,0:T(8,128)(2,1)S(1)}, bf16[1024,128]{1,0:T(8,128)(2,1)}, u32[]{:S(2)}, u32[]{:S(2)}) collective-permute-start(bf16[1024,128]{1,0:T(8,128)(2,1)S(1)} %shard_map.103), channel_id=1, source_target_pairs={{0,2},{2,0},{1,3},{3,1},{4,6},{6,4},{5,7},{7,5},{8,10},{10,8},{9,1... | collective-permute-start | bytes 786440 | tf_op jit(solution)/shard_map/ppermute | solution.py:36
  15.6 16.0 %collective-permute-start = (bf16[256,640]{1,0:T(8,128)(2,1)S(1)}, bf16[256,640]{1,0:T(8,128)(2,1)}, u32[]{:S(2)}, u32[]{:S(2)}) collective-permute-start(bf16[256,640]{1,0:T(8,128)(2,1)S(1)} %shard_map.104.here), channel_id=1, source_target_pairs={{0,2},{2,0},{1,3},{3,1},{4,6},{6,4},{5,7},{7,5},{8,10},{10,8},{9,1... | collective-permute-start | bytes 983048 | tf_op jit(solution)/shard_map/ppermute | solution.py:36
  17.1 25.3 %collective-permute-start.5 = (bf16[256,1024]{1,0:T(8,128)(2,1)}, bf16[256,1024]{1,0:T(8,128)(2,1)}, u32[]{:S(2)}, u32[]{:S(2)}) collective-permute-start(bf16[256,1024]{1,0:T(8,128)(2,1)} %shard_map.105), channel_id=1, source_target_pairs={{0,2},{2,0},{1,3},{3,1},{4,6},{6,4},{5,7},{7,5},{8,10},{10,8},{9,1... | collective-permute-start | bytes 1572872 | tf_op jit(solution)/shard_map/ppermute | solution.py:36
  26.2 16.3 %collective-permute-start.4 = (bf16[1024,256]{1,0:T(8,128)(2,1)S(1)}, bf16[1024,256]{1,0:T(8,128)(2,1)}, u32[]{:S(2)}, u32[]{:S(2)}) collective-permute-start(bf16[1024,256]{1,0:T(8,128)(2,1)S(1)} %shard_map.106.refs_0_.rest_0_.own), channel_id=1, source_target_pairs={{0,4},{4,0},{8,12},{12,8},{1,5},{5,1},{9,13},{13,9},{2,6},{6,2},{1... | collective-permute-start | bytes 1572872 | tf_op jit(solution)/shard_map/ppermute | solution.py:40
  38.3 19.3 %collective-permute-start.7 = (bf16[1024,256]{1,0:T(8,128)(2,1)}, bf16[1024,256]{1,0:T(8,128)(2,1)}, u32[]{:S(2)}, u32[]{:S(2)}) collective-permute-start(bf16[1024,256]{1,0:T(8,128)(2,1)} %shard_map.109.refs_0_.own), channel_id=1, source_target_pairs={{0,4},{4,0},{8,12},{12,8},{1,5},{5,1},{9,13},{13,9},{2,6},{6,2},{1... | collective-permute-start | bytes 1572872 | tf_op jit(solution)/shard_map/ppermute | solution.py:40
  45.1 41.1 %collective-permute-start.10 = (bf16[1024,512]{1,0:T(8,128)(2,1)}, bf16[1024,512]{1,0:T(8,128)(2,1)}, u32[]{:S(2)}, u32[]{:S(2)}) collective-permute-start(bf16[1024,512]{1,0:T(8,128)(2,1)} %shard_map.111), channel_id=1, source_target_pairs={{4,8},{8,4},{5,9},{9,5},{6,10},{10,6},{7,11},{11,7},{20,24},{24,20... | collective-permute-start | bytes 3145736 | tf_op jit(solution)/shard_map/ppermute | solution.py:40
  46.7 39.4 %collective-permute-start.9 = (bf16[1024,512]{1,0:T(8,128)(2,1)}, bf16[1024,512]{1,0:T(8,128)(2,1)}, u32[]{:S(2)}, u32[]{:S(2)}) collective-permute-start(bf16[1024,512]{1,0:T(8,128)(2,1)} %shard_map.111), channel_id=1, source_target_pairs={{0,16},{16,0},{1,17},{17,1},{2,18},{18,2},{3,19},{19,3},{4,20},{20... | collective-permute-start | bytes 3145736 | tf_op jit(solution)/shard_map/ppermute | solution.py:36
  50.1 46.4 %collective-permute-start.13 = (bf16[512,1024]{1,0:T(8,128)(2,1)S(1)}, bf16[512,1024]{1,0:T(8,128)(2,1)S(1)}, u32[]{:S(2)}, u32[]{:S(2)}) collective-permute-start(bf16[512,1024]{1,0:T(8,128)(2,1)S(1)} %shard_map.112.x_here.x_mine.tokens), channel_id=1, source_target_pairs={{0,4},{12,8},{1,5},{13,9},{2,6},{14,10},{3,7},{15,11},{16,20},{28,... | collective-permute-start | bytes 3145736 | tf_op jit(solution)/shard_map/ppermute | solution.py:40
  59.5 39.4 %collective-permute-start.12 = (bf16[1024,512]{1,0:T(8,128)(2,1)S(1)}, bf16[1024,512]{1,0:T(8,128)(2,1)}, u32[]{:S(2)}, u32[]{:S(2)}) collective-permute-start(bf16[1024,512]{1,0:T(8,128)(2,1)S(1)} %shard_map.114), channel_id=1, source_target_pairs={{4,8},{8,4},{5,9},{9,5},{6,10},{10,6},{7,11},{11,7},{20,24},{24,20... | collective-permute-start | bytes 3145736 | tf_op jit(solution)/shard_map/ppermute | solution.py:40
  61.2 21.1 %collective-permute-start.6 = (bf16[512,256]{1,0:T(8,128)(2,1)S(1)}, bf16[512,256]{1,0:T(8,128)(2,1)S(1)}, u32[]{:S(2)}, u32[]{:S(2)}) collective-permute-start(bf16[512,256]{1,0:T(8,128)(2,1)S(1)} %get-tuple-element.95), channel_id=1, source_target_pairs={{0,4},{12,8},{1,5},{13,9},{2,6},{14,10},{3,7},{15,11},{16,20},{28,... | collective-permute-start | bytes 786440 | tf_op jit(solution)/shard_map/ppermute | solution.py:40
  83.9 12.0 %collective-permute-start.8 = (bf16[256,1024]{1,0:T(8,128)(2,1)S(1)}, bf16[256,1024]{1,0:T(8,128)(2,1)S(1)}, u32[]{:S(2)}, u32[]{:S(2)}) collective-permute-start(bf16[256,1024]{1,0:T(8,128)(2,1)S(1)} %shard_map.116), channel_id=1, source_target_pairs={{0,2},{2,0},{1,3},{3,1},{4,6},{6,4},{5,7},{7,5},{8,10},{10,8},{9,1... | collective-permute-start | bytes 1572872 | tf_op jit(solution)/shard_map/ppermute | solution.py:36
  86.1 12.7 %collective-permute-start.11 = (bf16[1024,256]{1,0:T(8,128)(2,1)}, bf16[1024,256]{1,0:T(8,128)(2,1)S(1)}, u32[]{:S(2)}, u32[]{:S(2)}) collective-permute-start(bf16[1024,256]{1,0:T(8,128)(2,1)} %collective-permute-done.7.refs_1_.near), channel_id=1, source_target_pairs={{0,16},{16,0},{1,17},{17,1},{2,18},{18,2},{3,19},{19,3},{4,20},{20... | collective-permute-start | bytes 1572872 | tf_op jit(solution)/shard_map/ppermute | solution.py:36
  86.6 24.5 %collective-permute-start.18 = (bf16[1024,512]{1,0:T(8,128)(2,1)}, bf16[1024,512]{1,0:T(8,128)(2,1)}, u32[]{:S(2)}, u32[]{:S(2)}) collective-permute-start(bf16[1024,512]{1,0:T(8,128)(2,1)} %collective-permute-done.10.crossed), channel_id=1, source_target_pairs={{4,0},{8,12},{5,1},{9,13},{6,2},{10,14},{7,3},{11,15},{20,16},{24,... | collective-permute-start | bytes 3145736 | tf_op jit(solution)/shard_map/ppermute | solution.py:40
  99.7 27.6 %collective-permute-start.17 = (bf16[512,1024]{1,0:T(8,128)(2,1)S(1)}, bf16[512,1024]{1,0:T(8,128)(2,1)}, u32[]{:S(2)}, u32[]{:S(2)}) collective-permute-start(bf16[512,1024]{1,0:T(8,128)(2,1)S(1)} %shard_map.118.x_here.x_other.tokens), channel_id=1, source_target_pairs={{0,4},{12,8},{1,5},{13,9},{2,6},{14,10},{3,7},{15,11},{16,20},{28,... | collective-permute-start | bytes 3145736 | tf_op jit(solution)/shard_map/ppermute | solution.py:40
  105.1 25.3 %collective-permute-start.16 = (bf16[1024,512]{1,0:T(8,128)(2,1)}, bf16[1024,512]{1,0:T(8,128)(2,1)}, u32[]{:S(2)}, u32[]{:S(2)}) collective-permute-start(bf16[1024,512]{1,0:T(8,128)(2,1)} %shard_map.119), channel_id=1, source_target_pairs={{4,8},{8,4},{5,9},{9,5},{6,10},{10,6},{7,11},{11,7},{20,24},{24,20... | collective-permute-start | bytes 3145736 | tf_op jit(solution)/shard_map/ppermute | solution.py:40
  106.8 27.5 %collective-permute-start.15 = (bf16[1024,512]{1,0:T(8,128)(2,1)}, bf16[1024,512]{1,0:T(8,128)(2,1)}, u32[]{:S(2)}, u32[]{:S(2)}) collective-permute-start(bf16[1024,512]{1,0:T(8,128)(2,1)} %collective-permute-done.12.crossed), channel_id=1, source_target_pairs={{4,0},{8,12},{5,1},{9,13},{6,2},{10,14},{7,3},{11,15},{20,16},{24,... | collective-permute-start | bytes 3145736 | tf_op jit(solution)/shard_map/ppermute | solution.py:40
  112.8 31.1 %collective-permute-start.20 = (bf16[1024,512]{1,0:T(8,128)(2,1)S(1)}, bf16[1024,512]{1,0:T(8,128)(2,1)S(1)}, u32[]{:S(2)}, u32[]{:S(2)}) collective-permute-start(bf16[1024,512]{1,0:T(8,128)(2,1)S(1)} %shard_map.121.rest_2_.far), channel_id=1, source_target_pairs={{0,16},{16,0},{1,17},{17,1},{2,18},{18,2},{3,19},{19,3},{4,20},{20... | collective-permute-start | bytes 3145736 | tf_op jit(solution)/shard_map/ppermute | solution.py:36
  129.7 30.7 %collective-permute-start.26 = (bf16[1024,512]{1,0:T(8,128)(2,1)S(1)}, bf16[1024,512]{1,0:T(8,128)(2,1)S(1)}, u32[]{:S(2)}, u32[]{:S(2)}) collective-permute-start(bf16[1024,512]{1,0:T(8,128)(2,1)S(1)} %shard_map.122), channel_id=1, source_target_pairs={{4,8},{8,4},{5,9},{9,5},{6,10},{10,6},{7,11},{11,7},{20,24},{24,20... | collective-permute-start | bytes 3145736 | tf_op jit(solution)/shard_map/ppermute | solution.py:40
  135.9 36.3 %collective-permute-start.19 = (bf16[1024,512]{1,0:T(8,128)(2,1)S(1)}, bf16[1024,512]{1,0:T(8,128)(2,1)S(1)}, u32[]{:S(2)}, u32[]{:S(2)}) collective-permute-start(bf16[1024,512]{1,0:T(8,128)(2,1)S(1)} %shard_map.124.far), channel_id=1, source_target_pairs={{0,16},{16,0},{1,17},{17,1},{2,18},{18,2},{3,19},{19,3},{4,20},{20... | collective-permute-start | bytes 3145736 | tf_op jit(solution)/shard_map/ppermute | solution.py:36
  136.9 15.2 %collective-permute-start.23 = (bf16[1024,256]{1,0:T(8,128)(2,1)S(1)}, bf16[1024,256]{1,0:T(8,128)(2,1)S(1)}, u32[]{:S(2)}, u32[]{:S(2)}) collective-permute-start(bf16[1024,256]{1,0:T(8,128)(2,1)S(1)} %shard_map.123), channel_id=1, source_target_pairs={{4,0},{8,12},{5,1},{9,13},{6,2},{10,14},{7,3},{11,15},{20,16},{24,... | collective-permute-start | bytes 1572872 | tf_op jit(solution)/shard_map/ppermute | solution.py:40
  142.1 16.6 %collective-permute-start.22 = (bf16[256,1024]{1,0:T(8,128)(2,1)S(1)}, bf16[256,1024]{1,0:T(8,128)(2,1)S(1)}, u32[]{:S(2)}, u32[]{:S(2)}) collective-permute-start(bf16[256,1024]{1,0:T(8,128)(2,1)S(1)} %get-tuple-element.116), channel_id=1, source_target_pairs={{0,2},{2,0},{1,3},{3,1},{4,6},{6,4},{5,7},{7,5},{8,10},{10,8},{9,1... | collective-permute-start | bytes 1572872 | tf_op jit(solution)/shard_map/ppermute | solution.py:36
  158.8 11.9 %collective-permute-start.24 = (f32[512,128]{1,0:T(8,128)S(1)}, f32[512,128]{1,0:T(8,128)S(1)}, u32[]{:S(2)}, u32[]{:S(2)}) collective-permute-start(f32[512,128]{1,0:T(8,128)S(1)} %shard_map.129.part), channel_id=1, source_target_pairs={{0,2},{2,0},{1,3},{3,1},{4,6},{6,4},{5,7},{7,5},{8,10},{10,8},{9,1... | collective-permute-start | bytes 786440 | tf_op jit(solution)/shard_map/ppermute | solution.py:36
  160.9 19.2 %collective-permute-start.31 = (bf16[1024,256]{1,0:T(8,128)(2,1)S(1)}, bf16[1024,256]{1,0:T(8,128)(2,1)S(1)}, u32[]{:S(2)}, u32[]{:S(2)}) collective-permute-start(bf16[1024,256]{1,0:T(8,128)(2,1)S(1)} %shard_map.130), channel_id=1, source_target_pairs={{4,0},{8,12},{5,1},{9,13},{6,2},{10,14},{7,3},{11,15},{20,16},{24,... | collective-permute-start | bytes 1572872 | tf_op jit(solution)/shard_map/ppermute | solution.py:40
  (38 other events, 349.0 us)

commit v11 on v10

--- a/solution.py
+++ b/solution.py
@@ -437,16 +437,12 @@
             got,
         )[0]
 
-    up_sent = kernel_call(up_sent_kernel, [like(number, size, kvq)], up)[0]
-    up_all = lax.all_to_all(
-        done(up_sent), ("fsdp", "own"), split_axis=0, concat_axis=0, tiled=True
-    ).reshape(number * size, kvq)
-    down_got = swap(done(rows_at(2, step(down), eighth)), "own")
+    down_got = swap(done(rows_at(2, down, eighth)), "own")
     packet_here = done(
         kernel_call(packet_kernel, [like(rows, kv + size)], step(cotangent), token_adapter)[0]
     )
     packet = swap(packet_here, "own")
-    x_got = [swap(done(columns_at(2, step(tokens))), "own")]
+    down_got, packet = step(down_got, packet)
     down_piece = done(
         copy_call(
             lambda n, a, o: [
@@ -456,51 +452,58 @@
             [like(eighth, wide)],
             starts,
             down,
-            step(down_got),
+            down_got,
         )[0]
     )
     down_near = along(down_piece, NEIGHBOURS)
-    packet, up_all = step(packet, up_all)
+    up_sent = kernel_call(up_sent_kernel, [like(number, size, kvq)], step(up))[0]
+    up_all = lax.all_to_all(
+        done(up_sent), ("fsdp", "own"), split_axis=0, concat_axis=0, tiled=True
+    ).reshape(number * size, kvq)
     dy_half, ids, dy_quarter = kernel_call(
         unpack_kernel,
         [like(both, kv), like(both, size), like(both, kvq)],
         packet_here,
-        packet,
+        step(packet),
         scalars=flags,
     )
-    compact = like(both, size, kind=f32)
-    back_part = done(kernel_call(back_kernel, [compact], ids, dy_quarter, up_all)[0])
-    back_tp = swap(back_part, "tp")
+    done(dy_quarter)
+    x_got = [swap(done(columns_at(2, step(tokens))), "own")]
     weight_here = done(rows_at(0, step(frozen_value_weight), eighth))
     weight_near = along(weight_here, NEIGHBOURS)
+    crossing = done(side_by_side(down_piece, step(down_near)))
+    down_crossed = along(crossing, MIDDLE)
+    compact = like(both, size, kind=f32)
+    back_part = done(
+        kernel_call(back_kernel, [compact], ids, dy_quarter, step(up_all))[0]
+    )
+    back_tp = swap(back_part, "tp")
+    down_other = swap(crossing, "rep")
+    crossing = done(side_by_side(weight_here, step(weight_near)))
+    weight_crossed = along(crossing, MIDDLE)
     back_part = done(kernel_call(add_kernel, [compact], back_part, step(back_tp))[0])
     back_got = swap(back_part, "own")
-    down_near, x_got[0] = step(down_near, x_got[0])
-    crossing = done(side_by_side(down_piece, down_near))
-    down_crossed = along(crossing, MIDDLE)
-    down_other = swap(crossing, "rep")
-    x_mine = done(tokens_of(0, tokens, step(x_got[0])))
-    x_in = [along(x_mine, INWARD)]
+    back_got, x_got[0] = step(back_got, x_got[0])
     back_wide, back_sent = kernel_call(
         back_end_kernel,
         [like(both, number * size), like(both, wide)],
         ids,
         back_part,
-        step(back_got),
+        back_got,
         scalars=numbers,
     )
     back_in = along(done(back_sent), INWARD)
-    crossing = done(side_by_side(weight_here, step(weight_near)))
-    weight_crossed = along(crossing, MIDDLE)
+    x_got.append(swap(done(columns_at(3, step(tokens))), "own"))
+    x_mine = done(tokens_of(0, tokens, step(x_got[0])))
+    back_in, down_crossed = step(back_in, down_crossed)
     back_in_wide = done(
         kernel_call(
-            spread_in_kernel, [like(both, number * size)], step(back_in), scalars=numbers
-        )[0]
-    )
-    x_got.append(swap(done(columns_at(3, step(tokens))), "own"))
+            spread_in_kernel, [like(both, number * size)], back_in, scalars=numbers
+        )[0]
+    )
+    down_outer = along(down_crossed, OUTWARD)
+    x_in = [along(step(x_mine), INWARD)]
     weight_other = done(rows_at(1, step(frozen_value_weight), eighth))
-    down_crossed = done(step(down_crossed))
-    down_outer = along(down_crossed, OUTWARD)
     weight_near, down_other = step(weight_near, down_other)
     weight_near_other = swap(done(weight_near), "rep")
     x_other = done(tokens_of(1, tokens, step(x_got[1])))

time: 214 us -> 239 us (1.12)
  waiting for transfers between devices: 80.6 us -> 106 us
    ppermute x16, waiting for transfers between devices: 40.8 us -> 54.7 us  [along(): return lax.ppermute(value, 'fsdp', pairs)]
    ppermute x20, waiting for transfers between devices: 39.8 us -> 51.8 us  [swap(): return lax.ppermute(value, axis, PAIR)]
    ppermute x20, starting transfers between devices: 18.2 us -> 21.5 us  [swap(): return lax.ppermute(value, axis, PAIR)]
    ppermute x16, starting transfers between devices: 34.9 us -> 31.9 us  [along(): return lax.ppermute(value, 'fsdp', pairs)]
    unnamed x51 -> x61, local copies, waits for them, and re-layouts: 8.71 us -> 10.4 us
  transfers between devices with their start and end apart: 37 -> 37, of which waited for: 17 -> 17; matrix products, arithmetic and copies ran while one was open for 1% -> 0% of each run, Pallas kernels for 26% -> 22%
where the time goes in v11:
time: 239 us; the launch traced here: 238 us
  waiting for transfers between devices  106 us (44%)
  Pallas kernels  59.7 us (25%)
  starting transfers between devices  59.4 us (25%)
  local copies, waits for them, and re-layouts  10.6 us (4%)
    pallas_call x39, Pallas kernels, kernel_call(): pl.pallas_call(body, out_shape=list(outs), in_specs=specs, out_specs=[pl....  59.7 us
    ppermute x16, waiting for transfers between devices, along(): return lax.ppermute(value, 'fsdp', pairs)  54.7 us
    ppermute x20, waiting for transfers between devices, swap(): return lax.ppermute(value, axis, PAIR)  51.8 us
    ppermute x16, starting transfers between devices, along(): return lax.ppermute(value, 'fsdp', pairs)  31.9 us
    ppermute x20, starting transfers between devices, swap(): return lax.ppermute(value, axis, PAIR)  21.5 us
    unnamed x61, local copies, waits for them, and re-layouts  10.4 us
    all_to_all x1, starting transfers between devices, body_line(): lax.all_to_all(done(up_sent), ('fsdp', 'own'), split_axis=0, concat_axis=...  6.05 us
  transfers between devices with their start and end apart: 37, of which 17 were waited for; matrix products, arithmetic and copies ran while one was open for 0% of the time, Pallas kernels for 22%

profile of v11, /device:TPU:0, one launch (start us, length us, event | category | flops | bytes accessed | tf_op | source)
XLA Modules:
  0.0 237.6 jit_solution(3049806878029990545)
XLA Ops:
  4.4 3.0 %collective-permute-start.1 = (bf16[256,640]{1,0:T(8,128)(2,1)S(1)}, bf16[256,640]{1,0:T(8,128)(2,1)S(1)}, u32[]{:S(2)}, u32[]{:S(2)}) collective-permute-start(bf16[256,640]{1,0:T(8,128)(2,1)S(1)} %shard_map.103.here), channel_id=1, source_target_pairs={{0,2},{2,0},{1,3},{3,1},{4,6},{6,4},{5,7},{7,5},{8,10},{10,8},{9,1... | collective-permute-start | bytes 983048 | tf_op jit(solution)/shard_map/ppermute | solution.py:36
  7.5 13.2 %collective-permute-done.refs_1_ = bf16[1024,128]{1,0:T(8,128)(2,1)S(1)} collective-permute-done((bf16[1024,128]{1,0:T(8,128)(2,1)S(1)}, bf16[1024,128]{1,0:T(8,128)(2,1)S(1)}, u32[]{:S(2)}, u32[]{:S(2)}) %collective-permute-start) | collective-permute-done | bytes 262176 | tf_op jit(solution)/shard_map/ppermute | solution.py:36
  24.3 6.1 %all-to-all-start = ((bf16[8,128,256]{2,1,0:T(8,128)(2,1)}), bf16[8,128,256]{2,1,0:T(8,128)(2,1)}, u32[]{:S(2)}, u32[]{:S(2)}) async-start(bf16[8,128,256]{2,1,0:T(8,128)(2,1)} %shard_map.105), calls=%async_computation | async-start | bytes 1048576 | tf_op jit(solution)/shard_map/all_to_all | solution.py:460
  36.4 17.6 %collective-permute-done.2.refs_1_.rest_1_.near = bf16[1024,256]{1,0:T(8,128)(2,1)} collective-permute-done((bf16[1024,256]{1,0:T(8,128)(2,1)S(1)}, bf16[1024,256]{1,0:T(8,128)(2,1)}, u32[]{:S(2)}, u32[]{:S(2)}) %collective-permute-start.2) | collective-permute-done | bytes 524320 | tf_op jit(solution)/shard_map/ppermute | solution.py:40
  68.7 6.3 %collective-permute-done.6.refs_1_ = bf16[256,1024]{1,0:T(8,128)(2,1)} collective-permute-done((bf16[256,1024]{1,0:T(8,128)(2,1)}, bf16[256,1024]{1,0:T(8,128)(2,1)}, u32[]{:S(2)}, u32[]{:S(2)}) %collective-permute-start.6) | collective-permute-done | bytes 524320 | tf_op jit(solution)/shard_map/ppermute | solution.py:36
  74.9 5.1 %collective-permute-done.5.got = f32[512,128]{1,0:T(8,128)S(1)} collective-permute-done((f32[512,128]{1,0:T(8,128)S(1)}, f32[512,128]{1,0:T(8,128)S(1)}, u32[]{:S(2)}, u32[]{:S(2)}) %collective-permute-start.5) | collective-permute-done | bytes 262176 | tf_op jit(solution)/shard_map/ppermute | solution.py:36
  82.9 5.1 %collective-permute-start.9 = (bf16[512,256]{1,0:T(8,128)(2,1)S(1)}, bf16[512,256]{1,0:T(8,128)(2,1)S(1)}, u32[]{:S(2)}, u32[]{:S(2)}) collective-permute-start(bf16[512,256]{1,0:T(8,128)(2,1)S(1)} %get-tuple-element.97), channel_id=1, source_target_pairs={{0,4},{12,8},{1,5},{13,9},{2,6},{14,10},{3,7},{15,11},{16,20},{28,... | collective-permute-start | bytes 786440 | tf_op jit(solution)/shard_map/ppermute | solution.py:40
  90.7 2.8 %collective-permute-done.9.packet = bf16[512,256]{1,0:T(8,128)(2,1)S(1)} collective-permute-done((bf16[512,256]{1,0:T(8,128)(2,1)S(1)}, bf16[512,256]{1,0:T(8,128)(2,1)S(1)}, u32[]{:S(2)}, u32[]{:S(2)}) %collective-permute-start.9) | collective-permute-done | bytes 262176 | tf_op jit(solution)/shard_map/ppermute | solution.py:40
  94.4 4.5 %collective-permute-start.13 = (bf16[512,1024]{1,0:T(8,128)(2,1)S(1)}, bf16[512,1024]{1,0:T(8,128)(2,1)S(1)}, u32[]{:S(2)}, u32[]{:S(2)}) collective-permute-start(bf16[512,1024]{1,0:T(8,128)(2,1)S(1)} %shard_map.115.x_here.x_mine.tokens), channel_id=1, source_target_pairs={{0,4},{12,8},{1,5},{13,9},{2,6},{14,10},{3,7},{15,11},{16,20},{28,... | collective-permute-start | bytes 3145736 | tf_op jit(solution)/shard_map/ppermute | solution.py:40
  106.2 6.7 %collective-permute-done.7.refs_1_ = bf16[256,1024]{1,0:T(8,128)(2,1)S(1)} collective-permute-done((bf16[256,1024]{1,0:T(8,128)(2,1)S(1)}, bf16[256,1024]{1,0:T(8,128)(2,1)S(1)}, u32[]{:S(2)}, u32[]{:S(2)}) %collective-permute-start.7) | collective-permute-done | bytes 524320 | tf_op jit(solution)/shard_map/ppermute | solution.py:36
  113.6 6.6 %collective-permute-done.13.x_in = bf16[512,1024]{1,0:T(8,128)(2,1)S(1)} collective-permute-done((bf16[512,1024]{1,0:T(8,128)(2,1)S(1)}, bf16[512,1024]{1,0:T(8,128)(2,1)S(1)}, u32[]{:S(2)}, u32[]{:S(2)}) %collective-permute-start.13) | collective-permute-done | bytes 1048608 | tf_op jit(solution)/shard_map/ppermute | solution.py:40
  123.4 5.4 %collective-permute-start.17 = (bf16[512,1024]{1,0:T(8,128)(2,1)S(1)}, bf16[512,1024]{1,0:T(8,128)(2,1)}, u32[]{:S(2)}, u32[]{:S(2)}) collective-permute-start(bf16[512,1024]{1,0:T(8,128)(2,1)S(1)} %shard_map.118.x_here.x_other.tokens), channel_id=1, source_target_pairs={{0,4},{12,8},{1,5},{13,9},{2,6},{14,10},{3,7},{15,11},{16,20},{28,... | collective-permute-start | bytes 3145736 | tf_op jit(solution)/shard_map/ppermute | solution.py:40
  136.5 14.3 %collective-permute-done.17.x_in = bf16[512,1024]{1,0:T(8,128)(2,1)} collective-permute-done((bf16[512,1024]{1,0:T(8,128)(2,1)S(1)}, bf16[512,1024]{1,0:T(8,128)(2,1)}, u32[]{:S(2)}, u32[]{:S(2)}) %collective-permute-start.17) | collective-permute-done | bytes 1048608 | tf_op jit(solution)/shard_map/ppermute | solution.py:40
  162.6 3.6 %shard_map.125 = (bf16[256,1024]{1,0:T(8,128)(2,1)S(1)}, bf16[256,1024]{1,0:T(8,128)(2,1)S(1)}) custom-call(bf16[512,1024]{1,0:T(8,128)(2,1)S(1)} %shard_map.120.dy, bf16[512,1024]{1,0:T(8,128)(2,1)S(1)} %get-tuple-element.106.back, bf16[1024,256]{1,0:T(8,128)(2,1)S(1)} %copy-done.7, bf16[1024,256]{1,0:T(8,128)(2,1)} %collective-permute-done.4.refs_1_.near, ...), custom_call_target="tpu_custom_call" | custom-call | tf_op jit(solution)/shard_map/pallas_call | solution.py:48
  167.7 3.7 %shard_map.126.left = f32[512,128]{1,0:T(8,128)S(1)} custom-call(s32[24]{0:T(128)S(1)} %concatenate.3.numbers, bf16[512,128]{1,0:T(8,128)(2,1)S(1)} %get-tuple-element.88.ids, bf16[512,1024]{1,0:T(8,128)(2,1)S(1)} %shard_map.115.x_here.x_mine.tokens, bf16[512,1024]{1,0:T(8,128)(2,1)S(1)} %shard_map.118.x_here.x_other.tokens, ...), custom_call_target="tpu_custom_call" | custom-call | tf_op jit(solution)/shard_map/pallas_call | solution.py:48
  171.5 4.4 %collective-permute-done.23.outer = bf16[1024,256]{1,0:T(8,128)(2,1)S(1)} collective-permute-done((bf16[1024,256]{1,0:T(8,128)(2,1)S(1)}, bf16[1024,256]{1,0:T(8,128)(2,1)S(1)}, u32[]{:S(2)}, u32[]{:S(2)}) %collective-permute-start.23) | collective-permute-done | bytes 524320 | tf_op jit(solution)/shard_map/ppermute | solution.py:40
  178.0 3.9 %shard_map.128 = (f32[2,512,256]{2,1,0:T(8,128)S(1)}, f32[2,512,256]{2,1,0:T(8,128)S(1)}) custom-call(s32[5]{0:T(128)S(1)} %convert_element_type.3.flags, bf16[512,1024]{1,0:T(8,128)(2,1)S(1)} %shard_map.115.x_here.x_mine.tokens, bf16[1024,256]{1,0:T(8,128)(2,1)S(1)} %copy-done.7, bf16[1024,256]{1,0:T(8,128)(2,1)} %collective-permute-done.4.refs_1_.near, ...), custom_call_target="tpu_custom_call" | custom-call | tf_op jit(solution)/shard_map/pallas_call | solution.py:48
  185.9 5.3 %collective-permute-done.25.refs_2_ = bf16[1024,128]{1,0:T(8,128)(2,1)S(1)} collective-permute-done((bf16[1024,128]{1,0:T(8,128)(2,1)S(1)}, bf16[1024,128]{1,0:T(8,128)(2,1)S(1)}, u32[]{:S(2)}, u32[]{:S(2)}) %collective-permute-start.25) | collective-permute-done | bytes 262176 | tf_op jit(solution)/shard_map/ppermute | solution.py:36
  196.1 3.6 %shard_map.132 = (bf16[256,1024]{1,0:T(8,128)(2,1)S(1)}, bf16[256,1024]{1,0:T(8,128)(2,1)S(1)}) custom-call(bf16[512,1024]{1,0:T(8,128)(2,1)S(1)} %shard_map.120.dy, bf16[512,1024]{1,0:T(8,128)(2,1)S(1)} %get-tuple-element.106.back, bf16[1024,256]{1,0:T(8,128)(2,1)S(1)} %copy-done.11, bf16[1024,256]{1,0:T(8,128)(2,1)S(1)} %copy-done.17, ...), custom_call_target="tpu_custom_call" | custom-call | tf_op jit(solution)/shard_map/pallas_call | solution.py:48
  201.2 3.3 %collective-permute-start.29 = (bf16[256,256]{1,0:T(8,128)(2,1)S(1)}, bf16[256,256]{1,0:T(8,128)(2,1)S(1)}, u32[]{:S(2)}, u32[]{:S(2)}) collective-permute-start(bf16[256,256]{1,0:T(8,128)(2,1)S(1)} %get-tuple-element.135), channel_id=1, source_target_pairs={{0,8},{4,12},{8,0},{12,4},{1,9},{5,13},{9,1},{13,5},{2,10},{6,14},... | collective-permute-start | bytes 393224 | tf_op jit(solution)/shard_map/ppermute | solution.py:40
  208.4 3.3 %collective-permute-done.29.third = bf16[256,256]{1,0:T(8,128)(2,1)S(1)} collective-permute-done((bf16[256,256]{1,0:T(8,128)(2,1)S(1)}, bf16[256,256]{1,0:T(8,128)(2,1)S(1)}, u32[]{:S(2)}, u32[]{:S(2)}) %collective-permute-start.29) | collective-permute-done | bytes 131104 | tf_op jit(solution)/shard_map/ppermute | solution.py:40
  212.3 3.5 %shard_map.135 = (f32[2,512,256]{2,1,0:T(8,128)S(1)}, f32[2,512,256]{2,1,0:T(8,128)S(1)}) custom-call(s32[5]{0:T(128)S(1)} %convert_element_type.3.flags, bf16[512,1024]{1,0:T(8,128)(2,1)S(1)} %shard_map.118.x_here.x_other.tokens, bf16[1024,256]{1,0:T(8,128)(2,1)S(1)} %copy-done.11, bf16[1024,256]{1,0:T(8,128)(2,1)S(1)} %copy-done.17, ...), custom_call_target="tpu_custom_call" | custom-call | tf_op jit(solution)/shard_map/pallas_call | solution.py:48
  216.7 7.9 %collective-permute-done.33.refs_3_ = bf16[1024,128]{1,0:T(8,128)(2,1)S(1)} collective-permute-done((bf16[1024,128]{1,0:T(8,128)(2,1)S(1)}, bf16[1024,128]{1,0:T(8,128)(2,1)S(1)}, u32[]{:S(2)}, u32[]{:S(2)}) %collective-permute-start.33) | collective-permute-done | bytes 262176 | tf_op jit(solution)/shard_map/ppermute | solution.py:36
  229.5 4.5 %collective-permute-done.34.got = bf16[2,256,256]{2,1,0:T(8,128)(2,1)S(1)} collective-permute-done((bf16[2,256,256]{2,1,0:T(8,128)(2,1)S(1)}, bf16[2,256,256]{2,1,0:T(8,128)(2,1)S(1)}, u32[]{:S(2)}, u32[]{:S(2)}) %collective-permute-start.34) | collective-permute-done | bytes 262176 | tf_op jit(solution)/shard_map/ppermute | solution.py:36
  (156 shorter events, 92.7 us)
Async XLA Ops:
  4.4 16.3 %collective-permute-start.1 = (bf16[256,640]{1,0:T(8,128)(2,1)S(1)}, bf16[256,640]{1,0:T(8,128)(2,1)S(1)}, u32[]{:S(2)}, u32[]{:S(2)}) collective-permute-start(bf16[256,640]{1,0:T(8,128)(2,1)S(1)} %shard_map.103.here), channel_id=1, source_target_pairs={{0,2},{2,0},{1,3},{3,1},{4,6},{6,4},{5,7},{7,5},{8,10},{10,8},{9,1... | collective-permute-start | bytes 983048 | tf_op jit(solution)/shard_map/ppermute | solution.py:36
  7.4 13.3 %collective-permute-start = (bf16[1024,128]{1,0:T(8,128)(2,1)S(1)}, bf16[1024,128]{1,0:T(8,128)(2,1)S(1)}, u32[]{:S(2)}, u32[]{:S(2)}) collective-permute-start(bf16[1024,128]{1,0:T(8,128)(2,1)S(1)} %shard_map.102), channel_id=1, source_target_pairs={{0,2},{2,0},{1,3},{3,1},{4,6},{6,4},{5,7},{7,5},{8,10},{10,8},{9,1... | collective-permute-start | bytes 786440 | tf_op jit(solution)/shard_map/ppermute | solution.py:36
  24.3 33.9 %all-to-all-start = ((bf16[8,128,256]{2,1,0:T(8,128)(2,1)}), bf16[8,128,256]{2,1,0:T(8,128)(2,1)}, u32[]{:S(2)}, u32[]{:S(2)}) async-start(bf16[8,128,256]{2,1,0:T(8,128)(2,1)} %shard_map.105), calls=%async_computation | async-start | bytes 1048576 | tf_op jit(solution)/shard_map/all_to_all | solution.py:460
  30.4 23.6 %collective-permute-start.2 = (bf16[1024,256]{1,0:T(8,128)(2,1)S(1)}, bf16[1024,256]{1,0:T(8,128)(2,1)}, u32[]{:S(2)}, u32[]{:S(2)}) collective-permute-start(bf16[1024,256]{1,0:T(8,128)(2,1)S(1)} %shard_map.104.refs_0_.rest_0_.own), channel_id=1, source_target_pairs={{0,4},{4,0},{8,12},{12,8},{1,5},{5,1},{9,13},{13,9},{2,6},{6,2},{1... | collective-permute-start | bytes 1572872 | tf_op jit(solution)/shard_map/ppermute | solution.py:40
  36.3 26.6 %collective-permute-start.4 = (bf16[1024,256]{1,0:T(8,128)(2,1)S(1)}, bf16[1024,256]{1,0:T(8,128)(2,1)}, u32[]{:S(2)}, u32[]{:S(2)}) collective-permute-start(bf16[1024,256]{1,0:T(8,128)(2,1)S(1)} %shard_map.108.refs_0_.own), channel_id=1, source_target_pairs={{0,4},{4,0},{8,12},{12,8},{1,5},{5,1},{9,13},{13,9},{2,6},{6,2},{1... | collective-permute-start | bytes 1572872 | tf_op jit(solution)/shard_map/ppermute | solution.py:40
  56.6 34.1 %collective-permute-start.10 = (bf16[1024,512]{1,0:T(8,128)(2,1)}, bf16[1024,512]{1,0:T(8,128)(2,1)}, u32[]{:S(2)}, u32[]{:S(2)}) collective-permute-start(bf16[1024,512]{1,0:T(8,128)(2,1)} %shard_map.109), channel_id=1, source_target_pairs={{4,8},{8,4},{5,9},{9,5},{6,10},{10,6},{7,11},{11,7},{20,24},{24,20... | collective-permute-start | bytes 3145736 | tf_op jit(solution)/shard_map/ppermute | solution.py:40
  59.8 15.1 %collective-permute-start.6 = (bf16[256,1024]{1,0:T(8,128)(2,1)}, bf16[256,1024]{1,0:T(8,128)(2,1)}, u32[]{:S(2)}, u32[]{:S(2)}) collective-permute-start(bf16[256,1024]{1,0:T(8,128)(2,1)} %copy-done.22), channel_id=1, source_target_pairs={{0,2},{2,0},{1,3},{3,1},{4,6},{6,4},{5,7},{7,5},{8,10},{10,8},{9,1... | collective-permute-start | bytes 1572872 | tf_op jit(solution)/shard_map/ppermute | solution.py:36
  65.5 14.5 %collective-permute-start.5 = (f32[512,128]{1,0:T(8,128)S(1)}, f32[512,128]{1,0:T(8,128)S(1)}, u32[]{:S(2)}, u32[]{:S(2)}) collective-permute-start(f32[512,128]{1,0:T(8,128)S(1)} %shard_map.112.part), channel_id=1, source_target_pairs={{0,2},{2,0},{1,3},{3,1},{4,6},{6,4},{5,7},{7,5},{8,10},{10,8},{9,1... | collective-permute-start | bytes 786440 | tf_op jit(solution)/shard_map/ppermute | solution.py:36
  67.0 36.4 %collective-permute-start.8 = (bf16[1024,512]{1,0:T(8,128)(2,1)}, bf16[1024,512]{1,0:T(8,128)(2,1)}, u32[]{:S(2)}, u32[]{:S(2)}) collective-permute-start(bf16[1024,512]{1,0:T(8,128)(2,1)} %shard_map.109), channel_id=1, source_target_pairs={{0,16},{16,0},{1,17},{17,1},{2,18},{18,2},{3,19},{19,3},{4,20},{20... | collective-permute-start | bytes 3145736 | tf_op jit(solution)/shard_map/ppermute | solution.py:36
  94.4 25.8 %collective-permute-start.13 = (bf16[512,1024]{1,0:T(8,128)(2,1)S(1)}, bf16[512,1024]{1,0:T(8,128)(2,1)S(1)}, u32[]{:S(2)}, u32[]{:S(2)}) collective-permute-start(bf16[512,1024]{1,0:T(8,128)(2,1)S(1)} %shard_map.115.x_here.x_mine.tokens), channel_id=1, source_target_pairs={{0,4},{12,8},{1,5},{13,9},{2,6},{14,10},{3,7},{15,11},{16,20},{28,... | collective-permute-start | bytes 3145736 | tf_op jit(solution)/shard_map/ppermute | solution.py:40
  98.9 23.6 %collective-permute-start.12 = (bf16[1024,512]{1,0:T(8,128)(2,1)S(1)}, bf16[1024,512]{1,0:T(8,128)(2,1)}, u32[]{:S(2)}, u32[]{:S(2)}) collective-permute-start(bf16[1024,512]{1,0:T(8,128)(2,1)S(1)} %copy-done.19), channel_id=1, source_target_pairs={{4,8},{8,4},{5,9},{9,5},{6,10},{10,6},{7,11},{11,7},{20,24},{24,20... | collective-permute-start | bytes 3145736 | tf_op jit(solution)/shard_map/ppermute | solution.py:40
  100.5 12.4 %collective-permute-start.7 = (bf16[256,1024]{1,0:T(8,128)(2,1)S(1)}, bf16[256,1024]{1,0:T(8,128)(2,1)S(1)}, u32[]{:S(2)}, u32[]{:S(2)}) collective-permute-start(bf16[256,1024]{1,0:T(8,128)(2,1)S(1)} %shard_map.114), channel_id=1, source_target_pairs={{0,2},{2,0},{1,3},{3,1},{4,6},{6,4},{5,7},{7,5},{8,10},{10,8},{9,1... | collective-permute-start | bytes 1572872 | tf_op jit(solution)/shard_map/ppermute | solution.py:36
  103.4 19.1 %collective-permute-start.11 = (bf16[1024,256]{1,0:T(8,128)(2,1)}, bf16[1024,256]{1,0:T(8,128)(2,1)S(1)}, u32[]{:S(2)}, u32[]{:S(2)}) collective-permute-start(bf16[1024,256]{1,0:T(8,128)(2,1)} %collective-permute-done.4.refs_1_.near), channel_id=1, source_target_pairs={{0,16},{16,0},{1,17},{17,1},{2,18},{18,2},{3,19},{19,3},{4,20},{20... | collective-permute-start | bytes 1572872 | tf_op jit(solution)/shard_map/ppermute | solution.py:36
  104.9 28.2 %collective-permute-start.18 = (bf16[1024,512]{1,0:T(8,128)(2,1)}, bf16[1024,512]{1,0:T(8,128)(2,1)}, u32[]{:S(2)}, u32[]{:S(2)}) collective-permute-start(bf16[1024,512]{1,0:T(8,128)(2,1)} %collective-permute-done.10.crossed), channel_id=1, source_target_pairs={{4,0},{8,12},{5,1},{9,13},{6,2},{10,14},{7,3},{11,15},{20,16},{24,... | collective-permute-start | bytes 3145736 | tf_op jit(solution)/shard_map/ppermute | solution.py:40
  123.4 27.5 %collective-permute-start.17 = (bf16[512,1024]{1,0:T(8,128)(2,1)S(1)}, bf16[512,1024]{1,0:T(8,128)(2,1)}, u32[]{:S(2)}, u32[]{:S(2)}) collective-permute-start(bf16[512,1024]{1,0:T(8,128)(2,1)S(1)} %shard_map.118.x_here.x_other.tokens), channel_id=1, source_target_pairs={{0,4},{12,8},{1,5},{13,9},{2,6},{14,10},{3,7},{15,11},{16,20},{28,... | collective-permute-start | bytes 3145736 | tf_op jit(solution)/shard_map/ppermute | solution.py:40
  128.7 25.3 %collective-permute-start.16 = (bf16[1024,512]{1,0:T(8,128)(2,1)}, bf16[1024,512]{1,0:T(8,128)(2,1)}, u32[]{:S(2)}, u32[]{:S(2)}) collective-permute-start(bf16[1024,512]{1,0:T(8,128)(2,1)} %shard_map.119), channel_id=1, source_target_pairs={{4,8},{8,4},{5,9},{9,5},{6,10},{10,6},{7,11},{11,7},{20,24},{24,20... | collective-permute-start | bytes 3145736 | tf_op jit(solution)/shard_map/ppermute | solution.py:40
  130.4 27.5 %collective-permute-start.15 = (bf16[1024,512]{1,0:T(8,128)(2,1)}, bf16[1024,512]{1,0:T(8,128)(2,1)}, u32[]{:S(2)}, u32[]{:S(2)}) collective-permute-start(bf16[1024,512]{1,0:T(8,128)(2,1)} %collective-permute-done.12.crossed), channel_id=1, source_target_pairs={{4,0},{8,12},{5,1},{9,13},{6,2},{10,14},{7,3},{11,15},{20,16},{24,... | collective-permute-start | bytes 3145736 | tf_op jit(solution)/shard_map/ppermute | solution.py:40
  134.9 32.8 %collective-permute-start.20 = (bf16[1024,512]{1,0:T(8,128)(2,1)S(1)}, bf16[1024,512]{1,0:T(8,128)(2,1)S(1)}, u32[]{:S(2)}, u32[]{:S(2)}) collective-permute-start(bf16[1024,512]{1,0:T(8,128)(2,1)S(1)} %shard_map.121.rest_2_.far), channel_id=1, source_target_pairs={{0,16},{16,0},{1,17},{17,1},{2,18},{18,2},{3,19},{19,3},{4,20},{20... | collective-permute-start | bytes 3145736 | tf_op jit(solution)/shard_map/ppermute | solution.py:36
  153.3 30.8 %collective-permute-start.26 = (bf16[1024,512]{1,0:T(8,128)(2,1)S(1)}, bf16[1024,512]{1,0:T(8,128)(2,1)S(1)}, u32[]{:S(2)}, u32[]{:S(2)}) collective-permute-start(bf16[1024,512]{1,0:T(8,128)(2,1)S(1)} %shard_map.122), channel_id=1, source_target_pairs={{4,8},{8,4},{5,9},{9,5},{6,10},{10,6},{7,11},{11,7},{20,24},{24,20... | collective-permute-start | bytes 3145736 | tf_op jit(solution)/shard_map/ppermute | solution.py:40
  159.5 36.5 %collective-permute-start.19 = (bf16[1024,512]{1,0:T(8,128)(2,1)S(1)}, bf16[1024,512]{1,0:T(8,128)(2,1)S(1)}, u32[]{:S(2)}, u32[]{:S(2)}) collective-permute-start(bf16[1024,512]{1,0:T(8,128)(2,1)S(1)} %shard_map.124.far), channel_id=1, source_target_pairs={{0,16},{16,0},{1,17},{17,1},{2,18},{18,2},{3,19},{19,3},{4,20},{20... | collective-permute-start | bytes 3145736 | tf_op jit(solution)/shard_map/ppermute | solution.py:36
  161.1 14.8 %collective-permute-start.23 = (bf16[1024,256]{1,0:T(8,128)(2,1)S(1)}, bf16[1024,256]{1,0:T(8,128)(2,1)S(1)}, u32[]{:S(2)}, u32[]{:S(2)}) collective-permute-start(bf16[1024,256]{1,0:T(8,128)(2,1)S(1)} %shard_map.123), channel_id=1, source_target_pairs={{4,0},{8,12},{5,1},{9,13},{6,2},{10,14},{7,3},{11,15},{20,16},{24,... | collective-permute-start | bytes 1572872 | tf_op jit(solution)/shard_map/ppermute | solution.py:40
  166.2 17.3 %collective-permute-start.22 = (bf16[256,1024]{1,0:T(8,128)(2,1)S(1)}, bf16[256,1024]{1,0:T(8,128)(2,1)S(1)}, u32[]{:S(2)}, u32[]{:S(2)}) collective-permute-start(bf16[256,1024]{1,0:T(8,128)(2,1)S(1)} %get-tuple-element.120), channel_id=1, source_target_pairs={{0,2},{2,0},{1,3},{3,1},{4,6},{6,4},{5,7},{7,5},{8,10},{10,8},{9,1... | collective-permute-start | bytes 1572872 | tf_op jit(solution)/shard_map/ppermute | solution.py:36
  184.6 20.4 %collective-permute-start.31 = (bf16[1024,256]{1,0:T(8,128)(2,1)S(1)}, bf16[1024,256]{1,0:T(8,128)(2,1)S(1)}, u32[]{:S(2)}, u32[]{:S(2)}) collective-permute-start(bf16[1024,256]{1,0:T(8,128)(2,1)S(1)} %shard_map.130), channel_id=1, source_target_pairs={{4,0},{8,12},{5,1},{9,13},{6,2},{10,14},{7,3},{11,15},{20,16},{24,... | collective-permute-start | bytes 1572872 | tf_op jit(solution)/shard_map/ppermute | solution.py:40
  199.7 12.6 %collective-permute-start.27 = (bf16[256,1024]{1,0:T(8,128)(2,1)S(1)}, bf16[256,1024]{1,0:T(8,128)(2,1)S(1)}, u32[]{:S(2)}, u32[]{:S(2)}) collective-permute-start(bf16[256,1024]{1,0:T(8,128)(2,1)S(1)} %get-tuple-element.132), channel_id=1, source_target_pairs={{0,2},{2,0},{1,3},{3,1},{4,6},{6,4},{5,7},{7,5},{8,10},{10,8},{9,1... | collective-permute-start | bytes 1572872 | tf_op jit(solution)/shard_map/ppermute | solution.py:36
  (43 other events, 444.1 us)

commit v12 on v10

--- a/solution.py
+++ b/solution.py
@@ -479,8 +479,6 @@
     crossing = done(side_by_side(down_piece, down_near))
     down_crossed = along(crossing, MIDDLE)
     down_other = swap(crossing, "rep")
-    x_mine = done(tokens_of(0, tokens, step(x_got[0])))
-    x_in = [along(x_mine, INWARD)]
     back_wide, back_sent = kernel_call(
         back_end_kernel,
         [like(both, number * size), like(both, wide)],
@@ -492,12 +490,14 @@
     back_in = along(done(back_sent), INWARD)
     crossing = done(side_by_side(weight_here, step(weight_near)))
     weight_crossed = along(crossing, MIDDLE)
+    x_got.append(swap(done(columns_at(3, step(tokens))), "own"))
     back_in_wide = done(
         kernel_call(
             spread_in_kernel, [like(both, number * size)], step(back_in), scalars=numbers
         )[0]
     )
-    x_got.append(swap(done(columns_at(3, step(tokens))), "own"))
+    x_mine = done(tokens_of(0, tokens, step(x_got[0])))
+    x_in = [along(x_mine, INWARD)]
     weight_other = done(rows_at(1, step(frozen_value_weight), eighth))
     down_crossed = done(step(down_crossed))
     down_outer = along(down_crossed, OUTWARD)

time: 214 us -> 209 us (0.977)
  waiting for transfers between devices: 80.6 us -> 72.8 us
    ppermute x16, waiting for transfers between devices: 40.8 us -> 34.7 us  [along(): return lax.ppermute(value, 'fsdp', pairs)]
    unnamed x51 -> x55, local copies, waits for them, and re-layouts: 8.71 us -> 10.4 us
  transfers between devices with their start and end apart: 37 -> 37, of which waited for: 17 -> 16; matrix products, arithmetic and copies ran while one was open for 1% -> 1% of each run, Pallas kernels for 26% -> 27%
where the time goes in v12:
time: 209 us; the launch traced here: 208 us
  waiting for transfers between devices  72.8 us (35%)
  Pallas kernels  61.6 us (29%)
  starting transfers between devices  61.5 us (29%)
  local copies, waits for them, and re-layouts  10.6 us (5%)
    pallas_call x39, Pallas kernels, kernel_call(): pl.pallas_call(body, out_shape=list(outs), in_specs=specs, out_specs=[pl....  61.6 us
    ppermute x20, waiting for transfers between devices, swap(): return lax.ppermute(value, axis, PAIR)  38 us
    ppermute x16, starting transfers between devices, along(): return lax.ppermute(value, 'fsdp', pairs)  35.5 us
    ppermute x16, waiting for transfers between devices, along(): return lax.ppermute(value, 'fsdp', pairs)  34.7 us
    ppermute x20, starting transfers between devices, swap(): return lax.ppermute(value, axis, PAIR)  18.7 us
    unnamed x55, local copies, waits for them, and re-layouts  10.4 us
    all_to_all x1, starting transfers between devices, body_line(): lax.all_to_all(done(up_sent), ('fsdp', 'own'), split_axis=0, concat_axis=...  7.25 us
  transfers between devices with their start and end apart: 37, of which 16 were waited for; matrix products, arithmetic and copies ran while one was open for 1% of the time, Pallas kernels for 27%

profile of v12, /device:TPU:0, one launch (start us, length us, event | category | flops | bytes accessed | tf_op | source)
XLA Modules:
  0.0 207.8 jit_solution(3261078780770353940)
XLA Ops:
  2.5 7.3 %all-to-all-start = ((bf16[8,128,256]{2,1,0:T(8,128)(2,1)}), bf16[8,128,256]{2,1,0:T(8,128)(2,1)S(1)}, u32[]{:S(2)}, u32[]{:S(2)}) async-start(bf16[8,128,256]{2,1,0:T(8,128)(2,1)} %shard_map.102), calls=%async_computation | async-start | bytes 1048576 | tf_op jit(solution)/shard_map/all_to_all | solution.py:441
  19.2 5.4 %collective-permute-done.1.refs_1_ = bf16[1024,128]{1,0:T(8,128)(2,1)} collective-permute-done((bf16[1024,128]{1,0:T(8,128)(2,1)S(1)}, bf16[1024,128]{1,0:T(8,128)(2,1)}, u32[]{:S(2)}, u32[]{:S(2)}) %collective-permute-start.1) | collective-permute-done | bytes 262176 | tf_op jit(solution)/shard_map/ppermute | solution.py:36
  28.2 3.4 %collective-permute-done.there = bf16[256,640]{1,0:T(8,128)(2,1)} collective-permute-done((bf16[256,640]{1,0:T(8,128)(2,1)S(1)}, bf16[256,640]{1,0:T(8,128)(2,1)}, u32[]{:S(2)}, u32[]{:S(2)}) %collective-permute-start) | collective-permute-done | bytes 327712 | tf_op jit(solution)/shard_map/ppermute | solution.py:36
  42.4 2.6 %shard_map.111 = bf16[1024,512]{1,0:T(8,128)(2,1)} custom-call(s32[4]{0:T(128)S(1)} %pad_add_fusion.numbers, bf16[1024,256]{1,0:T(8,128)(2,1)S(1)} %shard_map.106.refs_0_.rest_0_.own, bf16[1024,256]{1,0:T(8,128)(2,1)} %collective-permute-done.5.refs_1_.rest_1_.near), custom_call_target="tpu_custom_call" | custom-call | tf_op jit(solution)/shard_map/pallas_call | solution.py:48
  51.7 4.0 %collective-permute-start.10 = (bf16[512,256]{1,0:T(8,128)(2,1)S(1)}, bf16[512,256]{1,0:T(8,128)(2,1)S(1)}, u32[]{:S(2)}, u32[]{:S(2)}) collective-permute-start(bf16[512,256]{1,0:T(8,128)(2,1)S(1)} %get-tuple-element.93), channel_id=1, source_target_pairs={{0,4},{12,8},{1,5},{13,9},{2,6},{14,10},{3,7},{15,11},{16,20},{28,... | collective-permute-start | bytes 786440 | tf_op jit(solution)/shard_map/ppermute | solution.py:40
  63.0 4.5 %collective-permute-start.13 = (bf16[512,1024]{1,0:T(8,128)(2,1)S(1)}, bf16[512,1024]{1,0:T(8,128)(2,1)S(1)}, u32[]{:S(2)}, u32[]{:S(2)}) collective-permute-start(bf16[512,1024]{1,0:T(8,128)(2,1)S(1)} %shard_map.116.x_here.x_mine.tokens), channel_id=1, source_target_pairs={{0,4},{12,8},{1,5},{13,9},{2,6},{14,10},{3,7},{15,11},{16,20},{28,... | collective-permute-start | bytes 3145736 | tf_op jit(solution)/shard_map/ppermute | solution.py:40
  74.6 6.1 %collective-permute-done.7.refs_1_ = bf16[256,1024]{1,0:T(8,128)(2,1)S(1)} collective-permute-done((bf16[256,1024]{1,0:T(8,128)(2,1)S(1)}, bf16[256,1024]{1,0:T(8,128)(2,1)S(1)}, u32[]{:S(2)}, u32[]{:S(2)}) %collective-permute-start.7) | collective-permute-done | bytes 524320 | tf_op jit(solution)/shard_map/ppermute | solution.py:36
  81.3 6.5 %collective-permute-done.13.x_in = bf16[512,1024]{1,0:T(8,128)(2,1)S(1)} collective-permute-done((bf16[512,1024]{1,0:T(8,128)(2,1)S(1)}, bf16[512,1024]{1,0:T(8,128)(2,1)S(1)}, u32[]{:S(2)}, u32[]{:S(2)}) %collective-permute-start.13) | collective-permute-done | bytes 1048608 | tf_op jit(solution)/shard_map/ppermute | solution.py:40
  87.8 2.3 %shard_map.119 = bf16[1024,512]{1,0:T(8,128)(2,1)} custom-call(bf16[512,1024]{1,0:T(8,128)(2,1)S(1)} %shard_map.116.x_here.x_mine.tokens, bf16[512,1024]{1,0:T(8,128)(2,1)S(1)} %get-tuple-element.104.back, bf16[512,1024]{1,0:T(8,128)(2,1)S(1)} %collective-permute-done.13.x_in, bf16[512,1024]{1,0:T(8,128)(2,1)S(1)} %shard_map.115.back_in), custom_call_target="tpu_custom_call" | custom-call | tf_op jit(solution)/shard_map/pallas_call | solution.py:48
  90.9 8.4 %collective-permute-start.17 = (bf16[512,1024]{1,0:T(8,128)(2,1)S(1)}, bf16[512,1024]{1,0:T(8,128)(2,1)}, u32[]{:S(2)}, u32[]{:S(2)}) collective-permute-start(bf16[512,1024]{1,0:T(8,128)(2,1)S(1)} %shard_map.118.x_here.x_other.tokens), channel_id=1, source_target_pairs={{0,4},{12,8},{1,5},{13,9},{2,6},{14,10},{3,7},{15,11},{16,20},{28,... | collective-permute-start | bytes 3145736 | tf_op jit(solution)/shard_map/ppermute | solution.py:40
  107.1 14.3 %collective-permute-done.17.x_in = bf16[512,1024]{1,0:T(8,128)(2,1)} collective-permute-done((bf16[512,1024]{1,0:T(8,128)(2,1)S(1)}, bf16[512,1024]{1,0:T(8,128)(2,1)}, u32[]{:S(2)}, u32[]{:S(2)}) %collective-permute-start.17) | collective-permute-done | bytes 1048608 | tf_op jit(solution)/shard_map/ppermute | solution.py:40
  121.4 2.5 %shard_map.122 = bf16[1024,512]{1,0:T(8,128)(2,1)S(1)} custom-call(bf16[512,1024]{1,0:T(8,128)(2,1)S(1)} %shard_map.118.x_here.x_other.tokens, bf16[512,1024]{1,0:T(8,128)(2,1)S(1)} %get-tuple-element.104.back, bf16[512,1024]{1,0:T(8,128)(2,1)} %collective-permute-done.17.x_in, bf16[512,1024]{1,0:T(8,128)(2,1)S(1)} %copy-done.3), custom_call_target="tpu_custom_call" | custom-call | tf_op jit(solution)/shard_map/pallas_call | solution.py:48
  126.4 2.1 %collective-permute-done.15.outer = bf16[1024,512]{1,0:T(8,128)(2,1)} collective-permute-done((bf16[1024,512]{1,0:T(8,128)(2,1)}, bf16[1024,512]{1,0:T(8,128)(2,1)}, u32[]{:S(2)}, u32[]{:S(2)}) %collective-permute-start.15) | collective-permute-done | bytes 1048608 | tf_op jit(solution)/shard_map/ppermute | solution.py:40
  133.2 3.7 %shard_map.125 = (bf16[256,1024]{1,0:T(8,128)(2,1)S(1)}, bf16[256,1024]{1,0:T(8,128)(2,1)S(1)}) custom-call(bf16[512,1024]{1,0:T(8,128)(2,1)S(1)} %shard_map.120.dy, bf16[512,1024]{1,0:T(8,128)(2,1)S(1)} %get-tuple-element.104.back, bf16[1024,256]{1,0:T(8,128)(2,1)} %shard_map.109.refs_0_.own, bf16[1024,256]{1,0:T(8,128)(2,1)} %collective-permute-done.2.refs_1_.near, ...), custom_call_target="tpu_custom_call" | custom-call | tf_op jit(solution)/shard_map/pallas_call | solution.py:48
  137.2 3.8 %shard_map.126.left = f32[512,128]{1,0:T(8,128)S(1)} custom-call(s32[24]{0:T(128)S(1)} %concatenate.3.numbers, bf16[512,128]{1,0:T(8,128)(2,1)S(1)} %get-tuple-element.86.ids, bf16[512,1024]{1,0:T(8,128)(2,1)S(1)} %shard_map.116.x_here.x_mine.tokens, bf16[512,1024]{1,0:T(8,128)(2,1)S(1)} %shard_map.118.x_here.x_other.tokens, ...), custom_call_target="tpu_custom_call" | custom-call | tf_op jit(solution)/shard_map/pallas_call | solution.py:48
  141.0 5.5 %collective-permute-done.23.outer = bf16[1024,256]{1,0:T(8,128)(2,1)S(1)} collective-permute-done((bf16[1024,256]{1,0:T(8,128)(2,1)S(1)}, bf16[1024,256]{1,0:T(8,128)(2,1)S(1)}, u32[]{:S(2)}, u32[]{:S(2)}) %collective-permute-start.23) | collective-permute-done | bytes 524320 | tf_op jit(solution)/shard_map/ppermute | solution.py:40
  148.6 4.1 %shard_map.128 = (f32[2,512,256]{2,1,0:T(8,128)S(1)}, f32[2,512,256]{2,1,0:T(8,128)S(1)}) custom-call(s32[5]{0:T(128)S(1)} %convert_element_type.3.flags, bf16[512,1024]{1,0:T(8,128)(2,1)S(1)} %shard_map.116.x_here.x_mine.tokens, bf16[1024,256]{1,0:T(8,128)(2,1)} %shard_map.109.refs_0_.own, bf16[1024,256]{1,0:T(8,128)(2,1)} %collective-permute-done.2.refs_1_.near, ...), custom_call_target="tpu_custom_call" | custom-call | tf_op jit(solution)/shard_map/pallas_call | solution.py:48
  156.7 5.3 %collective-permute-done.25.refs_2_ = bf16[1024,128]{1,0:T(8,128)(2,1)S(1)} collective-permute-done((bf16[1024,128]{1,0:T(8,128)(2,1)S(1)}, bf16[1024,128]{1,0:T(8,128)(2,1)S(1)}, u32[]{:S(2)}, u32[]{:S(2)}) %collective-permute-start.25) | collective-permute-done | bytes 262176 | tf_op jit(solution)/shard_map/ppermute | solution.py:36
  162.0 2.8 %collective-permute-done.24.got = f32[512,128]{1,0:T(8,128)S(1)} collective-permute-done((f32[512,128]{1,0:T(8,128)S(1)}, f32[512,128]{1,0:T(8,128)S(1)}, u32[]{:S(2)}, u32[]{:S(2)}) %collective-permute-start.24) | collective-permute-done | bytes 262176 | tf_op jit(solution)/shard_map/ppermute | solution.py:36
  166.3 3.6 %shard_map.132 = (bf16[256,1024]{1,0:T(8,128)(2,1)S(1)}, bf16[256,1024]{1,0:T(8,128)(2,1)S(1)}) custom-call(bf16[512,1024]{1,0:T(8,128)(2,1)S(1)} %shard_map.120.dy, bf16[512,1024]{1,0:T(8,128)(2,1)S(1)} %get-tuple-element.104.back, bf16[1024,256]{1,0:T(8,128)(2,1)S(1)} %copy-done.11, bf16[1024,256]{1,0:T(8,128)(2,1)S(1)} %copy-done.17, ...), custom_call_target="tpu_custom_call" | custom-call | tf_op jit(solution)/shard_map/pallas_call | solution.py:48
  179.1 2.8 %collective-permute-done.29.third = bf16[256,256]{1,0:T(8,128)(2,1)S(1)} collective-permute-done((bf16[256,256]{1,0:T(8,128)(2,1)S(1)}, bf16[256,256]{1,0:T(8,128)(2,1)S(1)}, u32[]{:S(2)}, u32[]{:S(2)}) %collective-permute-start.29) | collective-permute-done | bytes 131104 | tf_op jit(solution)/shard_map/ppermute | solution.py:40
  182.5 3.5 %shard_map.135 = (f32[2,512,256]{2,1,0:T(8,128)S(1)}, f32[2,512,256]{2,1,0:T(8,128)S(1)}) custom-call(s32[5]{0:T(128)S(1)} %convert_element_type.3.flags, bf16[512,1024]{1,0:T(8,128)(2,1)S(1)} %shard_map.118.x_here.x_other.tokens, bf16[1024,256]{1,0:T(8,128)(2,1)S(1)} %copy-done.11, bf16[1024,256]{1,0:T(8,128)(2,1)S(1)} %copy-done.17, ...), custom_call_target="tpu_custom_call" | custom-call | tf_op jit(solution)/shard_map/pallas_call | solution.py:48
  186.7 8.1 %collective-permute-done.33.refs_3_ = bf16[1024,128]{1,0:T(8,128)(2,1)S(1)} collective-permute-done((bf16[1024,128]{1,0:T(8,128)(2,1)S(1)}, bf16[1024,128]{1,0:T(8,128)(2,1)S(1)}, u32[]{:S(2)}, u32[]{:S(2)}) %collective-permute-start.33) | collective-permute-done | bytes 262176 | tf_op jit(solution)/shard_map/ppermute | solution.py:36
  199.7 4.5 %collective-permute-done.34.got = bf16[2,256,256]{2,1,0:T(8,128)(2,1)S(1)} collective-permute-done((bf16[2,256,256]{2,1,0:T(8,128)(2,1)S(1)}, bf16[2,256,256]{2,1,0:T(8,128)(2,1)S(1)}, u32[]{:S(2)}, u32[]{:S(2)}) %collective-permute-start.34) | collective-permute-done | bytes 262176 | tf_op jit(solution)/shard_map/ppermute | solution.py:36
  (150 shorter events, 89.7 us)
Async XLA Ops:
  2.5 29.1 %all-to-all-start = ((bf16[8,128,256]{2,1,0:T(8,128)(2,1)}), bf16[8,128,256]{2,1,0:T(8,128)(2,1)S(1)}, u32[]{:S(2)}, u32[]{:S(2)}) async-start(bf16[8,128,256]{2,1,0:T(8,128)(2,1)} %shard_map.102), calls=%async_computation | async-start | bytes 1048576 | tf_op jit(solution)/shard_map/all_to_all | solution.py:441
  11.7 12.9 %collective-permute-start.1 = (bf16[1024,128]{1,0:T(8,128)(2,1)S(1)}, bf16[1024,128]{1,0:T(8,128)(2,1)}, u32[]{:S(2)}, u32[]{:S(2)}) collective-permute-start(bf16[1024,128]{1,0:T(8,128)(2,1)S(1)} %shard_map.103), channel_id=1, source_target_pairs={{0,2},{2,0},{1,3},{3,1},{4,6},{6,4},{5,7},{7,5},{8,10},{10,8},{9,1... | collective-permute-start | bytes 786440 | tf_op jit(solution)/shard_map/ppermute | solution.py:36
  15.6 16.0 %collective-permute-start = (bf16[256,640]{1,0:T(8,128)(2,1)S(1)}, bf16[256,640]{1,0:T(8,128)(2,1)}, u32[]{:S(2)}, u32[]{:S(2)}) collective-permute-start(bf16[256,640]{1,0:T(8,128)(2,1)S(1)} %shard_map.104.here), channel_id=1, source_target_pairs={{0,2},{2,0},{1,3},{3,1},{4,6},{6,4},{5,7},{7,5},{8,10},{10,8},{9,1... | collective-permute-start | bytes 983048 | tf_op jit(solution)/shard_map/ppermute | solution.py:36
  17.1 25.3 %collective-permute-start.6 = (bf16[256,1024]{1,0:T(8,128)(2,1)}, bf16[256,1024]{1,0:T(8,128)(2,1)}, u32[]{:S(2)}, u32[]{:S(2)}) collective-permute-start(bf16[256,1024]{1,0:T(8,128)(2,1)} %shard_map.105), channel_id=1, source_target_pairs={{0,2},{2,0},{1,3},{3,1},{4,6},{6,4},{5,7},{7,5},{8,10},{10,8},{9,1... | collective-permute-start | bytes 1572872 | tf_op jit(solution)/shard_map/ppermute | solution.py:36
  26.2 16.3 %collective-permute-start.5 = (bf16[1024,256]{1,0:T(8,128)(2,1)S(1)}, bf16[1024,256]{1,0:T(8,128)(2,1)}, u32[]{:S(2)}, u32[]{:S(2)}) collective-permute-start(bf16[1024,256]{1,0:T(8,128)(2,1)S(1)} %shard_map.106.refs_0_.rest_0_.own), channel_id=1, source_target_pairs={{0,4},{4,0},{8,12},{12,8},{1,5},{5,1},{9,13},{13,9},{2,6},{6,2},{1... | collective-permute-start | bytes 1572872 | tf_op jit(solution)/shard_map/ppermute | solution.py:40
  38.3 17.4 %collective-permute-start.2 = (bf16[1024,256]{1,0:T(8,128)(2,1)}, bf16[1024,256]{1,0:T(8,128)(2,1)}, u32[]{:S(2)}, u32[]{:S(2)}) collective-permute-start(bf16[1024,256]{1,0:T(8,128)(2,1)} %shard_map.109.refs_0_.own), channel_id=1, source_target_pairs={{0,4},{4,0},{8,12},{12,8},{1,5},{5,1},{9,13},{13,9},{2,6},{6,2},{1... | collective-permute-start | bytes 1572872 | tf_op jit(solution)/shard_map/ppermute | solution.py:40
  45.1 26.7 %collective-permute-start.9 = (bf16[1024,512]{1,0:T(8,128)(2,1)}, bf16[1024,512]{1,0:T(8,128)(2,1)}, u32[]{:S(2)}, u32[]{:S(2)}) collective-permute-start(bf16[1024,512]{1,0:T(8,128)(2,1)} %shard_map.111), channel_id=1, source_target_pairs={{4,8},{8,4},{5,9},{9,5},{6,10},{10,6},{7,11},{11,7},{20,24},{24,20... | collective-permute-start | bytes 3145736 | tf_op jit(solution)/shard_map/ppermute | solution.py:40
  46.7 25.1 %collective-permute-start.8 = (bf16[1024,512]{1,0:T(8,128)(2,1)}, bf16[1024,512]{1,0:T(8,128)(2,1)}, u32[]{:S(2)}, u32[]{:S(2)}) collective-permute-start(bf16[1024,512]{1,0:T(8,128)(2,1)} %shard_map.111), channel_id=1, source_target_pairs={{0,16},{16,0},{1,17},{17,1},{2,18},{18,2},{3,19},{19,3},{4,20},{20... | collective-permute-start | bytes 3145736 | tf_op jit(solution)/shard_map/ppermute | solution.py:36
  63.0 24.7 %collective-permute-start.13 = (bf16[512,1024]{1,0:T(8,128)(2,1)S(1)}, bf16[512,1024]{1,0:T(8,128)(2,1)S(1)}, u32[]{:S(2)}, u32[]{:S(2)}) collective-permute-start(bf16[512,1024]{1,0:T(8,128)(2,1)S(1)} %shard_map.116.x_here.x_mine.tokens), channel_id=1, source_target_pairs={{0,4},{12,8},{1,5},{13,9},{2,6},{14,10},{3,7},{15,11},{16,20},{28,... | collective-permute-start | bytes 3145736 | tf_op jit(solution)/shard_map/ppermute | solution.py:40
  67.5 22.6 %collective-permute-start.12 = (bf16[1024,512]{1,0:T(8,128)(2,1)S(1)}, bf16[1024,512]{1,0:T(8,128)(2,1)}, u32[]{:S(2)}, u32[]{:S(2)}) collective-permute-start(bf16[1024,512]{1,0:T(8,128)(2,1)S(1)} %shard_map.113), channel_id=1, source_target_pairs={{4,8},{8,4},{5,9},{9,5},{6,10},{10,6},{7,11},{11,7},{20,24},{24,20... | collective-permute-start | bytes 3145736 | tf_op jit(solution)/shard_map/ppermute | solution.py:40
  69.1 11.5 %collective-permute-start.7 = (bf16[256,1024]{1,0:T(8,128)(2,1)S(1)}, bf16[256,1024]{1,0:T(8,128)(2,1)S(1)}, u32[]{:S(2)}, u32[]{:S(2)}) collective-permute-start(bf16[256,1024]{1,0:T(8,128)(2,1)S(1)} %shard_map.114), channel_id=1, source_target_pairs={{0,2},{2,0},{1,3},{3,1},{4,6},{6,4},{5,7},{7,5},{8,10},{10,8},{9,1... | collective-permute-start | bytes 1572872 | tf_op jit(solution)/shard_map/ppermute | solution.py:36
  71.8 18.3 %collective-permute-start.11 = (bf16[1024,256]{1,0:T(8,128)(2,1)}, bf16[1024,256]{1,0:T(8,128)(2,1)S(1)}, u32[]{:S(2)}, u32[]{:S(2)}) collective-permute-start(bf16[1024,256]{1,0:T(8,128)(2,1)} %collective-permute-done.2.refs_1_.near), channel_id=1, source_target_pairs={{0,16},{16,0},{1,17},{17,1},{2,18},{18,2},{3,19},{19,3},{4,20},{20... | collective-permute-start | bytes 1572872 | tf_op jit(solution)/shard_map/ppermute | solution.py:36
  73.3 30.4 %collective-permute-start.18 = (bf16[1024,512]{1,0:T(8,128)(2,1)}, bf16[1024,512]{1,0:T(8,128)(2,1)}, u32[]{:S(2)}, u32[]{:S(2)}) collective-permute-start(bf16[1024,512]{1,0:T(8,128)(2,1)} %collective-permute-done.9.crossed), channel_id=1, source_target_pairs={{4,0},{8,12},{5,1},{9,13},{6,2},{10,14},{7,3},{11,15},{20,16},{24,... | collective-permute-start | bytes 3145736 | tf_op jit(solution)/shard_map/ppermute | solution.py:40
  90.9 30.5 %collective-permute-start.17 = (bf16[512,1024]{1,0:T(8,128)(2,1)S(1)}, bf16[512,1024]{1,0:T(8,128)(2,1)}, u32[]{:S(2)}, u32[]{:S(2)}) collective-permute-start(bf16[512,1024]{1,0:T(8,128)(2,1)S(1)} %shard_map.118.x_here.x_other.tokens), channel_id=1, source_target_pairs={{0,4},{12,8},{1,5},{13,9},{2,6},{14,10},{3,7},{15,11},{16,20},{28,... | collective-permute-start | bytes 3145736 | tf_op jit(solution)/shard_map/ppermute | solution.py:40
  99.3 25.3 %collective-permute-start.16 = (bf16[1024,512]{1,0:T(8,128)(2,1)}, bf16[1024,512]{1,0:T(8,128)(2,1)}, u32[]{:S(2)}, u32[]{:S(2)}) collective-permute-start(bf16[1024,512]{1,0:T(8,128)(2,1)} %shard_map.119), channel_id=1, source_target_pairs={{4,8},{8,4},{5,9},{9,5},{6,10},{10,6},{7,11},{11,7},{20,24},{24,20... | collective-permute-start | bytes 3145736 | tf_op jit(solution)/shard_map/ppermute | solution.py:40
  101.0 27.5 %collective-permute-start.15 = (bf16[1024,512]{1,0:T(8,128)(2,1)}, bf16[1024,512]{1,0:T(8,128)(2,1)}, u32[]{:S(2)}, u32[]{:S(2)}) collective-permute-start(bf16[1024,512]{1,0:T(8,128)(2,1)} %collective-permute-done.12.crossed), channel_id=1, source_target_pairs={{4,0},{8,12},{5,1},{9,13},{6,2},{10,14},{7,3},{11,15},{20,16},{24,... | collective-permute-start | bytes 3145736 | tf_op jit(solution)/shard_map/ppermute | solution.py:40
  105.5 31.7 %collective-permute-start.20 = (bf16[1024,512]{1,0:T(8,128)(2,1)S(1)}, bf16[1024,512]{1,0:T(8,128)(2,1)S(1)}, u32[]{:S(2)}, u32[]{:S(2)}) collective-permute-start(bf16[1024,512]{1,0:T(8,128)(2,1)S(1)} %shard_map.121.rest_2_.far), channel_id=1, source_target_pairs={{0,16},{16,0},{1,17},{17,1},{2,18},{18,2},{3,19},{19,3},{4,20},{20... | collective-permute-start | bytes 3145736 | tf_op jit(solution)/shard_map/ppermute | solution.py:36
  123.9 31.0 %collective-permute-start.26 = (bf16[1024,512]{1,0:T(8,128)(2,1)S(1)}, bf16[1024,512]{1,0:T(8,128)(2,1)S(1)}, u32[]{:S(2)}, u32[]{:S(2)}) collective-permute-start(bf16[1024,512]{1,0:T(8,128)(2,1)S(1)} %shard_map.122), channel_id=1, source_target_pairs={{4,8},{8,4},{5,9},{9,5},{6,10},{10,6},{7,11},{11,7},{20,24},{24,20... | collective-permute-start | bytes 3145736 | tf_op jit(solution)/shard_map/ppermute | solution.py:40
  130.1 36.2 %collective-permute-start.19 = (bf16[1024,512]{1,0:T(8,128)(2,1)S(1)}, bf16[1024,512]{1,0:T(8,128)(2,1)S(1)}, u32[]{:S(2)}, u32[]{:S(2)}) collective-permute-start(bf16[1024,512]{1,0:T(8,128)(2,1)S(1)} %shard_map.124.far), channel_id=1, source_target_pairs={{0,16},{16,0},{1,17},{17,1},{2,18},{18,2},{3,19},{19,3},{4,20},{20... | collective-permute-start | bytes 3145736 | tf_op jit(solution)/shard_map/ppermute | solution.py:36
  131.7 14.9 %collective-permute-start.23 = (bf16[1024,256]{1,0:T(8,128)(2,1)S(1)}, bf16[1024,256]{1,0:T(8,128)(2,1)S(1)}, u32[]{:S(2)}, u32[]{:S(2)}) collective-permute-start(bf16[1024,256]{1,0:T(8,128)(2,1)S(1)} %shard_map.123), channel_id=1, source_target_pairs={{4,0},{8,12},{5,1},{9,13},{6,2},{10,14},{7,3},{11,15},{20,16},{24,... | collective-permute-start | bytes 1572872 | tf_op jit(solution)/shard_map/ppermute | solution.py:40
  136.9 17.1 %collective-permute-start.22 = (bf16[256,1024]{1,0:T(8,128)(2,1)S(1)}, bf16[256,1024]{1,0:T(8,128)(2,1)S(1)}, u32[]{:S(2)}, u32[]{:S(2)}) collective-permute-start(bf16[256,1024]{1,0:T(8,128)(2,1)S(1)} %get-tuple-element.116), channel_id=1, source_target_pairs={{0,2},{2,0},{1,3},{3,1},{4,6},{6,4},{5,7},{7,5},{8,10},{10,8},{9,1... | collective-permute-start | bytes 1572872 | tf_op jit(solution)/shard_map/ppermute | solution.py:36
  140.9 13.1 %collective-permute-start.21 = (f32[512,128]{1,0:T(8,128)S(1)}, f32[512,128]{1,0:T(8,128)S(1)}, u32[]{:S(2)}, u32[]{:S(2)}) collective-permute-start(f32[512,128]{1,0:T(8,128)S(1)} %shard_map.126.left), channel_id=1, source_target_pairs={{0,1},{1,0},{2,3},{3,2},{4,5},{5,4},{6,7},{7,6},{8,9},{9,8},{10,11... | collective-permute-start | bytes 786440 | tf_op jit(solution)/shard_map/ppermute | solution.py:36
  155.4 20.0 %collective-permute-start.31 = (bf16[1024,256]{1,0:T(8,128)(2,1)S(1)}, bf16[1024,256]{1,0:T(8,128)(2,1)S(1)}, u32[]{:S(2)}, u32[]{:S(2)}) collective-permute-start(bf16[1024,256]{1,0:T(8,128)(2,1)S(1)} %shard_map.130), channel_id=1, source_target_pairs={{4,0},{8,12},{5,1},{9,13},{6,2},{10,14},{7,3},{11,15},{20,16},{24,... | collective-permute-start | bytes 1572872 | tf_op jit(solution)/shard_map/ppermute | solution.py:40
  169.9 12.5 %collective-permute-start.27 = (bf16[256,1024]{1,0:T(8,128)(2,1)S(1)}, bf16[256,1024]{1,0:T(8,128)(2,1)S(1)}, u32[]{:S(2)}, u32[]{:S(2)}) collective-permute-start(bf16[256,1024]{1,0:T(8,128)(2,1)S(1)} %get-tuple-element.128), channel_id=1, source_target_pairs={{0,2},{2,0},{1,3},{3,1},{4,6},{6,4},{5,7},{7,5},{8,10},{10,8},{9,1... | collective-permute-start | bytes 1572872 | tf_op jit(solution)/shard_map/ppermute | solution.py:36
  (40 other events, 315.7 us)

commit v13 on v12

--- a/solution.py
+++ b/solution.py
@@ -471,10 +471,16 @@
     compact = like(both, size, kind=f32)
     back_part = done(kernel_call(back_kernel, [compact], ids, dy_quarter, up_all)[0])
     back_tp = swap(back_part, "tp")
+    dy_tp = swap(dy_half, "tp")
     weight_here = done(rows_at(0, step(frozen_value_weight), eighth))
     weight_near = along(weight_here, NEIGHBOURS)
     back_part = done(kernel_call(add_kernel, [compact], back_part, step(back_tp))[0])
     back_got = swap(back_part, "own")
+    dy_line = done(
+        kernel_call(
+            dy_line_kernel, [like(both, 2 * kv)], dy_half, step(dy_tp), scalars=places
+        )[0]
+    )
     down_near, x_got[0] = step(down_near, x_got[0])
     crossing = done(side_by_side(down_piece, down_near))
     down_crossed = along(crossing, MIDDLE)
@@ -546,34 +552,14 @@
     middle = [to_middle(0)]
     weight_crossed = done(step(weight_crossed))
     weight_outer = along(weight_crossed, OUTWARD)
-    dy_half, weight_near_other = step(dy_half, weight_near_other)
-    dy_tp = swap(dy_half, "tp")
-    dy_line = done(
-        kernel_call(
-            dy_line_kernel, [like(both, 2 * kv)], dy_half, step(dy_tp), scalars=places
-        )[0]
-    )
-    down_far = done(far_of(down_crossed, step(down_outer)))
+    down_outer, weight_near_other = step(down_outer, weight_near_other)
+    down_far = done(far_of(down_crossed, down_outer))
     down_far_other = swap(down_far, "rep")
     middle.append(to_middle(1))
     outward = [to_end(0, middle[0])]
     weight_far = done(far_of(weight_crossed, step(weight_outer)))
     weight_far_other = swap(weight_far, "rep")
     half_grad = [like(rows, eighth)] * 2
-    dx_mine, dx_sent = kernel_call(
-        dx_kernel,
-        half_grad,
-        step(dy_line),
-        back_wide,
-        weight_here,
-        weight_near,
-        weight_far,
-        down_piece,
-        down_near,
-        down_far,
-    )
-    dx_mine_got = swap(done(dx_sent), "own")
-
     low_part = done(
         kernel_call(
             low_kernel,
@@ -590,18 +576,30 @@
         )[0]
     )
     low_tp = swap(low_part, "tp")
-    grad_here, grad_sent = finish(0, middle[0], outward[0])
-    grad_got = swap(grad_sent, "own")
     blocks = [like(2, both, cols, kind=f32)] * 2
     y_first = kernel_call(
         y_kernel, blocks, step(x_mine), weight_here, weight_near, weight_far, scalars=flags
     )
     done(y_first[0])
-    low_tp, dx_mine_got = step(low_tp, dx_mine_got)
-    low_part = done(kernel_call(add_kernel, [compact], low_part, low_tp)[0])
+    low_part = done(kernel_call(add_kernel, [compact], low_part, step(low_tp))[0])
     low_got = swap(low_part, "own")
+    dx_mine, dx_sent = kernel_call(
+        dx_kernel,
+        half_grad,
+        step(dy_line),
+        back_wide,
+        weight_here,
+        weight_near,
+        weight_far,
+        down_piece,
+        down_near,
+        down_far,
+    )
+    dx_mine_got = swap(done(dx_sent), "own")
+    grad_here, grad_sent = finish(0, middle[0], outward[0])
+    grad_got = swap(grad_sent, "own")
     outward.append(to_end(1, middle[1]))
-    low_got, grad_got = step(low_got, grad_got)
+    low_got = step(low_got)
     delta, *up_parts = kernel_call(
         low_end_kernel,
         [like(both, kvq)] + [like(wide, kvq)] * 4,
@@ -614,6 +612,7 @@
     )
     done(delta)
     up_got = [around(up_parts[k], k) for k in (1, 2, 3)]
+    weight_far_other, dx_mine_got = step(weight_far_other, dx_mine_got)
     dx_other, dx_sent = kernel_call(
         dx_kernel,
         half_grad,
@@ -621,12 +620,12 @@
         back_wide,
         weight_other,
         weight_near_other,
-        step(weight_far_other),
+        weight_far_other,
         down_other,
         down_far_other,
     )
     dx_other_got = swap(done(dx_sent), "own")
-    grad_last, grad_sent = finish(1, middle[1], outward[1])
+    grad_last, grad_sent = finish(1, middle[1], outward[1], grad_got)
     grad_last_got = swap(grad_sent, "own")
     up_got = step(*up_got)
     up_mine, up_theirs = kernel_call(

time: 209 us -> 225 us (1.077)
  waiting for transfers between devices: 72.8 us -> 103 us
  Pallas kernels: 61.6 us -> 53 us
  starting transfers between devices: 61.5 us -> 56.4 us
    ppermute x20, waiting for transfers between devices: 38 us -> 73.5 us  [swap(): return lax.ppermute(value, axis, PAIR)]
    pallas_call x39, Pallas kernels: 61.6 us -> 53 us  [kernel_call(): pl.pallas_call(body, out_shape=list(outs), in_specs=specs, out_specs=[pl....]
    ppermute x16, starting transfers between devices: 35.5 us -> 28.7 us  [along(): return lax.ppermute(value, 'fsdp', pairs)]
    ppermute x16, waiting for transfers between devices: 34.7 us -> 29.9 us  [along(): return lax.ppermute(value, 'fsdp', pairs)]
    unnamed x55 -> x27, local copies, waits for them, and re-layouts: 10.4 us -> 9.05 us
  transfers between devices with their start and end apart: 37 -> 37, of which waited for: 16 -> 17; matrix products, arithmetic and copies ran while one was open for 1% -> 1% of each run, Pallas kernels for 27% -> 19%
where the time goes in v13:
time: 225 us; the launch traced here: 224 us
  waiting for transfers between devices  103 us (46%)
  starting transfers between devices  56.4 us (25%)
  Pallas kernels  53 us (24%)
  local copies, waits for them, and re-layouts  9.33 us (4%)
    ppermute x20, waiting for transfers between devices, swap(): return lax.ppermute(value, axis, PAIR)  73.5 us
    pallas_call x39, Pallas kernels, kernel_call(): pl.pallas_call(body, out_shape=list(outs), in_specs=specs, out_specs=[pl....  53 us
    ppermute x16, waiting for transfers between devices, along(): return lax.ppermute(value, 'fsdp', pairs)  29.9 us
    ppermute x16, starting transfers between devices, along(): return lax.ppermute(value, 'fsdp', pairs)  28.7 us
    ppermute x20, starting transfers between devices, swap(): return lax.ppermute(value, axis, PAIR)  20.5 us
    unnamed x27, local copies, waits for them, and re-layouts  9.05 us
    all_to_all x1, starting transfers between devices, body_line(): lax.all_to_all(done(up_sent), ('fsdp', 'own'), split_axis=0, concat_axis=...  7.25 us
  transfers between devices with their start and end apart: 37, of which 17 were waited for; matrix products, arithmetic and copies ran while one was open for 1% of the time, Pallas kernels for 19%

profile of v13, /device:TPU:0, one launch (start us, length us, event | category | flops | bytes accessed | tf_op | source)
XLA Modules:
  0.0 224.1 jit_solution(17519866636335656258)
XLA Ops:
  2.5 7.3 %all-to-all-start = ((bf16[8,128,256]{2,1,0:T(8,128)(2,1)}), bf16[8,128,256]{2,1,0:T(8,128)(2,1)S(1)}, u32[]{:S(2)}, u32[]{:S(2)}) async-start(bf16[8,128,256]{2,1,0:T(8,128)(2,1)} %shard_map.102), calls=%async_computation | async-start | bytes 1048576 | tf_op jit(solution)/shard_map/all_to_all | solution.py:441
  17.9 13.6 %collective-permute-done.1.refs_1_ = bf16[1024,128]{1,0:T(8,128)(2,1)} collective-permute-done((bf16[1024,128]{1,0:T(8,128)(2,1)}, bf16[1024,128]{1,0:T(8,128)(2,1)}, u32[]{:S(2)}, u32[]{:S(2)}) %collective-permute-start.1) | collective-permute-done | bytes 262176 | tf_op jit(solution)/shard_map/ppermute | solution.py:36
  44.6 6.6 %collective-permute-done.6.refs_1_ = bf16[256,1024]{1,0:T(8,128)(2,1)} collective-permute-done((bf16[256,1024]{1,0:T(8,128)(2,1)}, bf16[256,1024]{1,0:T(8,128)(2,1)}, u32[]{:S(2)}, u32[]{:S(2)}) %collective-permute-start.6) | collective-permute-done | bytes 524320 | tf_op jit(solution)/shard_map/ppermute | solution.py:36
  51.8 2.7 %shard_map.112 = bf16[1024,512]{1,0:T(8,128)(2,1)} custom-call(s32[4]{0:T(128)S(1)} %pad_add_fusion.numbers, bf16[1024,256]{1,0:T(8,128)(2,1)} %shard_map.106.refs_0_.own.rest_0_, bf16[1024,256]{1,0:T(8,128)(2,1)} %collective-permute-done.5.refs_1_.near.rest_1_), custom_call_target="tpu_custom_call" | custom-call | tf_op jit(solution)/shard_map/pallas_call | solution.py:48
  56.2 3.0 %collective-permute-start.2 = (bf16[1024,256]{1,0:T(8,128)(2,1)}, bf16[1024,256]{1,0:T(8,128)(2,1)}, u32[]{:S(2)}, u32[]{:S(2)}) collective-permute-start(bf16[1024,256]{1,0:T(8,128)(2,1)} %shard_map.109.refs_0_.own), channel_id=1, source_target_pairs={{0,4},{4,0},{8,12},{12,8},{1,5},{5,1},{9,13},{13,9},{2,6},{6,2},{1... | collective-permute-start | bytes 1572872 | tf_op jit(solution)/shard_map/ppermute | solution.py:40
  61.7 5.0 %collective-permute-done.4.got = f32[512,128]{1,0:T(8,128)} collective-permute-done((f32[512,128]{1,0:T(8,128)S(1)}, f32[512,128]{1,0:T(8,128)}, u32[]{:S(2)}, u32[]{:S(2)}) %collective-permute-start.4) | collective-permute-done | bytes 262176 | tf_op jit(solution)/shard_map/ppermute | solution.py:36
  78.4 4.5 %collective-permute-start.15 = (bf16[512,1024]{1,0:T(8,128)(2,1)S(1)}, bf16[512,1024]{1,0:T(8,128)(2,1)S(1)}, u32[]{:S(2)}, u32[]{:S(2)}) collective-permute-start(bf16[512,1024]{1,0:T(8,128)(2,1)S(1)} %shard_map.117.x_here.x_mine.tokens), channel_id=1, source_target_pairs={{0,4},{12,8},{1,5},{13,9},{2,6},{14,10},{3,7},{15,11},{16,20},{28,... | collective-permute-start | bytes 3145736 | tf_op jit(solution)/shard_map/ppermute | solution.py:40
  87.0 7.3 %collective-permute-done.9.own_near_other.rest_0_ = bf16[1024,512]{1,0:T(8,128)(2,1)S(1)} collective-permute-done((bf16[1024,512]{1,0:T(8,128)(2,1)}, bf16[1024,512]{1,0:T(8,128)(2,1)S(1)}, u32[]{:S(2)}, u32[]{:S(2)}) %collective-permute-start.9) | collective-permute-done | bytes 1048608 | tf_op jit(solution)/shard_map/ppermute | solution.py:36
  98.4 4.4 %collective-permute-start.18 = (bf16[512,1024]{1,0:T(8,128)(2,1)S(1)}, bf16[512,1024]{1,0:T(8,128)(2,1)S(1)}, u32[]{:S(2)}, u32[]{:S(2)}) collective-permute-start(bf16[512,1024]{1,0:T(8,128)(2,1)S(1)} %shard_map.119.x_here.x_other.tokens), channel_id=1, source_target_pairs={{0,4},{12,8},{1,5},{13,9},{2,6},{14,10},{3,7},{15,11},{16,20},{28,... | collective-permute-start | bytes 3145736 | tf_op jit(solution)/shard_map/ppermute | solution.py:40
  102.8 3.6 %collective-permute-done.15.x_in = bf16[512,1024]{1,0:T(8,128)(2,1)S(1)} collective-permute-done((bf16[512,1024]{1,0:T(8,128)(2,1)S(1)}, bf16[512,1024]{1,0:T(8,128)(2,1)S(1)}, u32[]{:S(2)}, u32[]{:S(2)}) %collective-permute-start.15) | collective-permute-done | bytes 1048608 | tf_op jit(solution)/shard_map/ppermute | solution.py:40
  112.6 13.8 %collective-permute-done.18.x_in = bf16[512,1024]{1,0:T(8,128)(2,1)S(1)} collective-permute-done((bf16[512,1024]{1,0:T(8,128)(2,1)S(1)}, bf16[512,1024]{1,0:T(8,128)(2,1)S(1)}, u32[]{:S(2)}, u32[]{:S(2)}) %collective-permute-start.18) | collective-permute-done | bytes 1048608 | tf_op jit(solution)/shard_map/ppermute | solution.py:40
  128.9 3.6 %collective-permute-done.16.outer = bf16[1024,512]{1,0:T(8,128)(2,1)S(1)} collective-permute-done((bf16[1024,512]{1,0:T(8,128)(2,1)S(1)}, bf16[1024,512]{1,0:T(8,128)(2,1)S(1)}, u32[]{:S(2)}, u32[]{:S(2)}) %collective-permute-start.16) | collective-permute-done | bytes 1048608 | tf_op jit(solution)/shard_map/ppermute | solution.py:40
  136.9 3.5 %shard_map.125.left = f32[512,128]{1,0:T(8,128)S(1)} custom-call(s32[24]{0:T(128)S(1)} %concatenate.3.numbers, bf16[512,128]{1,0:T(8,128)(2,1)S(1)} %get-tuple-element.84.ids, bf16[512,1024]{1,0:T(8,128)(2,1)S(1)} %shard_map.117.x_here.x_mine.tokens, bf16[512,1024]{1,0:T(8,128)(2,1)S(1)} %shard_map.119.x_here.x_other.tokens, ...), custom_call_target="tpu_custom_call" | custom-call | tf_op jit(solution)/shard_map/pallas_call | solution.py:48
  141.8 4.3 %shard_map.126 = (f32[2,512,256]{2,1,0:T(8,128)S(1)}, f32[2,512,256]{2,1,0:T(8,128)S(1)}) custom-call(s32[5]{0:T(128)S(1)} %convert_element_type.3.flags, bf16[512,1024]{1,0:T(8,128)(2,1)S(1)} %shard_map.117.x_here.x_mine.tokens, bf16[1024,256]{1,0:T(8,128)(2,1)} %shard_map.109.refs_0_.own, bf16[1024,256]{1,0:T(8,128)(2,1)} %collective-permute-done.2.refs_1_.near, ...), custom_call_target="tpu_custom_call" | custom-call | tf_op jit(solution)/shard_map/pallas_call | solution.py:48
  146.1 3.9 %shard_map.128 = (bf16[256,1024]{1,0:T(8,128)(2,1)S(1)}, bf16[256,1024]{1,0:T(8,128)(2,1)S(1)}) custom-call(bf16[512,1024]{1,0:T(8,128)(2,1)S(1)} %shard_map.111.dy, bf16[512,1024]{1,0:T(8,128)(2,1)S(1)} %get-tuple-element.103.back, bf16[1024,256]{1,0:T(8,128)(2,1)} %shard_map.109.refs_0_.own, bf16[1024,256]{1,0:T(8,128)(2,1)} %collective-permute-done.2.refs_1_.near, ...), custom_call_target="tpu_custom_call" | custom-call | tf_op jit(solution)/shard_map/pallas_call | solution.py:48
  152.1 4.6 %collective-permute-done.25.outer = bf16[1024,256]{1,0:T(8,128)(2,1)S(1)} collective-permute-done((bf16[1024,256]{1,0:T(8,128)(2,1)S(1)}, bf16[1024,256]{1,0:T(8,128)(2,1)S(1)}, u32[]{:S(2)}, u32[]{:S(2)}) %collective-permute-start.25) | collective-permute-done | bytes 524320 | tf_op jit(solution)/shard_map/ppermute | solution.py:40
  159.4 10.7 %collective-permute-done.23.got = f32[512,128]{1,0:T(8,128)S(1)} collective-permute-done((f32[512,128]{1,0:T(8,128)S(1)}, f32[512,128]{1,0:T(8,128)S(1)}, u32[]{:S(2)}, u32[]{:S(2)}) %collective-permute-start.23) | collective-permute-done | bytes 262176 | tf_op jit(solution)/shard_map/ppermute | solution.py:36
  171.6 2.4 %shard_map.132 = (bf16[256,1024]{1,0:T(8,128)(2,1)S(1)}, bf16[256,1024]{1,0:T(8,128)(2,1)S(1)}) custom-call(bf16[512,1024]{1,0:T(8,128)(2,1)S(1)} %shard_map.111.dy, bf16[512,1024]{1,0:T(8,128)(2,1)S(1)} %get-tuple-element.103.back, bf16[1024,256]{1,0:T(8,128)(2,1)S(1)} %shard_map.118.own, bf16[1024,256]{1,0:T(8,128)(2,1)S(1)} %collective-permute-done.13.near, ...), custom_call_target="tpu_custom_call" | custom-call | tf_op jit(solution)/shard_map/pallas_call | solution.py:48
  176.1 2.4 %collective-permute-start.27 = (bf16[256,256]{1,0:T(8,128)(2,1)S(1)}, bf16[256,256]{1,0:T(8,128)(2,1)S(1)}, u32[]{:S(2)}, u32[]{:S(2)}) collective-permute-start(bf16[256,256]{1,0:T(8,128)(2,1)S(1)} %get-tuple-element.126), channel_id=1, source_target_pairs={{0,4},{4,8},{8,12},{12,0},{1,5},{5,9},{9,13},{13,1},{2,6},{6,10},{... | collective-permute-start | bytes 393224 | tf_op jit(solution)/shard_map/ppermute | solution.py:40
  178.6 14.6 %collective-permute-done.31.refs_2_ = bf16[1024,128]{1,0:T(8,128)(2,1)S(1)} collective-permute-done((bf16[1024,128]{1,0:T(8,128)(2,1)S(1)}, bf16[1024,128]{1,0:T(8,128)(2,1)S(1)}, u32[]{:S(2)}, u32[]{:S(2)}) %collective-permute-start.31) | collective-permute-done | bytes 262176 | tf_op jit(solution)/shard_map/ppermute | solution.py:36
  195.6 2.6 %collective-permute-done.29.fourth = bf16[256,256]{1,0:T(8,128)(2,1)S(1)} collective-permute-done((bf16[256,256]{1,0:T(8,128)(2,1)S(1)}, bf16[256,256]{1,0:T(8,128)(2,1)S(1)}, u32[]{:S(2)}, u32[]{:S(2)}) %collective-permute-start.29) | collective-permute-done | bytes 131104 | tf_op jit(solution)/shard_map/ppermute | solution.py:40
  198.9 3.5 %shard_map.135 = (f32[2,512,256]{2,1,0:T(8,128)S(1)}, f32[2,512,256]{2,1,0:T(8,128)S(1)}) custom-call(s32[5]{0:T(128)S(1)} %convert_element_type.3.flags, bf16[512,1024]{1,0:T(8,128)(2,1)S(1)} %shard_map.119.x_here.x_other.tokens, bf16[1024,256]{1,0:T(8,128)(2,1)S(1)} %shard_map.118.own, bf16[1024,256]{1,0:T(8,128)(2,1)S(1)} %collective-permute-done.13.near, ...), custom_call_target="tpu_custom_call" | custom-call | tf_op jit(solution)/shard_map/pallas_call | solution.py:48
  204.0 7.2 %collective-permute-done.33.refs_3_ = bf16[1024,128]{1,0:T(8,128)(2,1)S(1)} collective-permute-done((bf16[1024,128]{1,0:T(8,128)(2,1)S(1)}, bf16[1024,128]{1,0:T(8,128)(2,1)S(1)}, u32[]{:S(2)}, u32[]{:S(2)}) %collective-permute-start.33) | collective-permute-done | bytes 262176 | tf_op jit(solution)/shard_map/ppermute | solution.py:36
  216.1 4.5 %collective-permute-done.34.got = bf16[2,256,256]{2,1,0:T(8,128)(2,1)S(1)} collective-permute-done((bf16[2,256,256]{2,1,0:T(8,128)(2,1)S(1)}, bf16[2,256,256]{2,1,0:T(8,128)(2,1)S(1)}, u32[]{:S(2)}, u32[]{:S(2)}) %collective-permute-start.34) | collective-permute-done | bytes 262176 | tf_op jit(solution)/shard_map/ppermute | solution.py:36
  (122 shorter events, 83.5 us)
Async XLA Ops:
  2.5 32.6 %all-to-all-start = ((bf16[8,128,256]{2,1,0:T(8,128)(2,1)}), bf16[8,128,256]{2,1,0:T(8,128)(2,1)S(1)}, u32[]{:S(2)}, u32[]{:S(2)}) async-start(bf16[8,128,256]{2,1,0:T(8,128)(2,1)} %shard_map.102), calls=%async_computation | async-start | bytes 1048576 | tf_op jit(solution)/shard_map/all_to_all | solution.py:441
  14.2 20.9 %collective-permute-start = (bf16[256,640]{1,0:T(8,128)(2,1)S(1)}, bf16[256,640]{1,0:T(8,128)(2,1)S(1)}, u32[]{:S(2)}, u32[]{:S(2)}) collective-permute-start(bf16[256,640]{1,0:T(8,128)(2,1)S(1)} %shard_map.104.here), channel_id=1, source_target_pairs={{0,2},{2,0},{1,3},{3,1},{4,6},{6,4},{5,7},{7,5},{8,10},{10,8},{9,1... | collective-permute-start | bytes 983048 | tf_op jit(solution)/shard_map/ppermute | solution.py:36
  16.3 15.2 %collective-permute-start.1 = (bf16[1024,128]{1,0:T(8,128)(2,1)}, bf16[1024,128]{1,0:T(8,128)(2,1)}, u32[]{:S(2)}, u32[]{:S(2)}) collective-permute-start(bf16[1024,128]{1,0:T(8,128)(2,1)} %copy-done.10), channel_id=1, source_target_pairs={{0,2},{2,0},{1,3},{3,1},{4,6},{6,4},{5,7},{7,5},{8,10},{10,8},{9,1... | collective-permute-start | bytes 786440 | tf_op jit(solution)/shard_map/ppermute | solution.py:36
  54.5 29.7 %collective-permute-start.10 = (bf16[1024,512]{1,0:T(8,128)(2,1)}, bf16[1024,512]{1,0:T(8,128)(2,1)}, u32[]{:S(2)}, u32[]{:S(2)}) collective-permute-start(bf16[1024,512]{1,0:T(8,128)(2,1)} %shard_map.112), channel_id=1, source_target_pairs={{4,8},{8,4},{5,9},{9,5},{6,10},{10,6},{7,11},{11,7},{20,24},{24,20... | collective-permute-start | bytes 3145736 | tf_op jit(solution)/shard_map/ppermute | solution.py:40
  56.2 16.1 %collective-permute-start.2 = (bf16[1024,256]{1,0:T(8,128)(2,1)}, bf16[1024,256]{1,0:T(8,128)(2,1)}, u32[]{:S(2)}, u32[]{:S(2)}) collective-permute-start(bf16[1024,256]{1,0:T(8,128)(2,1)} %shard_map.109.refs_0_.own), channel_id=1, source_target_pairs={{0,4},{4,0},{8,12},{12,8},{1,5},{5,1},{9,13},{13,9},{2,6},{6,2},{1... | collective-permute-start | bytes 1572872 | tf_op jit(solution)/shard_map/ppermute | solution.py:40
  70.7 23.6 %collective-permute-start.9 = (bf16[1024,512]{1,0:T(8,128)(2,1)}, bf16[1024,512]{1,0:T(8,128)(2,1)S(1)}, u32[]{:S(2)}, u32[]{:S(2)}) collective-permute-start(bf16[1024,512]{1,0:T(8,128)(2,1)} %shard_map.112), channel_id=1, source_target_pairs={{0,16},{16,0},{1,17},{17,1},{2,18},{18,2},{3,19},{19,3},{4,20},{20... | collective-permute-start | bytes 3145736 | tf_op jit(solution)/shard_map/ppermute | solution.py:36
  78.4 28.0 %collective-permute-start.15 = (bf16[512,1024]{1,0:T(8,128)(2,1)S(1)}, bf16[512,1024]{1,0:T(8,128)(2,1)S(1)}, u32[]{:S(2)}, u32[]{:S(2)}) collective-permute-start(bf16[512,1024]{1,0:T(8,128)(2,1)S(1)} %shard_map.117.x_here.x_mine.tokens), channel_id=1, source_target_pairs={{0,4},{12,8},{1,5},{13,9},{2,6},{14,10},{3,7},{15,11},{16,20},{28,... | collective-permute-start | bytes 3145736 | tf_op jit(solution)/shard_map/ppermute | solution.py:40
  82.8 25.6 %collective-permute-start.14 = (bf16[1024,512]{1,0:T(8,128)(2,1)S(1)}, bf16[1024,512]{1,0:T(8,128)(2,1)S(1)}, u32[]{:S(2)}, u32[]{:S(2)}) collective-permute-start(bf16[1024,512]{1,0:T(8,128)(2,1)S(1)} %shard_map.114), channel_id=1, source_target_pairs={{4,8},{8,4},{5,9},{9,5},{6,10},{10,6},{7,11},{11,7},{20,24},{24,20... | collective-permute-start | bytes 3145736 | tf_op jit(solution)/shard_map/ppermute | solution.py:40
  84.2 25.5 %collective-permute-start.12 = (bf16[1024,512]{1,0:T(8,128)(2,1)}, bf16[1024,512]{1,0:T(8,128)(2,1)S(1)}, u32[]{:S(2)}, u32[]{:S(2)}) collective-permute-start(bf16[1024,512]{1,0:T(8,128)(2,1)} %collective-permute-done.10.crossed), channel_id=1, source_target_pairs={{4,0},{8,12},{5,1},{9,13},{6,2},{10,14},{7,3},{11,15},{20,16},{24,... | collective-permute-start | bytes 3145736 | tf_op jit(solution)/shard_map/ppermute | solution.py:40
  94.3 15.4 %collective-permute-start.13 = (bf16[1024,256]{1,0:T(8,128)(2,1)}, bf16[1024,256]{1,0:T(8,128)(2,1)S(1)}, u32[]{:S(2)}, u32[]{:S(2)}) collective-permute-start(bf16[1024,256]{1,0:T(8,128)(2,1)} %collective-permute-done.2.refs_1_.near), channel_id=1, source_target_pairs={{0,16},{16,0},{1,17},{17,1},{2,18},{18,2},{3,19},{19,3},{4,20},{20... | collective-permute-start | bytes 1572872 | tf_op jit(solution)/shard_map/ppermute | solution.py:36
  98.4 28.0 %collective-permute-start.18 = (bf16[512,1024]{1,0:T(8,128)(2,1)S(1)}, bf16[512,1024]{1,0:T(8,128)(2,1)S(1)}, u32[]{:S(2)}, u32[]{:S(2)}) collective-permute-start(bf16[512,1024]{1,0:T(8,128)(2,1)S(1)} %shard_map.119.x_here.x_other.tokens), channel_id=1, source_target_pairs={{0,4},{12,8},{1,5},{13,9},{2,6},{14,10},{3,7},{15,11},{16,20},{28,... | collective-permute-start | bytes 3145736 | tf_op jit(solution)/shard_map/ppermute | solution.py:40
  107.6 20.8 %collective-permute-start.17 = (bf16[1024,512]{1,0:T(8,128)(2,1)S(1)}, bf16[1024,512]{1,0:T(8,128)(2,1)S(1)}, u32[]{:S(2)}, u32[]{:S(2)}) collective-permute-start(bf16[1024,512]{1,0:T(8,128)(2,1)S(1)} %shard_map.120), channel_id=1, source_target_pairs={{4,8},{8,4},{5,9},{9,5},{6,10},{10,6},{7,11},{11,7},{20,24},{24,20... | collective-permute-start | bytes 3145736 | tf_op jit(solution)/shard_map/ppermute | solution.py:40
  108.4 24.2 %collective-permute-start.16 = (bf16[1024,512]{1,0:T(8,128)(2,1)S(1)}, bf16[1024,512]{1,0:T(8,128)(2,1)S(1)}, u32[]{:S(2)}, u32[]{:S(2)}) collective-permute-start(bf16[1024,512]{1,0:T(8,128)(2,1)S(1)} %collective-permute-done.14.crossed), channel_id=1, source_target_pairs={{4,0},{8,12},{5,1},{9,13},{6,2},{10,14},{7,3},{11,15},{20,16},{24,... | collective-permute-start | bytes 3145736 | tf_op jit(solution)/shard_map/ppermute | solution.py:40
  111.0 25.8 %collective-permute-start.20 = (bf16[1024,512]{1,0:T(8,128)(2,1)S(1)}, bf16[1024,512]{1,0:T(8,128)(2,1)S(1)}, u32[]{:S(2)}, u32[]{:S(2)}) collective-permute-start(bf16[1024,512]{1,0:T(8,128)(2,1)S(1)} %shard_map.121.far.rest_2_), channel_id=1, source_target_pairs={{0,16},{16,0},{1,17},{17,1},{2,18},{18,2},{3,19},{19,3},{4,20},{20... | collective-permute-start | bytes 3145736 | tf_op jit(solution)/shard_map/ppermute | solution.py:36
  127.7 29.9 %collective-permute-start.24 = (bf16[1024,512]{1,0:T(8,128)(2,1)S(1)}, bf16[1024,512]{1,0:T(8,128)(2,1)S(1)}, u32[]{:S(2)}, u32[]{:S(2)}) collective-permute-start(bf16[1024,512]{1,0:T(8,128)(2,1)S(1)} %shard_map.122), channel_id=1, source_target_pairs={{4,8},{8,4},{5,9},{9,5},{6,10},{10,6},{7,11},{11,7},{20,24},{24,20... | collective-permute-start | bytes 3145736 | tf_op jit(solution)/shard_map/ppermute | solution.py:40
  133.2 38.4 %collective-permute-start.19 = (bf16[1024,512]{1,0:T(8,128)(2,1)S(1)}, bf16[1024,512]{1,0:T(8,128)(2,1)S(1)}, u32[]{:S(2)}, u32[]{:S(2)}) collective-permute-start(bf16[1024,512]{1,0:T(8,128)(2,1)S(1)} %shard_map.124.far), channel_id=1, source_target_pairs={{0,16},{16,0},{1,17},{17,1},{2,18},{18,2},{3,19},{19,3},{4,20},{20... | collective-permute-start | bytes 3145736 | tf_op jit(solution)/shard_map/ppermute | solution.py:36
  140.5 16.2 %collective-permute-start.25 = (bf16[1024,256]{1,0:T(8,128)(2,1)S(1)}, bf16[1024,256]{1,0:T(8,128)(2,1)S(1)}, u32[]{:S(2)}, u32[]{:S(2)}) collective-permute-start(bf16[1024,256]{1,0:T(8,128)(2,1)S(1)} %shard_map.123), channel_id=1, source_target_pairs={{4,0},{8,12},{5,1},{9,13},{6,2},{10,14},{7,3},{11,15},{20,16},{24,... | collective-permute-start | bytes 1572872 | tf_op jit(solution)/shard_map/ppermute | solution.py:40
  150.0 21.6 %collective-permute-start.22 = (bf16[256,1024]{1,0:T(8,128)(2,1)S(1)}, bf16[256,1024]{1,0:T(8,128)(2,1)S(1)}, u32[]{:S(2)}, u32[]{:S(2)}) collective-permute-start(bf16[256,1024]{1,0:T(8,128)(2,1)S(1)} %get-tuple-element.117), channel_id=1, source_target_pairs={{0,2},{2,0},{1,3},{3,1},{4,6},{6,4},{5,7},{7,5},{8,10},{10,8},{9,1... | collective-permute-start | bytes 1572872 | tf_op jit(solution)/shard_map/ppermute | solution.py:36
  151.5 18.5 %collective-permute-start.23 = (f32[512,128]{1,0:T(8,128)S(1)}, f32[512,128]{1,0:T(8,128)S(1)}, u32[]{:S(2)}, u32[]{:S(2)}) collective-permute-start(f32[512,128]{1,0:T(8,128)S(1)} %shard_map.127.part), channel_id=1, source_target_pairs={{0,2},{2,0},{1,3},{3,1},{4,6},{6,4},{5,7},{7,5},{8,10},{10,8},{9,1... | collective-permute-start | bytes 786440 | tf_op jit(solution)/shard_map/ppermute | solution.py:36
  158.1 36.7 %collective-permute-start.30 = (bf16[1024,256]{1,0:T(8,128)(2,1)S(1)}, bf16[1024,256]{1,0:T(8,128)(2,1)S(1)}, u32[]{:S(2)}, u32[]{:S(2)}) collective-permute-start(bf16[1024,256]{1,0:T(8,128)(2,1)S(1)} %shard_map.130), channel_id=1, source_target_pairs={{4,0},{8,12},{5,1},{9,13},{6,2},{10,14},{7,3},{11,15},{20,16},{24,... | collective-permute-start | bytes 1572872 | tf_op jit(solution)/shard_map/ppermute | solution.py:40
  174.0 24.8 %collective-permute-start.26 = (bf16[256,1024]{1,0:T(8,128)(2,1)S(1)}, bf16[256,1024]{1,0:T(8,128)(2,1)S(1)}, u32[]{:S(2)}, u32[]{:S(2)}) collective-permute-start(bf16[256,1024]{1,0:T(8,128)(2,1)S(1)} %get-tuple-element.124), channel_id=1, source_target_pairs={{0,2},{2,0},{1,3},{3,1},{4,6},{6,4},{5,7},{7,5},{8,10},{10,8},{9,1... | collective-permute-start | bytes 1572872 | tf_op jit(solution)/shard_map/ppermute | solution.py:36
  175.5 17.7 %collective-permute-start.31 = (bf16[1024,128]{1,0:T(8,128)(2,1)S(1)}, bf16[1024,128]{1,0:T(8,128)(2,1)S(1)}, u32[]{:S(2)}, u32[]{:S(2)}) collective-permute-start(bf16[1024,128]{1,0:T(8,128)(2,1)S(1)} %get-tuple-element.129), channel_id=1, source_target_pairs={{0,2},{2,0},{1,3},{3,1},{4,6},{6,4},{5,7},{7,5},{8,10},{10,8},{9,1... | collective-permute-start | bytes 786440 | tf_op jit(solution)/shard_map/ppermute | solution.py:36
  176.1 19.5 %collective-permute-start.27 = (bf16[256,256]{1,0:T(8,128)(2,1)S(1)}, bf16[256,256]{1,0:T(8,128)(2,1)S(1)}, u32[]{:S(2)}, u32[]{:S(2)}) collective-permute-start(bf16[256,256]{1,0:T(8,128)(2,1)S(1)} %get-tuple-element.126), channel_id=1, source_target_pairs={{0,4},{4,8},{8,12},{12,0},{1,5},{5,9},{9,13},{13,1},{2,6},{6,10},{... | collective-permute-start | bytes 393224 | tf_op jit(solution)/shard_map/ppermute | solution.py:40
  178.5 17.1 %collective-permute-start.28 = (bf16[256,256]{1,0:T(8,128)(2,1)S(1)}, bf16[256,256]{1,0:T(8,128)(2,1)S(1)}, u32[]{:S(2)}, u32[]{:S(2)}) collective-permute-start(bf16[256,256]{1,0:T(8,128)(2,1)S(1)} %get-tuple-element.127), channel_id=1, source_target_pairs={{0,8},{4,12},{8,0},{12,4},{1,9},{5,13},{9,1},{13,5},{2,10},{6,14},... | collective-permute-start | bytes 393224 | tf_op jit(solution)/shard_map/ppermute | solution.py:40
  (26 other events, 176.3 us)

commit v14 on v13

--- a/solution.py
+++ b/solution.py
@@ -471,16 +471,10 @@
     compact = like(both, size, kind=f32)
     back_part = done(kernel_call(back_kernel, [compact], ids, dy_quarter, up_all)[0])
     back_tp = swap(back_part, "tp")
-    dy_tp = swap(dy_half, "tp")
     weight_here = done(rows_at(0, step(frozen_value_weight), eighth))
     weight_near = along(weight_here, NEIGHBOURS)
     back_part = done(kernel_call(add_kernel, [compact], back_part, step(back_tp))[0])
     back_got = swap(back_part, "own")
-    dy_line = done(
-        kernel_call(
-            dy_line_kernel, [like(both, 2 * kv)], dy_half, step(dy_tp), scalars=places
-        )[0]
-    )
     down_near, x_got[0] = step(down_near, x_got[0])
     crossing = done(side_by_side(down_piece, down_near))
     down_crossed = along(crossing, MIDDLE)
@@ -557,6 +551,12 @@
     down_far_other = swap(down_far, "rep")
     middle.append(to_middle(1))
     outward = [to_end(0, middle[0])]
+    dy_tp = swap(step(dy_half), "tp")
+    dy_line = done(
+        kernel_call(
+            dy_line_kernel, [like(both, 2 * kv)], dy_half, step(dy_tp), scalars=places
+        )[0]
+    )
     weight_far = done(far_of(weight_crossed, step(weight_outer)))
     weight_far_other = swap(weight_far, "rep")
     half_grad = [like(rows, eighth)] * 2
@@ -583,7 +583,7 @@
     done(y_first[0])
     low_part = done(kernel_call(add_kernel, [compact], low_part, step(low_tp))[0])
     low_got = swap(low_part, "own")
-    dx_mine, dx_sent = kernel_call(
+    dx_mine, dx_first_sent = kernel_call(
         dx_kernel,
         half_grad,
         step(dy_line),
@@ -595,11 +595,13 @@
         down_near,
         down_far,
     )
-    dx_mine_got = swap(done(dx_sent), "own")
+    done(dx_mine)
     grad_here, grad_sent = finish(0, middle[0], outward[0])
-    grad_got = swap(grad_sent, "own")
     outward.append(to_end(1, middle[1]))
     low_got = step(low_got)
+    dx_first_sent, grad_sent, _ = lax.optimization_barrier((dx_first_sent, grad_sent, low_got))
+    grad_got = swap(grad_sent, "own")
+    dx_mine_got = swap(dx_first_sent, "own")
     delta, *up_parts = kernel_call(
         low_end_kernel,
         [like(both, kvq)] + [like(wide, kvq)] * 4,
@@ -612,7 +614,6 @@
     )
     done(delta)
     up_got = [around(up_parts[k], k) for k in (1, 2, 3)]
-    weight_far_other, dx_mine_got = step(weight_far_other, dx_mine_got)
     dx_other, dx_sent = kernel_call(
         dx_kernel,
         half_grad,
@@ -620,14 +621,14 @@
         back_wide,
         weight_other,
         weight_near_other,
-        weight_far_other,
+        step(weight_far_other),
         down_other,
         down_far_other,
     )
     dx_other_got = swap(done(dx_sent), "own")
-    grad_last, grad_sent = finish(1, middle[1], outward[1], grad_got)
+    grad_last, grad_sent = finish(1, middle[1], outward[1], dx_mine_got)
     grad_last_got = swap(grad_sent, "own")
-    up_got = step(*up_got)
+    *up_got, grad_got = step(*up_got, grad_got)
     up_mine, up_theirs = kernel_call(
         up_sum_kernel, [like(size, kvq)] * 2, up_parts[0], *up_got, scalars=numbers
     )

time: 225 us -> 220 us (0.978); the launches traced: 224 us -> 216 us
  waiting for transfers between devices: 103 us -> 84.6 us
  Pallas kernels: 53 us -> 59 us
  local copies, waits for them, and re-layouts: 9.33 us -> 13.8 us
    ppermute x20, waiting for transfers between devices: 73.5 us -> 45.2 us  [swap(): return lax.ppermute(value, axis, PAIR)]
    ppermute x16, waiting for transfers between devices: 29.9 us -> 39.4 us  [along(): return lax.ppermute(value, 'fsdp', pairs)]
    pallas_call x39, Pallas kernels: 53 us -> 59 us  [kernel_call(): pl.pallas_call(body, out_shape=list(outs), in_specs=specs, out_specs=[pl....]
    unnamed x27 -> x71, local copies, waits for them, and re-layouts: 9.05 us -> 13.6 us
    ppermute x16, starting transfers between devices: 28.7 us -> 31.7 us  [along(): return lax.ppermute(value, 'fsdp', pairs)]
  transfers between devices with their start and end apart: 37 -> 37, of which waited for: 17 -> 18; matrix products, arithmetic and copies ran while one was open for 1% -> 1% of each run, Pallas kernels for 19% -> 24%
where the time goes in v14:
time: 220 us; the launch traced here: 216 us
  waiting for transfers between devices  84.6 us (38%)
  Pallas kernels  59 us (27%)
  starting transfers between devices  57.4 us (26%)
  local copies, waits for them, and re-layouts  13.8 us (6%)
    pallas_call x39, Pallas kernels, kernel_call(): pl.pallas_call(body, out_shape=list(outs), in_specs=specs, out_specs=[pl....  59 us
    ppermute x20, waiting for transfers between devices, swap(): return lax.ppermute(value, axis, PAIR)  45.2 us
    ppermute x16, waiting for transfers between devices, along(): return lax.ppermute(value, 'fsdp', pairs)  39.4 us
    ppermute x16, starting transfers between devices, along(): return lax.ppermute(value, 'fsdp', pairs)  31.7 us
    ppermute x20, starting transfers between devices, swap(): return lax.ppermute(value, axis, PAIR)  18.5 us
    unnamed x71, local copies, waits for them, and re-layouts  13.6 us
    all_to_all x1, starting transfers between devices, body_line(): lax.all_to_all(done(up_sent), ('fsdp', 'own'), split_axis=0, concat_axis=...  7.25 us
  transfers between devices with their start and end apart: 37, of which 18 were waited for; matrix products, arithmetic and copies ran while one was open for 1% of the time, Pallas kernels for 24%

profile of v14, /device:TPU:0, one launch (start us, length us, event | category | flops | bytes accessed | tf_op | source)
XLA Modules:
  0.0 216.3 jit_solution(5128515335813280648)
XLA Ops:
  2.5 7.3 %all-to-all-start = ((bf16[8,128,256]{2,1,0:T(8,128)(2,1)}), bf16[8,128,256]{2,1,0:T(8,128)(2,1)S(1)}, u32[]{:S(2)}, u32[]{:S(2)}) async-start(bf16[8,128,256]{2,1,0:T(8,128)(2,1)} %shard_map.102), calls=%async_computation | async-start | bytes 1048576 | tf_op jit(solution)/shard_map/all_to_all | solution.py:441
  19.2 12.7 %collective-permute-done.1.refs_1_ = bf16[1024,128]{1,0:T(8,128)(2,1)} collective-permute-done((bf16[1024,128]{1,0:T(8,128)(2,1)S(1)}, bf16[1024,128]{1,0:T(8,128)(2,1)}, u32[]{:S(2)}, u32[]{:S(2)}) %collective-permute-start.1) | collective-permute-done | bytes 262176 | tf_op jit(solution)/shard_map/ppermute | solution.py:36
  44.9 8.5 %collective-permute-done.5.refs_1_.near.rest_1_ = bf16[1024,256]{1,0:T(8,128)(2,1)} collective-permute-done((bf16[1024,256]{1,0:T(8,128)(2,1)S(1)}, bf16[1024,256]{1,0:T(8,128)(2,1)}, u32[]{:S(2)}, u32[]{:S(2)}) %collective-permute-start.5) | collective-permute-done | bytes 524320 | tf_op jit(solution)/shard_map/ppermute | solution.py:40
  58.0 3.7 %collective-permute-start.10 = (bf16[512,256]{1,0:T(8,128)(2,1)S(1)}, bf16[512,256]{1,0:T(8,128)(2,1)S(1)}, u32[]{:S(2)}, u32[]{:S(2)}) collective-permute-start(bf16[512,256]{1,0:T(8,128)(2,1)S(1)} %get-tuple-element.94), channel_id=1, source_target_pairs={{0,4},{12,8},{1,5},{13,9},{2,6},{14,10},{3,7},{15,11},{16,20},{28,... | collective-permute-start | bytes 786440 | tf_op jit(solution)/shard_map/ppermute | solution.py:40
  66.5 2.4 %collective-permute-done.10.packet = bf16[512,256]{1,0:T(8,128)(2,1)S(1)} collective-permute-done((bf16[512,256]{1,0:T(8,128)(2,1)S(1)}, bf16[512,256]{1,0:T(8,128)(2,1)S(1)}, u32[]{:S(2)}, u32[]{:S(2)}) %collective-permute-start.10) | collective-permute-done | bytes 262176 | tf_op jit(solution)/shard_map/ppermute | solution.py:40
  71.8 4.5 %collective-permute-start.11 = (bf16[512,1024]{1,0:T(8,128)(2,1)S(1)}, bf16[512,1024]{1,0:T(8,128)(2,1)S(1)}, u32[]{:S(2)}, u32[]{:S(2)}) collective-permute-start(bf16[512,1024]{1,0:T(8,128)(2,1)S(1)} %shard_map.116.x_here.x_mine.tokens), channel_id=1, source_target_pairs={{0,4},{12,8},{1,5},{13,9},{2,6},{14,10},{3,7},{15,11},{16,20},{28,... | collective-permute-start | bytes 3145736 | tf_op jit(solution)/shard_map/ppermute | solution.py:40
  81.7 4.6 %collective-permute-done.8.own_near_other.rest_0_ = bf16[1024,512]{1,0:T(8,128)(2,1)S(1)} collective-permute-done((bf16[1024,512]{1,0:T(8,128)(2,1)S(1)}, bf16[1024,512]{1,0:T(8,128)(2,1)S(1)}, u32[]{:S(2)}, u32[]{:S(2)}) %collective-permute-start.8) | collective-permute-done | bytes 1048608 | tf_op jit(solution)/shard_map/ppermute | solution.py:36
  90.1 3.9 %collective-permute-start.13 = (bf16[512,1024]{1,0:T(8,128)(2,1)S(1)}, bf16[512,1024]{1,0:T(8,128)(2,1)S(1)}, u32[]{:S(2)}, u32[]{:S(2)}) collective-permute-start(bf16[512,1024]{1,0:T(8,128)(2,1)S(1)} %shard_map.118.x_here.x_other.tokens), channel_id=1, source_target_pairs={{0,4},{12,8},{1,5},{13,9},{2,6},{14,10},{3,7},{15,11},{16,20},{28,... | collective-permute-start | bytes 3145736 | tf_op jit(solution)/shard_map/ppermute | solution.py:40
  94.0 5.8 %collective-permute-done.11.x_in = bf16[512,1024]{1,0:T(8,128)(2,1)S(1)} collective-permute-done((bf16[512,1024]{1,0:T(8,128)(2,1)S(1)}, bf16[512,1024]{1,0:T(8,128)(2,1)S(1)}, u32[]{:S(2)}, u32[]{:S(2)}) %collective-permute-start.11) | collective-permute-done | bytes 1048608 | tf_op jit(solution)/shard_map/ppermute | solution.py:40
  104.7 8.4 %collective-permute-done.15.near = bf16[1024,256]{1,0:T(8,128)(2,1)S(1)} collective-permute-done((bf16[1024,256]{1,0:T(8,128)(2,1)}, bf16[1024,256]{1,0:T(8,128)(2,1)S(1)}, u32[]{:S(2)}, u32[]{:S(2)}) %collective-permute-start.15) | collective-permute-done | bytes 524320 | tf_op jit(solution)/shard_map/ppermute | solution.py:36
  116.3 4.6 %collective-permute-done.13.x_in = bf16[512,1024]{1,0:T(8,128)(2,1)S(1)} collective-permute-done((bf16[512,1024]{1,0:T(8,128)(2,1)S(1)}, bf16[512,1024]{1,0:T(8,128)(2,1)S(1)}, u32[]{:S(2)}, u32[]{:S(2)}) %collective-permute-start.13) | collective-permute-done | bytes 1048608 | tf_op jit(solution)/shard_map/ppermute | solution.py:40
  129.1 3.8 %collective-permute-done.18.outer = bf16[1024,512]{1,0:T(8,128)(2,1)} collective-permute-done((bf16[1024,512]{1,0:T(8,128)(2,1)}, bf16[1024,512]{1,0:T(8,128)(2,1)}, u32[]{:S(2)}, u32[]{:S(2)}) %collective-permute-start.18) | collective-permute-done | bytes 1048608 | tf_op jit(solution)/shard_map/ppermute | solution.py:40
  138.9 4.0 %shard_map.125.left = f32[512,128]{1,0:T(8,128)S(1)} custom-call(s32[24]{0:T(128)S(1)} %concatenate.3.numbers, bf16[512,128]{1,0:T(8,128)(2,1)S(1)} %get-tuple-element.87.ids, bf16[512,1024]{1,0:T(8,128)(2,1)S(1)} %shard_map.116.x_here.x_mine.tokens, bf16[512,1024]{1,0:T(8,128)(2,1)S(1)} %shard_map.118.x_here.x_other.tokens, ...), custom_call_target="tpu_custom_call" | custom-call | tf_op jit(solution)/shard_map/pallas_call | solution.py:48
  143.0 4.3 %shard_map.126 = (f32[2,512,256]{2,1,0:T(8,128)S(1)}, f32[2,512,256]{2,1,0:T(8,128)S(1)}) custom-call(s32[5]{0:T(128)S(1)} %convert_element_type.3.flags, bf16[512,1024]{1,0:T(8,128)(2,1)S(1)} %shard_map.116.x_here.x_mine.tokens, bf16[1024,256]{1,0:T(8,128)(2,1)} %shard_map.109.refs_0_.own, bf16[1024,256]{1,0:T(8,128)(2,1)} %collective-permute-done.2.refs_1_.near, ...), custom_call_target="tpu_custom_call" | custom-call | tf_op jit(solution)/shard_map/pallas_call | solution.py:48
  148.3 4.1 %shard_map.128 = (bf16[256,1024]{1,0:T(8,128)(2,1)S(1)}, bf16[256,1024]{1,0:T(8,128)(2,1)S(1)}) custom-call(bf16[512,1024]{1,0:T(8,128)(2,1)S(1)} %shard_map.123.dy, bf16[512,1024]{1,0:T(8,128)(2,1)S(1)} %get-tuple-element.105.back, bf16[1024,256]{1,0:T(8,128)(2,1)} %shard_map.109.refs_0_.own, bf16[1024,256]{1,0:T(8,128)(2,1)} %collective-permute-done.2.refs_1_.near, ...), custom_call_target="tpu_custom_call" | custom-call | tf_op jit(solution)/shard_map/pallas_call | solution.py:48
  152.4 3.9 %collective-permute-done.24.outer = bf16[1024,256]{1,0:T(8,128)(2,1)S(1)} collective-permute-done((bf16[1024,256]{1,0:T(8,128)(2,1)S(1)}, bf16[1024,256]{1,0:T(8,128)(2,1)S(1)}, u32[]{:S(2)}, u32[]{:S(2)}) %collective-permute-start.24) | collective-permute-done | bytes 524320 | tf_op jit(solution)/shard_map/ppermute | solution.py:40
  162.1 3.7 %shard_map.132 = (bf16[256,1024]{1,0:T(8,128)(2,1)S(1)}, bf16[256,1024]{1,0:T(8,128)(2,1)S(1)}) custom-call(bf16[512,1024]{1,0:T(8,128)(2,1)S(1)} %shard_map.123.dy, bf16[512,1024]{1,0:T(8,128)(2,1)S(1)} %get-tuple-element.105.back, bf16[1024,256]{1,0:T(8,128)(2,1)S(1)} %copy-done.11, bf16[1024,256]{1,0:T(8,128)(2,1)S(1)} %copy-done.23, ...), custom_call_target="tpu_custom_call" | custom-call | tf_op jit(solution)/shard_map/pallas_call | solution.py:48
  167.9 5.7 %collective-permute-start.26 = (bf16[256,256]{1,0:T(8,128)(2,1)S(1)}, bf16[256,256]{1,0:T(8,128)(2,1)S(1)}, u32[]{:S(2)}, u32[]{:S(2)}) collective-permute-start(bf16[256,256]{1,0:T(8,128)(2,1)S(1)} %get-tuple-element.130), channel_id=1, source_target_pairs={{0,4},{4,8},{8,12},{12,0},{1,5},{5,9},{9,13},{13,1},{2,6},{6,10},{... | collective-permute-start | bytes 393224 | tf_op jit(solution)/shard_map/ppermute | solution.py:40
  173.6 6.3 %collective-permute-done.30.outer = bf16[1024,256]{1,0:T(8,128)(2,1)S(1)} collective-permute-done((bf16[1024,256]{1,0:T(8,128)(2,1)S(1)}, bf16[1024,256]{1,0:T(8,128)(2,1)S(1)}, u32[]{:S(2)}, u32[]{:S(2)}) %collective-permute-start.30) | collective-permute-done | bytes 524320 | tf_op jit(solution)/shard_map/ppermute | solution.py:40
  183.9 4.1 %collective-permute-done.27.third = bf16[256,256]{1,0:T(8,128)(2,1)S(1)} collective-permute-done((bf16[256,256]{1,0:T(8,128)(2,1)S(1)}, bf16[256,256]{1,0:T(8,128)(2,1)S(1)}, u32[]{:S(2)}, u32[]{:S(2)}) %collective-permute-start.27) | collective-permute-done | bytes 131104 | tf_op jit(solution)/shard_map/ppermute | solution.py:40
  188.0 2.4 %collective-permute-done.29.refs_2_ = bf16[1024,128]{1,0:T(8,128)(2,1)S(1)} collective-permute-done((bf16[1024,128]{1,0:T(8,128)(2,1)S(1)}, bf16[1024,128]{1,0:T(8,128)(2,1)S(1)}, u32[]{:S(2)}, u32[]{:S(2)}) %collective-permute-start.29) | collective-permute-done | bytes 262176 | tf_op jit(solution)/shard_map/ppermute | solution.py:36
  191.0 3.5 %shard_map.135 = (f32[2,512,256]{2,1,0:T(8,128)S(1)}, f32[2,512,256]{2,1,0:T(8,128)S(1)}) custom-call(s32[5]{0:T(128)S(1)} %convert_element_type.3.flags, bf16[512,1024]{1,0:T(8,128)(2,1)S(1)} %shard_map.118.x_here.x_other.tokens, bf16[1024,256]{1,0:T(8,128)(2,1)S(1)} %copy-done.11, bf16[1024,256]{1,0:T(8,128)(2,1)S(1)} %copy-done.23, ...), custom_call_target="tpu_custom_call" | custom-call | tf_op jit(solution)/shard_map/pallas_call | solution.py:48
  195.0 8.4 %collective-permute-done.33.refs_3_ = bf16[1024,128]{1,0:T(8,128)(2,1)S(1)} collective-permute-done((bf16[1024,128]{1,0:T(8,128)(2,1)S(1)}, bf16[1024,128]{1,0:T(8,128)(2,1)S(1)}, u32[]{:S(2)}, u32[]{:S(2)}) %collective-permute-start.33) | collective-permute-done | bytes 262176 | tf_op jit(solution)/shard_map/ppermute | solution.py:36
  208.2 4.5 %collective-permute-done.34.got = bf16[2,256,256]{2,1,0:T(8,128)(2,1)S(1)} collective-permute-done((bf16[2,256,256]{2,1,0:T(8,128)(2,1)S(1)}, bf16[2,256,256]{2,1,0:T(8,128)(2,1)S(1)}, u32[]{:S(2)}, u32[]{:S(2)}) %collective-permute-start.34) | collective-permute-done | bytes 262176 | tf_op jit(solution)/shard_map/ppermute | solution.py:36
  (166 shorter events, 90.2 us)
Async XLA Ops:
  2.5 32.2 %all-to-all-start = ((bf16[8,128,256]{2,1,0:T(8,128)(2,1)}), bf16[8,128,256]{2,1,0:T(8,128)(2,1)S(1)}, u32[]{:S(2)}, u32[]{:S(2)}) async-start(bf16[8,128,256]{2,1,0:T(8,128)(2,1)} %shard_map.102), calls=%async_computation | async-start | bytes 1048576 | tf_op jit(solution)/shard_map/all_to_all | solution.py:441
  13.5 21.2 %collective-permute-start = (bf16[256,640]{1,0:T(8,128)(2,1)S(1)}, bf16[256,640]{1,0:T(8,128)(2,1)}, u32[]{:S(2)}, u32[]{:S(2)}) collective-permute-start(bf16[256,640]{1,0:T(8,128)(2,1)S(1)} %shard_map.104.here), channel_id=1, source_target_pairs={{0,2},{2,0},{1,3},{3,1},{4,6},{6,4},{5,7},{7,5},{8,10},{10,8},{9,1... | collective-permute-start | bytes 983048 | tf_op jit(solution)/shard_map/ppermute | solution.py:36
  15.6 16.3 %collective-permute-start.1 = (bf16[1024,128]{1,0:T(8,128)(2,1)S(1)}, bf16[1024,128]{1,0:T(8,128)(2,1)}, u32[]{:S(2)}, u32[]{:S(2)}) collective-permute-start(bf16[1024,128]{1,0:T(8,128)(2,1)S(1)} %shard_map.103), channel_id=1, source_target_pairs={{0,2},{2,0},{1,3},{3,1},{4,6},{6,4},{5,7},{7,5},{8,10},{10,8},{9,1... | collective-permute-start | bytes 786440 | tf_op jit(solution)/shard_map/ppermute | solution.py:36
  17.1 27.8 %collective-permute-start.6 = (bf16[256,1024]{1,0:T(8,128)(2,1)}, bf16[256,1024]{1,0:T(8,128)(2,1)}, u32[]{:S(2)}, u32[]{:S(2)}) collective-permute-start(bf16[256,1024]{1,0:T(8,128)(2,1)} %shard_map.105), channel_id=1, source_target_pairs={{0,2},{2,0},{1,3},{3,1},{4,6},{6,4},{5,7},{7,5},{8,10},{10,8},{9,1... | collective-permute-start | bytes 1572872 | tf_op jit(solution)/shard_map/ppermute | solution.py:36
  38.5 14.8 %collective-permute-start.5 = (bf16[1024,256]{1,0:T(8,128)(2,1)S(1)}, bf16[1024,256]{1,0:T(8,128)(2,1)}, u32[]{:S(2)}, u32[]{:S(2)}) collective-permute-start(bf16[1024,256]{1,0:T(8,128)(2,1)S(1)} %shard_map.106.refs_0_.own.rest_0_), channel_id=1, source_target_pairs={{0,4},{4,0},{8,12},{12,8},{1,5},{5,1},{9,13},{13,9},{2,6},{6,2},{1... | collective-permute-start | bytes 1572872 | tf_op jit(solution)/shard_map/ppermute | solution.py:40
  43.3 20.8 %collective-permute-start.2 = (bf16[1024,256]{1,0:T(8,128)(2,1)}, bf16[1024,256]{1,0:T(8,128)(2,1)}, u32[]{:S(2)}, u32[]{:S(2)}) collective-permute-start(bf16[1024,256]{1,0:T(8,128)(2,1)} %shard_map.109.refs_0_.own), channel_id=1, source_target_pairs={{0,4},{4,0},{8,12},{12,8},{1,5},{5,1},{9,13},{13,9},{2,6},{6,2},{1... | collective-permute-start | bytes 1572872 | tf_op jit(solution)/shard_map/ppermute | solution.py:40
  61.7 18.7 %collective-permute-start.9 = (bf16[1024,512]{1,0:T(8,128)(2,1)S(1)}, bf16[1024,512]{1,0:T(8,128)(2,1)S(1)}, u32[]{:S(2)}, u32[]{:S(2)}) collective-permute-start(bf16[1024,512]{1,0:T(8,128)(2,1)S(1)} %shard_map.111), channel_id=1, source_target_pairs={{4,8},{8,4},{5,9},{9,5},{6,10},{10,6},{7,11},{11,7},{20,24},{24,20... | collective-permute-start | bytes 3145736 | tf_op jit(solution)/shard_map/ppermute | solution.py:40
  62.4 23.8 %collective-permute-start.8 = (bf16[1024,512]{1,0:T(8,128)(2,1)S(1)}, bf16[1024,512]{1,0:T(8,128)(2,1)S(1)}, u32[]{:S(2)}, u32[]{:S(2)}) collective-permute-start(bf16[1024,512]{1,0:T(8,128)(2,1)S(1)} %shard_map.111), channel_id=1, source_target_pairs={{0,16},{16,0},{1,17},{17,1},{2,18},{18,2},{3,19},{19,3},{4,20},{20... | collective-permute-start | bytes 3145736 | tf_op jit(solution)/shard_map/ppermute | solution.py:36
  71.8 28.0 %collective-permute-start.11 = (bf16[512,1024]{1,0:T(8,128)(2,1)S(1)}, bf16[512,1024]{1,0:T(8,128)(2,1)S(1)}, u32[]{:S(2)}, u32[]{:S(2)}) collective-permute-start(bf16[512,1024]{1,0:T(8,128)(2,1)S(1)} %shard_map.116.x_here.x_mine.tokens), channel_id=1, source_target_pairs={{0,4},{12,8},{1,5},{13,9},{2,6},{14,10},{3,7},{15,11},{16,20},{28,... | collective-permute-start | bytes 3145736 | tf_op jit(solution)/shard_map/ppermute | solution.py:40
  76.3 13.2 %collective-permute-start.7 = (bf16[256,1024]{1,0:T(8,128)(2,1)S(1)}, bf16[256,1024]{1,0:T(8,128)(2,1)S(1)}, u32[]{:S(2)}, u32[]{:S(2)}) collective-permute-start(bf16[256,1024]{1,0:T(8,128)(2,1)S(1)} %shard_map.114), channel_id=1, source_target_pairs={{0,2},{2,0},{1,3},{3,1},{4,6},{6,4},{5,7},{7,5},{8,10},{10,8},{9,1... | collective-permute-start | bytes 1572872 | tf_op jit(solution)/shard_map/ppermute | solution.py:36
  77.3 26.2 %collective-permute-start.16 = (bf16[1024,512]{1,0:T(8,128)(2,1)S(1)}, bf16[1024,512]{1,0:T(8,128)(2,1)}, u32[]{:S(2)}, u32[]{:S(2)}) collective-permute-start(bf16[1024,512]{1,0:T(8,128)(2,1)S(1)} %shard_map.113), channel_id=1, source_target_pairs={{4,8},{8,4},{5,9},{9,5},{6,10},{10,6},{7,11},{11,7},{20,24},{24,20... | collective-permute-start | bytes 3145736 | tf_op jit(solution)/shard_map/ppermute | solution.py:40
  80.4 32.7 %collective-permute-start.14 = (bf16[1024,512]{1,0:T(8,128)(2,1)S(1)}, bf16[1024,512]{1,0:T(8,128)(2,1)S(1)}, u32[]{:S(2)}, u32[]{:S(2)}) collective-permute-start(bf16[1024,512]{1,0:T(8,128)(2,1)S(1)} %collective-permute-done.9.crossed), channel_id=1, source_target_pairs={{4,0},{8,12},{5,1},{9,13},{6,2},{10,14},{7,3},{11,15},{20,16},{24,... | collective-permute-start | bytes 3145736 | tf_op jit(solution)/shard_map/ppermute | solution.py:40
  90.1 30.7 %collective-permute-start.13 = (bf16[512,1024]{1,0:T(8,128)(2,1)S(1)}, bf16[512,1024]{1,0:T(8,128)(2,1)S(1)}, u32[]{:S(2)}, u32[]{:S(2)}) collective-permute-start(bf16[512,1024]{1,0:T(8,128)(2,1)S(1)} %shard_map.118.x_here.x_other.tokens), channel_id=1, source_target_pairs={{0,4},{12,8},{1,5},{13,9},{2,6},{14,10},{3,7},{15,11},{16,20},{28,... | collective-permute-start | bytes 3145736 | tf_op jit(solution)/shard_map/ppermute | solution.py:40
  101.1 22.0 %collective-permute-start.12 = (bf16[1024,512]{1,0:T(8,128)(2,1)S(1)}, bf16[1024,512]{1,0:T(8,128)(2,1)S(1)}, u32[]{:S(2)}, u32[]{:S(2)}) collective-permute-start(bf16[1024,512]{1,0:T(8,128)(2,1)S(1)} %shard_map.119), channel_id=1, source_target_pairs={{4,8},{8,4},{5,9},{9,5},{6,10},{10,6},{7,11},{11,7},{20,24},{24,20... | collective-permute-start | bytes 3145736 | tf_op jit(solution)/shard_map/ppermute | solution.py:40
  103.4 29.4 %collective-permute-start.18 = (bf16[1024,512]{1,0:T(8,128)(2,1)}, bf16[1024,512]{1,0:T(8,128)(2,1)}, u32[]{:S(2)}, u32[]{:S(2)}) collective-permute-start(bf16[1024,512]{1,0:T(8,128)(2,1)} %collective-permute-done.16.crossed), channel_id=1, source_target_pairs={{4,0},{8,12},{5,1},{9,13},{6,2},{10,14},{7,3},{11,15},{20,16},{24,... | collective-permute-start | bytes 3145736 | tf_op jit(solution)/shard_map/ppermute | solution.py:40
  114.7 24.2 %collective-permute-start.20 = (bf16[1024,512]{1,0:T(8,128)(2,1)}, bf16[1024,512]{1,0:T(8,128)(2,1)}, u32[]{:S(2)}, u32[]{:S(2)}) collective-permute-start(bf16[1024,512]{1,0:T(8,128)(2,1)} %shard_map.120.far.rest_2_), channel_id=1, source_target_pairs={{0,16},{16,0},{1,17},{17,1},{2,18},{18,2},{3,19},{19,3},{4,20},{20... | collective-permute-start | bytes 3145736 | tf_op jit(solution)/shard_map/ppermute | solution.py:36
  125.4 31.7 %collective-permute-start.23 = (bf16[1024,512]{1,0:T(8,128)(2,1)}, bf16[1024,512]{1,0:T(8,128)(2,1)}, u32[]{:S(2)}, u32[]{:S(2)}) collective-permute-start(bf16[1024,512]{1,0:T(8,128)(2,1)} %shard_map.121), channel_id=1, source_target_pairs={{4,8},{8,4},{5,9},{9,5},{6,10},{10,6},{7,11},{11,7},{20,24},{24,20... | collective-permute-start | bytes 3145736 | tf_op jit(solution)/shard_map/ppermute | solution.py:40
  134.5 27.6 %collective-permute-start.19 = (bf16[1024,512]{1,0:T(8,128)(2,1)S(1)}, bf16[1024,512]{1,0:T(8,128)(2,1)S(1)}, u32[]{:S(2)}, u32[]{:S(2)}) collective-permute-start(bf16[1024,512]{1,0:T(8,128)(2,1)S(1)} %shard_map.124.far), channel_id=1, source_target_pairs={{0,16},{16,0},{1,17},{17,1},{2,18},{18,2},{3,19},{19,3},{4,20},{20... | collective-permute-start | bytes 3145736 | tf_op jit(solution)/shard_map/ppermute | solution.py:36
  136.1 20.2 %collective-permute-start.24 = (bf16[1024,256]{1,0:T(8,128)(2,1)S(1)}, bf16[1024,256]{1,0:T(8,128)(2,1)S(1)}, u32[]{:S(2)}, u32[]{:S(2)}) collective-permute-start(bf16[1024,256]{1,0:T(8,128)(2,1)S(1)} %copy-done.29), channel_id=1, source_target_pairs={{4,0},{8,12},{5,1},{9,13},{6,2},{10,14},{7,3},{11,15},{20,16},{24,... | collective-permute-start | bytes 1572872 | tf_op jit(solution)/shard_map/ppermute | solution.py:40
  158.9 20.9 %collective-permute-start.30 = (bf16[1024,256]{1,0:T(8,128)(2,1)S(1)}, bf16[1024,256]{1,0:T(8,128)(2,1)S(1)}, u32[]{:S(2)}, u32[]{:S(2)}) collective-permute-start(bf16[1024,256]{1,0:T(8,128)(2,1)S(1)} %shard_map.130), channel_id=1, source_target_pairs={{4,0},{8,12},{5,1},{9,13},{6,2},{10,14},{7,3},{11,15},{20,16},{24,... | collective-permute-start | bytes 1572872 | tf_op jit(solution)/shard_map/ppermute | solution.py:40
  160.3 19.6 %collective-permute-start.31 = (bf16[256,1024]{1,0:T(8,128)(2,1)S(1)}, bf16[256,1024]{1,0:T(8,128)(2,1)S(1)}, u32[]{:S(2)}, u32[]{:S(2)}) collective-permute-start(bf16[256,1024]{1,0:T(8,128)(2,1)S(1)} %get-tuple-element.136), channel_id=1, source_target_pairs={{0,2},{2,0},{1,3},{3,1},{4,6},{6,4},{5,7},{7,5},{8,10},{10,8},{9,1... | collective-permute-start | bytes 1572872 | tf_op jit(solution)/shard_map/ppermute | solution.py:36
  165.8 25.3 %collective-permute-start.25 = (bf16[256,1024]{1,0:T(8,128)(2,1)S(1)}, bf16[256,1024]{1,0:T(8,128)(2,1)S(1)}, u32[]{:S(2)}, u32[]{:S(2)}) collective-permute-start(bf16[256,1024]{1,0:T(8,128)(2,1)S(1)} %get-tuple-element.128), channel_id=1, source_target_pairs={{0,2},{2,0},{1,3},{3,1},{4,6},{6,4},{5,7},{7,5},{8,10},{10,8},{9,1... | collective-permute-start | bytes 1572872 | tf_op jit(solution)/shard_map/ppermute | solution.py:36
  167.7 22.7 %collective-permute-start.29 = (bf16[1024,128]{1,0:T(8,128)(2,1)S(1)}, bf16[1024,128]{1,0:T(8,128)(2,1)S(1)}, u32[]{:S(2)}, u32[]{:S(2)}) collective-permute-start(bf16[1024,128]{1,0:T(8,128)(2,1)S(1)} %get-tuple-element.135), channel_id=1, source_target_pairs={{0,2},{2,0},{1,3},{3,1},{4,6},{6,4},{5,7},{7,5},{8,10},{10,8},{9,1... | collective-permute-start | bytes 786440 | tf_op jit(solution)/shard_map/ppermute | solution.py:36
  167.9 16.0 %collective-permute-start.26 = (bf16[256,256]{1,0:T(8,128)(2,1)S(1)}, bf16[256,256]{1,0:T(8,128)(2,1)S(1)}, u32[]{:S(2)}, u32[]{:S(2)}) collective-permute-start(bf16[256,256]{1,0:T(8,128)(2,1)S(1)} %get-tuple-element.130), channel_id=1, source_target_pairs={{0,4},{4,8},{8,12},{12,0},{1,5},{5,9},{9,13},{13,1},{2,6},{6,10},{... | collective-permute-start | bytes 393224 | tf_op jit(solution)/shard_map/ppermute | solution.py:40
  (48 other events, 362.6 us)

commit v15 on v12

--- a/solution.py
+++ b/solution.py
@@ -591,7 +591,6 @@
     )
     low_tp = swap(low_part, "tp")
     grad_here, grad_sent = finish(0, middle[0], outward[0])
-    grad_got = swap(grad_sent, "own")
     blocks = [like(2, both, cols, kind=f32)] * 2
     y_first = kernel_call(
         y_kernel, blocks, step(x_mine), weight_here, weight_near, weight_far, scalars=flags
@@ -601,7 +600,8 @@
     low_part = done(kernel_call(add_kernel, [compact], low_part, low_tp)[0])
     low_got = swap(low_part, "own")
     outward.append(to_end(1, middle[1]))
-    low_got, grad_got = step(low_got, grad_got)
+    low_got = step(low_got)
+    grad_got = swap(lax.optimization_barrier((grad_sent, low_got))[0], "own")
     delta, *up_parts = kernel_call(
         low_end_kernel,
         [like(both, kvq)] + [like(wide, kvq)] * 4,
@@ -628,12 +628,7 @@
     dx_other_got = swap(done(dx_sent), "own")
     grad_last, grad_sent = finish(1, middle[1], outward[1])
     grad_last_got = swap(grad_sent, "own")
-    up_got = step(*up_got)
-    up_mine, up_theirs = kernel_call(
-        up_sum_kernel, [like(size, kvq)] * 2, up_parts[0], *up_got, scalars=numbers
-    )
-    up_theirs = swap(done(up_theirs), "own")
-    x_other, dx_other_got = step(x_other, dx_other_got)
+    x_other, grad_got = step(x_other, grad_got)
     y_keep, y_sent = kernel_call(
         y_kernel,
         blocks,
@@ -645,7 +640,12 @@
         scalars=flags,
     )
     y_got = swap(done(y_sent), "tp")
-    y_got, grad_last_got = step(y_got, grad_last_got)
+    up_got = step(*up_got)
+    up_mine, up_theirs = kernel_call(
+        up_sum_kernel, [like(size, kvq)] * 2, up_parts[0], *up_got, scalars=numbers
+    )
+    up_theirs = swap(done(up_theirs), "own")
+    y_got = step(y_got)
     y_here, y_sent = kernel_call(
         y_sum_kernel,
         [like(2, rows, cols, kind=f32), like(2, rows, cols)],
@@ -665,7 +665,7 @@
 
         return copy_call(plan, [out], starts, *pieces)[0]
 
-    dx_other_got, _ = step(dx_other_got, dx_mine)
+    dx_other_got = step(dx_other_got)
     input_grad = done(
         in_place(1, like(rows, width), dx_mine, dx_other, dx_mine_got, dx_other_got)
     )

time: 209 us -> 201 us (0.962)
  waiting for transfers between devices: 72.8 us -> 68.6 us
  starting transfers between devices: 61.5 us -> 57.4 us
    ppermute x20, waiting for transfers between devices: 38 us -> 29.7 us  [swap(): return lax.ppermute(value, axis, PAIR)]
    ppermute x16, waiting for transfers between devices: 34.7 us -> 38.9 us  [along(): return lax.ppermute(value, 'fsdp', pairs)]
    ppermute x16, starting transfers between devices: 35.5 us -> 31.8 us  [along(): return lax.ppermute(value, 'fsdp', pairs)]
  transfers between devices with their start and end apart: 37 -> 37, of which waited for: 16 -> 18; matrix products, arithmetic and copies ran while one was open for 1% -> 1% of each run, Pallas kernels for 27% -> 28%
where the time goes in v15:
time: 201 us; the launch traced here: 200 us
  waiting for transfers between devices  68.6 us (34%)
  Pallas kernels  61.7 us (31%)
  starting transfers between devices  57.4 us (29%)
  local copies, waits for them, and re-layouts  10.6 us (5%)
    pallas_call x39, Pallas kernels, kernel_call(): pl.pallas_call(body, out_shape=list(outs), in_specs=specs, out_specs=[pl....  61.7 us
    ppermute x16, waiting for transfers between devices, along(): return lax.ppermute(value, 'fsdp', pairs)  38.9 us
    ppermute x16, starting transfers between devices, along(): return lax.ppermute(value, 'fsdp', pairs)  31.8 us
    ppermute x20, waiting for transfers between devices, swap(): return lax.ppermute(value, axis, PAIR)  29.7 us
    ppermute x20, starting transfers between devices, swap(): return lax.ppermute(value, axis, PAIR)  18.4 us
    unnamed x55, local copies, waits for them, and re-layouts  10.4 us
    all_to_all x1, starting transfers between devices, body_line(): lax.all_to_all(done(up_sent), ('fsdp', 'own'), split_axis=0, concat_axis=...  7.25 us
  transfers between devices with their start and end apart: 37, of which 18 were waited for; matrix products, arithmetic and copies ran while one was open for 1% of the time, Pallas kernels for 28%

profile of v15, /device:TPU:0, one launch (start us, length us, event | category | flops | bytes accessed | tf_op | source)
XLA Modules:
  0.0 199.7 jit_solution(13671752744336661522)
XLA Ops:
  2.5 7.3 %all-to-all-start = ((bf16[8,128,256]{2,1,0:T(8,128)(2,1)}), bf16[8,128,256]{2,1,0:T(8,128)(2,1)S(1)}, u32[]{:S(2)}, u32[]{:S(2)}) async-start(bf16[8,128,256]{2,1,0:T(8,128)(2,1)} %shard_map.102), calls=%async_computation | async-start | bytes 1048576 | tf_op jit(solution)/shard_map/all_to_all | solution.py:441
  19.2 5.4 %collective-permute-done.1.refs_1_ = bf16[1024,128]{1,0:T(8,128)(2,1)} collective-permute-done((bf16[1024,128]{1,0:T(8,128)(2,1)S(1)}, bf16[1024,128]{1,0:T(8,128)(2,1)}, u32[]{:S(2)}, u32[]{:S(2)}) %collective-permute-start.1) | collective-permute-done | bytes 262176 | tf_op jit(solution)/shard_map/ppermute | solution.py:36
  28.2 3.4 %collective-permute-done.there = bf16[256,640]{1,0:T(8,128)(2,1)} collective-permute-done((bf16[256,640]{1,0:T(8,128)(2,1)S(1)}, bf16[256,640]{1,0:T(8,128)(2,1)}, u32[]{:S(2)}, u32[]{:S(2)}) %collective-permute-start) | collective-permute-done | bytes 327712 | tf_op jit(solution)/shard_map/ppermute | solution.py:36
  42.4 2.6 %shard_map.111 = bf16[1024,512]{1,0:T(8,128)(2,1)} custom-call(s32[4]{0:T(128)S(1)} %pad_add_fusion.numbers, bf16[1024,256]{1,0:T(8,128)(2,1)S(1)} %shard_map.106.refs_0_.rest_0_.own, bf16[1024,256]{1,0:T(8,128)(2,1)} %collective-permute-done.5.refs_1_.rest_1_.near), custom_call_target="tpu_custom_call" | custom-call | tf_op jit(solution)/shard_map/pallas_call | solution.py:48
  51.7 4.0 %collective-permute-start.10 = (bf16[512,256]{1,0:T(8,128)(2,1)S(1)}, bf16[512,256]{1,0:T(8,128)(2,1)S(1)}, u32[]{:S(2)}, u32[]{:S(2)}) collective-permute-start(bf16[512,256]{1,0:T(8,128)(2,1)S(1)} %get-tuple-element.92), channel_id=1, source_target_pairs={{0,4},{12,8},{1,5},{13,9},{2,6},{14,10},{3,7},{15,11},{16,20},{28,... | collective-permute-start | bytes 786440 | tf_op jit(solution)/shard_map/ppermute | solution.py:40
  63.0 4.5 %collective-permute-start.11 = (bf16[512,1024]{1,0:T(8,128)(2,1)S(1)}, bf16[512,1024]{1,0:T(8,128)(2,1)S(1)}, u32[]{:S(2)}, u32[]{:S(2)}) collective-permute-start(bf16[512,1024]{1,0:T(8,128)(2,1)S(1)} %shard_map.116.x_here.x_mine.tokens), channel_id=1, source_target_pairs={{0,4},{12,8},{1,5},{13,9},{2,6},{14,10},{3,7},{15,11},{16,20},{28,... | collective-permute-start | bytes 3145736 | tf_op jit(solution)/shard_map/ppermute | solution.py:40
  74.6 6.1 %collective-permute-done.7.refs_1_ = bf16[256,1024]{1,0:T(8,128)(2,1)S(1)} collective-permute-done((bf16[256,1024]{1,0:T(8,128)(2,1)S(1)}, bf16[256,1024]{1,0:T(8,128)(2,1)S(1)}, u32[]{:S(2)}, u32[]{:S(2)}) %collective-permute-start.7) | collective-permute-done | bytes 524320 | tf_op jit(solution)/shard_map/ppermute | solution.py:36
  81.3 3.7 %collective-permute-start.13 = (bf16[512,1024]{1,0:T(8,128)(2,1)S(1)}, bf16[512,1024]{1,0:T(8,128)(2,1)}, u32[]{:S(2)}, u32[]{:S(2)}) collective-permute-start(bf16[512,1024]{1,0:T(8,128)(2,1)S(1)} %shard_map.118.x_here.x_other.tokens), channel_id=1, source_target_pairs={{0,4},{12,8},{1,5},{13,9},{2,6},{14,10},{3,7},{15,11},{16,20},{28,... | collective-permute-start | bytes 3145736 | tf_op jit(solution)/shard_map/ppermute | solution.py:40
  85.0 6.0 %collective-permute-done.11.x_in = bf16[512,1024]{1,0:T(8,128)(2,1)S(1)} collective-permute-done((bf16[512,1024]{1,0:T(8,128)(2,1)S(1)}, bf16[512,1024]{1,0:T(8,128)(2,1)S(1)}, u32[]{:S(2)}, u32[]{:S(2)}) %collective-permute-start.11) | collective-permute-done | bytes 1048608 | tf_op jit(solution)/shard_map/ppermute | solution.py:40
  101.7 8.5 %collective-permute-done.13.x_in = bf16[512,1024]{1,0:T(8,128)(2,1)} collective-permute-done((bf16[512,1024]{1,0:T(8,128)(2,1)S(1)}, bf16[512,1024]{1,0:T(8,128)(2,1)}, u32[]{:S(2)}, u32[]{:S(2)}) %collective-permute-start.13) | collective-permute-done | bytes 1048608 | tf_op jit(solution)/shard_map/ppermute | solution.py:40
  110.3 2.5 %shard_map.122 = bf16[1024,512]{1,0:T(8,128)(2,1)S(1)} custom-call(bf16[512,1024]{1,0:T(8,128)(2,1)S(1)} %shard_map.118.x_here.x_other.tokens, bf16[512,1024]{1,0:T(8,128)(2,1)S(1)} %get-tuple-element.102.back, bf16[512,1024]{1,0:T(8,128)(2,1)} %collective-permute-done.13.x_in, bf16[512,1024]{1,0:T(8,128)(2,1)S(1)} %copy-done.3), custom_call_target="tpu_custom_call" | custom-call | tf_op jit(solution)/shard_map/pallas_call | solution.py:48
  116.7 8.5 %collective-permute-done.20.outer = bf16[1024,512]{1,0:T(8,128)(2,1)} collective-permute-done((bf16[1024,512]{1,0:T(8,128)(2,1)}, bf16[1024,512]{1,0:T(8,128)(2,1)}, u32[]{:S(2)}, u32[]{:S(2)}) %collective-permute-start.20) | collective-permute-done | bytes 1048608 | tf_op jit(solution)/shard_map/ppermute | solution.py:40
  126.9 3.7 %shard_map.125 = (bf16[256,1024]{1,0:T(8,128)(2,1)S(1)}, bf16[256,1024]{1,0:T(8,128)(2,1)S(1)}) custom-call(bf16[512,1024]{1,0:T(8,128)(2,1)S(1)} %shard_map.120.dy, bf16[512,1024]{1,0:T(8,128)(2,1)S(1)} %get-tuple-element.102.back, bf16[1024,256]{1,0:T(8,128)(2,1)} %shard_map.109.refs_0_.own, bf16[1024,256]{1,0:T(8,128)(2,1)} %collective-permute-done.2.refs_1_.near, ...), custom_call_target="tpu_custom_call" | custom-call | tf_op jit(solution)/shard_map/pallas_call | solution.py:48
  132.6 3.7 %shard_map.126.left = f32[512,128]{1,0:T(8,128)S(1)} custom-call(s32[24]{0:T(128)S(1)} %concatenate.3.numbers, bf16[512,128]{1,0:T(8,128)(2,1)S(1)} %get-tuple-element.85.ids, bf16[512,1024]{1,0:T(8,128)(2,1)S(1)} %shard_map.116.x_here.x_mine.tokens, bf16[512,1024]{1,0:T(8,128)(2,1)S(1)} %shard_map.118.x_here.x_other.tokens, ...), custom_call_target="tpu_custom_call" | custom-call | tf_op jit(solution)/shard_map/pallas_call | solution.py:48
  136.4 3.0 %collective-permute-done.18.outer = bf16[1024,256]{1,0:T(8,128)(2,1)S(1)} collective-permute-done((bf16[1024,256]{1,0:T(8,128)(2,1)S(1)}, bf16[1024,256]{1,0:T(8,128)(2,1)S(1)}, u32[]{:S(2)}, u32[]{:S(2)}) %collective-permute-start.18) | collective-permute-done | bytes 524320 | tf_op jit(solution)/shard_map/ppermute | solution.py:40
  141.4 4.1 %shard_map.128 = (f32[2,512,256]{2,1,0:T(8,128)S(1)}, f32[2,512,256]{2,1,0:T(8,128)S(1)}) custom-call(s32[5]{0:T(128)S(1)} %convert_element_type.3.flags, bf16[512,1024]{1,0:T(8,128)(2,1)S(1)} %shard_map.116.x_here.x_mine.tokens, bf16[1024,256]{1,0:T(8,128)(2,1)} %shard_map.109.refs_0_.own, bf16[1024,256]{1,0:T(8,128)(2,1)} %collective-permute-done.2.refs_1_.near, ...), custom_call_target="tpu_custom_call" | custom-call | tf_op jit(solution)/shard_map/pallas_call | solution.py:48
  148.7 3.9 %collective-permute-done.23.got = f32[512,128]{1,0:T(8,128)S(1)} collective-permute-done((f32[512,128]{1,0:T(8,128)S(1)}, f32[512,128]{1,0:T(8,128)S(1)}, u32[]{:S(2)}, u32[]{:S(2)}) %collective-permute-start.23) | collective-permute-done | bytes 262176 | tf_op jit(solution)/shard_map/ppermute | solution.py:36
  155.6 3.6 %shard_map.132 = (bf16[256,1024]{1,0:T(8,128)(2,1)S(1)}, bf16[256,1024]{1,0:T(8,128)(2,1)S(1)}) custom-call(bf16[512,1024]{1,0:T(8,128)(2,1)S(1)} %shard_map.120.dy, bf16[512,1024]{1,0:T(8,128)(2,1)S(1)} %get-tuple-element.102.back, bf16[1024,256]{1,0:T(8,128)(2,1)S(1)} %copy-done.11, bf16[1024,256]{1,0:T(8,128)(2,1)S(1)} %copy-done.17, ...), custom_call_target="tpu_custom_call" | custom-call | tf_op jit(solution)/shard_map/pallas_call | solution.py:48
  159.2 2.3 %collective-permute-done.26.outer = bf16[1024,256]{1,0:T(8,128)(2,1)S(1)} collective-permute-done((bf16[1024,256]{1,0:T(8,128)(2,1)S(1)}, bf16[1024,256]{1,0:T(8,128)(2,1)S(1)}, u32[]{:S(2)}, u32[]{:S(2)}) %collective-permute-start.26) | collective-permute-done | bytes 524320 | tf_op jit(solution)/shard_map/ppermute | solution.py:40
  163.6 3.5 %shard_map.134 = (f32[2,512,256]{2,1,0:T(8,128)S(1)}, f32[2,512,256]{2,1,0:T(8,128)S(1)}) custom-call(s32[5]{0:T(128)S(1)} %convert_element_type.3.flags, bf16[512,1024]{1,0:T(8,128)(2,1)S(1)} %shard_map.118.x_here.x_other.tokens, bf16[1024,256]{1,0:T(8,128)(2,1)S(1)} %copy-done.11, bf16[1024,256]{1,0:T(8,128)(2,1)S(1)} %copy-done.17, ...), custom_call_target="tpu_custom_call" | custom-call | tf_op jit(solution)/shard_map/pallas_call | solution.py:48
  172.9 3.4 %collective-permute-done.29.second = bf16[256,256]{1,0:T(8,128)(2,1)S(1)} collective-permute-done((bf16[256,256]{1,0:T(8,128)(2,1)S(1)}, bf16[256,256]{1,0:T(8,128)(2,1)S(1)}, u32[]{:S(2)}, u32[]{:S(2)}) %collective-permute-start.29) | collective-permute-done | bytes 131104 | tf_op jit(solution)/shard_map/ppermute | solution.py:40
  176.3 4.8 %collective-permute-done.30.third = bf16[256,256]{1,0:T(8,128)(2,1)S(1)} collective-permute-done((bf16[256,256]{1,0:T(8,128)(2,1)S(1)}, bf16[256,256]{1,0:T(8,128)(2,1)S(1)}, u32[]{:S(2)}, u32[]{:S(2)}) %collective-permute-start.30) | collective-permute-done | bytes 131104 | tf_op jit(solution)/shard_map/ppermute | solution.py:40
  188.0 3.8 %collective-permute-done.32.got = bf16[2,256,256]{2,1,0:T(8,128)(2,1)S(1)} collective-permute-done((bf16[2,256,256]{2,1,0:T(8,128)(2,1)S(1)}, bf16[2,256,256]{2,1,0:T(8,128)(2,1)S(1)}, u32[]{:S(2)}, u32[]{:S(2)}) %collective-permute-start.32) | collective-permute-done | bytes 262176 | tf_op jit(solution)/shard_map/ppermute | solution.py:36
  192.5 4.3 %collective-permute-done.34.refs_3_ = bf16[1024,128]{1,0:T(8,128)(2,1)S(1)} collective-permute-done((bf16[1024,128]{1,0:T(8,128)(2,1)S(1)}, bf16[1024,128]{1,0:T(8,128)(2,1)S(1)}, u32[]{:S(2)}, u32[]{:S(2)}) %collective-permute-start.34) | collective-permute-done | bytes 262176 | tf_op jit(solution)/shard_map/ppermute | solution.py:36
  (150 shorter events, 91.9 us)
Async XLA Ops:
  2.5 29.1 %all-to-all-start = ((bf16[8,128,256]{2,1,0:T(8,128)(2,1)}), bf16[8,128,256]{2,1,0:T(8,128)(2,1)S(1)}, u32[]{:S(2)}, u32[]{:S(2)}) async-start(bf16[8,128,256]{2,1,0:T(8,128)(2,1)} %shard_map.102), calls=%async_computation | async-start | bytes 1048576 | tf_op jit(solution)/shard_map/all_to_all | solution.py:441
  15.6 16.0 %collective-permute-start = (bf16[256,640]{1,0:T(8,128)(2,1)S(1)}, bf16[256,640]{1,0:T(8,128)(2,1)}, u32[]{:S(2)}, u32[]{:S(2)}) collective-permute-start(bf16[256,640]{1,0:T(8,128)(2,1)S(1)} %shard_map.104.here), channel_id=1, source_target_pairs={{0,2},{2,0},{1,3},{3,1},{4,6},{6,4},{5,7},{7,5},{8,10},{10,8},{9,1... | collective-permute-start | bytes 983048 | tf_op jit(solution)/shard_map/ppermute | solution.py:36
  17.1 25.3 %collective-permute-start.6 = (bf16[256,1024]{1,0:T(8,128)(2,1)}, bf16[256,1024]{1,0:T(8,128)(2,1)}, u32[]{:S(2)}, u32[]{:S(2)}) collective-permute-start(bf16[256,1024]{1,0:T(8,128)(2,1)} %shard_map.105), channel_id=1, source_target_pairs={{0,2},{2,0},{1,3},{3,1},{4,6},{6,4},{5,7},{7,5},{8,10},{10,8},{9,1... | collective-permute-start | bytes 1572872 | tf_op jit(solution)/shard_map/ppermute | solution.py:36
  26.2 16.3 %collective-permute-start.5 = (bf16[1024,256]{1,0:T(8,128)(2,1)S(1)}, bf16[1024,256]{1,0:T(8,128)(2,1)}, u32[]{:S(2)}, u32[]{:S(2)}) collective-permute-start(bf16[1024,256]{1,0:T(8,128)(2,1)S(1)} %shard_map.106.refs_0_.rest_0_.own), channel_id=1, source_target_pairs={{0,4},{4,0},{8,12},{12,8},{1,5},{5,1},{9,13},{13,9},{2,6},{6,2},{1... | collective-permute-start | bytes 1572872 | tf_op jit(solution)/shard_map/ppermute | solution.py:40
  38.3 17.4 %collective-permute-start.2 = (bf16[1024,256]{1,0:T(8,128)(2,1)}, bf16[1024,256]{1,0:T(8,128)(2,1)}, u32[]{:S(2)}, u32[]{:S(2)}) collective-permute-start(bf16[1024,256]{1,0:T(8,128)(2,1)} %shard_map.109.refs_0_.own), channel_id=1, source_target_pairs={{0,4},{4,0},{8,12},{12,8},{1,5},{5,1},{9,13},{13,9},{2,6},{6,2},{1... | collective-permute-start | bytes 1572872 | tf_op jit(solution)/shard_map/ppermute | solution.py:40
  45.1 26.7 %collective-permute-start.9 = (bf16[1024,512]{1,0:T(8,128)(2,1)}, bf16[1024,512]{1,0:T(8,128)(2,1)}, u32[]{:S(2)}, u32[]{:S(2)}) collective-permute-start(bf16[1024,512]{1,0:T(8,128)(2,1)} %shard_map.111), channel_id=1, source_target_pairs={{4,8},{8,4},{5,9},{9,5},{6,10},{10,6},{7,11},{11,7},{20,24},{24,20... | collective-permute-start | bytes 3145736 | tf_op jit(solution)/shard_map/ppermute | solution.py:40
  46.7 25.1 %collective-permute-start.8 = (bf16[1024,512]{1,0:T(8,128)(2,1)}, bf16[1024,512]{1,0:T(8,128)(2,1)}, u32[]{:S(2)}, u32[]{:S(2)}) collective-permute-start(bf16[1024,512]{1,0:T(8,128)(2,1)} %shard_map.111), channel_id=1, source_target_pairs={{0,16},{16,0},{1,17},{17,1},{2,18},{18,2},{3,19},{19,3},{4,20},{20... | collective-permute-start | bytes 3145736 | tf_op jit(solution)/shard_map/ppermute | solution.py:36
  63.0 28.0 %collective-permute-start.11 = (bf16[512,1024]{1,0:T(8,128)(2,1)S(1)}, bf16[512,1024]{1,0:T(8,128)(2,1)S(1)}, u32[]{:S(2)}, u32[]{:S(2)}) collective-permute-start(bf16[512,1024]{1,0:T(8,128)(2,1)S(1)} %shard_map.116.x_here.x_mine.tokens), channel_id=1, source_target_pairs={{0,4},{12,8},{1,5},{13,9},{2,6},{14,10},{3,7},{15,11},{16,20},{28,... | collective-permute-start | bytes 3145736 | tf_op jit(solution)/shard_map/ppermute | solution.py:40
  67.5 25.8 %collective-permute-start.16 = (bf16[1024,512]{1,0:T(8,128)(2,1)S(1)}, bf16[1024,512]{1,0:T(8,128)(2,1)}, u32[]{:S(2)}, u32[]{:S(2)}) collective-permute-start(bf16[1024,512]{1,0:T(8,128)(2,1)S(1)} %shard_map.113), channel_id=1, source_target_pairs={{4,8},{8,4},{5,9},{9,5},{6,10},{10,6},{7,11},{11,7},{20,24},{24,20... | collective-permute-start | bytes 3145736 | tf_op jit(solution)/shard_map/ppermute | solution.py:40
  71.8 21.5 %collective-permute-start.15 = (bf16[1024,256]{1,0:T(8,128)(2,1)}, bf16[1024,256]{1,0:T(8,128)(2,1)S(1)}, u32[]{:S(2)}, u32[]{:S(2)}) collective-permute-start(bf16[1024,256]{1,0:T(8,128)(2,1)} %collective-permute-done.2.refs_1_.near), channel_id=1, source_target_pairs={{0,16},{16,0},{1,17},{17,1},{2,18},{18,2},{3,19},{19,3},{4,20},{20... | collective-permute-start | bytes 1572872 | tf_op jit(solution)/shard_map/ppermute | solution.py:36
  73.3 25.8 %collective-permute-start.14 = (bf16[1024,512]{1,0:T(8,128)(2,1)}, bf16[1024,512]{1,0:T(8,128)(2,1)}, u32[]{:S(2)}, u32[]{:S(2)}) collective-permute-start(bf16[1024,512]{1,0:T(8,128)(2,1)} %collective-permute-done.9.crossed), channel_id=1, source_target_pairs={{4,0},{8,12},{5,1},{9,13},{6,2},{10,14},{7,3},{11,15},{20,16},{24,... | collective-permute-start | bytes 3145736 | tf_op jit(solution)/shard_map/ppermute | solution.py:40
  81.3 28.9 %collective-permute-start.13 = (bf16[512,1024]{1,0:T(8,128)(2,1)S(1)}, bf16[512,1024]{1,0:T(8,128)(2,1)}, u32[]{:S(2)}, u32[]{:S(2)}) collective-permute-start(bf16[512,1024]{1,0:T(8,128)(2,1)S(1)} %shard_map.118.x_here.x_other.tokens), channel_id=1, source_target_pairs={{0,4},{12,8},{1,5},{13,9},{2,6},{14,10},{3,7},{15,11},{16,20},{28,... | collective-permute-start | bytes 3145736 | tf_op jit(solution)/shard_map/ppermute | solution.py:40
  94.2 19.3 %collective-permute-start.12 = (bf16[1024,512]{1,0:T(8,128)(2,1)}, bf16[1024,512]{1,0:T(8,128)(2,1)}, u32[]{:S(2)}, u32[]{:S(2)}) collective-permute-start(bf16[1024,512]{1,0:T(8,128)(2,1)} %shard_map.119), channel_id=1, source_target_pairs={{4,8},{8,4},{5,9},{9,5},{6,10},{10,6},{7,11},{11,7},{20,24},{24,20... | collective-permute-start | bytes 3145736 | tf_op jit(solution)/shard_map/ppermute | solution.py:40
  95.8 29.3 %collective-permute-start.20 = (bf16[1024,512]{1,0:T(8,128)(2,1)}, bf16[1024,512]{1,0:T(8,128)(2,1)}, u32[]{:S(2)}, u32[]{:S(2)}) collective-permute-start(bf16[1024,512]{1,0:T(8,128)(2,1)} %collective-permute-done.16.crossed), channel_id=1, source_target_pairs={{4,0},{8,12},{5,1},{9,13},{6,2},{10,14},{7,3},{11,15},{20,16},{24,... | collective-permute-start | bytes 3145736 | tf_op jit(solution)/shard_map/ppermute | solution.py:40
  100.7 31.8 %collective-permute-start.19 = (bf16[1024,512]{1,0:T(8,128)(2,1)S(1)}, bf16[1024,512]{1,0:T(8,128)(2,1)S(1)}, u32[]{:S(2)}, u32[]{:S(2)}) collective-permute-start(bf16[1024,512]{1,0:T(8,128)(2,1)S(1)} %shard_map.121.rest_2_.far), channel_id=1, source_target_pairs={{0,16},{16,0},{1,17},{17,1},{2,18},{18,2},{3,19},{19,3},{4,20},{20... | collective-permute-start | bytes 3145736 | tf_op jit(solution)/shard_map/ppermute | solution.py:36
  112.8 34.1 %collective-permute-start.24 = (bf16[1024,512]{1,0:T(8,128)(2,1)S(1)}, bf16[1024,512]{1,0:T(8,128)(2,1)S(1)}, u32[]{:S(2)}, u32[]{:S(2)}) collective-permute-start(bf16[1024,512]{1,0:T(8,128)(2,1)S(1)} %shard_map.122), channel_id=1, source_target_pairs={{4,8},{8,4},{5,9},{9,5},{6,10},{10,6},{7,11},{11,7},{20,24},{24,20... | collective-permute-start | bytes 3145736 | tf_op jit(solution)/shard_map/ppermute | solution.py:40
  115.2 24.1 %collective-permute-start.18 = (bf16[1024,256]{1,0:T(8,128)(2,1)S(1)}, bf16[1024,256]{1,0:T(8,128)(2,1)S(1)}, u32[]{:S(2)}, u32[]{:S(2)}) collective-permute-start(bf16[1024,256]{1,0:T(8,128)(2,1)S(1)} %shard_map.123), channel_id=1, source_target_pairs={{4,0},{8,12},{5,1},{9,13},{6,2},{10,14},{7,3},{11,15},{20,16},{24,... | collective-permute-start | bytes 1572872 | tf_op jit(solution)/shard_map/ppermute | solution.py:40
  130.7 14.8 %collective-permute-start.22 = (bf16[256,1024]{1,0:T(8,128)(2,1)S(1)}, bf16[256,1024]{1,0:T(8,128)(2,1)S(1)}, u32[]{:S(2)}, u32[]{:S(2)}) collective-permute-start(bf16[256,1024]{1,0:T(8,128)(2,1)S(1)} %get-tuple-element.114), channel_id=1, source_target_pairs={{0,2},{2,0},{1,3},{3,1},{4,6},{6,4},{5,7},{7,5},{8,10},{10,8},{9,1... | collective-permute-start | bytes 1572872 | tf_op jit(solution)/shard_map/ppermute | solution.py:36
  131.0 24.6 %collective-permute-start.27 = (bf16[1024,512]{1,0:T(8,128)(2,1)S(1)}, bf16[1024,512]{1,0:T(8,128)(2,1)S(1)}, u32[]{:S(2)}, u32[]{:S(2)}) collective-permute-start(bf16[1024,512]{1,0:T(8,128)(2,1)S(1)} %shard_map.124.far), channel_id=1, source_target_pairs={{0,16},{16,0},{1,17},{17,1},{2,18},{18,2},{3,19},{19,3},{4,20},{20... | collective-permute-start | bytes 3145736 | tf_op jit(solution)/shard_map/ppermute | solution.py:36
  147.4 14.2 %collective-permute-start.26 = (bf16[1024,256]{1,0:T(8,128)(2,1)S(1)}, bf16[1024,256]{1,0:T(8,128)(2,1)S(1)}, u32[]{:S(2)}, u32[]{:S(2)}) collective-permute-start(bf16[1024,256]{1,0:T(8,128)(2,1)S(1)} %shard_map.130), channel_id=1, source_target_pairs={{4,0},{8,12},{5,1},{9,13},{6,2},{10,14},{7,3},{11,15},{20,16},{24,... | collective-permute-start | bytes 1572872 | tf_op jit(solution)/shard_map/ppermute | solution.py:40
  167.1 14.7 %collective-permute-start.28 = (f32[2,512,256]{2,1,0:T(8,128)S(1)}, f32[2,512,256]{2,1,0:T(8,128)S(1)}, u32[]{:S(2)}, u32[]{:S(2)}) collective-permute-start(f32[2,512,256]{2,1,0:T(8,128)S(1)} %get-tuple-element.134), channel_id=1, source_target_pairs={{0,1},{1,0},{2,3},{3,2},{4,5},{5,4},{6,7},{7,6},{8,9},{9,8},{10,11... | collective-permute-start | bytes 3145736 | tf_op jit(solution)/shard_map/ppermute | solution.py:36
  167.2 18.7 %collective-permute-start.33 = (bf16[256,1024]{1,0:T(8,128)(2,1)S(1)}, bf16[256,1024]{1,0:T(8,128)(2,1)S(1)}, u32[]{:S(2)}, u32[]{:S(2)}) collective-permute-start(bf16[256,1024]{1,0:T(8,128)(2,1)S(1)} %get-tuple-element.128), channel_id=1, source_target_pairs={{0,2},{2,0},{1,3},{3,1},{4,6},{6,4},{5,7},{7,5},{8,10},{10,8},{9,1... | collective-permute-start | bytes 1572872 | tf_op jit(solution)/shard_map/ppermute | solution.py:36
  183.8 13.0 %collective-permute-start.34 = (bf16[1024,128]{1,0:T(8,128)(2,1)S(1)}, bf16[1024,128]{1,0:T(8,128)(2,1)S(1)}, u32[]{:S(2)}, u32[]{:S(2)}) collective-permute-start(bf16[1024,128]{1,0:T(8,128)(2,1)S(1)} %get-tuple-element.152), channel_id=1, source_target_pairs={{0,2},{2,0},{1,3},{3,1},{4,6},{6,4},{5,7},{7,5},{8,10},{10,8},{9,1... | collective-permute-start | bytes 786440 | tf_op jit(solution)/shard_map/ppermute | solution.py:36
  184.6 13.9 %collective-permute-start.35 = (bf16[128,256]{1,0:T(8,128)(2,1)S(1)}, bf16[128,256]{1,0:T(8,128)(2,1)S(1)}, u32[]{:S(2)}, u32[]{:S(2)}) collective-permute-start(bf16[128,256]{1,0:T(8,128)(2,1)S(1)} %get-tuple-element.142), channel_id=1, source_target_pairs={{0,2},{2,0},{1,3},{3,1},{4,6},{6,4},{5,7},{7,5},{8,10},{10,8},{9,1... | collective-permute-start | bytes 196616 | tf_op jit(solution)/shard_map/ppermute | solution.py:36
  (40 other events, 307.8 us)

commit v16 on v12

--- a/solution.py
+++ b/solution.py
@@ -591,7 +591,6 @@
     )
     low_tp = swap(low_part, "tp")
     grad_here, grad_sent = finish(0, middle[0], outward[0])
-    grad_got = swap(grad_sent, "own")
     blocks = [like(2, both, cols, kind=f32)] * 2
     y_first = kernel_call(
         y_kernel, blocks, step(x_mine), weight_here, weight_near, weight_far, scalars=flags
@@ -601,7 +600,8 @@
     low_part = done(kernel_call(add_kernel, [compact], low_part, low_tp)[0])
     low_got = swap(low_part, "own")
     outward.append(to_end(1, middle[1]))
-    low_got, grad_got = step(low_got, grad_got)
+    low_got = step(low_got)
+    grad_got = swap(lax.optimization_barrier((grad_sent, low_got))[0], "own")
     delta, *up_parts = kernel_call(
         low_end_kernel,
         [like(both, kvq)] + [like(wide, kvq)] * 4,
@@ -628,7 +628,7 @@
     dx_other_got = swap(done(dx_sent), "own")
     grad_last, grad_sent = finish(1, middle[1], outward[1])
     grad_last_got = swap(grad_sent, "own")
-    up_got = step(*up_got)
+    *up_got, grad_got = step(*up_got, grad_got)
     up_mine, up_theirs = kernel_call(
         up_sum_kernel, [like(size, kvq)] * 2, up_parts[0], *up_got, scalars=numbers
     )
@@ -645,7 +645,7 @@
         scalars=flags,
     )
     y_got = swap(done(y_sent), "tp")
-    y_got, grad_last_got = step(y_got, grad_last_got)
+    y_got = step(y_got)
     y_here, y_sent = kernel_call(
         y_sum_kernel,
         [like(2, rows, cols, kind=f32), like(2, rows, cols)],
@@ -665,7 +665,7 @@
 
         return copy_call(plan, [out], starts, *pieces)[0]
 
-    dx_other_got, _ = step(dx_other_got, dx_mine)
+    dx_other_got = step(dx_other_got)
     input_grad = done(
         in_place(1, like(rows, width), dx_mine, dx_other, dx_mine_got, dx_other_got)
     )

time: 209 us -> 205 us (0.981)
  starting transfers between devices: 61.5 us -> 53.6 us
  waiting for transfers between devices: 72.8 us -> 76.7 us
    ppermute x16, starting transfers between devices: 35.5 us -> 29.3 us  [along(): return lax.ppermute(value, 'fsdp', pairs)]
    ppermute x16, waiting for transfers between devices: 34.7 us -> 38.2 us  [along(): return lax.ppermute(value, 'fsdp', pairs)]
  transfers between devices with their start and end apart: 37 -> 37, of which waited for: 16 -> 19; matrix products, arithmetic and copies ran while one was open for 1% -> 1% of each run, Pallas kernels for 27% -> 27%
where the time goes in v16:
time: 205 us; the launch traced here: 204 us
  waiting for transfers between devices  76.7 us (37%)
  Pallas kernels  61.4 us (30%)
  starting transfers between devices  53.6 us (26%)
  local copies, waits for them, and re-layouts  10.6 us (5%)
    pallas_call x39, Pallas kernels, kernel_call(): pl.pallas_call(body, out_shape=list(outs), in_specs=specs, out_specs=[pl....  61.4 us
    ppermute x20, waiting for transfers between devices, swap(): return lax.ppermute(value, axis, PAIR)  38.5 us
    ppermute x16, waiting for transfers between devices, along(): return lax.ppermute(value, 'fsdp', pairs)  38.2 us
    ppermute x16, starting transfers between devices, along(): return lax.ppermute(value, 'fsdp', pairs)  29.3 us
    ppermute x20, starting transfers between devices, swap(): return lax.ppermute(value, axis, PAIR)  17 us
    unnamed x55, local copies, waits for them, and re-layouts  10.4 us
    all_to_all x1, starting transfers between devices, body_line(): lax.all_to_all(done(up_sent), ('fsdp', 'own'), split_axis=0, concat_axis=...  7.25 us
  transfers between devices with their start and end apart: 37, of which 19 were waited for; matrix products, arithmetic and copies ran while one was open for 1% of the time, Pallas kernels for 27%

profile of v16, /device:TPU:0, one launch (start us, length us, event | category | flops | bytes accessed | tf_op | source)
XLA Modules:
  0.0 203.7 jit_solution(10899279529829046883)
XLA Ops:
  2.5 7.3 %all-to-all-start = ((bf16[8,128,256]{2,1,0:T(8,128)(2,1)}), bf16[8,128,256]{2,1,0:T(8,128)(2,1)S(1)}, u32[]{:S(2)}, u32[]{:S(2)}) async-start(bf16[8,128,256]{2,1,0:T(8,128)(2,1)} %shard_map.102), calls=%async_computation | async-start | bytes 1048576 | tf_op jit(solution)/shard_map/all_to_all | solution.py:441
  19.2 5.4 %collective-permute-done.1.refs_1_ = bf16[1024,128]{1,0:T(8,128)(2,1)} collective-permute-done((bf16[1024,128]{1,0:T(8,128)(2,1)S(1)}, bf16[1024,128]{1,0:T(8,128)(2,1)}, u32[]{:S(2)}, u32[]{:S(2)}) %collective-permute-start.1) | collective-permute-done | bytes 262176 | tf_op jit(solution)/shard_map/ppermute | solution.py:36
  28.2 3.4 %collective-permute-done.there = bf16[256,640]{1,0:T(8,128)(2,1)} collective-permute-done((bf16[256,640]{1,0:T(8,128)(2,1)S(1)}, bf16[256,640]{1,0:T(8,128)(2,1)}, u32[]{:S(2)}, u32[]{:S(2)}) %collective-permute-start) | collective-permute-done | bytes 327712 | tf_op jit(solution)/shard_map/ppermute | solution.py:36
  42.4 2.6 %shard_map.111 = bf16[1024,512]{1,0:T(8,128)(2,1)} custom-call(s32[4]{0:T(128)S(1)} %pad_add_fusion.numbers, bf16[1024,256]{1,0:T(8,128)(2,1)S(1)} %shard_map.106.refs_0_.rest_0_.own, bf16[1024,256]{1,0:T(8,128)(2,1)} %collective-permute-done.5.refs_1_.rest_1_.near), custom_call_target="tpu_custom_call" | custom-call | tf_op jit(solution)/shard_map/pallas_call | solution.py:48
  51.7 4.0 %collective-permute-start.10 = (bf16[512,256]{1,0:T(8,128)(2,1)S(1)}, bf16[512,256]{1,0:T(8,128)(2,1)S(1)}, u32[]{:S(2)}, u32[]{:S(2)}) collective-permute-start(bf16[512,256]{1,0:T(8,128)(2,1)S(1)} %get-tuple-element.93), channel_id=1, source_target_pairs={{0,4},{12,8},{1,5},{13,9},{2,6},{14,10},{3,7},{15,11},{16,20},{28,... | collective-permute-start | bytes 786440 | tf_op jit(solution)/shard_map/ppermute | solution.py:40
  63.0 4.5 %collective-permute-start.13 = (bf16[512,1024]{1,0:T(8,128)(2,1)S(1)}, bf16[512,1024]{1,0:T(8,128)(2,1)S(1)}, u32[]{:S(2)}, u32[]{:S(2)}) collective-permute-start(bf16[512,1024]{1,0:T(8,128)(2,1)S(1)} %shard_map.116.x_here.x_mine.tokens), channel_id=1, source_target_pairs={{0,4},{12,8},{1,5},{13,9},{2,6},{14,10},{3,7},{15,11},{16,20},{28,... | collective-permute-start | bytes 3145736 | tf_op jit(solution)/shard_map/ppermute | solution.py:40
  74.6 6.1 %collective-permute-done.7.refs_1_ = bf16[256,1024]{1,0:T(8,128)(2,1)S(1)} collective-permute-done((bf16[256,1024]{1,0:T(8,128)(2,1)S(1)}, bf16[256,1024]{1,0:T(8,128)(2,1)S(1)}, u32[]{:S(2)}, u32[]{:S(2)}) %collective-permute-start.7) | collective-permute-done | bytes 524320 | tf_op jit(solution)/shard_map/ppermute | solution.py:36
  81.3 3.7 %collective-permute-start.17 = (bf16[512,1024]{1,0:T(8,128)(2,1)S(1)}, bf16[512,1024]{1,0:T(8,128)(2,1)}, u32[]{:S(2)}, u32[]{:S(2)}) collective-permute-start(bf16[512,1024]{1,0:T(8,128)(2,1)S(1)} %shard_map.118.x_here.x_other.tokens), channel_id=1, source_target_pairs={{0,4},{12,8},{1,5},{13,9},{2,6},{14,10},{3,7},{15,11},{16,20},{28,... | collective-permute-start | bytes 3145736 | tf_op jit(solution)/shard_map/ppermute | solution.py:40
  85.0 6.0 %collective-permute-done.13.x_in = bf16[512,1024]{1,0:T(8,128)(2,1)S(1)} collective-permute-done((bf16[512,1024]{1,0:T(8,128)(2,1)S(1)}, bf16[512,1024]{1,0:T(8,128)(2,1)S(1)}, u32[]{:S(2)}, u32[]{:S(2)}) %collective-permute-start.13) | collective-permute-done | bytes 1048608 | tf_op jit(solution)/shard_map/ppermute | solution.py:40
  101.7 8.5 %collective-permute-done.17.x_in = bf16[512,1024]{1,0:T(8,128)(2,1)} collective-permute-done((bf16[512,1024]{1,0:T(8,128)(2,1)S(1)}, bf16[512,1024]{1,0:T(8,128)(2,1)}, u32[]{:S(2)}, u32[]{:S(2)}) %collective-permute-start.17) | collective-permute-done | bytes 1048608 | tf_op jit(solution)/shard_map/ppermute | solution.py:40
  110.3 2.5 %shard_map.122 = bf16[1024,512]{1,0:T(8,128)(2,1)S(1)} custom-call(bf16[512,1024]{1,0:T(8,128)(2,1)S(1)} %shard_map.118.x_here.x_other.tokens, bf16[512,1024]{1,0:T(8,128)(2,1)S(1)} %get-tuple-element.104.back, bf16[512,1024]{1,0:T(8,128)(2,1)} %collective-permute-done.17.x_in, bf16[512,1024]{1,0:T(8,128)(2,1)S(1)} %copy-done.3), custom_call_target="tpu_custom_call" | custom-call | tf_op jit(solution)/shard_map/pallas_call | solution.py:48
  115.2 9.9 %collective-permute-done.15.outer = bf16[1024,512]{1,0:T(8,128)(2,1)} collective-permute-done((bf16[1024,512]{1,0:T(8,128)(2,1)}, bf16[1024,512]{1,0:T(8,128)(2,1)}, u32[]{:S(2)}, u32[]{:S(2)}) %collective-permute-start.15) | collective-permute-done | bytes 1048608 | tf_op jit(solution)/shard_map/ppermute | solution.py:40
  129.5 3.7 %shard_map.125 = (bf16[256,1024]{1,0:T(8,128)(2,1)S(1)}, bf16[256,1024]{1,0:T(8,128)(2,1)S(1)}) custom-call(bf16[512,1024]{1,0:T(8,128)(2,1)S(1)} %shard_map.120.dy, bf16[512,1024]{1,0:T(8,128)(2,1)S(1)} %get-tuple-element.104.back, bf16[1024,256]{1,0:T(8,128)(2,1)} %shard_map.109.refs_0_.own, bf16[1024,256]{1,0:T(8,128)(2,1)} %collective-permute-done.2.refs_1_.near, ...), custom_call_target="tpu_custom_call" | custom-call | tf_op jit(solution)/shard_map/pallas_call | solution.py:48
  133.9 3.7 %shard_map.126.left = f32[512,128]{1,0:T(8,128)S(1)} custom-call(s32[24]{0:T(128)S(1)} %concatenate.3.numbers, bf16[512,128]{1,0:T(8,128)(2,1)S(1)} %get-tuple-element.86.ids, bf16[512,1024]{1,0:T(8,128)(2,1)S(1)} %shard_map.116.x_here.x_mine.tokens, bf16[512,1024]{1,0:T(8,128)(2,1)S(1)} %shard_map.118.x_here.x_other.tokens, ...), custom_call_target="tpu_custom_call" | custom-call | tf_op jit(solution)/shard_map/pallas_call | solution.py:48
  137.7 5.5 %collective-permute-done.23.outer = bf16[1024,256]{1,0:T(8,128)(2,1)S(1)} collective-permute-done((bf16[1024,256]{1,0:T(8,128)(2,1)S(1)}, bf16[1024,256]{1,0:T(8,128)(2,1)S(1)}, u32[]{:S(2)}, u32[]{:S(2)}) %collective-permute-start.23) | collective-permute-done | bytes 524320 | tf_op jit(solution)/shard_map/ppermute | solution.py:40
  145.2 4.1 %shard_map.128 = (f32[2,512,256]{2,1,0:T(8,128)S(1)}, f32[2,512,256]{2,1,0:T(8,128)S(1)}) custom-call(s32[5]{0:T(128)S(1)} %convert_element_type.3.flags, bf16[512,1024]{1,0:T(8,128)(2,1)S(1)} %shard_map.116.x_here.x_mine.tokens, bf16[1024,256]{1,0:T(8,128)(2,1)} %shard_map.109.refs_0_.own, bf16[1024,256]{1,0:T(8,128)(2,1)} %collective-permute-done.2.refs_1_.near, ...), custom_call_target="tpu_custom_call" | custom-call | tf_op jit(solution)/shard_map/pallas_call | solution.py:48
  151.9 4.4 %collective-permute-done.24.got = f32[512,128]{1,0:T(8,128)S(1)} collective-permute-done((f32[512,128]{1,0:T(8,128)S(1)}, f32[512,128]{1,0:T(8,128)S(1)}, u32[]{:S(2)}, u32[]{:S(2)}) %collective-permute-start.24) | collective-permute-done | bytes 262176 | tf_op jit(solution)/shard_map/ppermute | solution.py:36
  157.8 3.6 %shard_map.132 = (bf16[256,1024]{1,0:T(8,128)(2,1)S(1)}, bf16[256,1024]{1,0:T(8,128)(2,1)S(1)}) custom-call(bf16[512,1024]{1,0:T(8,128)(2,1)S(1)} %shard_map.120.dy, bf16[512,1024]{1,0:T(8,128)(2,1)S(1)} %get-tuple-element.104.back, bf16[1024,256]{1,0:T(8,128)(2,1)S(1)} %copy-done.11, bf16[1024,256]{1,0:T(8,128)(2,1)S(1)} %copy-done.17, ...), custom_call_target="tpu_custom_call" | custom-call | tf_op jit(solution)/shard_map/pallas_call | solution.py:48
  170.8 2.9 %collective-permute-done.28.third = bf16[256,256]{1,0:T(8,128)(2,1)S(1)} collective-permute-done((bf16[256,256]{1,0:T(8,128)(2,1)S(1)}, bf16[256,256]{1,0:T(8,128)(2,1)S(1)}, u32[]{:S(2)}, u32[]{:S(2)}) %collective-permute-start.28) | collective-permute-done | bytes 131104 | tf_op jit(solution)/shard_map/ppermute | solution.py:40
  173.6 4.9 %collective-permute-done.30.refs_2_ = bf16[1024,128]{1,0:T(8,128)(2,1)S(1)} collective-permute-done((bf16[1024,128]{1,0:T(8,128)(2,1)S(1)}, bf16[1024,128]{1,0:T(8,128)(2,1)S(1)}, u32[]{:S(2)}, u32[]{:S(2)}) %collective-permute-start.30) | collective-permute-done | bytes 262176 | tf_op jit(solution)/shard_map/ppermute | solution.py:36
  179.2 3.5 %shard_map.135 = (f32[2,512,256]{2,1,0:T(8,128)S(1)}, f32[2,512,256]{2,1,0:T(8,128)S(1)}) custom-call(s32[5]{0:T(128)S(1)} %convert_element_type.3.flags, bf16[512,1024]{1,0:T(8,128)(2,1)S(1)} %shard_map.118.x_here.x_other.tokens, bf16[1024,256]{1,0:T(8,128)(2,1)S(1)} %copy-done.11, bf16[1024,256]{1,0:T(8,128)(2,1)S(1)} %copy-done.17, ...), custom_call_target="tpu_custom_call" | custom-call | tf_op jit(solution)/shard_map/pallas_call | solution.py:48
  182.7 2.6 %collective-permute-done.32.got = f32[2,512,256]{2,1,0:T(8,128)S(1)} collective-permute-done((f32[2,512,256]{2,1,0:T(8,128)S(1)}, f32[2,512,256]{2,1,0:T(8,128)S(1)}, u32[]{:S(2)}, u32[]{:S(2)}) %collective-permute-start.32) | collective-permute-done | bytes 1048608 | tf_op jit(solution)/shard_map/ppermute | solution.py:36
  190.8 4.5 %collective-permute-done.33.got = bf16[2,256,256]{2,1,0:T(8,128)(2,1)S(1)} collective-permute-done((bf16[2,256,256]{2,1,0:T(8,128)(2,1)S(1)}, bf16[2,256,256]{2,1,0:T(8,128)(2,1)S(1)}, u32[]{:S(2)}, u32[]{:S(2)}) %collective-permute-start.33) | collective-permute-done | bytes 262176 | tf_op jit(solution)/shard_map/ppermute | solution.py:36
  196.0 4.8 %collective-permute-done.34.refs_3_ = bf16[1024,128]{1,0:T(8,128)(2,1)S(1)} collective-permute-done((bf16[1024,128]{1,0:T(8,128)(2,1)S(1)}, bf16[1024,128]{1,0:T(8,128)(2,1)S(1)}, u32[]{:S(2)}, u32[]{:S(2)}) %collective-permute-start.34) | collective-permute-done | bytes 262176 | tf_op jit(solution)/shard_map/ppermute | solution.py:36
  (150 shorter events, 90.5 us)
Async XLA Ops:
  2.5 29.1 %all-to-all-start = ((bf16[8,128,256]{2,1,0:T(8,128)(2,1)}), bf16[8,128,256]{2,1,0:T(8,128)(2,1)S(1)}, u32[]{:S(2)}, u32[]{:S(2)}) async-start(bf16[8,128,256]{2,1,0:T(8,128)(2,1)} %shard_map.102), calls=%async_computation | async-start | bytes 1048576 | tf_op jit(solution)/shard_map/all_to_all | solution.py:441
  15.6 16.0 %collective-permute-start = (bf16[256,640]{1,0:T(8,128)(2,1)S(1)}, bf16[256,640]{1,0:T(8,128)(2,1)}, u32[]{:S(2)}, u32[]{:S(2)}) collective-permute-start(bf16[256,640]{1,0:T(8,128)(2,1)S(1)} %shard_map.104.here), channel_id=1, source_target_pairs={{0,2},{2,0},{1,3},{3,1},{4,6},{6,4},{5,7},{7,5},{8,10},{10,8},{9,1... | collective-permute-start | bytes 983048 | tf_op jit(solution)/shard_map/ppermute | solution.py:36
  17.1 25.3 %collective-permute-start.6 = (bf16[256,1024]{1,0:T(8,128)(2,1)}, bf16[256,1024]{1,0:T(8,128)(2,1)}, u32[]{:S(2)}, u32[]{:S(2)}) collective-permute-start(bf16[256,1024]{1,0:T(8,128)(2,1)} %shard_map.105), channel_id=1, source_target_pairs={{0,2},{2,0},{1,3},{3,1},{4,6},{6,4},{5,7},{7,5},{8,10},{10,8},{9,1... | collective-permute-start | bytes 1572872 | tf_op jit(solution)/shard_map/ppermute | solution.py:36
  26.2 16.3 %collective-permute-start.5 = (bf16[1024,256]{1,0:T(8,128)(2,1)S(1)}, bf16[1024,256]{1,0:T(8,128)(2,1)}, u32[]{:S(2)}, u32[]{:S(2)}) collective-permute-start(bf16[1024,256]{1,0:T(8,128)(2,1)S(1)} %shard_map.106.refs_0_.rest_0_.own), channel_id=1, source_target_pairs={{0,4},{4,0},{8,12},{12,8},{1,5},{5,1},{9,13},{13,9},{2,6},{6,2},{1... | collective-permute-start | bytes 1572872 | tf_op jit(solution)/shard_map/ppermute | solution.py:40
  38.3 17.4 %collective-permute-start.2 = (bf16[1024,256]{1,0:T(8,128)(2,1)}, bf16[1024,256]{1,0:T(8,128)(2,1)}, u32[]{:S(2)}, u32[]{:S(2)}) collective-permute-start(bf16[1024,256]{1,0:T(8,128)(2,1)} %shard_map.109.refs_0_.own), channel_id=1, source_target_pairs={{0,4},{4,0},{8,12},{12,8},{1,5},{5,1},{9,13},{13,9},{2,6},{6,2},{1... | collective-permute-start | bytes 1572872 | tf_op jit(solution)/shard_map/ppermute | solution.py:40
  45.1 26.7 %collective-permute-start.9 = (bf16[1024,512]{1,0:T(8,128)(2,1)}, bf16[1024,512]{1,0:T(8,128)(2,1)}, u32[]{:S(2)}, u32[]{:S(2)}) collective-permute-start(bf16[1024,512]{1,0:T(8,128)(2,1)} %shard_map.111), channel_id=1, source_target_pairs={{4,8},{8,4},{5,9},{9,5},{6,10},{10,6},{7,11},{11,7},{20,24},{24,20... | collective-permute-start | bytes 3145736 | tf_op jit(solution)/shard_map/ppermute | solution.py:40
  46.7 25.1 %collective-permute-start.8 = (bf16[1024,512]{1,0:T(8,128)(2,1)}, bf16[1024,512]{1,0:T(8,128)(2,1)}, u32[]{:S(2)}, u32[]{:S(2)}) collective-permute-start(bf16[1024,512]{1,0:T(8,128)(2,1)} %shard_map.111), channel_id=1, source_target_pairs={{0,16},{16,0},{1,17},{17,1},{2,18},{18,2},{3,19},{19,3},{4,20},{20... | collective-permute-start | bytes 3145736 | tf_op jit(solution)/shard_map/ppermute | solution.py:36
  63.0 28.0 %collective-permute-start.13 = (bf16[512,1024]{1,0:T(8,128)(2,1)S(1)}, bf16[512,1024]{1,0:T(8,128)(2,1)S(1)}, u32[]{:S(2)}, u32[]{:S(2)}) collective-permute-start(bf16[512,1024]{1,0:T(8,128)(2,1)S(1)} %shard_map.116.x_here.x_mine.tokens), channel_id=1, source_target_pairs={{0,4},{12,8},{1,5},{13,9},{2,6},{14,10},{3,7},{15,11},{16,20},{28,... | collective-permute-start | bytes 3145736 | tf_op jit(solution)/shard_map/ppermute | solution.py:40
  67.5 25.8 %collective-permute-start.12 = (bf16[1024,512]{1,0:T(8,128)(2,1)S(1)}, bf16[1024,512]{1,0:T(8,128)(2,1)}, u32[]{:S(2)}, u32[]{:S(2)}) collective-permute-start(bf16[1024,512]{1,0:T(8,128)(2,1)S(1)} %shard_map.113), channel_id=1, source_target_pairs={{4,8},{8,4},{5,9},{9,5},{6,10},{10,6},{7,11},{11,7},{20,24},{24,20... | collective-permute-start | bytes 3145736 | tf_op jit(solution)/shard_map/ppermute | solution.py:40
  71.8 21.5 %collective-permute-start.11 = (bf16[1024,256]{1,0:T(8,128)(2,1)}, bf16[1024,256]{1,0:T(8,128)(2,1)S(1)}, u32[]{:S(2)}, u32[]{:S(2)}) collective-permute-start(bf16[1024,256]{1,0:T(8,128)(2,1)} %collective-permute-done.2.refs_1_.near), channel_id=1, source_target_pairs={{0,16},{16,0},{1,17},{17,1},{2,18},{18,2},{3,19},{19,3},{4,20},{20... | collective-permute-start | bytes 1572872 | tf_op jit(solution)/shard_map/ppermute | solution.py:36
  73.3 25.8 %collective-permute-start.18 = (bf16[1024,512]{1,0:T(8,128)(2,1)}, bf16[1024,512]{1,0:T(8,128)(2,1)}, u32[]{:S(2)}, u32[]{:S(2)}) collective-permute-start(bf16[1024,512]{1,0:T(8,128)(2,1)} %collective-permute-done.9.crossed), channel_id=1, source_target_pairs={{4,0},{8,12},{5,1},{9,13},{6,2},{10,14},{7,3},{11,15},{20,16},{24,... | collective-permute-start | bytes 3145736 | tf_op jit(solution)/shard_map/ppermute | solution.py:40
  81.3 28.9 %collective-permute-start.17 = (bf16[512,1024]{1,0:T(8,128)(2,1)S(1)}, bf16[512,1024]{1,0:T(8,128)(2,1)}, u32[]{:S(2)}, u32[]{:S(2)}) collective-permute-start(bf16[512,1024]{1,0:T(8,128)(2,1)S(1)} %shard_map.118.x_here.x_other.tokens), channel_id=1, source_target_pairs={{0,4},{12,8},{1,5},{13,9},{2,6},{14,10},{3,7},{15,11},{16,20},{28,... | collective-permute-start | bytes 3145736 | tf_op jit(solution)/shard_map/ppermute | solution.py:40
  94.2 19.3 %collective-permute-start.16 = (bf16[1024,512]{1,0:T(8,128)(2,1)}, bf16[1024,512]{1,0:T(8,128)(2,1)}, u32[]{:S(2)}, u32[]{:S(2)}) collective-permute-start(bf16[1024,512]{1,0:T(8,128)(2,1)} %shard_map.119), channel_id=1, source_target_pairs={{4,8},{8,4},{5,9},{9,5},{6,10},{10,6},{7,11},{11,7},{20,24},{24,20... | collective-permute-start | bytes 3145736 | tf_op jit(solution)/shard_map/ppermute | solution.py:40
  95.8 29.3 %collective-permute-start.15 = (bf16[1024,512]{1,0:T(8,128)(2,1)}, bf16[1024,512]{1,0:T(8,128)(2,1)}, u32[]{:S(2)}, u32[]{:S(2)}) collective-permute-start(bf16[1024,512]{1,0:T(8,128)(2,1)} %collective-permute-done.12.crossed), channel_id=1, source_target_pairs={{4,0},{8,12},{5,1},{9,13},{6,2},{10,14},{7,3},{11,15},{20,16},{24,... | collective-permute-start | bytes 3145736 | tf_op jit(solution)/shard_map/ppermute | solution.py:40
  100.7 33.2 %collective-permute-start.20 = (bf16[1024,512]{1,0:T(8,128)(2,1)S(1)}, bf16[1024,512]{1,0:T(8,128)(2,1)S(1)}, u32[]{:S(2)}, u32[]{:S(2)}) collective-permute-start(bf16[1024,512]{1,0:T(8,128)(2,1)S(1)} %shard_map.121.rest_2_.far), channel_id=1, source_target_pairs={{0,16},{16,0},{1,17},{17,1},{2,18},{18,2},{3,19},{19,3},{4,20},{20... | collective-permute-start | bytes 3145736 | tf_op jit(solution)/shard_map/ppermute | solution.py:36
  112.8 37.3 %collective-permute-start.25 = (bf16[1024,512]{1,0:T(8,128)(2,1)S(1)}, bf16[1024,512]{1,0:T(8,128)(2,1)S(1)}, u32[]{:S(2)}, u32[]{:S(2)}) collective-permute-start(bf16[1024,512]{1,0:T(8,128)(2,1)S(1)} %shard_map.122), channel_id=1, source_target_pairs={{4,8},{8,4},{5,9},{9,5},{6,10},{10,6},{7,11},{11,7},{20,24},{24,20... | collective-permute-start | bytes 3145736 | tf_op jit(solution)/shard_map/ppermute | solution.py:40
  126.8 31.0 %collective-permute-start.19 = (bf16[1024,512]{1,0:T(8,128)(2,1)S(1)}, bf16[1024,512]{1,0:T(8,128)(2,1)S(1)}, u32[]{:S(2)}, u32[]{:S(2)}) collective-permute-start(bf16[1024,512]{1,0:T(8,128)(2,1)S(1)} %shard_map.124.far), channel_id=1, source_target_pairs={{0,16},{16,0},{1,17},{17,1},{2,18},{18,2},{3,19},{19,3},{4,20},{20... | collective-permute-start | bytes 3145736 | tf_op jit(solution)/shard_map/ppermute | solution.py:36
  128.1 15.2 %collective-permute-start.23 = (bf16[1024,256]{1,0:T(8,128)(2,1)S(1)}, bf16[1024,256]{1,0:T(8,128)(2,1)S(1)}, u32[]{:S(2)}, u32[]{:S(2)}) collective-permute-start(bf16[1024,256]{1,0:T(8,128)(2,1)S(1)} %shard_map.123), channel_id=1, source_target_pairs={{4,0},{8,12},{5,1},{9,13},{6,2},{10,14},{7,3},{11,15},{20,16},{24,... | collective-permute-start | bytes 1572872 | tf_op jit(solution)/shard_map/ppermute | solution.py:40
  133.3 16.1 %collective-permute-start.22 = (bf16[256,1024]{1,0:T(8,128)(2,1)S(1)}, bf16[256,1024]{1,0:T(8,128)(2,1)S(1)}, u32[]{:S(2)}, u32[]{:S(2)}) collective-permute-start(bf16[256,1024]{1,0:T(8,128)(2,1)S(1)} %get-tuple-element.116), channel_id=1, source_target_pairs={{0,2},{2,0},{1,3},{3,1},{4,6},{6,4},{5,7},{7,5},{8,10},{10,8},{9,1... | collective-permute-start | bytes 1572872 | tf_op jit(solution)/shard_map/ppermute | solution.py:36
  150.6 16.7 %collective-permute-start.31 = (bf16[1024,256]{1,0:T(8,128)(2,1)S(1)}, bf16[1024,256]{1,0:T(8,128)(2,1)S(1)}, u32[]{:S(2)}, u32[]{:S(2)}) collective-permute-start(bf16[1024,256]{1,0:T(8,128)(2,1)S(1)} %shard_map.130), channel_id=1, source_target_pairs={{4,0},{8,12},{5,1},{9,13},{6,2},{10,14},{7,3},{11,15},{20,16},{24,... | collective-permute-start | bytes 1572872 | tf_op jit(solution)/shard_map/ppermute | solution.py:40
  161.4 17.7 %collective-permute-start.26 = (bf16[256,1024]{1,0:T(8,128)(2,1)S(1)}, bf16[256,1024]{1,0:T(8,128)(2,1)S(1)}, u32[]{:S(2)}, u32[]{:S(2)}) collective-permute-start(bf16[256,1024]{1,0:T(8,128)(2,1)S(1)} %get-tuple-element.127), channel_id=1, source_target_pairs={{0,2},{2,0},{1,3},{3,1},{4,6},{6,4},{5,7},{7,5},{8,10},{10,8},{9,1... | collective-permute-start | bytes 1572872 | tf_op jit(solution)/shard_map/ppermute | solution.py:36
  162.0 16.5 %collective-permute-start.30 = (bf16[1024,128]{1,0:T(8,128)(2,1)S(1)}, bf16[1024,128]{1,0:T(8,128)(2,1)S(1)}, u32[]{:S(2)}, u32[]{:S(2)}) collective-permute-start(bf16[1024,128]{1,0:T(8,128)(2,1)S(1)} %get-tuple-element.133), channel_id=1, source_target_pairs={{0,2},{2,0},{1,3},{3,1},{4,6},{6,4},{5,7},{7,5},{8,10},{10,8},{9,1... | collective-permute-start | bytes 786440 | tf_op jit(solution)/shard_map/ppermute | solution.py:36
  186.7 14.1 %collective-permute-start.34 = (bf16[1024,128]{1,0:T(8,128)(2,1)S(1)}, bf16[1024,128]{1,0:T(8,128)(2,1)S(1)}, u32[]{:S(2)}, u32[]{:S(2)}) collective-permute-start(bf16[1024,128]{1,0:T(8,128)(2,1)S(1)} %get-tuple-element.154), channel_id=1, source_target_pairs={{0,2},{2,0},{1,3},{3,1},{4,6},{6,4},{5,7},{7,5},{8,10},{10,8},{9,1... | collective-permute-start | bytes 786440 | tf_op jit(solution)/shard_map/ppermute | solution.py:36
  188.2 14.3 %collective-permute-start.35 = (bf16[128,256]{1,0:T(8,128)(2,1)S(1)}, bf16[128,256]{1,0:T(8,128)(2,1)S(1)}, u32[]{:S(2)}, u32[]{:S(2)}) collective-permute-start(bf16[128,256]{1,0:T(8,128)(2,1)S(1)} %get-tuple-element.139), channel_id=1, source_target_pairs={{0,2},{2,0},{1,3},{3,1},{4,6},{6,4},{5,7},{7,5},{8,10},{10,8},{9,1... | collective-permute-start | bytes 196616 | tf_op jit(solution)/shard_map/ppermute | solution.py:36
  (40 other events, 292.7 us)

commit v17 on v16

--- a/solution.py
+++ b/solution.py
@@ -626,14 +626,14 @@
         down_far_other,
     )
     dx_other_got = swap(done(dx_sent), "own")
-    grad_last, grad_sent = finish(1, middle[1], outward[1])
+    grad_last, grad_sent = finish(1, middle[1], outward[1], grad_got)
     grad_last_got = swap(grad_sent, "own")
-    *up_got, grad_got = step(*up_got, grad_got)
+    up_got = step(*up_got)
     up_mine, up_theirs = kernel_call(
         up_sum_kernel, [like(size, kvq)] * 2, up_parts[0], *up_got, scalars=numbers
     )
     up_theirs = swap(done(up_theirs), "own")
-    x_other, dx_other_got = step(x_other, dx_other_got)
+    x_other, dx_other_got, grad_last_got = step(x_other, dx_other_got, grad_last_got)
     y_keep, y_sent = kernel_call(
         y_kernel,
         blocks,

time: 205 us -> 202 us (0.985)
  waiting for transfers between devices: 76.7 us -> 72.6 us
    ppermute x20, waiting for transfers between devices: 38.5 us -> 33.3 us  [swap(): return lax.ppermute(value, axis, PAIR)]
  transfers between devices with their start and end apart: 37 -> 37, of which waited for: 19 -> 19; matrix products, arithmetic and copies ran while one was open for 1% -> 1% of each run, Pallas kernels for 27% -> 28%
where the time goes in v17:
time: 202 us; the launch traced here: 201 us
  waiting for transfers between devices  72.6 us (36%)
  Pallas kernels  61.4 us (30%)
  starting transfers between devices  54.8 us (27%)
  local copies, waits for them, and re-layouts  10.6 us (5%)
    pallas_call x39, Pallas kernels, kernel_call(): pl.pallas_call(body, out_shape=list(outs), in_specs=specs, out_specs=[pl....  61.4 us
    ppermute x16, waiting for transfers between devices, along(): return lax.ppermute(value, 'fsdp', pairs)  39.3 us
    ppermute x20, waiting for transfers between devices, swap(): return lax.ppermute(value, axis, PAIR)  33.3 us
    ppermute x16, starting transfers between devices, along(): return lax.ppermute(value, 'fsdp', pairs)  30.9 us
    ppermute x20, starting transfers between devices, swap(): return lax.ppermute(value, axis, PAIR)  16.6 us
    unnamed x55, local copies, waits for them, and re-layouts  10.4 us
    all_to_all x1, starting transfers between devices, body_line(): lax.all_to_all(done(up_sent), ('fsdp', 'own'), split_axis=0, concat_axis=...  7.25 us
  transfers between devices with their start and end apart: 37, of which 19 were waited for; matrix products, arithmetic and copies ran while one was open for 1% of the time, Pallas kernels for 28%

profile of v17, /device:TPU:0, one launch (start us, length us, event | category | flops | bytes accessed | tf_op | source)
XLA Modules:
  0.0 200.7 jit_solution(16236771363773332738)
XLA Ops:
  2.5 7.3 %all-to-all-start = ((bf16[8,128,256]{2,1,0:T(8,128)(2,1)}), bf16[8,128,256]{2,1,0:T(8,128)(2,1)S(1)}, u32[]{:S(2)}, u32[]{:S(2)}) async-start(bf16[8,128,256]{2,1,0:T(8,128)(2,1)} %shard_map.102), calls=%async_computation | async-start | bytes 1048576 | tf_op jit(solution)/shard_map/all_to_all | solution.py:441
  19.2 5.4 %collective-permute-done.1.refs_1_ = bf16[1024,128]{1,0:T(8,128)(2,1)} collective-permute-done((bf16[1024,128]{1,0:T(8,128)(2,1)S(1)}, bf16[1024,128]{1,0:T(8,128)(2,1)}, u32[]{:S(2)}, u32[]{:S(2)}) %collective-permute-start.1) | collective-permute-done | bytes 262176 | tf_op jit(solution)/shard_map/ppermute | solution.py:36
  28.2 3.4 %collective-permute-done.there = bf16[256,640]{1,0:T(8,128)(2,1)} collective-permute-done((bf16[256,640]{1,0:T(8,128)(2,1)S(1)}, bf16[256,640]{1,0:T(8,128)(2,1)}, u32[]{:S(2)}, u32[]{:S(2)}) %collective-permute-start) | collective-permute-done | bytes 327712 | tf_op jit(solution)/shard_map/ppermute | solution.py:36
  42.4 2.6 %shard_map.111 = bf16[1024,512]{1,0:T(8,128)(2,1)} custom-call(s32[4]{0:T(128)S(1)} %pad_add_fusion.numbers, bf16[1024,256]{1,0:T(8,128)(2,1)S(1)} %shard_map.106.refs_0_.rest_0_.own, bf16[1024,256]{1,0:T(8,128)(2,1)} %collective-permute-done.5.refs_1_.rest_1_.near), custom_call_target="tpu_custom_call" | custom-call | tf_op jit(solution)/shard_map/pallas_call | solution.py:48
  51.7 4.0 %collective-permute-start.10 = (bf16[512,256]{1,0:T(8,128)(2,1)S(1)}, bf16[512,256]{1,0:T(8,128)(2,1)S(1)}, u32[]{:S(2)}, u32[]{:S(2)}) collective-permute-start(bf16[512,256]{1,0:T(8,128)(2,1)S(1)} %get-tuple-element.93), channel_id=1, source_target_pairs={{0,4},{12,8},{1,5},{13,9},{2,6},{14,10},{3,7},{15,11},{16,20},{28,... | collective-permute-start | bytes 786440 | tf_op jit(solution)/shard_map/ppermute | solution.py:40
  63.0 4.5 %collective-permute-start.13 = (bf16[512,1024]{1,0:T(8,128)(2,1)S(1)}, bf16[512,1024]{1,0:T(8,128)(2,1)S(1)}, u32[]{:S(2)}, u32[]{:S(2)}) collective-permute-start(bf16[512,1024]{1,0:T(8,128)(2,1)S(1)} %shard_map.116.x_here.x_mine.tokens), channel_id=1, source_target_pairs={{0,4},{12,8},{1,5},{13,9},{2,6},{14,10},{3,7},{15,11},{16,20},{28,... | collective-permute-start | bytes 3145736 | tf_op jit(solution)/shard_map/ppermute | solution.py:40
  74.6 6.1 %collective-permute-done.7.refs_1_ = bf16[256,1024]{1,0:T(8,128)(2,1)S(1)} collective-permute-done((bf16[256,1024]{1,0:T(8,128)(2,1)S(1)}, bf16[256,1024]{1,0:T(8,128)(2,1)S(1)}, u32[]{:S(2)}, u32[]{:S(2)}) %collective-permute-start.7) | collective-permute-done | bytes 524320 | tf_op jit(solution)/shard_map/ppermute | solution.py:36
  81.3 3.7 %collective-permute-start.17 = (bf16[512,1024]{1,0:T(8,128)(2,1)S(1)}, bf16[512,1024]{1,0:T(8,128)(2,1)}, u32[]{:S(2)}, u32[]{:S(2)}) collective-permute-start(bf16[512,1024]{1,0:T(8,128)(2,1)S(1)} %shard_map.118.x_here.x_other.tokens), channel_id=1, source_target_pairs={{0,4},{12,8},{1,5},{13,9},{2,6},{14,10},{3,7},{15,11},{16,20},{28,... | collective-permute-start | bytes 3145736 | tf_op jit(solution)/shard_map/ppermute | solution.py:40
  85.0 6.0 %collective-permute-done.13.x_in = bf16[512,1024]{1,0:T(8,128)(2,1)S(1)} collective-permute-done((bf16[512,1024]{1,0:T(8,128)(2,1)S(1)}, bf16[512,1024]{1,0:T(8,128)(2,1)S(1)}, u32[]{:S(2)}, u32[]{:S(2)}) %collective-permute-start.13) | collective-permute-done | bytes 1048608 | tf_op jit(solution)/shard_map/ppermute | solution.py:40
  91.0 2.3 %shard_map.119 = bf16[1024,512]{1,0:T(8,128)(2,1)} custom-call(bf16[512,1024]{1,0:T(8,128)(2,1)S(1)} %shard_map.116.x_here.x_mine.tokens, bf16[512,1024]{1,0:T(8,128)(2,1)S(1)} %get-tuple-element.104.back, bf16[512,1024]{1,0:T(8,128)(2,1)S(1)} %collective-permute-done.13.x_in, bf16[512,1024]{1,0:T(8,128)(2,1)S(1)} %shard_map.115.back_in), custom_call_target="tpu_custom_call" | custom-call | tf_op jit(solution)/shard_map/pallas_call | solution.py:48
  101.7 8.5 %collective-permute-done.17.x_in = bf16[512,1024]{1,0:T(8,128)(2,1)} collective-permute-done((bf16[512,1024]{1,0:T(8,128)(2,1)S(1)}, bf16[512,1024]{1,0:T(8,128)(2,1)}, u32[]{:S(2)}, u32[]{:S(2)}) %collective-permute-start.17) | collective-permute-done | bytes 1048608 | tf_op jit(solution)/shard_map/ppermute | solution.py:40
  110.3 2.5 %shard_map.122 = bf16[1024,512]{1,0:T(8,128)(2,1)S(1)} custom-call(bf16[512,1024]{1,0:T(8,128)(2,1)S(1)} %shard_map.118.x_here.x_other.tokens, bf16[512,1024]{1,0:T(8,128)(2,1)S(1)} %get-tuple-element.104.back, bf16[512,1024]{1,0:T(8,128)(2,1)} %collective-permute-done.17.x_in, bf16[512,1024]{1,0:T(8,128)(2,1)S(1)} %copy-done.3), custom_call_target="tpu_custom_call" | custom-call | tf_op jit(solution)/shard_map/pallas_call | solution.py:48
  115.2 9.9 %collective-permute-done.15.outer = bf16[1024,512]{1,0:T(8,128)(2,1)} collective-permute-done((bf16[1024,512]{1,0:T(8,128)(2,1)}, bf16[1024,512]{1,0:T(8,128)(2,1)}, u32[]{:S(2)}, u32[]{:S(2)}) %collective-permute-start.15) | collective-permute-done | bytes 1048608 | tf_op jit(solution)/shard_map/ppermute | solution.py:40
  129.5 3.7 %shard_map.125 = (bf16[256,1024]{1,0:T(8,128)(2,1)S(1)}, bf16[256,1024]{1,0:T(8,128)(2,1)S(1)}) custom-call(bf16[512,1024]{1,0:T(8,128)(2,1)S(1)} %shard_map.120.dy, bf16[512,1024]{1,0:T(8,128)(2,1)S(1)} %get-tuple-element.104.back, bf16[1024,256]{1,0:T(8,128)(2,1)} %shard_map.109.refs_0_.own, bf16[1024,256]{1,0:T(8,128)(2,1)} %collective-permute-done.2.refs_1_.near, ...), custom_call_target="tpu_custom_call" | custom-call | tf_op jit(solution)/shard_map/pallas_call | solution.py:48
  133.9 3.7 %shard_map.126.left = f32[512,128]{1,0:T(8,128)S(1)} custom-call(s32[24]{0:T(128)S(1)} %concatenate.3.numbers, bf16[512,128]{1,0:T(8,128)(2,1)S(1)} %get-tuple-element.86.ids, bf16[512,1024]{1,0:T(8,128)(2,1)S(1)} %shard_map.116.x_here.x_mine.tokens, bf16[512,1024]{1,0:T(8,128)(2,1)S(1)} %shard_map.118.x_here.x_other.tokens, ...), custom_call_target="tpu_custom_call" | custom-call | tf_op jit(solution)/shard_map/pallas_call | solution.py:48
  137.7 5.5 %collective-permute-done.23.outer = bf16[1024,256]{1,0:T(8,128)(2,1)S(1)} collective-permute-done((bf16[1024,256]{1,0:T(8,128)(2,1)S(1)}, bf16[1024,256]{1,0:T(8,128)(2,1)S(1)}, u32[]{:S(2)}, u32[]{:S(2)}) %collective-permute-start.23) | collective-permute-done | bytes 524320 | tf_op jit(solution)/shard_map/ppermute | solution.py:40
  145.2 4.1 %shard_map.128 = (f32[2,512,256]{2,1,0:T(8,128)S(1)}, f32[2,512,256]{2,1,0:T(8,128)S(1)}) custom-call(s32[5]{0:T(128)S(1)} %convert_element_type.3.flags, bf16[512,1024]{1,0:T(8,128)(2,1)S(1)} %shard_map.116.x_here.x_mine.tokens, bf16[1024,256]{1,0:T(8,128)(2,1)} %shard_map.109.refs_0_.own, bf16[1024,256]{1,0:T(8,128)(2,1)} %collective-permute-done.2.refs_1_.near, ...), custom_call_target="tpu_custom_call" | custom-call | tf_op jit(solution)/shard_map/pallas_call | solution.py:48
  151.9 4.4 %collective-permute-done.24.got = f32[512,128]{1,0:T(8,128)S(1)} collective-permute-done((f32[512,128]{1,0:T(8,128)S(1)}, f32[512,128]{1,0:T(8,128)S(1)}, u32[]{:S(2)}, u32[]{:S(2)}) %collective-permute-start.24) | collective-permute-done | bytes 262176 | tf_op jit(solution)/shard_map/ppermute | solution.py:36
  158.4 3.6 %shard_map.132 = (bf16[256,1024]{1,0:T(8,128)(2,1)S(1)}, bf16[256,1024]{1,0:T(8,128)(2,1)S(1)}) custom-call(bf16[512,1024]{1,0:T(8,128)(2,1)S(1)} %shard_map.120.dy, bf16[512,1024]{1,0:T(8,128)(2,1)S(1)} %get-tuple-element.104.back, bf16[1024,256]{1,0:T(8,128)(2,1)S(1)} %copy-done.11, bf16[1024,256]{1,0:T(8,128)(2,1)S(1)} %copy-done.17, ...), custom_call_target="tpu_custom_call" | custom-call | tf_op jit(solution)/shard_map/pallas_call | solution.py:48
  172.5 3.1 %collective-permute-done.30.second = bf16[256,256]{1,0:T(8,128)(2,1)S(1)} collective-permute-done((bf16[256,256]{1,0:T(8,128)(2,1)S(1)}, bf16[256,256]{1,0:T(8,128)(2,1)S(1)}, u32[]{:S(2)}, u32[]{:S(2)}) %collective-permute-start.30) | collective-permute-done | bytes 131104 | tf_op jit(solution)/shard_map/ppermute | solution.py:40
  175.6 2.8 %collective-permute-done.31.third = bf16[256,256]{1,0:T(8,128)(2,1)S(1)} collective-permute-done((bf16[256,256]{1,0:T(8,128)(2,1)S(1)}, bf16[256,256]{1,0:T(8,128)(2,1)S(1)}, u32[]{:S(2)}, u32[]{:S(2)}) %collective-permute-start.31) | collective-permute-done | bytes 131104 | tf_op jit(solution)/shard_map/ppermute | solution.py:40
  181.1 3.5 %shard_map.135 = (f32[2,512,256]{2,1,0:T(8,128)S(1)}, f32[2,512,256]{2,1,0:T(8,128)S(1)}) custom-call(s32[5]{0:T(128)S(1)} %convert_element_type.3.flags, bf16[512,1024]{1,0:T(8,128)(2,1)S(1)} %shard_map.118.x_here.x_other.tokens, bf16[1024,256]{1,0:T(8,128)(2,1)S(1)} %copy-done.11, bf16[1024,256]{1,0:T(8,128)(2,1)S(1)} %copy-done.17, ...), custom_call_target="tpu_custom_call" | custom-call | tf_op jit(solution)/shard_map/pallas_call | solution.py:48
  184.6 2.6 %collective-permute-done.33.got = f32[2,512,256]{2,1,0:T(8,128)S(1)} collective-permute-done((f32[2,512,256]{2,1,0:T(8,128)S(1)}, f32[2,512,256]{2,1,0:T(8,128)S(1)}, u32[]{:S(2)}, u32[]{:S(2)}) %collective-permute-start.33) | collective-permute-done | bytes 1048608 | tf_op jit(solution)/shard_map/ppermute | solution.py:36
  192.2 4.9 %collective-permute-done.34.got = bf16[2,256,256]{2,1,0:T(8,128)(2,1)S(1)} collective-permute-done((bf16[2,256,256]{2,1,0:T(8,128)(2,1)S(1)}, bf16[2,256,256]{2,1,0:T(8,128)(2,1)S(1)}, u32[]{:S(2)}, u32[]{:S(2)}) %collective-permute-start.34) | collective-permute-done | bytes 262176 | tf_op jit(solution)/shard_map/ppermute | solution.py:36
  (150 shorter events, 91.3 us)
Async XLA Ops:
  2.5 29.1 %all-to-all-start = ((bf16[8,128,256]{2,1,0:T(8,128)(2,1)}), bf16[8,128,256]{2,1,0:T(8,128)(2,1)S(1)}, u32[]{:S(2)}, u32[]{:S(2)}) async-start(bf16[8,128,256]{2,1,0:T(8,128)(2,1)} %shard_map.102), calls=%async_computation | async-start | bytes 1048576 | tf_op jit(solution)/shard_map/all_to_all | solution.py:441
  11.7 12.9 %collective-permute-start.1 = (bf16[1024,128]{1,0:T(8,128)(2,1)S(1)}, bf16[1024,128]{1,0:T(8,128)(2,1)}, u32[]{:S(2)}, u32[]{:S(2)}) collective-permute-start(bf16[1024,128]{1,0:T(8,128)(2,1)S(1)} %shard_map.103), channel_id=1, source_target_pairs={{0,2},{2,0},{1,3},{3,1},{4,6},{6,4},{5,7},{7,5},{8,10},{10,8},{9,1... | collective-permute-start | bytes 786440 | tf_op jit(solution)/shard_map/ppermute | solution.py:36
  15.6 16.0 %collective-permute-start = (bf16[256,640]{1,0:T(8,128)(2,1)S(1)}, bf16[256,640]{1,0:T(8,128)(2,1)}, u32[]{:S(2)}, u32[]{:S(2)}) collective-permute-start(bf16[256,640]{1,0:T(8,128)(2,1)S(1)} %shard_map.104.here), channel_id=1, source_target_pairs={{0,2},{2,0},{1,3},{3,1},{4,6},{6,4},{5,7},{7,5},{8,10},{10,8},{9,1... | collective-permute-start | bytes 983048 | tf_op jit(solution)/shard_map/ppermute | solution.py:36
  17.1 25.3 %collective-permute-start.6 = (bf16[256,1024]{1,0:T(8,128)(2,1)}, bf16[256,1024]{1,0:T(8,128)(2,1)}, u32[]{:S(2)}, u32[]{:S(2)}) collective-permute-start(bf16[256,1024]{1,0:T(8,128)(2,1)} %shard_map.105), channel_id=1, source_target_pairs={{0,2},{2,0},{1,3},{3,1},{4,6},{6,4},{5,7},{7,5},{8,10},{10,8},{9,1... | collective-permute-start | bytes 1572872 | tf_op jit(solution)/shard_map/ppermute | solution.py:36
  26.2 16.3 %collective-permute-start.5 = (bf16[1024,256]{1,0:T(8,128)(2,1)S(1)}, bf16[1024,256]{1,0:T(8,128)(2,1)}, u32[]{:S(2)}, u32[]{:S(2)}) collective-permute-start(bf16[1024,256]{1,0:T(8,128)(2,1)S(1)} %shard_map.106.refs_0_.rest_0_.own), channel_id=1, source_target_pairs={{0,4},{4,0},{8,12},{12,8},{1,5},{5,1},{9,13},{13,9},{2,6},{6,2},{1... | collective-permute-start | bytes 1572872 | tf_op jit(solution)/shard_map/ppermute | solution.py:40
  38.3 17.4 %collective-permute-start.2 = (bf16[1024,256]{1,0:T(8,128)(2,1)}, bf16[1024,256]{1,0:T(8,128)(2,1)}, u32[]{:S(2)}, u32[]{:S(2)}) collective-permute-start(bf16[1024,256]{1,0:T(8,128)(2,1)} %shard_map.109.refs_0_.own), channel_id=1, source_target_pairs={{0,4},{4,0},{8,12},{12,8},{1,5},{5,1},{9,13},{13,9},{2,6},{6,2},{1... | collective-permute-start | bytes 1572872 | tf_op jit(solution)/shard_map/ppermute | solution.py:40
  45.1 26.7 %collective-permute-start.9 = (bf16[1024,512]{1,0:T(8,128)(2,1)}, bf16[1024,512]{1,0:T(8,128)(2,1)}, u32[]{:S(2)}, u32[]{:S(2)}) collective-permute-start(bf16[1024,512]{1,0:T(8,128)(2,1)} %shard_map.111), channel_id=1, source_target_pairs={{4,8},{8,4},{5,9},{9,5},{6,10},{10,6},{7,11},{11,7},{20,24},{24,20... | collective-permute-start | bytes 3145736 | tf_op jit(solution)/shard_map/ppermute | solution.py:40
  46.7 25.1 %collective-permute-start.8 = (bf16[1024,512]{1,0:T(8,128)(2,1)}, bf16[1024,512]{1,0:T(8,128)(2,1)}, u32[]{:S(2)}, u32[]{:S(2)}) collective-permute-start(bf16[1024,512]{1,0:T(8,128)(2,1)} %shard_map.111), channel_id=1, source_target_pairs={{0,16},{16,0},{1,17},{17,1},{2,18},{18,2},{3,19},{19,3},{4,20},{20... | collective-permute-start | bytes 3145736 | tf_op jit(solution)/shard_map/ppermute | solution.py:36
  63.0 28.0 %collective-permute-start.13 = (bf16[512,1024]{1,0:T(8,128)(2,1)S(1)}, bf16[512,1024]{1,0:T(8,128)(2,1)S(1)}, u32[]{:S(2)}, u32[]{:S(2)}) collective-permute-start(bf16[512,1024]{1,0:T(8,128)(2,1)S(1)} %shard_map.116.x_here.x_mine.tokens), channel_id=1, source_target_pairs={{0,4},{12,8},{1,5},{13,9},{2,6},{14,10},{3,7},{15,11},{16,20},{28,... | collective-permute-start | bytes 3145736 | tf_op jit(solution)/shard_map/ppermute | solution.py:40
  67.5 25.8 %collective-permute-start.12 = (bf16[1024,512]{1,0:T(8,128)(2,1)S(1)}, bf16[1024,512]{1,0:T(8,128)(2,1)}, u32[]{:S(2)}, u32[]{:S(2)}) collective-permute-start(bf16[1024,512]{1,0:T(8,128)(2,1)S(1)} %shard_map.113), channel_id=1, source_target_pairs={{4,8},{8,4},{5,9},{9,5},{6,10},{10,6},{7,11},{11,7},{20,24},{24,20... | collective-permute-start | bytes 3145736 | tf_op jit(solution)/shard_map/ppermute | solution.py:40
  71.8 21.5 %collective-permute-start.11 = (bf16[1024,256]{1,0:T(8,128)(2,1)}, bf16[1024,256]{1,0:T(8,128)(2,1)S(1)}, u32[]{:S(2)}, u32[]{:S(2)}) collective-permute-start(bf16[1024,256]{1,0:T(8,128)(2,1)} %collective-permute-done.2.refs_1_.near), channel_id=1, source_target_pairs={{0,16},{16,0},{1,17},{17,1},{2,18},{18,2},{3,19},{19,3},{4,20},{20... | collective-permute-start | bytes 1572872 | tf_op jit(solution)/shard_map/ppermute | solution.py:36
  73.3 25.8 %collective-permute-start.18 = (bf16[1024,512]{1,0:T(8,128)(2,1)}, bf16[1024,512]{1,0:T(8,128)(2,1)}, u32[]{:S(2)}, u32[]{:S(2)}) collective-permute-start(bf16[1024,512]{1,0:T(8,128)(2,1)} %collective-permute-done.9.crossed), channel_id=1, source_target_pairs={{4,0},{8,12},{5,1},{9,13},{6,2},{10,14},{7,3},{11,15},{20,16},{24,... | collective-permute-start | bytes 3145736 | tf_op jit(solution)/shard_map/ppermute | solution.py:40
  81.3 28.9 %collective-permute-start.17 = (bf16[512,1024]{1,0:T(8,128)(2,1)S(1)}, bf16[512,1024]{1,0:T(8,128)(2,1)}, u32[]{:S(2)}, u32[]{:S(2)}) collective-permute-start(bf16[512,1024]{1,0:T(8,128)(2,1)S(1)} %shard_map.118.x_here.x_other.tokens), channel_id=1, source_target_pairs={{0,4},{12,8},{1,5},{13,9},{2,6},{14,10},{3,7},{15,11},{16,20},{28,... | collective-permute-start | bytes 3145736 | tf_op jit(solution)/shard_map/ppermute | solution.py:40
  94.2 19.3 %collective-permute-start.16 = (bf16[1024,512]{1,0:T(8,128)(2,1)}, bf16[1024,512]{1,0:T(8,128)(2,1)}, u32[]{:S(2)}, u32[]{:S(2)}) collective-permute-start(bf16[1024,512]{1,0:T(8,128)(2,1)} %shard_map.119), channel_id=1, source_target_pairs={{4,8},{8,4},{5,9},{9,5},{6,10},{10,6},{7,11},{11,7},{20,24},{24,20... | collective-permute-start | bytes 3145736 | tf_op jit(solution)/shard_map/ppermute | solution.py:40
  95.8 29.3 %collective-permute-start.15 = (bf16[1024,512]{1,0:T(8,128)(2,1)}, bf16[1024,512]{1,0:T(8,128)(2,1)}, u32[]{:S(2)}, u32[]{:S(2)}) collective-permute-start(bf16[1024,512]{1,0:T(8,128)(2,1)} %collective-permute-done.12.crossed), channel_id=1, source_target_pairs={{4,0},{8,12},{5,1},{9,13},{6,2},{10,14},{7,3},{11,15},{20,16},{24,... | collective-permute-start | bytes 3145736 | tf_op jit(solution)/shard_map/ppermute | solution.py:40
  100.7 33.2 %collective-permute-start.20 = (bf16[1024,512]{1,0:T(8,128)(2,1)S(1)}, bf16[1024,512]{1,0:T(8,128)(2,1)S(1)}, u32[]{:S(2)}, u32[]{:S(2)}) collective-permute-start(bf16[1024,512]{1,0:T(8,128)(2,1)S(1)} %shard_map.121.rest_2_.far), channel_id=1, source_target_pairs={{0,16},{16,0},{1,17},{17,1},{2,18},{18,2},{3,19},{19,3},{4,20},{20... | collective-permute-start | bytes 3145736 | tf_op jit(solution)/shard_map/ppermute | solution.py:36
  112.8 37.3 %collective-permute-start.25 = (bf16[1024,512]{1,0:T(8,128)(2,1)S(1)}, bf16[1024,512]{1,0:T(8,128)(2,1)S(1)}, u32[]{:S(2)}, u32[]{:S(2)}) collective-permute-start(bf16[1024,512]{1,0:T(8,128)(2,1)S(1)} %shard_map.122), channel_id=1, source_target_pairs={{4,8},{8,4},{5,9},{9,5},{6,10},{10,6},{7,11},{11,7},{20,24},{24,20... | collective-permute-start | bytes 3145736 | tf_op jit(solution)/shard_map/ppermute | solution.py:40
  126.8 31.7 %collective-permute-start.19 = (bf16[1024,512]{1,0:T(8,128)(2,1)S(1)}, bf16[1024,512]{1,0:T(8,128)(2,1)S(1)}, u32[]{:S(2)}, u32[]{:S(2)}) collective-permute-start(bf16[1024,512]{1,0:T(8,128)(2,1)S(1)} %shard_map.124.far), channel_id=1, source_target_pairs={{0,16},{16,0},{1,17},{17,1},{2,18},{18,2},{3,19},{19,3},{4,20},{20... | collective-permute-start | bytes 3145736 | tf_op jit(solution)/shard_map/ppermute | solution.py:36
  128.1 15.2 %collective-permute-start.23 = (bf16[1024,256]{1,0:T(8,128)(2,1)S(1)}, bf16[1024,256]{1,0:T(8,128)(2,1)S(1)}, u32[]{:S(2)}, u32[]{:S(2)}) collective-permute-start(bf16[1024,256]{1,0:T(8,128)(2,1)S(1)} %shard_map.123), channel_id=1, source_target_pairs={{4,0},{8,12},{5,1},{9,13},{6,2},{10,14},{7,3},{11,15},{20,16},{24,... | collective-permute-start | bytes 1572872 | tf_op jit(solution)/shard_map/ppermute | solution.py:40
  133.3 16.1 %collective-permute-start.22 = (bf16[256,1024]{1,0:T(8,128)(2,1)S(1)}, bf16[256,1024]{1,0:T(8,128)(2,1)S(1)}, u32[]{:S(2)}, u32[]{:S(2)}) collective-permute-start(bf16[256,1024]{1,0:T(8,128)(2,1)S(1)} %get-tuple-element.116), channel_id=1, source_target_pairs={{0,2},{2,0},{1,3},{3,1},{4,6},{6,4},{5,7},{7,5},{8,10},{10,8},{9,1... | collective-permute-start | bytes 1572872 | tf_op jit(solution)/shard_map/ppermute | solution.py:36
  137.7 11.7 %collective-permute-start.21 = (f32[512,128]{1,0:T(8,128)S(1)}, f32[512,128]{1,0:T(8,128)S(1)}, u32[]{:S(2)}, u32[]{:S(2)}) collective-permute-start(f32[512,128]{1,0:T(8,128)S(1)} %shard_map.126.left), channel_id=1, source_target_pairs={{0,1},{1,0},{2,3},{3,2},{4,5},{5,4},{6,7},{7,6},{8,9},{9,8},{10,11... | collective-permute-start | bytes 786440 | tf_op jit(solution)/shard_map/ppermute | solution.py:36
  150.6 14.0 %collective-permute-start.27 = (bf16[1024,256]{1,0:T(8,128)(2,1)S(1)}, bf16[1024,256]{1,0:T(8,128)(2,1)S(1)}, u32[]{:S(2)}, u32[]{:S(2)}) collective-permute-start(bf16[1024,256]{1,0:T(8,128)(2,1)S(1)} %shard_map.130), channel_id=1, source_target_pairs={{4,0},{8,12},{5,1},{9,13},{6,2},{10,14},{7,3},{11,15},{20,16},{24,... | collective-permute-start | bytes 1572872 | tf_op jit(solution)/shard_map/ppermute | solution.py:40
  162.0 17.1 %collective-permute-start.26 = (bf16[256,1024]{1,0:T(8,128)(2,1)S(1)}, bf16[256,1024]{1,0:T(8,128)(2,1)S(1)}, u32[]{:S(2)}, u32[]{:S(2)}) collective-permute-start(bf16[256,1024]{1,0:T(8,128)(2,1)S(1)} %get-tuple-element.127), channel_id=1, source_target_pairs={{0,2},{2,0},{1,3},{3,1},{4,6},{6,4},{5,7},{7,5},{8,10},{10,8},{9,1... | collective-permute-start | bytes 1572872 | tf_op jit(solution)/shard_map/ppermute | solution.py:36
  168.5 12.5 %collective-permute-start.29 = (bf16[1024,128]{1,0:T(8,128)(2,1)S(1)}, bf16[1024,128]{1,0:T(8,128)(2,1)S(1)}, u32[]{:S(2)}, u32[]{:S(2)}) collective-permute-start(bf16[1024,128]{1,0:T(8,128)(2,1)S(1)} %get-tuple-element.131), channel_id=1, source_target_pairs={{0,2},{2,0},{1,3},{3,1},{4,6},{6,4},{5,7},{7,5},{8,10},{10,8},{9,1... | collective-permute-start | bytes 786440 | tf_op jit(solution)/shard_map/ppermute | solution.py:36
  (40 other events, 289.0 us)

commit v18 on v15

--- a/solution.py
+++ b/solution.py
@@ -640,11 +640,6 @@
         scalars=flags,
     )
     y_got = swap(done(y_sent), "tp")
-    up_got = step(*up_got)
-    up_mine, up_theirs = kernel_call(
-        up_sum_kernel, [like(size, kvq)] * 2, up_parts[0], *up_got, scalars=numbers
-    )
-    up_theirs = swap(done(up_theirs), "own")
     y_got = step(y_got)
     y_here, y_sent = kernel_call(
         y_sum_kernel,
@@ -655,6 +650,11 @@
         scalars=flags,
     )
     y_got = swap(done(y_sent), "own")
+    up_got = step(*up_got)
+    up_mine, up_theirs = kernel_call(
+        up_sum_kernel, [like(size, kvq)] * 2, up_parts[0], *up_got, scalars=numbers
+    )
+    up_theirs = swap(done(up_theirs), "own")
 
     def in_place(axis, out, *pieces):
         def plan(n, a, o):

time: 201 us -> 197 us (0.980)
    ppermute x16, starting transfers between devices: 31.8 us -> 29.8 us  [along(): return lax.ppermute(value, 'fsdp', pairs)]
  transfers between devices with their start and end apart: 37 -> 37, of which waited for: 18 -> 20; matrix products, arithmetic and copies ran while one was open for 1% -> 1% of each run, Pallas kernels for 28% -> 29%
where the time goes in v18:
time: 197 us; the launch traced here: 196 us
  waiting for transfers between devices  66.9 us (34%)
  Pallas kernels  61.6 us (31%)
  starting transfers between devices  55.6 us (28%)
  local copies, waits for them, and re-layouts  10.6 us (5%)
    pallas_call x39, Pallas kernels, kernel_call(): pl.pallas_call(body, out_shape=list(outs), in_specs=specs, out_specs=[pl....  61.6 us
    ppermute x16, waiting for transfers between devices, along(): return lax.ppermute(value, 'fsdp', pairs)  38.6 us
    ppermute x16, starting transfers between devices, along(): return lax.ppermute(value, 'fsdp', pairs)  29.8 us
    ppermute x20, waiting for transfers between devices, swap(): return lax.ppermute(value, axis, PAIR)  28.3 us
    ppermute x20, starting transfers between devices, swap(): return lax.ppermute(value, axis, PAIR)  18.5 us
    unnamed x55, local copies, waits for them, and re-layouts  10.4 us
    all_to_all x1, starting transfers between devices, body_line(): lax.all_to_all(done(up_sent), ('fsdp', 'own'), split_axis=0, concat_axis=...  7.25 us
  transfers between devices with their start and end apart: 37, of which 20 were waited for; matrix products, arithmetic and copies ran while one was open for 1% of the time, Pallas kernels for 29%

profile of v18, /device:TPU:0, one launch (start us, length us, event | category | flops | bytes accessed | tf_op | source)
XLA Modules:
  0.0 196.0 jit_solution(15614362801775487885)
XLA Ops:
  2.5 7.3 %all-to-all-start = ((bf16[8,128,256]{2,1,0:T(8,128)(2,1)}), bf16[8,128,256]{2,1,0:T(8,128)(2,1)S(1)}, u32[]{:S(2)}, u32[]{:S(2)}) async-start(bf16[8,128,256]{2,1,0:T(8,128)(2,1)} %shard_map.102), calls=%async_computation | async-start | bytes 1048576 | tf_op jit(solution)/shard_map/all_to_all | solution.py:441
  11.7 2.1 %collective-permute-start.1 = (bf16[1024,128]{1,0:T(8,128)(2,1)S(1)}, bf16[1024,128]{1,0:T(8,128)(2,1)}, u32[]{:S(2)}, u32[]{:S(2)}) collective-permute-start(bf16[1024,128]{1,0:T(8,128)(2,1)S(1)} %shard_map.103), channel_id=1, source_target_pairs={{0,2},{2,0},{1,3},{3,1},{4,6},{6,4},{5,7},{7,5},{8,10},{10,8},{9,1... | collective-permute-start | bytes 786440 | tf_op jit(solution)/shard_map/ppermute | solution.py:36
  19.2 5.4 %collective-permute-done.1.refs_1_ = bf16[1024,128]{1,0:T(8,128)(2,1)} collective-permute-done((bf16[1024,128]{1,0:T(8,128)(2,1)S(1)}, bf16[1024,128]{1,0:T(8,128)(2,1)}, u32[]{:S(2)}, u32[]{:S(2)}) %collective-permute-start.1) | collective-permute-done | bytes 262176 | tf_op jit(solution)/shard_map/ppermute | solution.py:36
  28.2 3.4 %collective-permute-done.there = bf16[256,640]{1,0:T(8,128)(2,1)} collective-permute-done((bf16[256,640]{1,0:T(8,128)(2,1)S(1)}, bf16[256,640]{1,0:T(8,128)(2,1)}, u32[]{:S(2)}, u32[]{:S(2)}) %collective-permute-start) | collective-permute-done | bytes 327712 | tf_op jit(solution)/shard_map/ppermute | solution.py:36
  42.4 2.6 %shard_map.111 = bf16[1024,512]{1,0:T(8,128)(2,1)} custom-call(s32[4]{0:T(128)S(1)} %pad_add_fusion.numbers, bf16[1024,256]{1,0:T(8,128)(2,1)S(1)} %shard_map.106.refs_0_.rest_0_.own, bf16[1024,256]{1,0:T(8,128)(2,1)} %collective-permute-done.5.refs_1_.rest_1_.near), custom_call_target="tpu_custom_call" | custom-call | tf_op jit(solution)/shard_map/pallas_call | solution.py:48
  51.7 4.0 %collective-permute-start.10 = (bf16[512,256]{1,0:T(8,128)(2,1)S(1)}, bf16[512,256]{1,0:T(8,128)(2,1)S(1)}, u32[]{:S(2)}, u32[]{:S(2)}) collective-permute-start(bf16[512,256]{1,0:T(8,128)(2,1)S(1)} %get-tuple-element.92), channel_id=1, source_target_pairs={{0,4},{12,8},{1,5},{13,9},{2,6},{14,10},{3,7},{15,11},{16,20},{28,... | collective-permute-start | bytes 786440 | tf_op jit(solution)/shard_map/ppermute | solution.py:40
  63.0 4.5 %collective-permute-start.11 = (bf16[512,1024]{1,0:T(8,128)(2,1)S(1)}, bf16[512,1024]{1,0:T(8,128)(2,1)S(1)}, u32[]{:S(2)}, u32[]{:S(2)}) collective-permute-start(bf16[512,1024]{1,0:T(8,128)(2,1)S(1)} %shard_map.116.x_here.x_mine.tokens), channel_id=1, source_target_pairs={{0,4},{12,8},{1,5},{13,9},{2,6},{14,10},{3,7},{15,11},{16,20},{28,... | collective-permute-start | bytes 3145736 | tf_op jit(solution)/shard_map/ppermute | solution.py:40
  74.6 6.1 %collective-permute-done.7.refs_1_ = bf16[256,1024]{1,0:T(8,128)(2,1)S(1)} collective-permute-done((bf16[256,1024]{1,0:T(8,128)(2,1)S(1)}, bf16[256,1024]{1,0:T(8,128)(2,1)S(1)}, u32[]{:S(2)}, u32[]{:S(2)}) %collective-permute-start.7) | collective-permute-done | bytes 524320 | tf_op jit(solution)/shard_map/ppermute | solution.py:36
  81.3 3.7 %collective-permute-start.13 = (bf16[512,1024]{1,0:T(8,128)(2,1)S(1)}, bf16[512,1024]{1,0:T(8,128)(2,1)}, u32[]{:S(2)}, u32[]{:S(2)}) collective-permute-start(bf16[512,1024]{1,0:T(8,128)(2,1)S(1)} %shard_map.118.x_here.x_other.tokens), channel_id=1, source_target_pairs={{0,4},{12,8},{1,5},{13,9},{2,6},{14,10},{3,7},{15,11},{16,20},{28,... | collective-permute-start | bytes 3145736 | tf_op jit(solution)/shard_map/ppermute | solution.py:40
  85.0 6.0 %collective-permute-done.11.x_in = bf16[512,1024]{1,0:T(8,128)(2,1)S(1)} collective-permute-done((bf16[512,1024]{1,0:T(8,128)(2,1)S(1)}, bf16[512,1024]{1,0:T(8,128)(2,1)S(1)}, u32[]{:S(2)}, u32[]{:S(2)}) %collective-permute-start.11) | collective-permute-done | bytes 1048608 | tf_op jit(solution)/shard_map/ppermute | solution.py:40
  91.0 2.3 %shard_map.119 = bf16[1024,512]{1,0:T(8,128)(2,1)} custom-call(bf16[512,1024]{1,0:T(8,128)(2,1)S(1)} %shard_map.116.x_here.x_mine.tokens, bf16[512,1024]{1,0:T(8,128)(2,1)S(1)} %get-tuple-element.102.back, bf16[512,1024]{1,0:T(8,128)(2,1)S(1)} %collective-permute-done.11.x_in, bf16[512,1024]{1,0:T(8,128)(2,1)S(1)} %shard_map.115.back_in), custom_call_target="tpu_custom_call" | custom-call | tf_op jit(solution)/shard_map/pallas_call | solution.py:48
  101.7 8.5 %collective-permute-done.13.x_in = bf16[512,1024]{1,0:T(8,128)(2,1)} collective-permute-done((bf16[512,1024]{1,0:T(8,128)(2,1)S(1)}, bf16[512,1024]{1,0:T(8,128)(2,1)}, u32[]{:S(2)}, u32[]{:S(2)}) %collective-permute-start.13) | collective-permute-done | bytes 1048608 | tf_op jit(solution)/shard_map/ppermute | solution.py:40
  110.3 2.5 %shard_map.122 = bf16[1024,512]{1,0:T(8,128)(2,1)S(1)} custom-call(bf16[512,1024]{1,0:T(8,128)(2,1)S(1)} %shard_map.118.x_here.x_other.tokens, bf16[512,1024]{1,0:T(8,128)(2,1)S(1)} %get-tuple-element.102.back, bf16[512,1024]{1,0:T(8,128)(2,1)} %collective-permute-done.13.x_in, bf16[512,1024]{1,0:T(8,128)(2,1)S(1)} %copy-done.3), custom_call_target="tpu_custom_call" | custom-call | tf_op jit(solution)/shard_map/pallas_call | solution.py:48
  116.7 8.5 %collective-permute-done.20.outer = bf16[1024,512]{1,0:T(8,128)(2,1)} collective-permute-done((bf16[1024,512]{1,0:T(8,128)(2,1)}, bf16[1024,512]{1,0:T(8,128)(2,1)}, u32[]{:S(2)}, u32[]{:S(2)}) %collective-permute-start.20) | collective-permute-done | bytes 1048608 | tf_op jit(solution)/shard_map/ppermute | solution.py:40
  126.9 3.7 %shard_map.125 = (bf16[256,1024]{1,0:T(8,128)(2,1)S(1)}, bf16[256,1024]{1,0:T(8,128)(2,1)S(1)}) custom-call(bf16[512,1024]{1,0:T(8,128)(2,1)S(1)} %shard_map.120.dy, bf16[512,1024]{1,0:T(8,128)(2,1)S(1)} %get-tuple-element.102.back, bf16[1024,256]{1,0:T(8,128)(2,1)} %shard_map.109.refs_0_.own, bf16[1024,256]{1,0:T(8,128)(2,1)} %collective-permute-done.2.refs_1_.near, ...), custom_call_target="tpu_custom_call" | custom-call | tf_op jit(solution)/shard_map/pallas_call | solution.py:48
  132.6 3.7 %shard_map.126.left = f32[512,128]{1,0:T(8,128)S(1)} custom-call(s32[24]{0:T(128)S(1)} %concatenate.3.numbers, bf16[512,128]{1,0:T(8,128)(2,1)S(1)} %get-tuple-element.85.ids, bf16[512,1024]{1,0:T(8,128)(2,1)S(1)} %shard_map.116.x_here.x_mine.tokens, bf16[512,1024]{1,0:T(8,128)(2,1)S(1)} %shard_map.118.x_here.x_other.tokens, ...), custom_call_target="tpu_custom_call" | custom-call | tf_op jit(solution)/shard_map/pallas_call | solution.py:48
  136.4 3.0 %collective-permute-done.18.outer = bf16[1024,256]{1,0:T(8,128)(2,1)S(1)} collective-permute-done((bf16[1024,256]{1,0:T(8,128)(2,1)S(1)}, bf16[1024,256]{1,0:T(8,128)(2,1)S(1)}, u32[]{:S(2)}, u32[]{:S(2)}) %collective-permute-start.18) | collective-permute-done | bytes 524320 | tf_op jit(solution)/shard_map/ppermute | solution.py:40
  141.4 4.1 %shard_map.128 = (f32[2,512,256]{2,1,0:T(8,128)S(1)}, f32[2,512,256]{2,1,0:T(8,128)S(1)}) custom-call(s32[5]{0:T(128)S(1)} %convert_element_type.3.flags, bf16[512,1024]{1,0:T(8,128)(2,1)S(1)} %shard_map.116.x_here.x_mine.tokens, bf16[1024,256]{1,0:T(8,128)(2,1)} %shard_map.109.refs_0_.own, bf16[1024,256]{1,0:T(8,128)(2,1)} %collective-permute-done.2.refs_1_.near, ...), custom_call_target="tpu_custom_call" | custom-call | tf_op jit(solution)/shard_map/pallas_call | solution.py:48
  148.7 3.9 %collective-permute-done.23.got = f32[512,128]{1,0:T(8,128)S(1)} collective-permute-done((f32[512,128]{1,0:T(8,128)S(1)}, f32[512,128]{1,0:T(8,128)S(1)}, u32[]{:S(2)}, u32[]{:S(2)}) %collective-permute-start.23) | collective-permute-done | bytes 262176 | tf_op jit(solution)/shard_map/ppermute | solution.py:36
  155.6 3.6 %shard_map.132 = (bf16[256,1024]{1,0:T(8,128)(2,1)S(1)}, bf16[256,1024]{1,0:T(8,128)(2,1)S(1)}) custom-call(bf16[512,1024]{1,0:T(8,128)(2,1)S(1)} %shard_map.120.dy, bf16[512,1024]{1,0:T(8,128)(2,1)S(1)} %get-tuple-element.102.back, bf16[1024,256]{1,0:T(8,128)(2,1)S(1)} %copy-done.11, bf16[1024,256]{1,0:T(8,128)(2,1)S(1)} %copy-done.17, ...), custom_call_target="tpu_custom_call" | custom-call | tf_op jit(solution)/shard_map/pallas_call | solution.py:48
  159.2 2.3 %collective-permute-done.26.outer = bf16[1024,256]{1,0:T(8,128)(2,1)S(1)} collective-permute-done((bf16[1024,256]{1,0:T(8,128)(2,1)S(1)}, bf16[1024,256]{1,0:T(8,128)(2,1)S(1)}, u32[]{:S(2)}, u32[]{:S(2)}) %collective-permute-start.26) | collective-permute-done | bytes 524320 | tf_op jit(solution)/shard_map/ppermute | solution.py:40
  163.6 3.5 %shard_map.134 = (f32[2,512,256]{2,1,0:T(8,128)S(1)}, f32[2,512,256]{2,1,0:T(8,128)S(1)}) custom-call(s32[5]{0:T(128)S(1)} %convert_element_type.3.flags, bf16[512,1024]{1,0:T(8,128)(2,1)S(1)} %shard_map.118.x_here.x_other.tokens, bf16[1024,256]{1,0:T(8,128)(2,1)S(1)} %copy-done.11, bf16[1024,256]{1,0:T(8,128)(2,1)S(1)} %copy-done.17, ...), custom_call_target="tpu_custom_call" | custom-call | tf_op jit(solution)/shard_map/pallas_call | solution.py:48
  176.0 5.9 %collective-permute-done.32.third = bf16[256,256]{1,0:T(8,128)(2,1)S(1)} collective-permute-done((bf16[256,256]{1,0:T(8,128)(2,1)S(1)}, bf16[256,256]{1,0:T(8,128)(2,1)S(1)}, u32[]{:S(2)}, u32[]{:S(2)}) %collective-permute-start.32) | collective-permute-done | bytes 131104 | tf_op jit(solution)/shard_map/ppermute | solution.py:40
  188.3 4.9 %collective-permute-done.34.refs_3_ = bf16[1024,128]{1,0:T(8,128)(2,1)S(1)} collective-permute-done((bf16[1024,128]{1,0:T(8,128)(2,1)S(1)}, bf16[1024,128]{1,0:T(8,128)(2,1)S(1)}, u32[]{:S(2)}, u32[]{:S(2)}) %collective-permute-start.34) | collective-permute-done | bytes 262176 | tf_op jit(solution)/shard_map/ppermute | solution.py:36
  (150 shorter events, 89.4 us)
Async XLA Ops:
  2.5 29.1 %all-to-all-start = ((bf16[8,128,256]{2,1,0:T(8,128)(2,1)}), bf16[8,128,256]{2,1,0:T(8,128)(2,1)S(1)}, u32[]{:S(2)}, u32[]{:S(2)}) async-start(bf16[8,128,256]{2,1,0:T(8,128)(2,1)} %shard_map.102), calls=%async_computation | async-start | bytes 1048576 | tf_op jit(solution)/shard_map/all_to_all | solution.py:441
  11.7 12.9 %collective-permute-start.1 = (bf16[1024,128]{1,0:T(8,128)(2,1)S(1)}, bf16[1024,128]{1,0:T(8,128)(2,1)}, u32[]{:S(2)}, u32[]{:S(2)}) collective-permute-start(bf16[1024,128]{1,0:T(8,128)(2,1)S(1)} %shard_map.103), channel_id=1, source_target_pairs={{0,2},{2,0},{1,3},{3,1},{4,6},{6,4},{5,7},{7,5},{8,10},{10,8},{9,1... | collective-permute-start | bytes 786440 | tf_op jit(solution)/shard_map/ppermute | solution.py:36
  15.6 16.0 %collective-permute-start = (bf16[256,640]{1,0:T(8,128)(2,1)S(1)}, bf16[256,640]{1,0:T(8,128)(2,1)}, u32[]{:S(2)}, u32[]{:S(2)}) collective-permute-start(bf16[256,640]{1,0:T(8,128)(2,1)S(1)} %shard_map.104.here), channel_id=1, source_target_pairs={{0,2},{2,0},{1,3},{3,1},{4,6},{6,4},{5,7},{7,5},{8,10},{10,8},{9,1... | collective-permute-start | bytes 983048 | tf_op jit(solution)/shard_map/ppermute | solution.py:36
  17.1 25.3 %collective-permute-start.6 = (bf16[256,1024]{1,0:T(8,128)(2,1)}, bf16[256,1024]{1,0:T(8,128)(2,1)}, u32[]{:S(2)}, u32[]{:S(2)}) collective-permute-start(bf16[256,1024]{1,0:T(8,128)(2,1)} %shard_map.105), channel_id=1, source_target_pairs={{0,2},{2,0},{1,3},{3,1},{4,6},{6,4},{5,7},{7,5},{8,10},{10,8},{9,1... | collective-permute-start | bytes 1572872 | tf_op jit(solution)/shard_map/ppermute | solution.py:36
  26.2 16.3 %collective-permute-start.5 = (bf16[1024,256]{1,0:T(8,128)(2,1)S(1)}, bf16[1024,256]{1,0:T(8,128)(2,1)}, u32[]{:S(2)}, u32[]{:S(2)}) collective-permute-start(bf16[1024,256]{1,0:T(8,128)(2,1)S(1)} %shard_map.106.refs_0_.rest_0_.own), channel_id=1, source_target_pairs={{0,4},{4,0},{8,12},{12,8},{1,5},{5,1},{9,13},{13,9},{2,6},{6,2},{1... | collective-permute-start | bytes 1572872 | tf_op jit(solution)/shard_map/ppermute | solution.py:40
  38.3 17.4 %collective-permute-start.2 = (bf16[1024,256]{1,0:T(8,128)(2,1)}, bf16[1024,256]{1,0:T(8,128)(2,1)}, u32[]{:S(2)}, u32[]{:S(2)}) collective-permute-start(bf16[1024,256]{1,0:T(8,128)(2,1)} %shard_map.109.refs_0_.own), channel_id=1, source_target_pairs={{0,4},{4,0},{8,12},{12,8},{1,5},{5,1},{9,13},{13,9},{2,6},{6,2},{1... | collective-permute-start | bytes 1572872 | tf_op jit(solution)/shard_map/ppermute | solution.py:40
  45.1 26.7 %collective-permute-start.9 = (bf16[1024,512]{1,0:T(8,128)(2,1)}, bf16[1024,512]{1,0:T(8,128)(2,1)}, u32[]{:S(2)}, u32[]{:S(2)}) collective-permute-start(bf16[1024,512]{1,0:T(8,128)(2,1)} %shard_map.111), channel_id=1, source_target_pairs={{4,8},{8,4},{5,9},{9,5},{6,10},{10,6},{7,11},{11,7},{20,24},{24,20... | collective-permute-start | bytes 3145736 | tf_op jit(solution)/shard_map/ppermute | solution.py:40
  46.7 25.1 %collective-permute-start.8 = (bf16[1024,512]{1,0:T(8,128)(2,1)}, bf16[1024,512]{1,0:T(8,128)(2,1)}, u32[]{:S(2)}, u32[]{:S(2)}) collective-permute-start(bf16[1024,512]{1,0:T(8,128)(2,1)} %shard_map.111), channel_id=1, source_target_pairs={{0,16},{16,0},{1,17},{17,1},{2,18},{18,2},{3,19},{19,3},{4,20},{20... | collective-permute-start | bytes 3145736 | tf_op jit(solution)/shard_map/ppermute | solution.py:36
  63.0 28.0 %collective-permute-start.11 = (bf16[512,1024]{1,0:T(8,128)(2,1)S(1)}, bf16[512,1024]{1,0:T(8,128)(2,1)S(1)}, u32[]{:S(2)}, u32[]{:S(2)}) collective-permute-start(bf16[512,1024]{1,0:T(8,128)(2,1)S(1)} %shard_map.116.x_here.x_mine.tokens), channel_id=1, source_target_pairs={{0,4},{12,8},{1,5},{13,9},{2,6},{14,10},{3,7},{15,11},{16,20},{28,... | collective-permute-start | bytes 3145736 | tf_op jit(solution)/shard_map/ppermute | solution.py:40
  67.5 25.8 %collective-permute-start.16 = (bf16[1024,512]{1,0:T(8,128)(2,1)S(1)}, bf16[1024,512]{1,0:T(8,128)(2,1)}, u32[]{:S(2)}, u32[]{:S(2)}) collective-permute-start(bf16[1024,512]{1,0:T(8,128)(2,1)S(1)} %shard_map.113), channel_id=1, source_target_pairs={{4,8},{8,4},{5,9},{9,5},{6,10},{10,6},{7,11},{11,7},{20,24},{24,20... | collective-permute-start | bytes 3145736 | tf_op jit(solution)/shard_map/ppermute | solution.py:40
  71.8 21.5 %collective-permute-start.15 = (bf16[1024,256]{1,0:T(8,128)(2,1)}, bf16[1024,256]{1,0:T(8,128)(2,1)S(1)}, u32[]{:S(2)}, u32[]{:S(2)}) collective-permute-start(bf16[1024,256]{1,0:T(8,128)(2,1)} %collective-permute-done.2.refs_1_.near), channel_id=1, source_target_pairs={{0,16},{16,0},{1,17},{17,1},{2,18},{18,2},{3,19},{19,3},{4,20},{20... | collective-permute-start | bytes 1572872 | tf_op jit(solution)/shard_map/ppermute | solution.py:36
  73.3 25.8 %collective-permute-start.14 = (bf16[1024,512]{1,0:T(8,128)(2,1)}, bf16[1024,512]{1,0:T(8,128)(2,1)}, u32[]{:S(2)}, u32[]{:S(2)}) collective-permute-start(bf16[1024,512]{1,0:T(8,128)(2,1)} %collective-permute-done.9.crossed), channel_id=1, source_target_pairs={{4,0},{8,12},{5,1},{9,13},{6,2},{10,14},{7,3},{11,15},{20,16},{24,... | collective-permute-start | bytes 3145736 | tf_op jit(solution)/shard_map/ppermute | solution.py:40
  81.3 28.9 %collective-permute-start.13 = (bf16[512,1024]{1,0:T(8,128)(2,1)S(1)}, bf16[512,1024]{1,0:T(8,128)(2,1)}, u32[]{:S(2)}, u32[]{:S(2)}) collective-permute-start(bf16[512,1024]{1,0:T(8,128)(2,1)S(1)} %shard_map.118.x_here.x_other.tokens), channel_id=1, source_target_pairs={{0,4},{12,8},{1,5},{13,9},{2,6},{14,10},{3,7},{15,11},{16,20},{28,... | collective-permute-start | bytes 3145736 | tf_op jit(solution)/shard_map/ppermute | solution.py:40
  94.2 19.3 %collective-permute-start.12 = (bf16[1024,512]{1,0:T(8,128)(2,1)}, bf16[1024,512]{1,0:T(8,128)(2,1)}, u32[]{:S(2)}, u32[]{:S(2)}) collective-permute-start(bf16[1024,512]{1,0:T(8,128)(2,1)} %shard_map.119), channel_id=1, source_target_pairs={{4,8},{8,4},{5,9},{9,5},{6,10},{10,6},{7,11},{11,7},{20,24},{24,20... | collective-permute-start | bytes 3145736 | tf_op jit(solution)/shard_map/ppermute | solution.py:40
  95.8 29.3 %collective-permute-start.20 = (bf16[1024,512]{1,0:T(8,128)(2,1)}, bf16[1024,512]{1,0:T(8,128)(2,1)}, u32[]{:S(2)}, u32[]{:S(2)}) collective-permute-start(bf16[1024,512]{1,0:T(8,128)(2,1)} %collective-permute-done.16.crossed), channel_id=1, source_target_pairs={{4,0},{8,12},{5,1},{9,13},{6,2},{10,14},{7,3},{11,15},{20,16},{24,... | collective-permute-start | bytes 3145736 | tf_op jit(solution)/shard_map/ppermute | solution.py:40
  100.7 31.8 %collective-permute-start.19 = (bf16[1024,512]{1,0:T(8,128)(2,1)S(1)}, bf16[1024,512]{1,0:T(8,128)(2,1)S(1)}, u32[]{:S(2)}, u32[]{:S(2)}) collective-permute-start(bf16[1024,512]{1,0:T(8,128)(2,1)S(1)} %shard_map.121.rest_2_.far), channel_id=1, source_target_pairs={{0,16},{16,0},{1,17},{17,1},{2,18},{18,2},{3,19},{19,3},{4,20},{20... | collective-permute-start | bytes 3145736 | tf_op jit(solution)/shard_map/ppermute | solution.py:36
  112.8 34.1 %collective-permute-start.24 = (bf16[1024,512]{1,0:T(8,128)(2,1)S(1)}, bf16[1024,512]{1,0:T(8,128)(2,1)S(1)}, u32[]{:S(2)}, u32[]{:S(2)}) collective-permute-start(bf16[1024,512]{1,0:T(8,128)(2,1)S(1)} %shard_map.122), channel_id=1, source_target_pairs={{4,8},{8,4},{5,9},{9,5},{6,10},{10,6},{7,11},{11,7},{20,24},{24,20... | collective-permute-start | bytes 3145736 | tf_op jit(solution)/shard_map/ppermute | solution.py:40
  115.2 24.1 %collective-permute-start.18 = (bf16[1024,256]{1,0:T(8,128)(2,1)S(1)}, bf16[1024,256]{1,0:T(8,128)(2,1)S(1)}, u32[]{:S(2)}, u32[]{:S(2)}) collective-permute-start(bf16[1024,256]{1,0:T(8,128)(2,1)S(1)} %shard_map.123), channel_id=1, source_target_pairs={{4,0},{8,12},{5,1},{9,13},{6,2},{10,14},{7,3},{11,15},{20,16},{24,... | collective-permute-start | bytes 1572872 | tf_op jit(solution)/shard_map/ppermute | solution.py:40
  130.7 14.8 %collective-permute-start.22 = (bf16[256,1024]{1,0:T(8,128)(2,1)S(1)}, bf16[256,1024]{1,0:T(8,128)(2,1)S(1)}, u32[]{:S(2)}, u32[]{:S(2)}) collective-permute-start(bf16[256,1024]{1,0:T(8,128)(2,1)S(1)} %get-tuple-element.114), channel_id=1, source_target_pairs={{0,2},{2,0},{1,3},{3,1},{4,6},{6,4},{5,7},{7,5},{8,10},{10,8},{9,1... | collective-permute-start | bytes 1572872 | tf_op jit(solution)/shard_map/ppermute | solution.py:36
  131.0 24.6 %collective-permute-start.27 = (bf16[1024,512]{1,0:T(8,128)(2,1)S(1)}, bf16[1024,512]{1,0:T(8,128)(2,1)S(1)}, u32[]{:S(2)}, u32[]{:S(2)}) collective-permute-start(bf16[1024,512]{1,0:T(8,128)(2,1)S(1)} %shard_map.124.far), channel_id=1, source_target_pairs={{0,16},{16,0},{1,17},{17,1},{2,18},{18,2},{3,19},{19,3},{4,20},{20... | collective-permute-start | bytes 3145736 | tf_op jit(solution)/shard_map/ppermute | solution.py:36
  147.4 14.2 %collective-permute-start.26 = (bf16[1024,256]{1,0:T(8,128)(2,1)S(1)}, bf16[1024,256]{1,0:T(8,128)(2,1)S(1)}, u32[]{:S(2)}, u32[]{:S(2)}) collective-permute-start(bf16[1024,256]{1,0:T(8,128)(2,1)S(1)} %shard_map.130), channel_id=1, source_target_pairs={{4,0},{8,12},{5,1},{9,13},{6,2},{10,14},{7,3},{11,15},{20,16},{24,... | collective-permute-start | bytes 1572872 | tf_op jit(solution)/shard_map/ppermute | solution.py:40
  167.2 17.2 %collective-permute-start.30 = (bf16[256,1024]{1,0:T(8,128)(2,1)S(1)}, bf16[256,1024]{1,0:T(8,128)(2,1)S(1)}, u32[]{:S(2)}, u32[]{:S(2)}) collective-permute-start(bf16[256,1024]{1,0:T(8,128)(2,1)S(1)} %get-tuple-element.128), channel_id=1, source_target_pairs={{0,2},{2,0},{1,3},{3,1},{4,6},{6,4},{5,7},{7,5},{8,10},{10,8},{9,1... | collective-permute-start | bytes 1572872 | tf_op jit(solution)/shard_map/ppermute | solution.py:36
  170.5 17.0 %collective-permute-start.29 = (bf16[2,256,256]{2,1,0:T(8,128)(2,1)S(1)}, bf16[2,256,256]{2,1,0:T(8,128)(2,1)S(1)}, u32[]{:S(2)}, u32[]{:S(2)}) collective-permute-start(bf16[2,256,256]{2,1,0:T(8,128)(2,1)S(1)} %get-tuple-element.137), channel_id=1, source_target_pairs={{0,2},{2,0},{1,3},{3,1},{4,6},{6,4},{5,7},{7,5},{8,10},{10,8},{9,1... | collective-permute-start | bytes 786440 | tf_op jit(solution)/shard_map/ppermute | solution.py:36
  171.4 21.8 %collective-permute-start.34 = (bf16[1024,128]{1,0:T(8,128)(2,1)S(1)}, bf16[1024,128]{1,0:T(8,128)(2,1)S(1)}, u32[]{:S(2)}, u32[]{:S(2)}) collective-permute-start(bf16[1024,128]{1,0:T(8,128)(2,1)S(1)} %get-tuple-element.152), channel_id=1, source_target_pairs={{0,2},{2,0},{1,3},{3,1},{4,6},{6,4},{5,7},{7,5},{8,10},{10,8},{9,1... | collective-permute-start | bytes 786440 | tf_op jit(solution)/shard_map/ppermute | solution.py:36
  (40 other events, 293.4 us)
